TPU v7x, 32 devices: a whole 2x2x4 slice. The times are simulated.
32 devices in a mesh: dp: 8 (over z, y), expert: 4 (over x, core).
Axes of the slice: x: 2, y: 2, z: 4, core: 2. Of those that a mesh axis runs over, the one named last changes fastest.
Arguments:
- patches: bfloat16 [32768, 768], P(('dp', 'expert')), may hold values from -6 to 6
- lengths: int32 [128, 3], P(('dp', 'expert')), may hold values from 1 to 196, 256 in all within a row
- slot_mask: int32 [128, 256], P(('dp', 'expert')), may hold values from 0 to 1
- expert_picks: int32 [32768, 2], P(('dp', 'expert')), may hold values from 0 to 7, all different within a row
- priority_rank: int32 [32, 1024], P(('dp', 'expert')), may hold values from 0 to 1023, each once within a row
- class_labels: int32 [18432, 384], P(('dp', 'expert')), may hold values 0 or 1
- dense_weights: float32 [5, 768, 768], P(None, ('dp', 'expert')), may hold values from -0.21875 to 0.21875
- dense_first: float32 [5, 768, 768], P(None, ('dp', 'expert')), may hold values from -9.1552734e-05 to 9.1552734e-05
- dense_second: float32 [5, 768, 768], P(None, ('dp', 'expert')), may hold values from 2.8257017e-12 to 1.1302807e-09
- dense_average: float32 [5, 768, 768], P(None, ('dp', 'expert')), may hold values from -0.21875 to 0.21875
- router_weights: float32 [768, 8], P(('dp', 'expert')), may hold values from -0.15625 to 0.15625
- router_first: float32 [768, 8], P(('dp', 'expert')), may hold values from -9.1552734e-05 to 9.1552734e-05
- router_second: float32 [768, 8], P(('dp', 'expert')), may hold values from 2.8257017e-12 to 1.1302807e-11
- router_average: float32 [768, 8], P(('dp', 'expert')), may hold values from -0.15625 to 0.15625
- norm_params: float32 [6, 768], P(None, ('dp', 'expert')), may hold values from -2 to 2
- norm_first: float32 [6, 768], P(None, ('dp', 'expert')), may hold values from -0.0012207031 to 0.0012207031
- norm_second: float32 [6, 768], P(None, ('dp', 'expert')), may hold values from 6.3578287e-10 to 2.5431315e-09
- norm_average: float32 [6, 768], P(None, ('dp', 'expert')), may hold values from 0.5 to 1.5
- expert_in: float32 [8, 3072, 768], P('expert', 'dp'), may hold values from -0.21875 to 0.21875
- in_first: float32 [8, 3072, 768], P('expert', 'dp'), may hold values from -9.1552734e-05 to 9.1552734e-05
- in_second: float32 [8, 3072, 768], P('expert', 'dp'), may hold values from 2.8257017e-12 to 1.1302807e-11
- in_average: float32 [8, 3072, 768], P('expert', 'dp'), may hold values from -0.21875 to 0.21875
- expert_out: float32 [8, 3072, 768], P('expert', 'dp'), may hold values from -0.875 to 0.875
- out_first: float32 [8, 3072, 768], P('expert', 'dp'), may hold values from -2.2888184e-05 to 2.2888184e-05
- out_second: float32 [8, 3072, 768], P('expert', 'dp'), may hold values from 1.7660636e-13 to 7.064254e-13
- out_average: float32 [8, 3072, 768], P('expert', 'dp'), may hold values from -0.875 to 0.875
- head_weights: float32 [18432, 768], P(('dp', 'expert')), may hold values from -1 to 1
- head_first: float32 [18432, 768], P(('dp', 'expert')), may hold values from -0.0004272461 to 0.0004272461
- head_second: float32 [18432, 768], P(('dp', 'expert')), may hold values from 1.4128508e-11 to 5.6514033e-11
- head_average: float32 [18432, 768], P(('dp', 'expert')), may hold values from -0.4375 to 0.4375
Outputs:
- loss_value: float32 [], replicated
- importance: float32 [8], replicated
- grad_norm: float32 [], replicated
- dense_new: float32 [5, 768, 768], P(None, ('dp', 'expert'))
- dense_first_new: float32 [5, 768, 768], P(None, ('dp', 'expert'))
- dense_second_new: float32 [5, 768, 768], P(None, ('dp', 'expert'))
- dense_average_new: float32 [5, 768, 768], P(None, ('dp', 'expert'))
- router_new: float32 [768, 8], P(('dp', 'expert'))
- router_first_new: float32 [768, 8], P(('dp', 'expert'))
- router_second_new: float32 [768, 8], P(('dp', 'expert'))
- router_average_new: float32 [768, 8], P(('dp', 'expert'))
- norm_new: float32 [6, 768], P(None, ('dp', 'expert'))
- norm_first_new: float32 [6, 768], P(None, ('dp', 'expert'))
- norm_second_new: float32 [6, 768], P(None, ('dp', 'expert'))
- norm_average_new: float32 [6, 768], P(None, ('dp', 'expert'))
- in_new: float32 [8, 3072, 768], P('expert', 'dp')
- in_first_new: float32 [8, 3072, 768], P('expert', 'dp')
- in_second_new: float32 [8, 3072, 768], P('expert', 'dp')
- in_average_new: float32 [8, 3072, 768], P('expert', 'dp')
- out_new: float32 [8, 3072, 768], P('expert', 'dp')
- out_first_new: float32 [8, 3072, 768], P('expert', 'dp')
- out_second_new: float32 [8, 3072, 768], P('expert', 'dp')
- out_average_new: float32 [8, 3072, 768], P('expert', 'dp')
- head_new: float32 [18432, 768], P(('dp', 'expert'))
- head_first_new: float32 [18432, 768], P(('dp', 'expert'))
- head_second_new: float32 [18432, 768], P(('dp', 'expert'))
- head_average_new: float32 [18432, 768], P(('dp', 'expert'))
All inputs are finite; a program needn't handle non-finite values. No bound on the sum of `class_labels` on one device may be relied on, other than what follows from the above.
Results may differ from a plain program's by a relative error of at most 0.018.
The roundings to bfloat16 on the way count: a program that leaves them out, or rounds other values in their place, can miss the bound.
Values may be sent and summed in bfloat16 or wider, within the bound.
A program may use at most 320 MiB of HBM per device.

v0:
```python
import jax
import jax.numpy as jnp
from jax import lax
from jax.sharding import PartitionSpec as P

HEADS = 12
TOP = 2
STEP_COUNT = 10


high_prec = lax.Precision.HIGHEST
eps_norm = 1e-06
aux_weight = 0.01
clip_limit = 1.0
base_rate = 0.05
norm_rate = 0.5
beta_first = 0.9
beta_second = 0.999
weight_decay = 0.1
polyak_decay = 0.7
adam_eps = 1e-08
mask_fill = -1e30


def layer_norm(values, gain, shift):
    centre = values - jnp.mean(values, -1, keepdims=True)
    spread = jnp.mean(centre * centre, -1, keepdims=True)
    return centre * lax.rsqrt(spread + eps_norm) * gain + shift


def softmax_rows(logits):
    top_val = jnp.max(logits, -1, keepdims=True)
    powers = jnp.exp(logits - top_val)
    return powers / jnp.sum(powers, -1, keepdims=True)


def route(pick_ids, valid_flat, rank_ids, n_experts, capacity):
    columns = jnp.arange(n_experts, dtype=jnp.int32)
    first_hot = (pick_ids[:, 0:1] == columns[None, :]).astype(jnp.float32) * valid_flat[:, None]
    second_hot = (pick_ids[:, 1:2] == columns[None, :]).astype(jnp.float32) * valid_flat[:, None]
    before = (rank_ids[None, :] < rank_ids[:, None]).astype(jnp.float32)
    first_pos = jnp.sum(first_hot * jnp.dot(before, first_hot, precision=high_prec), 1)
    second_pos = jnp.sum(
        second_hot
        * (jnp.dot(before, second_hot, precision=high_prec) + jnp.sum(first_hot, 0)[None, :]),
        1,
    )
    first_kept = valid_flat * (first_pos < capacity).astype(jnp.float32)
    second_kept = valid_flat * (second_pos < capacity).astype(jnp.float32)
    return (first_pos.astype(jnp.int32), second_pos.astype(jnp.int32), first_kept, second_kept)


def adam_update(weight, first_state, second_state, average_state, gradient, factor, step_rate):
    clipped = gradient * factor
    first_new = beta_first * first_state + (1.0 - beta_first) * clipped
    second_new = beta_second * second_state + (1.0 - beta_second) * clipped * clipped
    first_hat = first_new / (1.0 - beta_first**STEP_COUNT)
    second_hat = second_new / (1.0 - beta_second**STEP_COUNT)
    weight_new = weight - step_rate * (
        first_hat / (jnp.sqrt(second_hat) + adam_eps) + weight_decay * weight
    )
    average_new = polyak_decay * average_state + (1.0 - polyak_decay) * weight_new
    return (weight_new, first_new, second_new, average_new)


def to_experts(buffer):
    return lax.all_to_all(buffer, "expert", split_axis=1, concat_axis=1, tiled=True)


def from_experts(buffer):
    return lax.all_to_all(buffer, "expert", split_axis=1, concat_axis=1, tiled=True)


def split_heads(proj_qkv, allow_mask, n_heads):
    n_rows, n_slots_row = (allow_mask.shape[0], allow_mask.shape[1])
    head_dim = proj_qkv.shape[-1] // n_heads
    shaped = proj_qkv.reshape(3, n_rows, n_slots_row, n_heads, head_dim)
    scores = jnp.einsum(
        "rqhd,rkhd->rhqk", shaped[0], shaped[1], preferred_element_type=jnp.float32
    ) * head_dim ** (-0.5)
    return (shaped, jnp.where(allow_mask[:, None], scores, mask_fill), head_dim ** (-0.5))


def attention_forward(proj_qkv, allow_mask, n_heads):
    shaped, masked, unused_scale = split_heads(proj_qkv, allow_mask, n_heads)
    top_val = jnp.max(masked, -1, keepdims=True)
    powers = jnp.exp(masked - top_val)
    totals = jnp.sum(powers, -1, keepdims=True)
    att_probs = powers / totals
    output = jnp.einsum(
        "rhqk,rkhd->rqhd",
        att_probs.astype(jnp.bfloat16),
        shaped[2],
        preferred_element_type=jnp.float32,
    )
    return (
        output.astype(jnp.bfloat16).reshape(proj_qkv.shape[1], proj_qkv.shape[2]),
        top_val + jnp.log(totals),
    )


def attention_backward(proj_qkv, allow_mask, log_total, d_output, n_heads):
    shaped, masked, score_scale = split_heads(proj_qkv, allow_mask, n_heads)
    att_probs = jnp.exp(masked - log_total)
    grad_out = d_output.reshape(shaped.shape[1:])
    d_probs = jnp.einsum("rqhd,rkhd->rhqk", grad_out, shaped[2], preferred_element_type=jnp.float32)
    d_values = jnp.einsum(
        "rhqk,rqhd->rkhd",
        att_probs.astype(jnp.bfloat16),
        grad_out,
        preferred_element_type=jnp.float32,
    )
    d_scores = (att_probs * (d_probs - jnp.sum(att_probs * d_probs, -1, keepdims=True))).astype(
        jnp.bfloat16
    )
    d_query = (
        jnp.einsum("rhqk,rkhd->rqhd", d_scores, shaped[1], preferred_element_type=jnp.float32)
        * score_scale
    )
    d_keys = (
        jnp.einsum("rhqk,rqhd->rkhd", d_scores, shaped[0], preferred_element_type=jnp.float32)
        * score_scale
    )
    stacked = jnp.stack([d_query, d_keys, d_values]).astype(jnp.bfloat16)
    return stacked.reshape(proj_qkv.shape)


def body(
    patches,
    lengths,
    slot_mask,
    expert_picks,
    priority_rank,
    class_labels,
    dense_weights,
    dense_first,
    dense_second,
    dense_average,
    router_weights,
    router_first,
    router_second,
    router_average,
    norm_params,
    norm_first,
    norm_second,
    norm_average,
    expert_in,
    in_first,
    in_second,
    in_average,
    expert_out,
    out_first,
    out_second,
    out_average,
    head_weights,
    head_first,
    head_second,
    head_average,
):
    layer_b, router_b, norm_b = (
        lax.all_gather(dense_weights.astype(jnp.bfloat16), ("dp", "expert"), axis=1, tiled=True),
        lax.all_gather(router_weights.astype(jnp.bfloat16), ("dp", "expert"), axis=0, tiled=True),
        lax.all_gather(norm_params.astype(jnp.bfloat16), ("dp", "expert"), axis=1, tiled=True),
    )
    gain_rows = norm_b.astype(jnp.float32)
    rows_here, n_slots_row = slot_mask.shape
    tokens = rows_here * n_slots_row
    model_width = layer_b.shape[2]
    n_expert = lax.axis_size("expert")
    per_dev = expert_in.shape[0]
    n_experts = per_dev * n_expert
    capacity = (21 * tokens * TOP + 20 * n_experts - 1) // (20 * n_experts)
    n_slots = n_experts * capacity
    valid = slot_mask.astype(jnp.float32)
    positions = jnp.arange(n_slots_row, dtype=jnp.int32)
    bounds = jnp.cumsum(lengths, 1)
    segment = jnp.sum((positions[None, :, None] >= bounds[:, None, :]).astype(jnp.int32), -1)
    diagonal = positions[:, None] == positions[None, :]
    allowed = (segment[:, :, None] == segment[:, None, :]) & (
        (valid[:, None, :] > 0) | diagonal[None]
    )
    member = (
        segment[:, None, :] == jnp.arange(lengths.shape[1], dtype=jnp.int32)[None, :, None]
    ).astype(jnp.float32) * valid[:, None, :]
    pooling = member / jnp.maximum(jnp.sum(member, -1, keepdims=True), 1.0)
    valid_flat = valid.reshape(tokens)
    x_zero = jnp.dot(patches, layer_b[0], preferred_element_type=jnp.float32)
    a_one = layer_norm(x_zero, gain_rows[0], gain_rows[3]).astype(jnp.bfloat16)
    proj_qkv = jnp.einsum(
        "td,kde->kte", a_one, layer_b[1:4], preferred_element_type=jnp.float32
    ).astype(jnp.bfloat16)
    att_out, log_total = attention_forward(proj_qkv, allowed, HEADS)
    x_one = x_zero + jnp.dot(att_out, layer_b[4], preferred_element_type=jnp.float32)
    a_two = layer_norm(x_one, gain_rows[1], gain_rows[4]).astype(jnp.bfloat16)
    router_probs = softmax_rows(jnp.dot(a_two, router_b, preferred_element_type=jnp.float32))
    importance = lax.psum(jnp.sum(router_probs * valid_flat[:, None], 0), ("dp", "expert"))
    pos_one, pos_two, kept_one, kept_two = route(
        expert_picks, valid_flat, priority_rank[0], n_experts, capacity
    )
    pick_one = expert_picks[:, 0]
    pick_two = expert_picks[:, 1]
    slot_one = jnp.where(
        kept_one > 0, (pick_one % per_dev * n_expert + pick_one // per_dev) * capacity + pos_one, 0
    )
    slot_two = jnp.where(
        kept_two > 0, (pick_two % per_dev * n_expert + pick_two // per_dev) * capacity + pos_two, 0
    )
    columns = jnp.arange(n_experts, dtype=jnp.int32)
    hot_one = (pick_one[:, None] == columns[None]).astype(jnp.float32)
    hot_two = (pick_two[:, None] == columns[None]).astype(jnp.float32)
    gate_one = jnp.sum(router_probs * hot_one, 1) * kept_one
    gate_two = jnp.sum(router_probs * hot_two, 1) * kept_two
    slot_ids = jnp.arange(n_slots, dtype=jnp.int32)
    match_one = ((slot_one[None, :] == slot_ids[:, None]) & (kept_one[None, :] > 0)).astype(
        jnp.float32
    )
    match_two = ((slot_two[None, :] == slot_ids[:, None]) & (kept_two[None, :] > 0)).astype(
        jnp.float32
    )
    token_ids = jnp.arange(tokens).astype(jnp.float32)
    slot_owner = (
        jnp.dot(match_one, token_ids, precision=high_prec)
        + jnp.dot(match_two, token_ids, precision=high_prec)
    ).astype(jnp.int32)
    slot_live = jnp.sum(match_one, 1) + jnp.sum(match_two, 1)
    slot_gate = jnp.dot(match_one, gate_one, precision=high_prec) + jnp.dot(
        match_two, gate_two, precision=high_prec
    )
    send_rows = (
        jnp.take(a_two, slot_owner, axis=0) * slot_live[:, None].astype(jnp.bfloat16)
    ).reshape(per_dev, n_slots // per_dev, model_width)
    arrived = to_experts(send_rows)
    in_b = expert_in.astype(jnp.bfloat16)
    out_b = expert_out.astype(jnp.bfloat16)
    w_one, w_two = (
        lax.all_gather(in_b, "dp", axis=1, tiled=True),
        lax.all_gather(out_b, "dp", axis=1, tiled=True),
    )
    hidden = jnp.einsum("esd,efd->esf", arrived, w_one, preferred_element_type=jnp.float32)
    activated = jax.nn.gelu(hidden).astype(jnp.bfloat16)
    result = jnp.einsum(
        "esf,efd->esd", activated, w_two, preferred_element_type=jnp.float32
    ).astype(jnp.bfloat16)
    back_rows = from_experts(result).reshape(n_slots, model_width)
    back_one = jnp.take(back_rows, slot_one, axis=0).astype(jnp.float32)
    back_two = jnp.take(back_rows, slot_two, axis=0).astype(jnp.float32)
    x_two = x_one + gate_one[:, None] * back_one + gate_two[:, None] * back_two
    pooled = jnp.einsum(
        "ris,rsd->rid",
        pooling,
        x_two.reshape(rows_here, n_slots_row, model_width),
        precision=high_prec,
    ).reshape(-1, model_width)
    gathered = lax.all_gather(
        layer_norm(pooled, gain_rows[2], gain_rows[5]).astype(jnp.bfloat16),
        ("dp", "expert"),
        axis=0,
        tiled=True,
    )
    head_b = head_weights.astype(jnp.bfloat16)
    logits = jnp.dot(head_b, gathered.T, preferred_element_type=jnp.float32)
    labels = class_labels.astype(jnp.float32)
    n_images = gathered.shape[0]
    local_loss = jnp.sum(jnp.logaddexp(logits, 0.0) - labels * logits) / n_images
    centre = jnp.mean(importance)
    spread = jnp.mean((importance - centre) ** 2)
    d_imp = aux_weight * (
        2.0 * (importance - centre) / (n_experts * centre * centre)
        - 2.0 * spread / (n_experts * centre * centre * centre)
    )
    d_logits = ((jax.nn.sigmoid(logits) - labels) / n_images).astype(jnp.bfloat16)
    g_head = jnp.dot(d_logits, gathered, preferred_element_type=jnp.float32)
    d_rows = lax.psum_scatter(
        jnp.dot(d_logits.T, head_b, preferred_element_type=jnp.float32),
        ("dp", "expert"),
        scatter_dimension=0,
        tiled=True,
    )
    unused_out, norm_back = jax.vjp(layer_norm, pooled, gain_rows[2], gain_rows[5])
    d_pooled, g_gain_three, g_shift_three = norm_back(d_rows)
    d_two = jnp.einsum(
        "ris,rid->rsd", pooling, d_pooled.reshape(rows_here, -1, model_width), precision=high_prec
    ).reshape(tokens, model_width)
    d_gate_one = kept_one * jnp.sum(d_two * back_one, 1)
    d_gate_two = kept_two * jnp.sum(d_two * back_two, 1)
    d_send = (
        (jnp.take(d_two, slot_owner, axis=0) * slot_gate[:, None])
        .astype(jnp.bfloat16)
        .reshape(per_dev, n_slots // per_dev, model_width)
    )
    d_all = to_experts(d_send)
    g_two = jnp.einsum("esf,esd->efd", activated, d_all, preferred_element_type=jnp.float32)
    d_act = jnp.einsum("esd,efd->esf", d_all, w_two, preferred_element_type=jnp.float32)
    d_hidden = jax.vjp(jax.nn.gelu, hidden)[1](d_act)[0].astype(jnp.bfloat16)
    d_inputs = jnp.einsum(
        "esf,efd->esd", d_hidden, w_one, preferred_element_type=jnp.float32
    ).astype(jnp.bfloat16)
    g_one = jnp.einsum("esf,esd->efd", d_hidden, arrived, preferred_element_type=jnp.float32)
    g_one, g_two = (
        lax.psum_scatter(g_one.astype(jnp.bfloat16), "dp", scatter_dimension=1, tiled=True).astype(
            jnp.float32
        ),
        lax.psum_scatter(g_two.astype(jnp.bfloat16), "dp", scatter_dimension=1, tiled=True).astype(
            jnp.float32
        ),
    )
    d_back = from_experts(d_inputs).reshape(n_slots, model_width)
    d_a_two = jnp.take(d_back, slot_one, axis=0).astype(jnp.float32) * kept_one[:, None]
    d_a_two = d_a_two + jnp.take(d_back, slot_two, axis=0).astype(jnp.float32) * kept_two[:, None]
    d_probs = (
        hot_one * d_gate_one[:, None]
        + hot_two * d_gate_two[:, None]
        + valid_flat[:, None] * d_imp[None, :]
    )
    d_router = (
        router_probs * (d_probs - jnp.sum(router_probs * d_probs, 1, keepdims=True))
    ).astype(jnp.bfloat16)
    g_router = jnp.dot(a_two.T, d_router, preferred_element_type=jnp.float32)
    d_a_two = d_a_two + jnp.dot(d_router, router_b.T, preferred_element_type=jnp.float32)
    unused_out, norm_back = jax.vjp(layer_norm, x_one, gain_rows[1], gain_rows[4])
    d_x_one, g_gain_two, g_shift_two = norm_back(d_a_two)
    d_x_one = d_x_one + d_two
    d_att_b = d_x_one.astype(jnp.bfloat16)
    g_out_proj = jnp.dot(att_out.T, d_att_b, preferred_element_type=jnp.float32)
    d_att_out = jnp.dot(d_att_b, layer_b[4].T, preferred_element_type=jnp.float32).astype(
        jnp.bfloat16
    )
    d_qkv = attention_backward(proj_qkv, allowed, log_total, d_att_out, HEADS)
    g_qkv = jnp.einsum("td,kte->kde", a_one, d_qkv, preferred_element_type=jnp.float32)
    d_a_one = jnp.einsum("kte,kde->td", d_qkv, layer_b[1:4], preferred_element_type=jnp.float32)
    unused_out, norm_back = jax.vjp(layer_norm, x_zero, gain_rows[0], gain_rows[3])
    d_x_zero, g_gain_one, g_shift_one = norm_back(d_a_one)
    d_x_zero = (d_x_zero + d_x_one).astype(jnp.bfloat16)
    g_embed = jnp.dot(patches.T, d_x_zero, preferred_element_type=jnp.float32)
    g_layers = jnp.concatenate([g_embed[None], g_qkv, g_out_proj[None]], 0)
    g_norms = jnp.stack(
        [g_gain_one, g_gain_two, g_gain_three, g_shift_one, g_shift_two, g_shift_three]
    )
    g_layers, g_router, g_norms = (
        lax.psum_scatter(g_layers, ("dp", "expert"), scatter_dimension=1, tiled=True),
        lax.psum_scatter(g_router, ("dp", "expert"), scatter_dimension=0, tiled=True),
        lax.psum_scatter(g_norms, ("dp", "expert"), scatter_dimension=1, tiled=True),
    )
    squares = (
        jnp.sum(g_layers * g_layers) + jnp.sum(g_router * g_router) + jnp.sum(g_norms * g_norms)
    )
    squares = squares + jnp.sum(g_one * g_one) + jnp.sum(g_two * g_two) + jnp.sum(g_head * g_head)
    loss_sum, square_sum = lax.psum((local_loss, squares), ("dp", "expert"))
    grad_norm = jnp.sqrt(square_sum)
    factor = jnp.minimum(1.0, clip_limit / grad_norm)
    loss_value = loss_sum + aux_weight * spread / (centre * centre)
    dense_out = adam_update(
        dense_weights, dense_first, dense_second, dense_average, g_layers, factor, base_rate
    )
    router_out = adam_update(
        router_weights, router_first, router_second, router_average, g_router, factor, base_rate
    )
    norm_out = adam_update(
        norm_params, norm_first, norm_second, norm_average, g_norms, factor, norm_rate
    )
    in_out = adam_update(expert_in, in_first, in_second, in_average, g_one, factor, base_rate)
    out_out = adam_update(expert_out, out_first, out_second, out_average, g_two, factor, base_rate)
    head_out = adam_update(
        head_weights, head_first, head_second, head_average, g_head, factor, base_rate
    )
    return (
        loss_value,
        importance,
        grad_norm,
        dense_out[0],
        dense_out[1],
        dense_out[2],
        dense_out[3],
        router_out[0],
        router_out[1],
        router_out[2],
        router_out[3],
        norm_out[0],
        norm_out[1],
        norm_out[2],
        norm_out[3],
        in_out[0],
        in_out[1],
        in_out[2],
        in_out[3],
        out_out[0],
        out_out[1],
        out_out[2],
        out_out[3],
        head_out[0],
        head_out[1],
        head_out[2],
        head_out[3],
    )


def solution(mesh):
    placed = (
        P(("dp", "expert"), None),
        P(("dp", "expert"), None),
        P(("dp", "expert"), None),
        P(("dp", "expert"), None),
        P(("dp", "expert"), None),
        P(("dp", "expert"), None),
        P(None, ("dp", "expert"), None),
        P(None, ("dp", "expert"), None),
        P(None, ("dp", "expert"), None),
        P(None, ("dp", "expert"), None),
        P(("dp", "expert"), None),
        P(("dp", "expert"), None),
        P(("dp", "expert"), None),
        P(("dp", "expert"), None),
        P(None, ("dp", "expert")),
        P(None, ("dp", "expert")),
        P(None, ("dp", "expert")),
        P(None, ("dp", "expert")),
        P("expert", "dp", None),
        P("expert", "dp", None),
        P("expert", "dp", None),
        P("expert", "dp", None),
        P("expert", "dp", None),
        P("expert", "dp", None),
        P("expert", "dp", None),
        P("expert", "dp", None),
        P(("dp", "expert"), None),
        P(("dp", "expert"), None),
        P(("dp", "expert"), None),
        P(("dp", "expert"), None),
    )
    return jax.shard_map(
        body,
        mesh=mesh,
        in_specs=placed,
        out_specs=(
            P(),
            P(),
            P(),
            P(None, ("dp", "expert"), None),
            P(None, ("dp", "expert"), None),
            P(None, ("dp", "expert"), None),
            P(None, ("dp", "expert"), None),
            P(("dp", "expert"), None),
            P(("dp", "expert"), None),
            P(("dp", "expert"), None),
            P(("dp", "expert"), None),
            P(None, ("dp", "expert")),
            P(None, ("dp", "expert")),
            P(None, ("dp", "expert")),
            P(None, ("dp", "expert")),
            P("expert", "dp", None),
            P("expert", "dp", None),
            P("expert", "dp", None),
            P("expert", "dp", None),
            P("expert", "dp", None),
            P("expert", "dp", None),
            P("expert", "dp", None),
            P("expert", "dp", None),
            P(("dp", "expert"), None),
            P(("dp", "expert"), None),
            P(("dp", "expert"), None),
            P(("dp", "expert"), None),
        ),
        check_vma=False,
    )
```

profile of v0, /device:TPU:0, one launch (start us, length us, event | category | flops | bytes accessed | tf_op | source)
XLA Modules:
  0.0 1631.6 jit_solution(12169330662072750665)
XLA Ops:
  15.2 43.5 %all-gather = bf16[32,24,6]{1,2,0:T(8,128)(2,1)S(1)} all-gather(bf16[1,24,6]{1,2,0:T(8,128)(2,1)S(1)} %convert_bitcast_fusion.2), channel_id=1, replica_groups=mesh['dp'=8,'expert'=4] {'dp','expert'}, dimensions={0}, use_global_device_ids=true | all-gather | bytes 9504 | tf_op jit(solution)/shard_map/all_gather | solution.py:163
  59.0 37.4 %all-gather.1 = bf16[32,24,8]{1,2,0:T(8,128)(2,1)S(1)} all-gather(bf16[1,24,8]{1,2,0:T(8,128)(2,1)S(1)} %convert_bitcast_fusion.1), channel_id=1, replica_groups=mesh['dp'=8,'expert'=4] {'dp','expert'}, dimensions={0}, use_global_device_ids=true | all-gather | bytes 12672 | tf_op jit(solution)/shard_map/all_gather | solution.py:162
  192.0 42.0 %all_to_all.20 = bf16[2,1076,768]{2,0,1:T(2,128)(2,1)} all-to-all(bf16[2,1076,768]{2,0,1:T(2,128)(2,1)S(1)} %copy.223), channel_id=1, replica_groups=mesh['dp'=8,'expert'=4] {'expert'}, dimensions={1} | all-to-all | bytes 6610944 | tf_op jit(solution)/shard_map/all_to_all | solution.py:67
  234.0 19.2 %fusion.49 = f32[2,1076,3072]{2,1,0:T(8,128)} fusion(bf16[2,3072,768]{2,1,0:T(8,128)(2,1)} %all-gather.9.cloned.1.call-done, bf16[2,1076,768]{2,0,1:T(2,128)(2,1)} %all_to_all.20), kind=kOutput, calls=%fused_computation.98 | convolution fusion | flops 10154409984 | bytes 39186432 | tf_op jit(solution)/shard_map/esd,efd->esf/dot_general | solution.py:239
  253.2 107.9 %all-gather.11.cloned.1.call-done = bf16[2,3072,768]{2,1,0:T(8,128)(2,1)} async-done(((bf16[2,384,768]{2,1,0:T(8,128)(2,1)}), bf16[2,3072,768]{2,1,0:T(8,128)(2,1)}) %all-gather.11.cloned.1.call-update) | async-done | bytes 9437200 | tf_op jit(solution)/shard_map/all_gather | solution.py:237
  361.2 18.9 %convolution_convert_fusion.3 = bf16[2,1076,768]{2,1,0:T(8,128)(2,1)S(1)} fusion(bf16[2,3072,768]{2,1,0:T(8,128)(2,1)} %all-gather.11.cloned.1.call-done, f32[2,1076,3072]{2,1,0:T(8,128)} %fusion.49), kind=kOutput, calls=%fused_computation.50 | convolution fusion | flops 10215561216 | bytes 39186432 | tf_op jit(solution)/shard_map/esf,efd->esd/dot_general | solution.py:241
  380.1 22.2 %copy.225 = bf16[2,1076,768]{2,0,1:T(2,128)(2,1)} copy(bf16[2,1076,768]{2,1,0:T(8,128)(2,1)S(1)} %convolution_convert_fusion.3) | data formatting | bytes 6610944 | tf_op jit(solution)/shard_map/convert_element_type | solution.py:243
  407.3 38.5 %all-to-all-done.1 = bf16[2,1076,768]{2,0,1:T(2,128)(2,1)} async-done(((bf16[2,1076,768]{2,0,1:T(2,128)(2,1)}), bf16[2,1076,768]{2,0,1:T(2,128)(2,1)}, u32[]{:S(2)}, u32[]{:S(2)}) %all-to-all-start.1) | async-done | bytes 3305504 | tf_op jit(solution)/shard_map/all_to_all | solution.py:71
  474.0 42.2 %all-gather.2 = bf16[32,12,768]{2,1,0:T(8,128)(2,1)} all-gather(bf16[1,12,768]{2,1,0:T(8,128)(2,1)S(1)} %fusion.128), channel_id=1, replica_groups=mesh['dp'=8,'expert'=4] {'dp','expert'}, dimensions={0}, use_global_device_ids=true | all-gather | bytes 608256 | tf_op jit(solution)/shard_map/all_gather | solution.py:254
  524.5 74.8 %fusion = f32[16,768]{1,0:T(8,128)S(1)} fusion(f32[384,768]{1,0:T(8,128)} %fusion.120), kind=kCustom, calls=%all-reduce-scatter | all-reduce-scatter fusion | flops 393217 | bytes 1228800
  629.4 12.3 concatenate.6
  677.0 42.4 %all_to_all.21 = bf16[2,1076,768]{2,0,1:T(2,128)(2,1)} all-to-all(bf16[2,1076,768]{2,0,1:T(2,128)(2,1)S(1)} %copy.227), channel_id=1, replica_groups=mesh['dp'=8,'expert'=4] {'expert'}, dimensions={1} | all-to-all | bytes 6610944 | tf_op jit(solution)/shard_map/all_to_all | solution.py:67
  719.3 32.8 %fusion.7 = bf16[2,1076,3072]{2,1,0:T(8,128)(2,1)} fusion(f32[2,1076,3072]{2,1,0:T(8,128)} %fusion.49, bf16[2,3072,768]{2,1,0:T(8,128)(2,1)} %all-gather.11.cloned.1.call-done, bf16[2,1076,768]{2,0,1:T(2,128)(2,1)} %all_to_all.21), kind=kOutput, calls=%fused_computation.14 | convolution fusion | flops 10286628864 | bytes 52408320 | tf_op jit(solution)/shard_map/esd,efd->esf/dot_general | solution.py:293
  752.1 16.5 %convolution_convert_fusion.2 = bf16[2,1076,768]{2,1,0:T(8,128)(2,1)S(1)} fusion(bf16[2,1076,3072]{2,1,0:T(8,128)(2,1)} %fusion.7, bf16[2,3072,768]{2,1,0:T(8,128)(2,1)} %all-gather.9.cloned.1.call-done), kind=kOutput, calls=%fused_computation.49 | convolution fusion | flops 10156062720 | bytes 25964544 | tf_op jit(solution)/shard_map/esf,efd->esd/dot_general | solution.py:295
  768.6 22.2 %copy.229 = bf16[2,1076,768]{2,0,1:T(2,128)(2,1)} copy(bf16[2,1076,768]{2,1,0:T(8,128)(2,1)S(1)} %convolution_convert_fusion.2) | data formatting | bytes 6610944 | tf_op jit(solution)/shard_map/convert_element_type | solution.py:297
  795.7 69.8 %psum.22 = f32[8]{0:T(128)S(1)} all-reduce(f32[8]{0:T(128)S(1)} %copy-done.122), channel_id=1, replica_groups=mesh['dp'=8,'expert'=4] {'dp','expert'}, use_global_device_ids=true, to_apply=%region_23.25 | all-reduce | flops 8 | bytes 64 | tf_op jit(solution)/shard_map/psum | solution.py:196
  994.6 16.3 %copy.248 = f32[5,768,768]{2,0,1:T(8,128)} copy(f32[5,768,768]{1,2,0:T(8,128)} %pad_maximum_fusion) | data formatting | bytes 23592960 | tf_op jit(solution)/shard_map/concatenate | solution.py:335
  1011.0 18.8 %convolution_convert_fusion.1 = bf16[2,3072,768]{2,1,0:T(8,128)(2,1)} fusion(bf16[2,1076,3072]{2,1,0:T(8,128)(2,1)} %fusion.7, bf16[2,1076,768]{2,0,1:T(2,128)(2,1)} %all_to_all.20), kind=kOutput, calls=%fused_computation.36 | convolution fusion | flops 10159128576 | bytes 25964544 | tf_op jit(solution)/shard_map/esf,esd->efd/dot_general | solution.py:298
  1029.9 24.2 %convolution_convert_fusion = bf16[2,3072,768]{2,1,0:T(8,128)(2,1)} fusion(bf16[2,1076,768]{2,0,1:T(2,128)(2,1)} %all_to_all.21, f32[2,1076,3072]{2,1,0:T(8,128)} %fusion.49), kind=kOutput, calls=%fused_computation.35 | convolution fusion | flops 10218627072 | bytes 39186432 | tf_op jit(solution)/shard_map/esf,esd->efd/dot_general | solution.py:292
  1061.5 42.9 %all-reduce.5 = (f32[768,8]{0,1:T(8,128)S(1)}, f32[6,768]{1,0:T(8,128)S(1)}) all-reduce(f32[768,8]{0,1:T(8,128)S(1)} %fusion.193, f32[6,768]{1,0:T(8,128)S(1)} %stack.25), channel_id=4, replica_groups=mesh['dp'=8,'expert'=4] {'dp','expert'}, use_global_device_ids=true, to_apply=%region_39.41.clone | all-reduce | flops 10752 | bytes 86016
  1105.7 113.9 %reduce-scatter.8.cloned.1.call-done = f32[5,24,768]{2,0,1:T(8,128)} async-done(((f32[5,768,768]{2,0,1:T(8,128)}), f32[5,24,768]{2,0,1:T(8,128)}) %reduce-scatter.8.cloned.1.call-update) | async-done | bytes 368656 | tf_op jit(solution)/shard_map/reduce_scatter | solution.py:340
  1223.4 162.1 %reduce-scatter.10.cloned.1.call-done = bf16[2,384,768]{2,1,0:T(8,128)(2,1)} async-done(((bf16[2,3072,768]{2,1,0:T(8,128)(2,1)}), bf16[2,384,768]{2,1,0:T(8,128)(2,1)}) %reduce-scatter.10.cloned.1.call-update) | async-done | bytes 1179664 | tf_op jit(solution)/shard_map/reduce_scatter | solution.py:300
  1388.6 162.9 %reduce-scatter.12.cloned.1.call-done = bf16[2,384,768]{2,1,0:T(8,128)(2,1)} async-done(((bf16[2,3072,768]{2,1,0:T(8,128)(2,1)}), bf16[2,384,768]{2,1,0:T(8,128)(2,1)}) %reduce-scatter.12.cloned.1.call-update) | async-done | bytes 1179664 | tf_op jit(solution)/shard_map/reduce_scatter | solution.py:303
  1555.4 39.6 %all-reduce.4 = (f32[]{:T(128)}, f32[]{:T(128)}) all-reduce(f32[]{:T(128)S(6)} %div.232, f32[]{:T(128)S(6)} %add.395), channel_id=1, replica_groups=mesh['dp'=8,'expert'=4] {'dp','expert'}, use_global_device_ids=true, to_apply=%region_21.23 | all-reduce | flops 2 | bytes 16 | tf_op jit(solution)/shard_map/psum | solution.py:348
  (455 shorter events, 379.5 us)
Async XLA Ops:
  7.2 92.4 %all-gather.7.cloned.1.call-start = ((), (), s32[]{:S(2)}) async-start(), calls=%async_computation.7 | async-start | bytes 6082560 | tf_op jit(solution)/shard_map/all_gather | solution.py:161
  9.1 224.9 %all-gather.9.cloned.1.call-start = ((), (), s32[]{:S(2)}) async-start(), calls=%async_computation.8 | async-start | bytes 10616832 | tf_op jit(solution)/shard_map/all_gather | solution.py:236
  12.0 349.2 %all-gather.11.cloned.1.call-start = ((), (), s32[]{:S(2)}) async-start(), calls=%async_computation.9 | async-start | bytes 10616832 | tf_op jit(solution)/shard_map/all_gather | solution.py:237
  402.2 43.6 %all-to-all-start.1 = ((bf16[2,1076,768]{2,0,1:T(2,128)(2,1)}), bf16[2,1076,768]{2,0,1:T(2,128)(2,1)}, u32[]{:S(2)}, u32[]{:S(2)}) async-start(bf16[2,1076,768]{2,0,1:T(2,128)(2,1)} %copy.225), calls=%async_computation.1 | async-start | bytes 6610944 | tf_op jit(solution)/shard_map/all_to_all | solution.py:71
  599.4 16.4 %collective-permute-start.6 = (f32[16,768]{1,0:T(8,128)S(1)}, f32[16,768]{1,0:T(8,128)S(1)}, u32[]{:S(2)}, u32[]{:S(2)}) collective-permute-start(f32[16,768]{1,0:T(8,128)S(1)} %fusion), channel_id=1, source_target_pairs={{0,7},{1,8},{2,9},{3,10},{4,11},{5,12},{6,13},{7,14},{8,15},{9,16}... | collective-permute-start | bytes 147464
  600.7 22.3 %collective-permute-start.5 = (f32[16,768]{1,0:T(8,128)S(1)}, f32[16,768]{1,0:T(8,128)S(1)}, u32[]{:S(2)}, u32[]{:S(2)}) collective-permute-start(f32[16,768]{1,0:T(8,128)S(1)} %fusion), channel_id=1, source_target_pairs={{0,6},{1,7},{2,8},{3,9},{4,10},{5,11},{6,12},{7,13},{8,14},{9,15},... | collective-permute-start | bytes 147464
  602.0 11.9 collective-permute-start.7
  607.5 21.8 %collective-permute-start.4 = (f32[16,768]{1,0:T(8,128)S(1)}, f32[16,768]{1,0:T(8,128)S(1)}, u32[]{:S(2)}, u32[]{:S(2)}) collective-permute-start(f32[16,768]{1,0:T(8,128)S(1)} %fusion), channel_id=1, source_target_pairs={{0,5},{1,6},{2,7},{3,8},{4,9},{5,10},{6,11},{7,12},{8,13},{9,14},{... | collective-permute-start | bytes 147464
  608.8 20.6 %collective-permute-start.3 = (f32[16,768]{1,0:T(8,128)S(1)}, f32[16,768]{1,0:T(8,128)S(1)}, u32[]{:S(2)}, u32[]{:S(2)}) collective-permute-start(f32[16,768]{1,0:T(8,128)S(1)} %fusion), channel_id=1, source_target_pairs={{0,4},{1,5},{2,6},{3,7},{4,8},{5,9},{6,10},{7,11},{8,12},{9,13},{1... | collective-permute-start | bytes 147464
  613.9 15.5 collective-permute-start.2
  615.8 13.6 collective-permute-start.1
  622.9 6.5 collective-permute-start
  790.8 81.4 %all-to-all-start.3 = ((bf16[2,1076,768]{2,0,1:T(2,128)(2,1)}), bf16[2,1076,768]{2,0,1:T(2,128)(2,1)}, u32[]{:S(2)}, u32[]{:S(2)}) async-start(bf16[2,1076,768]{2,0,1:T(2,128)(2,1)} %copy.229), calls=%async_computation.3 | async-start | bytes 6610944 | tf_op jit(solution)/shard_map/all_to_all | solution.py:71
  795.6 424.1 %reduce-scatter.8.cloned.1.call-start = ((), (), s32[]{:S(2)}) async-start(), calls=%async_computation.10 | async-start | bytes 19464192 | tf_op jit(solution)/shard_map/reduce_scatter | solution.py:340
  1011.0 374.5 %reduce-scatter.10.cloned.1.call-start = ((), (), s32[]{:S(2)}) async-start(), calls=%async_computation.11 | async-start | bytes 10616832 | tf_op jit(solution)/shard_map/reduce_scatter | solution.py:300
  1029.8 521.7 %reduce-scatter.12.cloned.1.call-start = ((), (), s32[]{:S(2)}) async-start(), calls=%async_computation.12 | async-start | bytes 10616832 | tf_op jit(solution)/shard_map/reduce_scatter | solution.py:303
  1057.0 539.3 %copy-start.95 = (f32[6,24]{1,0:T(8,128)S(1)}, f32[6,24]{1,0:T(8,128)}, u32[]{:S(2)}) copy-start(f32[6,24]{1,0:T(8,128)} %param.46) | copy-start | bytes 1732
  1057.1 539.3 %copy-start.109 = (f32[6,24]{1,0:T(8,128)S(1)}, f32[6,24]{1,0:T(8,128)}, u32[]{:S(2)}) copy-start(f32[6,24]{1,0:T(8,128)} %param.49) | copy-start | bytes 1732
  1057.1 539.3 %copy-start.110 = (f32[6,24]{1,0:T(8,128)S(1)}, f32[6,24]{1,0:T(8,128)}, u32[]{:S(2)}) copy-start(f32[6,24]{1,0:T(8,128)} %param.47) | copy-start | bytes 1732
  1057.1 539.3 %copy-start.111 = (f32[6,24]{1,0:T(8,128)S(1)}, f32[6,24]{1,0:T(8,128)}, u32[]{:S(2)}) copy-start(f32[6,24]{1,0:T(8,128)} %param.48) | copy-start | bytes 1732
  1057.1 540.0 %copy-start.97 = (f32[24,8]{0,1:T(8,128)S(1)}, f32[24,8]{0,1:T(8,128)}, u32[]{:S(2)}) copy-start(f32[24,8]{0,1:T(8,128)} %param.42) | copy-start | bytes 2308
  1057.1 539.9 %copy-start.112 = (f32[24,8]{0,1:T(8,128)S(1)}, f32[24,8]{0,1:T(8,128)}, u32[]{:S(2)}) copy-start(f32[24,8]{0,1:T(8,128)} %param.45) | copy-start | bytes 2308
  1057.1 539.9 %copy-start.113 = (f32[24,8]{0,1:T(8,128)S(1)}, f32[24,8]{0,1:T(8,128)}, u32[]{:S(2)}) copy-start(f32[24,8]{0,1:T(8,128)} %param.43) | copy-start | bytes 2308
  1057.1 539.9 %copy-start.114 = (f32[24,8]{0,1:T(8,128)S(1)}, f32[24,8]{0,1:T(8,128)}, u32[]{:S(2)}) copy-start(f32[24,8]{0,1:T(8,128)} %param.44) | copy-start | bytes 2308
  (122 other events, 3396.2 us)
Sparse Core Ops, SparseCore 0:
  11.6 71.2 all-gather.6
  85.6 136.4 all-gather.8
  224.9 136.2 all-gather.10
  1011.1 208.5 reduce-scatter.7
  1223.1 162.3 reduce-scatter.9
  1388.9 162.5 reduce-scatter.11
where the time goes:
time: 1640 us; the launch traced here: 1630 us
  waiting for transfers between devices  586 us (36%)
  blocking collectives  435 us (27%)
  matrix products  247 us (15%)
  local copies, waits for them, and re-layouts  222 us (14%)
  other arithmetic  82.3 us (5%)
  starting transfers between devices  31.3 us (2%)
  between operations  28.8 us (2%)
    reduce_scatter x1, waiting for transfers between devices, body(): lax.psum_scatter(g_two.astype(jnp.bfloat16), 'dp', scatter_dimension=1, t...  163 us
    reduce_scatter x1, waiting for transfers between devices, body(): lax.psum_scatter(g_one.astype(jnp.bfloat16), 'dp', scatter_dimension=1, t...  162 us
    unnamed x2, blocking collectives  118 us
    reduce_scatter x1, waiting for transfers between devices, body(): lax.psum_scatter(g_layers, ('dp', 'expert'), scatter_dimension=1, tiled=T...  114 us
    all_gather x1, waiting for transfers between devices, body(): lax.all_gather(out_b, 'dp', axis=1, tiled=True)  108 us
    all_to_all x2, blocking collectives, to_experts(): lax.all_to_all(buffer, 'expert', split_axis=1, concat_axis=1, tiled=True)  84.4 us
    psum x1, blocking collectives, body(): lax.psum(jnp.sum(router_probs * valid_flat[:, None], 0), ('dp', 'expert'))  69.8 us
    all_gather x1, blocking collectives, body(): lax.all_gather(norm_params.astype(jnp.bfloat16), ('dp', 'expert'), axis=1...  43.5 us
  transfers between devices with their start and end apart: 16, of which 5 were waited for; matrix products, arithmetic and copies ran while one was open for 11% of the time, Pallas kernels for 0%

commit v1 on v0

v1 whole, which is shorter than its diff:
```python
import functools

import jax
import jax.numpy as jnp
import numpy as np
from jax import lax
from jax.sharding import Mesh
from jax.sharding import PartitionSpec as P

HEADS = 12
TOP = 2
STEP_COUNT = 10
QUAD = 4

high_prec = lax.Precision.HIGHEST
eps_norm = 1e-06
aux_weight = 0.01
clip_limit = 1.0
base_rate = 0.05
norm_rate = 0.5
beta_first = 0.9
beta_second = 0.999
weight_decay = 0.1
polyak_decay = 0.7
adam_eps = 1e-08
mask_fill = -1e30

ALL = ("g", "r", "x", "c")
MEMBERS = ("x", "r")


def layer_norm(values, gain, shift):
    centre = values - jnp.mean(values, -1, keepdims=True)
    spread = jnp.mean(centre * centre, -1, keepdims=True)
    return centre * lax.rsqrt(spread + eps_norm) * gain + shift


def softmax_rows(logits):
    top_val = jnp.max(logits, -1, keepdims=True)
    powers = jnp.exp(logits - top_val)
    return powers / jnp.sum(powers, -1, keepdims=True)


def route(pick_ids, valid_flat, rank_ids, n_experts, capacity, padded):
    columns = jnp.arange(n_experts, dtype=jnp.int32)
    first_hot = (pick_ids[:, 0:1] == columns[None, :]).astype(jnp.float32) * valid_flat[:, None]
    second_hot = (pick_ids[:, 1:2] == columns[None, :]).astype(jnp.float32) * valid_flat[:, None]
    before = (rank_ids[None, :] < rank_ids[:, None]).astype(jnp.bfloat16)
    hot = jnp.concatenate([first_hot, second_hot], 1)
    ahead = jnp.dot(before, hot.astype(jnp.bfloat16), preferred_element_type=jnp.float32)
    first_pos = jnp.sum(first_hot * ahead[:, :n_experts], 1)
    second_pos = jnp.sum(second_hot * (ahead[:, n_experts:] + jnp.sum(first_hot, 0)[None, :]), 1)
    first_kept = valid_flat * (first_pos < capacity).astype(jnp.float32)
    second_kept = valid_flat * (second_pos < capacity).astype(jnp.float32)
    first_slot = jnp.where(
        first_kept > 0, pick_ids[:, 0] * padded + first_pos.astype(jnp.int32), -1
    )
    second_slot = jnp.where(
        second_kept > 0, pick_ids[:, 1] * padded + second_pos.astype(jnp.int32), -1
    )
    return (first_slot, second_slot, first_kept, second_kept)


def adam_update(weight, first_state, second_state, average_state, gradient, factor, step_rate):
    clipped = gradient * factor
    first_new = beta_first * first_state + (1.0 - beta_first) * clipped
    second_new = beta_second * second_state + (1.0 - beta_second) * clipped * clipped
    first_hat = first_new / (1.0 - beta_first**STEP_COUNT)
    second_hat = second_new / (1.0 - beta_second**STEP_COUNT)
    weight_new = weight - step_rate * (
        first_hat / (jnp.sqrt(second_hat) + adam_eps) + weight_decay * weight
    )
    average_new = polyak_decay * average_state + (1.0 - polyak_decay) * weight_new
    return (weight_new, first_new, second_new, average_new)


def split_heads(proj_qkv, allow_mask, n_heads):
    n_rows, n_slots_row = (allow_mask.shape[0], allow_mask.shape[1])
    head_dim = proj_qkv.shape[-1] // n_heads
    shaped = proj_qkv.reshape(3, n_rows, n_slots_row, n_heads, head_dim)
    scores = jnp.einsum(
        "rqhd,rkhd->rhqk", shaped[0], shaped[1], preferred_element_type=jnp.float32
    ) * head_dim ** (-0.5)
    return (shaped, jnp.where(allow_mask[:, None], scores, mask_fill), head_dim ** (-0.5))


def attention_forward(proj_qkv, allow_mask, n_heads):
    shaped, masked, unused_scale = split_heads(proj_qkv, allow_mask, n_heads)
    top_val = jnp.max(masked, -1, keepdims=True)
    powers = jnp.exp(masked - top_val)
    totals = jnp.sum(powers, -1, keepdims=True)
    att_probs = powers / totals
    output = jnp.einsum(
        "rhqk,rkhd->rqhd",
        att_probs.astype(jnp.bfloat16),
        shaped[2],
        preferred_element_type=jnp.float32,
    )
    return (
        output.astype(jnp.bfloat16).reshape(proj_qkv.shape[1], proj_qkv.shape[2]),
        top_val + jnp.log(totals),
    )


def attention_backward(proj_qkv, allow_mask, log_total, d_output, n_heads):
    shaped, masked, score_scale = split_heads(proj_qkv, allow_mask, n_heads)
    att_probs = jnp.exp(masked - log_total)
    grad_out = d_output.reshape(shaped.shape[1:])
    d_probs = jnp.einsum("rqhd,rkhd->rhqk", grad_out, shaped[2], preferred_element_type=jnp.float32)
    d_values = jnp.einsum(
        "rhqk,rqhd->rkhd",
        att_probs.astype(jnp.bfloat16),
        grad_out,
        preferred_element_type=jnp.float32,
    )
    d_scores = (att_probs * (d_probs - jnp.sum(att_probs * d_probs, -1, keepdims=True))).astype(
        jnp.bfloat16
    )
    d_query = (
        jnp.einsum("rhqk,rkhd->rqhd", d_scores, shaped[1], preferred_element_type=jnp.float32)
        * score_scale
    )
    d_keys = (
        jnp.einsum("rhqk,rqhd->rkhd", d_scores, shaped[0], preferred_element_type=jnp.float32)
        * score_scale
    )
    stacked = jnp.stack([d_query, d_keys, d_values]).astype(jnp.bfloat16)
    return stacked.reshape(proj_qkv.shape)


def shard_moves(n_blocks):
    span = 2 * n_blocks
    moves = []
    for step in range(span):
        pairs = []
        for place in range(QUAD * n_blocks):
            for core in range(2):
                target = (place + step) % span
                src = place * 2 + core
                dst = (target // 2 * QUAD + 2 * core + target % 2) * 2 + place // span
                pairs.append((src, dst))
        moves.append(pairs)
    return moves


def swap_cores(value):
    return lax.ppermute(value, "c", [(0, 1), (1, 0)])


def fetch_experts(expert_in, expert_out, n_blocks):
    place = lax.axis_index("g") * QUAD + lax.axis_index("r")
    odd = lax.rem(place, 2) == 1
    both = jnp.stack([expert_in, expert_out], 1).astype(jnp.bfloat16)
    ordered = [jnp.where(odd, both[1], both[0]), jnp.where(odd, both[0], both[1])]
    return [
        lax.ppermute(ordered[step % 2], ("g", "r", "c"), pairs)
        for step, pairs in enumerate(shard_moves(n_blocks))
    ]


def return_experts(parts, n_blocks):
    place = lax.axis_index("g") * QUAD + lax.axis_index("r")
    odd = lax.rem(place, 2) == 1
    sums = [None, None]
    for step, pairs in enumerate(shard_moves(n_blocks)):
        back = lax.ppermute(parts[step], ("g", "r", "c"), [(dst, src) for src, dst in pairs])
        back = back.astype(jnp.float32)
        sums[step % 2] = back if sums[step % 2] is None else sums[step % 2] + back
    zero, one = jnp.where(odd, sums[1], sums[0]), jnp.where(odd, sums[0], sums[1])
    return jnp.stack([zero[0], one[0]]), jnp.stack([zero[1], one[1]])


def to_members(value):
    return lax.all_to_all(value, MEMBERS, split_axis=0, concat_axis=0, tiled=True)


def body(
    patches,
    lengths,
    slot_mask,
    expert_picks,
    priority_rank,
    class_labels,
    dense_weights,
    dense_first,
    dense_second,
    dense_average,
    router_weights,
    router_first,
    router_second,
    router_average,
    norm_params,
    norm_first,
    norm_second,
    norm_average,
    expert_in,
    in_first,
    in_second,
    in_average,
    expert_out,
    out_first,
    out_second,
    out_average,
    head_weights,
    head_first,
    head_second,
    head_average,
):
    n_blocks = lax.axis_size("g")
    layer_b, router_b, norm_b = (
        lax.all_gather(dense_weights.astype(jnp.bfloat16), ALL, axis=1, tiled=True),
        lax.all_gather(router_weights.astype(jnp.bfloat16), ALL, axis=0, tiled=True),
        lax.all_gather(norm_params.astype(jnp.bfloat16), ALL, axis=1, tiled=True),
    )
    own_chunks = fetch_experts(expert_in, expert_out, n_blocks)
    own_half = jnp.stack(own_chunks, 1)
    other_half = swap_cores(own_half)
    w_one = jnp.concatenate([own_half[0], other_half[0]], 0)
    w_two = jnp.concatenate([own_half[1], other_half[1]], 0)
    gain_rows = norm_b.astype(jnp.float32)
    rows_here, n_slots_row = slot_mask.shape
    tokens = rows_here * n_slots_row
    model_width = layer_b.shape[2]
    n_experts = router_weights.shape[1]
    n_images = lengths.shape[0] * lengths.shape[1]
    capacity = (21 * tokens * TOP + 20 * n_experts - 1) // (20 * n_experts)
    padded = (capacity + 15) // 16 * 16
    n_slots = n_experts * padded
    w_one = w_one.reshape(-1, model_width)
    w_two = w_two.reshape(-1, model_width)
    valid = slot_mask.astype(jnp.float32)
    positions = jnp.arange(n_slots_row, dtype=jnp.int32)
    bounds = jnp.cumsum(lengths, 1)
    segment = jnp.sum((positions[None, :, None] >= bounds[:, None, :]).astype(jnp.int32), -1)
    diagonal = positions[:, None] == positions[None, :]
    allowed = (segment[:, :, None] == segment[:, None, :]) & (
        (valid[:, None, :] > 0) | diagonal[None]
    )
    member = (
        segment[:, None, :] == jnp.arange(lengths.shape[1], dtype=jnp.int32)[None, :, None]
    ).astype(jnp.float32) * valid[:, None, :]
    pooling = member / jnp.maximum(jnp.sum(member, -1, keepdims=True), 1.0)
    valid_flat = valid.reshape(tokens)
    pool_flat = jnp.sum(pooling, 1).reshape(tokens)
    image_flat = (segment + jnp.arange(rows_here)[:, None] * lengths.shape[1]).reshape(tokens)
    slot_one, slot_two, kept_one, kept_two = route(
        expert_picks, valid_flat, priority_rank[0], n_experts, capacity, padded
    )
    x_zero = jnp.dot(patches, layer_b[0], preferred_element_type=jnp.float32)
    a_one = layer_norm(x_zero, gain_rows[0], gain_rows[3]).astype(jnp.bfloat16)
    proj_qkv = jnp.einsum(
        "td,kde->kte", a_one, layer_b[1:4], preferred_element_type=jnp.float32
    ).astype(jnp.bfloat16)
    att_out, log_total = attention_forward(proj_qkv, allowed, HEADS)
    x_one = x_zero + jnp.dot(att_out, layer_b[4], preferred_element_type=jnp.float32)
    a_two = layer_norm(x_one, gain_rows[1], gain_rows[4]).astype(jnp.bfloat16)
    router_probs = softmax_rows(jnp.dot(a_two, router_b, preferred_element_type=jnp.float32))
    importance = lax.psum(jnp.sum(router_probs * valid_flat[:, None], 0), ALL)
    pick_one = expert_picks[:, 0]
    pick_two = expert_picks[:, 1]
    columns = jnp.arange(n_experts, dtype=jnp.int32)
    hot_one = (pick_one[:, None] == columns[None]).astype(jnp.float32)
    hot_two = (pick_two[:, None] == columns[None]).astype(jnp.float32)
    gate_one = jnp.sum(router_probs * hot_one, 1) * kept_one
    gate_two = jnp.sum(router_probs * hot_two, 1) * kept_two
    slot_ids = jnp.arange(n_slots, dtype=jnp.int32)
    match_one = slot_one[None, :] == slot_ids[:, None]
    match_two = slot_two[None, :] == slot_ids[:, None]
    match = (match_one | match_two).astype(jnp.bfloat16)
    send_rows = (
        jnp.dot(match, a_two, preferred_element_type=jnp.float32)
        .astype(jnp.bfloat16)
        .reshape(n_experts, padded, model_width)
    )
    held = jnp.where(match_one | match_two, 1.0, 0.0)
    slot_gate = jnp.sum(
        jnp.where(match_one, gate_one[None], 0.0) + jnp.where(match_two, gate_two[None], 0.0), 1
    )
    slot_pool = jnp.sum(held * pool_flat[None], 1)
    slot_image = jnp.sum(held * image_flat.astype(jnp.float32)[None], 1)
    details = jnp.stack([slot_gate, slot_pool, slot_image]).reshape(3, n_experts, padded)
    arrived = to_members(send_rows)
    details = to_members(details.transpose(1, 0, 2))
    got_gate, got_pool, got_image = details[:, 0], details[:, 1], details[:, 2]
    image_hot = (
        got_image[:, :, None] == jnp.arange(n_images).astype(jnp.float32)[None, None]
    ).astype(jnp.float32) * got_pool[:, :, None]
    rows_all = arrived.reshape(n_slots, model_width)
    hidden = jnp.dot(rows_all, w_one.T, preferred_element_type=jnp.float32)
    activated = jax.nn.gelu(hidden).astype(jnp.bfloat16)
    result = jnp.dot(activated, w_two, preferred_element_type=jnp.float32).astype(jnp.bfloat16)
    result = result.reshape(n_experts, padded, model_width).astype(jnp.float32)
    part_pooled = jnp.einsum(
        "dsi,dsw->diw", image_hot * got_gate[:, :, None], result, precision=high_prec
    )
    pooled = jnp.einsum(
        "ris,rsd->rid",
        pooling,
        x_one.reshape(rows_here, n_slots_row, model_width),
        precision=high_prec,
    ).reshape(-1, model_width)
    pooled = pooled + jnp.sum(to_members(part_pooled), 0)
    gathered = lax.all_gather(
        layer_norm(pooled, gain_rows[2], gain_rows[5]).astype(jnp.bfloat16),
        ALL,
        axis=0,
        tiled=True,
    )
    head_b = head_weights.astype(jnp.bfloat16)
    logits = jnp.dot(head_b, gathered.T, preferred_element_type=jnp.float32)
    labels = class_labels.astype(jnp.float32)
    n_images_all = gathered.shape[0]
    local_loss = jnp.sum(jnp.logaddexp(logits, 0.0) - labels * logits) / n_images_all
    centre = jnp.mean(importance)
    spread = jnp.mean((importance - centre) ** 2)
    d_imp = aux_weight * (
        2.0 * (importance - centre) / (n_experts * centre * centre)
        - 2.0 * spread / (n_experts * centre * centre * centre)
    )
    d_logits = ((jax.nn.sigmoid(logits) - labels) / n_images_all).astype(jnp.bfloat16)
    g_head = jnp.dot(d_logits, gathered, preferred_element_type=jnp.float32)
    d_rows = lax.psum_scatter(
        jnp.dot(d_logits.T, head_b, preferred_element_type=jnp.float32),
        ALL,
        scatter_dimension=0,
        tiled=True,
    )
    unused_out, norm_back = jax.vjp(layer_norm, pooled, gain_rows[2], gain_rows[5])
    d_pooled, g_gain_three, g_shift_three = norm_back(d_rows)
    d_two = jnp.einsum(
        "ris,rid->rsd", pooling, d_pooled.reshape(rows_here, -1, model_width), precision=high_prec
    ).reshape(tokens, model_width)
    d_pooled_all = lax.all_gather(d_pooled, MEMBERS, axis=0)
    d_two_slots = jnp.einsum("dsi,diw->dsw", image_hot, d_pooled_all, precision=high_prec)
    slot_d_gate = jnp.sum(d_two_slots * result, -1)
    d_all = (d_two_slots * got_gate[:, :, None]).astype(jnp.bfloat16).reshape(n_slots, model_width)
    d_act = jnp.dot(d_all, w_two.T, preferred_element_type=jnp.float32)
    d_hidden = jax.vjp(jax.nn.gelu, hidden)[1](d_act)[0].astype(jnp.bfloat16)
    d_inputs = jnp.dot(d_hidden, w_one, preferred_element_type=jnp.float32).astype(jnp.bfloat16)
    d_back = to_members(d_inputs.reshape(n_experts, padded, model_width))
    d_back = d_back.reshape(n_slots, model_width)
    back_gate = to_members(slot_d_gate).reshape(n_slots)
    g_two = jnp.dot(activated.T, d_all, preferred_element_type=jnp.float32)
    g_one = jnp.dot(d_hidden.T, rows_all, preferred_element_type=jnp.float32)
    half = g_one.shape[0] // 2
    grads = jnp.stack([g_one, g_two], 0).astype(jnp.bfloat16)
    summed = grads[:, :half].astype(jnp.float32) + swap_cores(grads[:, half:]).astype(jnp.float32)
    summed = summed.astype(jnp.bfloat16).reshape(2, 2 * n_blocks, -1, model_width)
    g_one, g_two = return_experts([summed[:, i] for i in range(2 * n_blocks)], n_blocks)
    d_gate_one = kept_one * jnp.take(back_gate, jnp.maximum(slot_one, 0), axis=0)
    d_gate_two = kept_two * jnp.take(back_gate, jnp.maximum(slot_two, 0), axis=0)
    d_a_two = lax.dot_general(
        match, d_back, (((0,), (0,)), ((), ())), preferred_element_type=jnp.float32
    )
    d_probs = (
        hot_one * d_gate_one[:, None]
        + hot_two * d_gate_two[:, None]
        + valid_flat[:, None] * d_imp[None, :]
    )
    d_router = (
        router_probs * (d_probs - jnp.sum(router_probs * d_probs, 1, keepdims=True))
    ).astype(jnp.bfloat16)
    g_router = jnp.dot(a_two.T, d_router, preferred_element_type=jnp.float32)
    d_a_two = d_a_two + jnp.dot(d_router, router_b.T, preferred_element_type=jnp.float32)
    unused_out, norm_back = jax.vjp(layer_norm, x_one, gain_rows[1], gain_rows[4])
    d_x_one, g_gain_two, g_shift_two = norm_back(d_a_two)
    d_x_one = d_x_one + d_two
    d_att_b = d_x_one.astype(jnp.bfloat16)
    g_out_proj = jnp.dot(att_out.T, d_att_b, preferred_element_type=jnp.float32)
    d_att_out = jnp.dot(d_att_b, layer_b[4].T, preferred_element_type=jnp.float32).astype(
        jnp.bfloat16
    )
    d_qkv = attention_backward(proj_qkv, allowed, log_total, d_att_out, HEADS)
    g_qkv = jnp.einsum("td,kte->kde", a_one, d_qkv, preferred_element_type=jnp.float32)
    d_a_one = jnp.einsum("kte,kde->td", d_qkv, layer_b[1:4], preferred_element_type=jnp.float32)
    unused_out, norm_back = jax.vjp(layer_norm, x_zero, gain_rows[0], gain_rows[3])
    d_x_zero, g_gain_one, g_shift_one = norm_back(d_a_one)
    d_x_zero = (d_x_zero + d_x_one).astype(jnp.bfloat16)
    g_embed = jnp.dot(patches.T, d_x_zero, preferred_element_type=jnp.float32)
    g_layers = jnp.concatenate([g_embed[None], g_qkv, g_out_proj[None]], 0)
    g_norms = jnp.stack(
        [g_gain_one, g_gain_two, g_gain_three, g_shift_one, g_shift_two, g_shift_three]
    )
    g_layers, g_router, g_norms = (
        lax.psum_scatter(
            g_layers.astype(jnp.bfloat16), ALL, scatter_dimension=1, tiled=True
        ).astype(jnp.float32),
        lax.psum_scatter(g_router, ALL, scatter_dimension=0, tiled=True),
        lax.psum_scatter(g_norms, ALL, scatter_dimension=1, tiled=True),
    )
    squares = (
        jnp.sum(g_layers * g_layers) + jnp.sum(g_router * g_router) + jnp.sum(g_norms * g_norms)
    )
    squares = squares + jnp.sum(g_one * g_one) + jnp.sum(g_two * g_two) + jnp.sum(g_head * g_head)
    loss_sum, square_sum = lax.psum((local_loss, squares), ALL)
    grad_norm = jnp.sqrt(square_sum)
    factor = jnp.minimum(1.0, clip_limit / grad_norm)
    loss_value = loss_sum + aux_weight * spread / (centre * centre)
    dense_out = adam_update(
        dense_weights, dense_first, dense_second, dense_average, g_layers, factor, base_rate
    )
    router_out = adam_update(
        router_weights, router_first, router_second, router_average, g_router, factor, base_rate
    )
    norm_out = adam_update(
        norm_params, norm_first, norm_second, norm_average, g_norms, factor, norm_rate
    )
    in_out = adam_update(expert_in, in_first, in_second, in_average, g_one, factor, base_rate)
    out_out = adam_update(expert_out, out_first, out_second, out_average, g_two, factor, base_rate)
    head_out = adam_update(
        head_weights, head_first, head_second, head_average, g_head, factor, base_rate
    )
    return (
        loss_value,
        importance,
        grad_norm,
        *dense_out,
        *router_out,
        *norm_out,
        *in_out,
        *out_out,
        *head_out,
    )


def solution(mesh):
    n_dp, n_expert = mesh.shape["dp"], mesh.shape["expert"]
    shaped = mesh.devices.reshape(n_dp // QUAD, QUAD, n_expert // 2, 2)
    fine = Mesh(shaped, ALL)
    rows = P(ALL, None)
    dense = P(None, ALL, None)
    norms = P(None, ALL)
    experts = P(("x", "c"), ("g", "r"), None)
    placed = (rows,) * 6 + (dense,) * 4 + (rows,) * 4 + (norms,) * 4 + (experts,) * 8 + (rows,) * 4
    results = (
        (P(),) * 3 + (dense,) * 4 + (rows,) * 4 + (norms,) * 4 + (experts,) * 8 + (rows,) * 4
    )
    return jax.shard_map(body, mesh=fine, in_specs=placed, out_specs=results, check_vma=False)
```

time: 1640 us -> 1120 us (0.68)
  waiting for transfers between devices: 586 us -> 38.2 us
  blocking collectives: 435 us -> 563 us
  local copies, waits for them, and re-layouts: 222 us -> 99 us
  starting transfers between devices: 31.3 us -> 70 us
  matrix products: 247 us -> 223 us
    reduce_scatter x3 -> x1, waiting for transfers between devices: 439 us -> 0.01 us  [body(): lax.psum_scatter(g_layers.astype(jnp.bfloat16), ALL, scatter_dimension=1,...]
    all_gather x2 -> x3, blocking collectives: 80.9 us -> 208 us  [the longest x1 110 us: body(): lax.all_gather(norm_params.astype(jnp.bfloat16), ALL, axis=1, tiled=True)]
    unnamed x2, blocking collectives: 118 us -> 231 us
    all_gather x3 -> x1, waiting for transfers between devices: 108 us -> 0.02 us  [body(): lax.all_gather(dense_weights.astype(jnp.bfloat16), ALL, axis=1, tiled=True)]
    all_to_all x2 -> x0, blocking collectives: 84.4 us -> none  [to_experts(): lax.all_to_all(buffer, 'expert', split_axis=1, concat_axis=1, tiled=True)]
    convert_element_type x4 -> x0, local copies, waits for them, and re-layouts: 50.1 us -> none  [the longest x1 22.2 us: body(): d_inputs = jnp.einsum('esf,efd->esd', d_hidden, w_one, preferred_element_...]
    gather x8 -> x2, local copies, waits for them, and re-layouts: 59 us -> 12.3 us  [the longest x1 6.15 us: body(): jnp.take(back_gate, jnp.maximum(slot_two, 0), axis=0)]
    ppermute x0 -> x10, starting transfers between devices: none -> 30.1 us  [the longest x4 16.7 us: fetch_experts(): lax.ppermute(ordered[step % 2], ('g', 'r', 'c'), pairs)]
  transfers between devices with their start and end apart: 16 -> 25, of which waited for: 5 -> 3; matrix products, arithmetic and copies ran while one was open for 11% -> 27% of each run, Pallas kernels for 0% -> 0%
where the time goes in v1:
time: 1120 us; the launch traced here: 1110 us
  blocking collectives  563 us (50%)
  matrix products  223 us (20%)
  local copies, waits for them, and re-layouts  99 us (9%)
  other arithmetic  86.7 us (8%)
  starting transfers between devices  70 us (6%)
  waiting for transfers between devices  38.2 us (3%)
  between operations  28.6 us (3%)
    unnamed x2, blocking collectives  231 us
    all_gather x1, blocking collectives, body(): lax.all_gather(norm_params.astype(jnp.bfloat16), ALL, axis=1, tiled=True)  110 us
    all_gather x1, blocking collectives, body(): lax.all_gather(router_weights.astype(jnp.bfloat16), ALL, axis=0, tiled=True)  70.2 us
    all_gather x1, blocking collectives, body(): lax.all_gather(layer_norm(pooled, gain_rows[2], gain_rows[5]).astype(jnp....  44.6 us
    psum x1, blocking collectives, body(): importance = lax.psum(jnp.sum(router_probs * valid_flat[:, None], 0), ALL)  40.6 us
    psum x1, blocking collectives, body(): loss_sum, square_sum = lax.psum((local_loss, squares), ALL)  38.8 us
    dot_general x1, matrix products, body(): d_act = jnp.dot(d_all, w_two.T, preferred_element_type=jnp.float32)  33.3 us
    all_to_all x5, waiting for transfers between devices, to_members(): lax.all_to_all(value, MEMBERS, split_axis=0, concat_axis=0, tiled=True)  30.5 us
  transfers between devices with their start and end apart: 25, of which 3 were waited for; matrix products, arithmetic and copies ran while one was open for 27% of the time, Pallas kernels for 0%

profile of v1, /device:TPU:0, one launch (start us, length us, event | category | flops | bytes accessed | tf_op | source)
XLA Modules:
  0.0 1108.3 jit_solution(4984558449201029843)
XLA Ops:
  13.0 10.5 collective-permute-start
  30.9 110.5 %all-gather.1 = bf16[32,24,6]{1,2,0:T(8,128)(2,1)S(1)} all-gather(bf16[1,24,6]{1,2,0:T(8,128)(2,1)S(1)} %convert_bitcast_fusion.6), channel_id=1, replica_groups=mesh['g'=2,'r'=4,'x'=2,'c'=2] {'g','r','x','c'}, dimensions={0}, use_global_device_ids=true | all-gather | bytes 9504 | tf_op jit(solution)/shard_map/all_gather | solution.py:213
  142.0 70.2 %all-gather.2 = bf16[32,24,8]{1,2,0:T(8,128)(2,1)S(1)} all-gather(bf16[1,24,8]{1,2,0:T(8,128)(2,1)S(1)} %convert_bitcast_fusion.5), channel_id=1, replica_groups=mesh['g'=2,'r'=4,'x'=2,'c'=2] {'g','r','x','c'}, dimensions={0}, use_global_device_ids=true | all-gather | bytes 12672 | tf_op jit(solution)/shard_map/all_gather | solution.py:212
  304.8 30.4 %all-to-all-done.1 = bf16[8,272,768]{2,1,0:T(8,128)(2,1)} async-done(((bf16[8,272,768]{2,1,0:T(8,128)(2,1)}), bf16[8,272,768]{2,1,0:T(8,128)(2,1)}, u32[]{:S(2)}, u32[]{:S(2)}) %all-to-all-start.1) | async-done | bytes 3342368 | tf_op jit(solution)/shard_map/all_to_all | solution.py:174
  335.3 25.4 %multiply_convert_fusion = (bf16[2176,3072]{1,0:T(8,128)(2,1)}, f32[2176,3072]{1,0:T(8,128)}) fusion(bf16[2176,768]{1,0:T(8,128)(2,1)} %bitcast.15, bf16[3072,768]{1,0:T(8,128)(2,1)} %bitcast.208), kind=kOutput, calls=%fused_computation.11 | convolution fusion | flops 10327818240 | bytes 48168960 | tf_op jit(solution)/shard_map/dot_general | solution.py:289
  360.7 15.2 %convolution_convert_fusion.3 = bf16[2176,768]{1,0:T(8,128)(2,1)S(1)} fusion(bf16[2176,3072]{1,0:T(8,128)(2,1)} %get-tuple-element.244, bf16[3072,768]{1,0:T(8,128)(2,1)} %bitcast.212), kind=kOutput, calls=%fused_computation.40 | convolution fusion | flops 10269327360 | bytes 21430272 | tf_op jit(solution)/shard_map/dot_general | solution.py:291
  384.5 40.6 %psum.22 = f32[8]{0:T(128)S(1)} all-reduce(f32[8]{0:T(128)S(1)} %get-tuple-element.147), channel_id=1, replica_groups=mesh['g'=2,'r'=4,'x'=2,'c'=2] {'g','r','x','c'}, use_global_device_ids=true, to_apply=%region_26.27 | all-reduce | flops 8 | bytes 64 | tf_op jit(solution)/shard_map/psum | solution.py:258
  435.0 44.6 %all-gather.3 = bf16[32,12,768]{2,1,0:T(8,128)(2,1)} all-gather(bf16[1,12,768]{2,1,0:T(8,128)(2,1)S(1)} %get-tuple-element.197), channel_id=1, replica_groups=mesh['g'=2,'r'=4,'x'=2,'c'=2] {'g','r','x','c'}, dimensions={0}, use_global_device_ids=true | all-gather | bytes 608256 | tf_op jit(solution)/shard_map/all_gather | solution.py:303
  487.3 74.0 %fusion = f32[16,768]{1,0:T(8,128)S(1)} fusion(f32[384,768]{1,0:T(8,128)} %fusion.74), kind=kCustom, calls=%all-reduce-scatter | all-reduce-scatter fusion | flops 393217 | bytes 1228800
  575.8 6.5 collective-permute-start.16
  586.0 27.5 %all-gather.4 = f32[8,12,768]{2,1,0:T(8,128)S(1)} all-gather(f32[1,12,768]{2,1,0:T(8,128)S(1)} %bitcast.220), channel_id=2, replica_groups=mesh['g'=2,'r'=4,'x'=2,'c'=2] {'x','r'}, dimensions={0}, use_global_device_ids=true | all-gather | bytes 331776 | tf_op jit(solution)/shard_map/all_gather | solution.py:333
  613.5 9.8 multiply_reduce_fusion.1
  627.2 33.3 %fusion.7 = bf16[2176,3072]{1,0:T(8,128)(2,1)} fusion(f32[2176,3072]{1,0:T(8,128)} %get-tuple-element.245, bf16[2176,768]{1,0:T(8,128)(2,1)} %bitcast.251, bf16[3072,768]{1,0:T(8,128)(2,1)} %bitcast.213), kind=kOutput, calls=%fused_computation.10 | convolution fusion | flops 10401349632 | bytes 48168960 | tf_op jit(solution)/shard_map/dot_general | solution.py:337
  660.6 15.0 %convolution_convert_fusion.2 = bf16[2176,768]{1,0:T(8,128)(2,1)} fusion(bf16[2176,3072]{1,0:T(8,128)(2,1)} %fusion.7, bf16[3072,768]{1,0:T(8,128)(2,1)S(1)} %bitcast.211), kind=kOutput, calls=%fused_computation.39 | convolution fusion | flops 10269327360 | bytes 21430272 | tf_op jit(solution)/shard_map/dot_general | solution.py:339
  680.7 15.4 %fusion.19 = bf16[1,3072,768]{2,1,0:T(8,128)(2,1)S(1)} fusion(bf16[2176,3072]{1,0:T(8,128)(2,1)} %get-tuple-element.244, bf16[2176,768]{1,0:T(8,128)(2,1)} %bitcast.252), kind=kOutput, calls=%fused_computation.52 | convolution fusion | flops 10270015488 | bytes 21430272 | tf_op jit(solution)/shard_map/dot_general | solution.py:343
  696.1 17.5 %fusion.18 = bf16[1,3072,768]{2,1,0:T(8,128)(2,1)S(1)} fusion(bf16[2176,3072]{1,0:T(8,128)(2,1)} %fusion.7, bf16[2176,768]{1,0:T(8,128)(2,1)} %bitcast.15), kind=kOutput, calls=%fused_computation.51 | convolution fusion | flops 10270015488 | bytes 21430272 | tf_op jit(solution)/shard_map/dot_general | solution.py:344
  757.1 7.9 multiply_reduce_fusion
  765.0 7.2 multiply_convert_fusion.1
  804.1 7.3 convert_bitcast_fusion.1
  826.3 12.2 %copy.266 = bf16[5,768,768]{2,0,1:T(8,128)(2,1)} copy(bf16[5,768,768]{1,2,0:T(8,128)(2,1)} %pad_maximum_fusion) | data formatting | bytes 11796480 | tf_op jit(solution)/shard_map/concatenate | solution.py:380
  848.1 10.4 collective-permute-start.8
  865.2 156.9 %all-reduce.5 = (f32[768,8]{0,1:T(8,128)S(1)}, f32[6,768]{1,0:T(8,128)S(1)}) all-reduce(f32[768,8]{0,1:T(8,128)S(1)} %fusion.144, f32[6,768]{1,0:T(8,128)S(1)} %stack.94), channel_id=5, replica_groups=mesh['g'=2,'r'=4,'x'=2,'c'=2] {'g','r','x','c'}, use_global_device_ids=true, to_apply=%region_41.43.clone | all-reduce | flops 10752 | bytes 86016
  1035.1 38.8 %all-reduce.4 = (f32[]{:T(128)}, f32[]{:T(128)}) all-reduce(f32[]{:T(128)S(6)} %div.208, f32[]{:T(128)S(6)} %add.348), channel_id=1, replica_groups=mesh['g'=2,'r'=4,'x'=2,'c'=2] {'g','r','x','c'}, use_global_device_ids=true, to_apply=%region_24.25 | all-reduce | flops 2 | bytes 16 | tf_op jit(solution)/shard_map/psum | solution.py:395
  1075.4 8.6 multiply_add_fusion
  (458 shorter events, 284.0 us)
Async XLA Ops:
  7.2 210.3 %all-gather.7.cloned.1.call-start = ((), (), s32[]{:S(2)}) async-start(), calls=%async_computation.6 | async-start | bytes 6082560 | tf_op jit(solution)/shard_map/all_gather | solution.py:211
  13.0 275.3 %collective-permute-start = (bf16[2,384,768]{2,1,0:T(8,128)(2,1)}, bf16[2,384,768]{2,1,0:T(8,128)(2,1)}, u32[]{:S(2)}, u32[]{:S(2)}) collective-permute-start(bf16[2,384,768]{2,1,0:T(8,128)(2,1)} %fusion.69), channel_id=1, source_target_pairs={{0,0},{1,8},{4,4},{5,12},{8,16},{9,24},{12,20},{13,28},{16,1},{17,... | collective-permute-start | bytes 3538952 | tf_op jit(solution)/shard_map/ppermute | solution.py:156
  23.5 264.8 %collective-permute-start.2 = (bf16[2,384,768]{2,1,0:T(8,128)(2,1)}, bf16[2,384,768]{2,1,0:T(8,128)(2,1)}, u32[]{:S(2)}, u32[]{:S(2)}) collective-permute-start(bf16[2,384,768]{2,1,0:T(8,128)(2,1)} %fusion.69), channel_id=1, source_target_pairs={{0,16},{1,24},{4,20},{5,28},{8,0},{9,8},{12,4},{13,12},{16,17},{17... | collective-permute-start | bytes 3538952 | tf_op jit(solution)/shard_map/ppermute | solution.py:156
  24.7 263.6 %collective-permute-start.1 = (bf16[2,384,768]{2,1,0:T(8,128)(2,1)}, bf16[2,384,768]{2,1,0:T(8,128)(2,1)}, u32[]{:S(2)}, u32[]{:S(2)}) collective-permute-start(bf16[2,384,768]{2,1,0:T(8,128)(2,1)} %fusion.66), channel_id=1, source_target_pairs={{0,4},{1,12},{4,16},{5,24},{8,20},{9,28},{12,0},{13,8},{16,5},{17,... | collective-permute-start | bytes 3538952 | tf_op jit(solution)/shard_map/ppermute | solution.py:156
  27.7 260.6 %collective-permute-start.3 = (bf16[2,384,768]{2,1,0:T(8,128)(2,1)}, bf16[2,384,768]{2,1,0:T(8,128)(2,1)}, u32[]{:S(2)}, u32[]{:S(2)}) collective-permute-start(bf16[2,384,768]{2,1,0:T(8,128)(2,1)} %fusion.66), channel_id=1, source_target_pairs={{0,20},{1,28},{4,0},{5,8},{8,4},{9,12},{12,16},{13,24},{16,21},{17... | collective-permute-start | bytes 3538952 | tf_op jit(solution)/shard_map/ppermute | solution.py:156
  274.0 9.2 all-to-all-start
  283.2 52.1 %all-to-all-start.1 = ((bf16[8,272,768]{2,1,0:T(8,128)(2,1)}), bf16[8,272,768]{2,1,0:T(8,128)(2,1)}, u32[]{:S(2)}, u32[]{:S(2)}) async-start(bf16[8,272,768]{2,1,0:T(8,128)(2,1)} %bitcast.216), calls=%async_computation.1 | async-start | bytes 6684672 | tf_op jit(solution)/shard_map/all_to_all | solution.py:174
  291.2 8.0 collective-permute-start.4
  380.3 46.1 %all-to-all-start.2 = ((f32[8,12,768]{2,1,0:T(8,128)}), f32[8,12,768]{2,1,0:T(8,128)}, u32[]{:S(2)}, u32[]{:S(2)}) async-start(f32[8,12,768]{2,1,0:T(8,128)} %fusion.84), calls=%async_computation.2 | async-start | bytes 786432 | tf_op jit(solution)/shard_map/all_to_all | solution.py:174
  561.4 9.8 collective-permute-start.10
  562.7 13.1 %collective-permute-start.11 = (f32[16,768]{1,0:T(8,128)S(1)}, f32[16,768]{1,0:T(8,128)S(1)}, u32[]{:S(2)}, u32[]{:S(2)}) collective-permute-start(f32[16,768]{1,0:T(8,128)S(1)} %fusion), channel_id=1, source_target_pairs={{0,2},{1,3},{2,4},{3,5},{4,6},{5,7},{6,8},{7,9},{8,10},{9,11},{10,... | collective-permute-start | bytes 147464
  567.2 15.1 %collective-permute-start.12 = (f32[16,768]{1,0:T(8,128)S(1)}, f32[16,768]{1,0:T(8,128)S(1)}, u32[]{:S(2)}, u32[]{:S(2)}) collective-permute-start(f32[16,768]{1,0:T(8,128)S(1)} %fusion), channel_id=1, source_target_pairs={{0,3},{1,4},{2,5},{3,6},{4,7},{5,8},{6,9},{7,10},{8,11},{9,12},{10... | collective-permute-start | bytes 147464
  568.5 13.8 %collective-permute-start.13 = (f32[16,768]{1,0:T(8,128)S(1)}, f32[16,768]{1,0:T(8,128)S(1)}, u32[]{:S(2)}, u32[]{:S(2)}) collective-permute-start(f32[16,768]{1,0:T(8,128)S(1)} %fusion), channel_id=1, source_target_pairs={{0,4},{1,5},{2,6},{3,7},{4,8},{5,9},{6,10},{7,11},{8,12},{9,13},{1... | collective-permute-start | bytes 147464
  569.8 12.5 %collective-permute-start.14 = (f32[16,768]{1,0:T(8,128)S(1)}, f32[16,768]{1,0:T(8,128)S(1)}, u32[]{:S(2)}, u32[]{:S(2)}) collective-permute-start(f32[16,768]{1,0:T(8,128)S(1)} %fusion), channel_id=1, source_target_pairs={{0,5},{1,6},{2,7},{3,8},{4,9},{5,10},{6,11},{7,12},{8,13},{9,14},{... | collective-permute-start | bytes 147464
  571.1 11.2 %collective-permute-start.15 = (f32[16,768]{1,0:T(8,128)S(1)}, f32[16,768]{1,0:T(8,128)S(1)}, u32[]{:S(2)}, u32[]{:S(2)}) collective-permute-start(f32[16,768]{1,0:T(8,128)S(1)} %fusion), channel_id=1, source_target_pairs={{0,6},{1,7},{2,8},{3,9},{4,10},{5,11},{6,12},{7,13},{8,14},{9,15},... | collective-permute-start | bytes 147464
  575.8 8.2 collective-permute-start.16
  623.9 51.7 %all-to-all-start.4 = ((f32[8,1,272]{2,1,0:T(1,128)}), f32[8,1,272]{2,1,0:T(1,128)S(1)}, u32[]{:S(2)}, u32[]{:S(2)}) async-start(f32[8,1,272]{2,1,0:T(1,128)} %all_to_all.22), calls=%async_computation.4 | async-start | bytes 24576 | tf_op jit(solution)/shard_map/all_to_all | solution.py:174
  675.6 59.1 %all-to-all-start.3 = ((bf16[8,272,768]{2,1,0:T(8,128)(2,1)}), bf16[8,272,768]{2,1,0:T(8,128)(2,1)}, u32[]{:S(2)}, u32[]{:S(2)}) async-start(bf16[8,272,768]{2,1,0:T(8,128)(2,1)} %bitcast.217), calls=%async_computation.3 | async-start | bytes 6684672 | tf_op jit(solution)/shard_map/all_to_all | solution.py:174
  680.6 348.9 %reduce-scatter.6.cloned.1.call-start = ((), (), s32[]{:S(2)}) async-start(), calls=%async_computation.7 | async-start | bytes 9732096 | tf_op jit(solution)/shard_map/reduce_scatter | solution.py:385
  717.3 121.3 %collective-permute-start.5 = (bf16[2,1536,768]{2,1,0:T(8,128)(2,1)}, bf16[2,1536,768]{2,1,0:T(8,128)(2,1)}, u32[]{:S(2)}, u32[]{:S(2)}) collective-permute-start(bf16[2,1536,768]{2,1,0:T(8,128)(2,1)} %pad_maximum_fusion.1), channel_id=1, source_target_pairs={{0,1},{1,0},{2,3},{3,2},{4,5},{5,4},{6,7},{7,6},{8,9},{9,8},{10,11... | collective-permute-start | bytes 14155784 | tf_op jit(solution)/shard_map/ppermute | solution.py:147
  845.2 178.2 %collective-permute-start.6 = (bf16[2,384,768]{2,1,0:T(8,128)(2,1)}, bf16[2,384,768]{2,1,0:T(8,128)(2,1)}, u32[]{:S(2)}, u32[]{:S(2)}) collective-permute-start(bf16[2,384,768]{2,1,0:T(8,128)(2,1)} %get-tuple-element.208), channel_id=1, source_target_pairs={{4,0},{12,1},{16,4},{24,5},{20,8},{28,9},{0,12},{8,13},{5,16},{13,... | collective-permute-start | bytes 3538952 | tf_op jit(solution)/shard_map/ppermute | solution.py:166
  848.1 175.3 %collective-permute-start.7 = (bf16[2,384,768]{2,1,0:T(8,128)(2,1)}, bf16[2,384,768]{2,1,0:T(8,128)(2,1)}, u32[]{:S(2)}, u32[]{:S(2)}) collective-permute-start(bf16[2,384,768]{2,1,0:T(8,128)(2,1)} %get-tuple-element.207), channel_id=1, source_target_pairs={{20,0},{28,1},{0,4},{8,5},{4,8},{12,9},{16,12},{24,13},{21,16},{29... | collective-permute-start | bytes 3538952 | tf_op jit(solution)/shard_map/ppermute | solution.py:166
  848.1 175.3 %collective-permute-start.8 = (bf16[2,384,768]{2,1,0:T(8,128)(2,1)}, bf16[2,384,768]{2,1,0:T(8,128)(2,1)}, u32[]{:S(2)}, u32[]{:S(2)}) collective-permute-start(bf16[2,384,768]{2,1,0:T(8,128)(2,1)} %get-tuple-element.206), channel_id=1, source_target_pairs={{0,0},{8,1},{4,4},{12,5},{16,8},{24,9},{20,12},{28,13},{1,16},{9,1... | collective-permute-start | bytes 3538952 | tf_op jit(solution)/shard_map/ppermute | solution.py:166
  858.5 164.9 %collective-permute-start.9 = (bf16[2,384,768]{2,1,0:T(8,128)(2,1)}, bf16[2,384,768]{2,1,0:T(8,128)(2,1)}, u32[]{:S(2)}, u32[]{:S(2)}) collective-permute-start(bf16[2,384,768]{2,1,0:T(8,128)(2,1)} %get-tuple-element.209), channel_id=1, source_target_pairs={{16,0},{24,1},{20,4},{28,5},{0,8},{8,9},{4,12},{12,13},{17,16},{25... | collective-permute-start | bytes 3538952 | tf_op jit(solution)/shard_map/ppermute | solution.py:166
  (123 other events, 2886.9 us)
Sparse Core Ops, SparseCore 0:
  11.6 123.7 all-gather.6
  838.7 180.7 reduce-scatter.5

commit v2 on v1

--- a/solution.py
+++ b/solution.py
@@ -1,9 +1,11 @@
 import functools
+import math
 
 import jax
 import jax.numpy as jnp
-import numpy as np
 from jax import lax
+from jax.experimental import pallas as pl
+from jax.experimental.pallas import tpu as pltpu
 from jax.sharding import Mesh
 from jax.sharding import PartitionSpec as P
 
@@ -126,6 +128,513 @@
     )
     stacked = jnp.stack([d_query, d_keys, d_values]).astype(jnp.bfloat16)
     return stacked.reshape(proj_qkv.shape)
+
+
+MESH_ID = pl.DeviceIdType.MESH
+VMEM = pltpu.VMEM
+ANY = pl.ANY
+MIB = 1 << 20
+
+
+def whole(space=None):
+    return pl.BlockSpec(memory_space=space or VMEM)
+
+
+def round_up(value, step):
+    return (value + step - 1) // step * step
+
+
+class Place:
+    def __init__(self, sizes):
+        self.G, self.X = sizes["g"], sizes["x"]
+        self.Z, self.Y = QUAD, sizes["g"]
+        self.chips = self.Z * self.Y * self.X
+        spot = lax.axis_index("g") * QUAD + lax.axis_index("r")
+        self.z, self.y = lax.div(spot, self.Y), lax.rem(spot, self.Y)
+        self.x, self.c = lax.axis_index("x"), lax.axis_index("c")
+        self.g, self.r = lax.axis_index("g"), lax.axis_index("r")
+        self.chip = spot * self.X + self.x
+        self.member = self.x * QUAD + self.r
+
+    def at(self, z=None, y=None, x=None, c=None):
+        spot = (self.z if z is None else z) * self.Y + (self.y if y is None else y)
+        return {
+            "g": lax.div(spot, QUAD),
+            "r": lax.rem(spot, QUAD),
+            "x": self.x if x is None else x,
+            "c": self.c if c is None else c,
+        }
+
+    def of_chip(self, chip):
+        spot = lax.div(chip, self.X)
+        return {
+            "g": lax.div(spot, QUAD),
+            "r": lax.rem(spot, QUAD),
+            "x": lax.rem(chip, self.X),
+            "c": self.c,
+        }
+
+    def of_member(self, member):
+        return {
+            "g": self.g,
+            "r": lax.rem(member, QUAD),
+            "x": lax.div(member, QUAD),
+            "c": self.c,
+        }
+
+    def sibling(self):
+        return self.at(c=1 - self.c)
+
+
+def greet(peers):
+    barrier = pltpu.get_barrier_semaphore()
+    for peer in peers:
+        pl.semaphore_signal(barrier, inc=1, device_id=peer, device_id_type=MESH_ID)
+    pl.semaphore_wait(barrier, len(peers))
+
+
+def send(src, dst, send_sem, recv_sem, peer):
+    return pltpu.make_async_remote_copy(
+        src_ref=src,
+        dst_ref=dst,
+        send_sem=send_sem,
+        recv_sem=recv_sem,
+        device_id=peer,
+        device_id_type=MESH_ID,
+    )
+
+
+def others(me, count):
+    return [lax.rem(me + step, count) for step in range(1, count)]
+
+
+def grid_peers(at):
+    peers = [at.at(z=z) for z in others(at.z, at.Z)]
+    peers += [at.at(y=y) for y in others(at.y, at.Y)]
+    peers += [at.at(x=x) for x in others(at.x, at.X)]
+    return peers + [at.sibling()]
+
+
+def gather_kernel(sizes, rows, mats, dense_ref, tail_ref, w_ref, gain_ref, router_ref, land, *sems):
+    at = Place(sizes)
+    Z, Y, X = at.Z, at.Y, at.X
+    depth = land.shape[4]
+    cut = depth // 2 // 16 * 16
+    first, second = pl.ds(0, cut), pl.ds(cut, depth - cut)
+    z_out, z_in, ya_out, ya_in, xb_out, xb_in, xa_out, xa_in, yb_out, yb_in, c_out, c_in = sems
+    block = jnp.concatenate([dense_ref[...].reshape(mats * rows, -1), tail_ref[...]], 0)
+    if block.shape[0] < depth:
+        block = jnp.pad(block, ((0, depth - block.shape[0]), (0, 0)))
+    mine = land.at[at.c, at.z, at.x, at.y]
+    mine[...] = block.astype(jnp.bfloat16)
+    greet(grid_peers(at))
+    started = []
+
+    def begin(copy):
+        copy.start()
+        started.append(copy)
+
+    order = [at.z] + [lax.rem(at.z + k, Z) for k in (1, 3, 2)]
+    for z in order[1:]:
+        begin(send(mine, mine, z_out.at[z], z_in.at[at.z], at.at(z=z)))
+
+    def one(z):
+        part = land.at[at.c, z, at.x, at.y]
+        for y in others(at.y, Y):
+            begin(send(part.at[first], part.at[first], ya_out.at[z, y], ya_in.at[z, at.y], at.at(y=y)))
+        for x in others(at.x, X):
+            begin(send(part.at[second], part.at[second], xb_out.at[z, x], xb_in.at[z, at.x], at.at(x=x)))
+
+    def two(z):
+        for y in others(at.y, Y):
+            part = land.at[at.c, z, at.x, y, first]
+            send(part, part, ya_out.at[z, y], ya_in.at[z, y], at.at(y=y)).wait_recv()
+        line = land.at[at.c, z, at.x, :, first]
+        for x in others(at.x, X):
+            begin(send(line, line, xa_out.at[z, x], xa_in.at[z, at.x], at.at(x=x)))
+        for x in others(at.x, X):
+            part = land.at[at.c, z, x, at.y, second]
+            send(part, part, xb_out.at[z, x], xb_in.at[z, x], at.at(x=x)).wait_recv()
+        line = land.at[at.c, z, :, at.y, second]
+        for y in others(at.y, Y):
+            begin(send(line, line, yb_out.at[z, y], yb_in.at[z, at.y], at.at(y=y)))
+
+    def three(z):
+        for x in others(at.x, X):
+            line = land.at[at.c, z, x, :, first]
+            send(line, line, xa_out.at[z, x], xa_in.at[z, x], at.at(x=x)).wait_recv()
+        for y in others(at.y, Y):
+            line = land.at[at.c, z, :, y, second]
+            send(line, line, yb_out.at[z, y], yb_in.at[z, y], at.at(y=y)).wait_recv()
+        plane = land.at[at.c, z]
+        begin(send(plane, plane, c_out.at[z], c_in.at[z], at.sibling()))
+
+    for step in range(Z + 2):
+        if step < Z:
+            if step > 0:
+                z = order[step]
+                part = land.at[at.c, z, at.x, at.y]
+                send(part, part, z_out.at[z], z_in.at[z], at.at(z=z)).wait_recv()
+            one(order[step])
+        if 0 <= step - 1 < Z:
+            two(order[step - 1])
+        if 0 <= step - 2 < Z:
+            three(order[step - 2])
+    for z in order:
+        plane = land.at[1 - at.c, z]
+        send(plane, plane, c_out.at[z], c_in.at[z], at.sibling()).wait_recv()
+    for copy in started:
+        copy.wait_send()
+    chips = [(z, y, x) for z in range(Z) for y in range(Y) for x in range(X)]
+    cores = [(c, z, x, y) for z, y, x in chips for c in range(2)]
+    group = 16 // math.gcd(16, rows)
+    for start in range(0, len(cores), group):
+        for mat in range(mats):
+            w_ref[mat, start * rows : (start + group) * rows] = jnp.concatenate(
+                [land[spot][mat * rows : (mat + 1) * rows] for spot in cores[start : start + group]], 0
+            )
+    base, count = mats * rows, tail_ref.shape[0]
+    tails = [land[spot][base : base + count].astype(jnp.float32) for spot in cores]
+    gain_ref[...] = jnp.concatenate([tail[:8, :rows] for tail in tails], 1)
+    router_ref[...] = jnp.concatenate([tail[:, 128 : 128 + rows] for tail in tails], 1)
+
+
+def gather_weights(sizes, dense, tail):
+    mats, rows, width = dense.shape
+    count = tail.shape[0]
+    depth = round_up(mats * rows + count, 16)
+    Z, Y, X = QUAD, sizes["g"], sizes["x"]
+    dma = pltpu.SemaphoreType.DMA
+    by_y, by_x = dma((Z, Y)), dma((Z, X))
+    return pl.pallas_call(
+        functools.partial(gather_kernel, sizes, rows, mats),
+        out_shape=(
+            jax.ShapeDtypeStruct((mats, width, width), jnp.bfloat16),
+            jax.ShapeDtypeStruct((8, width), jnp.float32),
+            jax.ShapeDtypeStruct((count, width), jnp.float32),
+        ),
+        in_specs=[whole()] * 2,
+        out_specs=(whole(),) * 3,
+        scratch_shapes=[VMEM((2, Z, X, Y, depth, width), jnp.bfloat16), dma((Z,)), dma((Z,))]
+        + [by_y, by_y, by_x, by_x, by_x, by_x, by_y, by_y, dma((Z,)), dma((Z,))],
+        compiler_params=pltpu.CompilerParams(
+            collective_id=1, has_side_effects=True, vmem_limit_bytes=48 * MIB
+        ),
+        name="gather_weights",
+    )(dense, tail)
+
+
+def scatter_kernel(sizes, g_ref, out_ref, hold, sib, got_xa, got_yb, got_ya, got_xb, got_z, *sems):
+    at = Place(sizes)
+    Z, Y, X = at.Z, at.Y, at.X
+    depth = g_ref.shape[4]
+    cut = depth // 2 // 16 * 16
+    first, second = pl.ds(0, cut), pl.ds(cut, depth - cut)
+    c_out, c_in, xa_out, xa_in, yb_out, yb_in, ya_out, ya_in, xb_out, xb_in, z_out, z_in = sems
+    greet(grid_peers(at))
+    started = []
+
+    def begin(copy):
+        copy.start()
+        started.append(copy)
+
+    wide = lambda value: value.astype(jnp.float32)
+    order = [lax.rem(at.z + k, Z) for k in (2, 1, 3)] + [at.z]
+    for z in order:
+        begin(send(g_ref.at[1 - at.c, z], sib.at[z], c_out.at[z], c_in.at[z], at.sibling()))
+
+    def one(z):
+        send(sib.at[z], sib.at[z], c_out.at[z], c_in.at[z], at.sibling()).wait_recv()
+        hold[z] = (wide(g_ref[at.c, z]) + wide(sib[z])).astype(jnp.bfloat16)
+        for x in others(at.x, X):
+            begin(send(hold.at[z, x, :, first], got_xa.at[z, at.x], xa_out.at[z, x], xa_in.at[z, at.x], at.at(x=x)))
+        for y in others(at.y, Y):
+            begin(send(hold.at[z, :, y, second], got_yb.at[z, at.y], yb_out.at[z, y], yb_in.at[z, at.y], at.at(y=y)))
+
+    def two(z):
+        total = wide(hold[z, at.x, :, first])
+        for x in others(at.x, X):
+            send(got_xa.at[z, x], got_xa.at[z, x], xa_out.at[z, x], xa_in.at[z, x], at.at(x=x)).wait_recv()
+            total = total + wide(got_xa[z, x])
+        hold[z, at.x, :, first] = total.astype(jnp.bfloat16)
+        for y in others(at.y, Y):
+            begin(send(hold.at[z, at.x, y, first], got_ya.at[z, at.y], ya_out.at[z, y], ya_in.at[z, at.y], at.at(y=y)))
+        total = wide(hold[z, :, at.y, second])
+        for y in others(at.y, Y):
+            send(got_yb.at[z, y], got_yb.at[z, y], yb_out.at[z, y], yb_in.at[z, y], at.at(y=y)).wait_recv()
+            total = total + wide(got_yb[z, y])
+        hold[z, :, at.y, second] = total.astype(jnp.bfloat16)
+        for x in others(at.x, X):
+            begin(send(hold.at[z, x, at.y, second], got_xb.at[z, at.x], xb_out.at[z, x], xb_in.at[z, at.x], at.at(x=x)))
+
+    def three(z, last):
+        total = wide(hold[z, at.x, at.y, first])
+        for y in others(at.y, Y):
+            send(got_ya.at[z, y], got_ya.at[z, y], ya_out.at[z, y], ya_in.at[z, y], at.at(y=y)).wait_recv()
+            total = total + wide(got_ya[z, y])
+        rest = wide(hold[z, at.x, at.y, second])
+        for x in others(at.x, X):
+            send(got_xb.at[z, x], got_xb.at[z, x], xb_out.at[z, x], xb_in.at[z, x], at.at(x=x)).wait_recv()
+            rest = rest + wide(got_xb[z, x])
+        if last:
+            out_ref[first] = total
+            out_ref[second] = rest
+            return
+        mine = hold.at[z, at.x, at.y]
+        mine[first] = total.astype(jnp.bfloat16)
+        mine[second] = rest.astype(jnp.bfloat16)
+        begin(send(mine, got_z.at[at.z], z_out.at[z], z_in.at[at.z], at.at(z=z)))
+
+    for step in range(Z + 2):
+        if step < Z:
+            one(order[step])
+        if 0 <= step - 1 < Z:
+            two(order[step - 1])
+        if 0 <= step - 2 < Z:
+            three(order[step - 2], step - 2 == Z - 1)
+    for z in order[:-1]:
+        send(got_z.at[z], got_z.at[z], z_out.at[z], z_in.at[z], at.at(z=z)).wait_recv()
+        out_ref[...] += wide(got_z[z])
+    for copy in started:
+        copy.wait_send()
+
+
+def scatter_dense(sizes, blocks):
+    unused, Z, X, Y, depth, width = blocks.shape
+    dma = pltpu.SemaphoreType.DMA
+    by_y, by_x, by_z = dma((Z, Y)), dma((Z, X)), dma((Z,))
+    cut = depth // 2 // 16 * 16
+    half = jnp.bfloat16
+    return pl.pallas_call(
+        functools.partial(scatter_kernel, sizes),
+        out_shape=jax.ShapeDtypeStruct((depth, width), jnp.float32),
+        in_specs=[whole()],
+        out_specs=whole(),
+        scratch_shapes=[
+            VMEM((Z, X, Y, depth, width), half),
+            VMEM((Z, X, Y, depth, width), half),
+            VMEM((Z, X, Y, cut, width), half),
+            VMEM((Z, Y, X, depth - cut, width), half),
+            VMEM((Z, Y, cut, width), half),
+            VMEM((Z, X, depth - cut, width), half),
+            VMEM((Z, depth, width), half),
+        ]
+        + [by_z, by_z, by_x, by_x, by_y, by_y, by_y, by_y, by_x, by_x, by_z, by_z],
+        compiler_params=pltpu.CompilerParams(
+            collective_id=2, has_side_effects=True, vmem_limit_bytes=48 * MIB
+        ),
+        name="scatter_dense",
+    )(blocks)
+
+
+def sums_kernel(sizes, in_ref, out_ref, land, out_sem, in_sem):
+    at = Place(sizes)
+    count = 2 * at.chips
+    me = at.chip * 2 + at.c
+    ids = others(me, count)
+
+    def peer(device):
+        spot = at.of_chip(lax.div(device, 2))
+        spot["c"] = lax.rem(device, 2)
+        return spot
+
+    greet([peer(device) for device in ids])
+    land[me] = in_ref[...]
+    copies = [send(in_ref, land.at[me], out_sem.at[d], in_sem.at[me], peer(d)) for d in ids]
+    for copy in copies:
+        copy.start()
+    for d in ids:
+        send(land.at[d], land.at[d], out_sem.at[d], in_sem.at[d], peer(d)).wait_recv()
+    out_ref[...] = jnp.sum(land[...], 0)
+    for copy in copies:
+        copy.wait_send()
+
+
+def share_sums(sizes, values):
+    count = sizes["g"] * QUAD * sizes["x"] * 2
+    dma = pltpu.SemaphoreType.DMA
+    return pl.pallas_call(
+        functools.partial(sums_kernel, sizes),
+        out_shape=jax.ShapeDtypeStruct(values.shape, jnp.float32),
+        in_specs=[whole()],
+        out_specs=whole(),
+        scratch_shapes=[VMEM((count, *values.shape), jnp.float32), dma((count,)), dma((count,))],
+        compiler_params=pltpu.CompilerParams(collective_id=3, has_side_effects=True),
+        name="share_sums",
+    )(values)
+
+
+IMAGE_PAD = 16
+
+
+def split_three(value):
+    high = value.astype(jnp.bfloat16)
+    rest = value - high.astype(jnp.float32)
+    middle = rest.astype(jnp.bfloat16)
+    return high, middle, (rest - middle.astype(jnp.float32)).astype(jnp.bfloat16)
+
+
+def dot_f32(left, right, dims):
+    return lax.dot_general(left, right, (dims, ((), ())), preferred_element_type=jnp.float32)
+
+
+NN = ((1,), (0,))
+NT = ((1,), (1,))
+TN = ((0,), (0,))
+
+
+def norm_parts(values):
+    centre = values - jnp.mean(values, -1, keepdims=True)
+    spread = jnp.mean(centre * centre, -1, keepdims=True)
+    scale = lax.rsqrt(spread + eps_norm)
+    return centre * scale, scale
+
+
+def norm_back(d_out, scaled, scale, gain):
+    pulled = d_out * gain
+    return scale * (
+        pulled
+        - jnp.mean(pulled, -1, keepdims=True)
+        - scaled * jnp.mean(pulled * scaled, -1, keepdims=True)
+    )
+
+
+def head_kernel(
+    sizes, images, part_ref, own_ref, imp_ref, gain_ref, head_ref, label_ref,
+    g_head_ref, d_pool_ref, own_d_ref, g_norm_ref, sums_ref, total_imp_ref,
+    in_part, rows, d_rows, d_sib, d_sum, d_in, head_b, labels, d_logits, *sems
+):
+    at = Place(sizes)
+    chips, members = at.chips, QUAD * at.X
+    devices = 2 * chips
+    p_out, p_in, r_out, r_in, s_out, s_in, d_out, d_in_sem, b_out, b_in = sems
+    width = own_ref.shape[1]
+    same_core = others(at.chip, chips)
+    greet([at.of_chip(chip) for chip in same_core] + [at.sibling()])
+    started = []
+
+    def begin(copy):
+        copy.start()
+        started.append(copy)
+
+    team = others(at.member, members)
+    for member in team:
+        begin(send(part_ref.at[member], in_part.at[at.member], p_out.at[member], p_in.at[at.member], at.of_member(member)))
+    in_part[at.member] = part_ref[at.member]
+    head_b[...] = head_ref[...].astype(jnp.bfloat16)
+    wide = devices * IMAGE_PAD
+    spot = lax.broadcasted_iota(jnp.int32, (label_ref.shape[1], wide), 1)
+    given = lax.broadcasted_iota(jnp.int32, (label_ref.shape[1], wide), 0)
+    image = lax.rem(spot, IMAGE_PAD)
+    device = lax.rem(lax.div(spot, IMAGE_PAD), chips) * 2 + lax.div(spot, IMAGE_PAD * chips)
+    chosen = ((device * images + image == given) & (image < images)).astype(jnp.bfloat16)
+    labels[...] = dot_f32(label_ref[...].astype(jnp.float32).astype(jnp.bfloat16), chosen, NN).astype(jnp.bfloat16)
+    for member in team:
+        send(in_part.at[member], in_part.at[member], p_out.at[member], p_in.at[member], at.of_member(member)).wait_recv()
+    pooled = own_ref[...] + jnp.sum(in_part[...], 0)
+    scaled, scale = norm_parts(pooled)
+    gain, shift = gain_ref[2:3], gain_ref[5:6]
+    a_three = scaled * gain + shift
+    row = lax.broadcasted_iota(jnp.int32, (IMAGE_PAD, width), 0)
+    block = jnp.where(row < images, a_three, 0.0)
+    pieces = split_three(imp_ref[...])
+    for index, piece in enumerate(pieces):
+        block = jnp.where(row == images + index, piece.astype(jnp.float32), block)
+    rows[at.c, at.chip] = block.astype(jnp.bfloat16)
+    mine = rows.at[at.c, at.chip]
+    for chip in same_core:
+        begin(send(mine, mine, r_out.at[chip], r_in.at[at.chip], at.of_chip(chip)))
+    for chip in same_core:
+        part = rows.at[at.c, chip]
+        send(part, part, r_out.at[chip], r_in.at[chip], at.of_chip(chip)).wait_recv()
+    begin(send(rows.at[at.c], rows.at[at.c], s_out.at[0], s_in.at[0], at.sibling()))
+    send(rows.at[1 - at.c], rows.at[1 - at.c], s_out.at[0], s_in.at[0], at.sibling()).wait_recv()
+    gathered = rows[...].reshape(wide, width)
+    in_block = lax.rem(lax.broadcasted_iota(jnp.int32, (wide, width), 0), IMAGE_PAD)
+    total = jnp.sum(jnp.where(in_block >= images, gathered.astype(jnp.float32), 0.0), 0, keepdims=True)
+    total_imp_ref[...] = jnp.broadcast_to(total, total_imp_ref.shape)
+    gathered = jnp.where(in_block < images, gathered.astype(jnp.float32), 0.0).astype(jnp.bfloat16)
+    logits = dot_f32(head_b[...], gathered, NT)
+    image = lax.rem(lax.broadcasted_iota(jnp.int32, logits.shape, 1), IMAGE_PAD)
+    count = devices * images
+    target = labels[...].astype(jnp.float32)
+    power = jnp.exp(-jnp.abs(logits))
+    loss = jnp.maximum(logits, 0.0) + jnp.log1p(power) - target * logits
+    loss = jnp.sum(jnp.where(image < images, loss, 0.0), 1, keepdims=True)
+    loss = jnp.sum(loss, 0, keepdims=True) / count
+    sums_ref[...] = jnp.broadcast_to(loss, sums_ref.shape)
+    chance = jnp.where(logits >= 0.0, 1.0, power) / (1.0 + power)
+    d_logits[...] = jnp.where(image < images, (chance - target) / count, 0.0).astype(jnp.bfloat16)
+    partial = dot_f32(d_logits[...], head_b[...], TN)
+    d_rows[...] = partial.reshape(d_rows.shape).astype(jnp.bfloat16)
+    begin(send(d_rows.at[1 - at.c], d_sib, s_out.at[1], s_in.at[1], at.sibling()))
+    g_head_ref[...] = dot_f32(d_logits[...], gathered, NN)
+    send(d_sib, d_sib, s_out.at[1], s_in.at[1], at.sibling()).wait_recv()
+    d_sum[...] = (d_rows[at.c].astype(jnp.float32) + d_sib[...].astype(jnp.float32)).astype(jnp.bfloat16)
+    for chip in same_core:
+        begin(send(d_sum.at[chip], d_in.at[at.chip], d_out.at[chip], d_in_sem.at[at.chip], at.of_chip(chip)))
+    d_in[at.chip] = d_sum[at.chip]
+    for chip in same_core:
+        send(d_in.at[chip], d_in.at[chip], d_out.at[chip], d_in_sem.at[chip], at.of_chip(chip)).wait_recv()
+    d_norm = jnp.sum(d_in[...].astype(jnp.float32), 0)
+    d_norm = jnp.where(row < images, d_norm, 0.0)
+    d_pooled = norm_back(d_norm, scaled, scale, gain)
+    d_pooled = jnp.where(row < images, d_pooled, 0.0)
+    d_gain = jnp.sum(d_norm * scaled, 0, keepdims=True)
+    d_shift = jnp.sum(d_norm, 0, keepdims=True)
+    line = lax.broadcasted_iota(jnp.int32, g_norm_ref.shape, 0)
+    g_norm_ref[...] = jnp.where(line == 2, d_gain, jnp.where(line == 5, d_shift, 0.0))
+    own_d_ref[...] = d_pooled
+    d_pool_ref[at.member] = d_pooled
+    mine = d_pool_ref.at[at.member]
+    for member in team:
+        begin(send(own_d_ref, mine, b_out.at[member], b_in.at[at.member], at.of_member(member)))
+    for member in team:
+        part = d_pool_ref.at[member]
+        send(part, part, b_out.at[member], b_in.at[member], at.of_member(member)).wait_recv()
+    for copy in started:
+        copy.wait_send()
+
+
+def head_step(sizes, images, part, own, imp, gains, head, label):
+    members = QUAD * sizes["x"]
+    chips = members * sizes["g"]
+    classes, width = head.shape
+    wide = 2 * chips * IMAGE_PAD
+    dma = pltpu.SemaphoreType.DMA
+    by_member, by_chip = dma((members,)), dma((chips,))
+    f32, half = jnp.float32, jnp.bfloat16
+    blocks = (chips, IMAGE_PAD, width)
+    return pl.pallas_call(
+        functools.partial(head_kernel, sizes, images),
+        out_shape=(
+            jax.ShapeDtypeStruct((classes, width), f32),
+            jax.ShapeDtypeStruct((members, IMAGE_PAD, width), f32),
+            jax.ShapeDtypeStruct((IMAGE_PAD, width), f32),
+            jax.ShapeDtypeStruct((8, width), f32),
+            jax.ShapeDtypeStruct((8, 128), f32),
+            jax.ShapeDtypeStruct((8, width), f32),
+        ),
+        in_specs=[whole()] * 6,
+        out_specs=(whole(),) * 6,
+        scratch_shapes=[
+            VMEM((members, IMAGE_PAD, width), f32),
+            VMEM((2, *blocks), half),
+            VMEM((2, *blocks), half),
+            VMEM(blocks, half),
+            VMEM(blocks, half),
+            VMEM(blocks, half),
+            VMEM((classes, width), half),
+            VMEM((classes, wide), half),
+            VMEM((classes, wide), half),
+        ]
+        + [by_member, by_member, by_chip, by_chip, dma((2,)), dma((2,)), by_chip, by_chip]
+        + [by_member, by_member],
+        compiler_params=pltpu.CompilerParams(
+            collective_id=4, has_side_effects=True, vmem_limit_bytes=56 * MIB
+        ),
+        name="head_step",
+    )(part, own, imp, gains, head, label)
 
 
 def shard_moves(n_blocks):
@@ -207,21 +716,23 @@
     head_average,
 ):
     n_blocks = lax.axis_size("g")
-    layer_b, router_b, norm_b = (
-        lax.all_gather(dense_weights.astype(jnp.bfloat16), ALL, axis=1, tiled=True),
-        lax.all_gather(router_weights.astype(jnp.bfloat16), ALL, axis=0, tiled=True),
-        lax.all_gather(norm_params.astype(jnp.bfloat16), ALL, axis=1, tiled=True),
-    )
-    own_chunks = fetch_experts(expert_in, expert_out, n_blocks)
+    sizes = {name: lax.axis_size(name) for name in ALL}
+    rows_own, n_experts = router_weights.shape
+    n_tail = max(8, n_experts)
+    tail = jnp.zeros((n_tail, dense_weights.shape[2]), jnp.float32)
+    tail = tail.at[:6, :rows_own].set(norm_params)
+    tail = tail.at[:n_experts, 128 : 128 + rows_own].set(router_weights.T)
+    layer_b, gain_rows, router_t = gather_weights(sizes, dense_weights, tail)
+    router_b = router_t[:n_experts].T.astype(jnp.bfloat16)
+    expert_in_now, expert_out_now, layer_b = lax.optimization_barrier((expert_in, expert_out, layer_b))
+    own_chunks = fetch_experts(expert_in_now, expert_out_now, n_blocks)
     own_half = jnp.stack(own_chunks, 1)
     other_half = swap_cores(own_half)
     w_one = jnp.concatenate([own_half[0], other_half[0]], 0)
     w_two = jnp.concatenate([own_half[1], other_half[1]], 0)
-    gain_rows = norm_b.astype(jnp.float32)
     rows_here, n_slots_row = slot_mask.shape
     tokens = rows_here * n_slots_row
     model_width = layer_b.shape[2]
-    n_experts = router_weights.shape[1]
     n_images = lengths.shape[0] * lengths.shape[1]
     capacity = (21 * tokens * TOP + 20 * n_experts - 1) // (20 * n_experts)
     padded = (capacity + 15) // 16 * 16
@@ -255,7 +766,7 @@
     x_one = x_zero + jnp.dot(att_out, layer_b[4], preferred_element_type=jnp.float32)
     a_two = layer_norm(x_one, gain_rows[1], gain_rows[4]).astype(jnp.bfloat16)
     router_probs = softmax_rows(jnp.dot(a_two, router_b, preferred_element_type=jnp.float32))
-    importance = lax.psum(jnp.sum(router_probs * valid_flat[:, None], 0), ALL)
+    part_importance = jnp.sum(router_probs * valid_flat[:, None], 0)
     pick_one = expert_picks[:, 0]
     pick_two = expert_picks[:, 1]
     columns = jnp.arange(n_experts, dtype=jnp.int32)
@@ -299,38 +810,30 @@
         x_one.reshape(rows_here, n_slots_row, model_width),
         precision=high_prec,
     ).reshape(-1, model_width)
-    pooled = pooled + jnp.sum(to_members(part_pooled), 0)
-    gathered = lax.all_gather(
-        layer_norm(pooled, gain_rows[2], gain_rows[5]).astype(jnp.bfloat16),
-        ALL,
-        axis=0,
-        tiled=True,
-    )
-    head_b = head_weights.astype(jnp.bfloat16)
-    logits = jnp.dot(head_b, gathered.T, preferred_element_type=jnp.float32)
-    labels = class_labels.astype(jnp.float32)
-    n_images_all = gathered.shape[0]
-    local_loss = jnp.sum(jnp.logaddexp(logits, 0.0) - labels * logits) / n_images_all
+    pad_rows = ((0, IMAGE_PAD - n_images), (0, 0))
+    g_head, d_pooled_all, d_pooled, g_norm_three, local_loss, importance = head_step(
+        sizes,
+        n_images,
+        jnp.pad(part_pooled, ((0, 0), *pad_rows)),
+        jnp.pad(pooled, pad_rows),
+        jnp.pad(part_importance, (0, model_width - n_experts))[None],
+        gain_rows,
+        head_weights,
+        class_labels,
+    )
+    importance = importance[0, :n_experts]
+    local_loss = local_loss[0, 0]
+    d_pooled_all = d_pooled_all[:, :n_images]
+    d_pooled = d_pooled[:n_images]
     centre = jnp.mean(importance)
     spread = jnp.mean((importance - centre) ** 2)
     d_imp = aux_weight * (
         2.0 * (importance - centre) / (n_experts * centre * centre)
         - 2.0 * spread / (n_experts * centre * centre * centre)
     )
-    d_logits = ((jax.nn.sigmoid(logits) - labels) / n_images_all).astype(jnp.bfloat16)
-    g_head = jnp.dot(d_logits, gathered, preferred_element_type=jnp.float32)
-    d_rows = lax.psum_scatter(
-        jnp.dot(d_logits.T, head_b, preferred_element_type=jnp.float32),
-        ALL,
-        scatter_dimension=0,
-        tiled=True,
-    )
-    unused_out, norm_back = jax.vjp(layer_norm, pooled, gain_rows[2], gain_rows[5])
-    d_pooled, g_gain_three, g_shift_three = norm_back(d_rows)
     d_two = jnp.einsum(
         "ris,rid->rsd", pooling, d_pooled.reshape(rows_here, -1, model_width), precision=high_prec
     ).reshape(tokens, model_width)
-    d_pooled_all = lax.all_gather(d_pooled, MEMBERS, axis=0)
     d_two_slots = jnp.einsum("dsi,diw->dsw", image_hot, d_pooled_all, precision=high_prec)
     slot_d_gate = jnp.sum(d_two_slots * result, -1)
     d_all = (d_two_slots * got_gate[:, :, None]).astype(jnp.bfloat16).reshape(n_slots, model_width)
@@ -378,21 +881,32 @@
     d_x_zero = (d_x_zero + d_x_one).astype(jnp.bfloat16)
     g_embed = jnp.dot(patches.T, d_x_zero, preferred_element_type=jnp.float32)
     g_layers = jnp.concatenate([g_embed[None], g_qkv, g_out_proj[None]], 0)
-    g_norms = jnp.stack(
-        [g_gain_one, g_gain_two, g_gain_three, g_shift_one, g_shift_two, g_shift_three]
-    )
-    g_layers, g_router, g_norms = (
-        lax.psum_scatter(
-            g_layers.astype(jnp.bfloat16), ALL, scatter_dimension=1, tiled=True
-        ).astype(jnp.float32),
-        lax.psum_scatter(g_router, ALL, scatter_dimension=0, tiled=True),
-        lax.psum_scatter(g_norms, ALL, scatter_dimension=1, tiled=True),
-    )
+    zero = jnp.zeros_like(g_gain_one)
+    g_norms = g_norm_three[:6] + jnp.stack(
+        [g_gain_one, g_gain_two, zero, g_shift_one, g_shift_two, zero]
+    )
+    def spread_rows(value):
+        value = value.reshape(value.shape[0], QUAD, n_blocks, sizes["x"], 2, rows_own, -1)
+        return value.transpose(4, 1, 3, 2, 0, 5, 6)
+
+    blocks = spread_rows(g_layers.astype(jnp.bfloat16))
+    blocks = blocks.reshape(*blocks.shape[:4], -1, model_width)
+    small = jnp.concatenate([g_norms, g_router.T], 0).astype(jnp.bfloat16)
+    small = spread_rows(small[..., None])[..., 0]
+    n_dense, n_small = blocks.shape[4], small.shape[4]
+    depth = round_up(n_dense + n_small, 16)
+    small = jnp.pad(small, ((0, 0),) * 4 + ((0, depth - n_dense - n_small), (0, model_width - rows_own)))
+    reduced = scatter_dense(sizes, jnp.concatenate([blocks, small], 4))
+    g_layers = reduced[:n_dense].reshape(-1, rows_own, model_width)
+    g_norms = reduced[n_dense : n_dense + 6, :rows_own]
+    g_router = reduced[n_dense + 6 : n_dense + n_small, :rows_own].T
     squares = (
         jnp.sum(g_layers * g_layers) + jnp.sum(g_router * g_router) + jnp.sum(g_norms * g_norms)
     )
     squares = squares + jnp.sum(g_one * g_one) + jnp.sum(g_two * g_two) + jnp.sum(g_head * g_head)
-    loss_sum, square_sum = lax.psum((local_loss, squares), ALL)
+    line = lax.broadcasted_iota(jnp.int32, (8, 128), 0)
+    all_sums = share_sums(sizes, jnp.where(line == 0, local_loss, squares))
+    loss_sum, square_sum = all_sums[0, 0], all_sums[1, 0]
     grad_norm = jnp.sqrt(square_sum)
     factor = jnp.minimum(1.0, clip_limit / grad_norm)
     loss_value = loss_sum + aux_weight * spread / (centre * centre)

time: 1120 us -> 673 us (0.60)
  blocking collectives: 563 us -> 0 us
  Pallas kernels: 0 us -> 143 us
  between operations: 28.6 us -> 14.6 us
  matrix products: 223 us -> 211 us
    all_gather x4 -> x0, blocking collectives: 253 us -> none  [the longest x1 110 us: body(): lax.all_gather(norm_params.astype(jnp.bfloat16), ALL, axis=1, tiled=True)]
    unnamed x2 -> x0, blocking collectives: 231 us -> none
    pallas_call x0 -> x4, Pallas kernels: none -> 143 us  [the longest x1 44.7 us: scatter_dense(): pl.pallas_call(functools.partial(scatter_kernel, sizes), out_shape=jax.Sh...]
    psum x2 -> x0, blocking collectives: 79.4 us -> none  [the longest x1 40.6 us: body(): importance = lax.psum(jnp.sum(router_probs * valid_flat[:, None], 0), ALL)]
    ppermute x2, starting transfers between devices: 0.07 us -> 19.7 us  [swap_cores(): return lax.ppermute(value, 'c', [(0, 1), (1, 0)])]
    unnamed x8 -> x0, starting transfers between devices: 18.9 us -> none
    all_to_all x5 -> x4, waiting for transfers between devices: 30.5 us -> 36.8 us  [to_members(): lax.all_to_all(value, MEMBERS, split_axis=0, concat_axis=0, tiled=True)]
  transfers between devices with their start and end apart: 25 -> 14, of which waited for: 3 -> 3; matrix products, arithmetic and copies ran while one was open for 27% -> 35% of each run, Pallas kernels for 0% -> 7%
where the time goes in v2:
time: 673 us; the launch traced here: 667 us
  matrix products  211 us (31%)
  Pallas kernels  143 us (21%)
  local copies, waits for them, and re-layouts  102 us (15%)
  other arithmetic  93.8 us (14%)
  starting transfers between devices  65.7 us (10%)
  waiting for transfers between devices  36.8 us (5%)
  between operations  14.6 us (2%)
    pallas_call x1, Pallas kernels, scatter_dense(): pl.pallas_call(functools.partial(scatter_kernel, sizes), out_shape=jax.Sh...  44.7 us
    pallas_call x1, Pallas kernels, gather_weights(): pl.pallas_call(functools.partial(gather_kernel, sizes, rows, mats), out_s...  44.6 us
    pallas_call x1, Pallas kernels, head_step(): pl.pallas_call(functools.partial(head_kernel, sizes, images), out_shape=(...  41.8 us
    all_to_all x4, waiting for transfers between devices, to_members(): lax.all_to_all(value, MEMBERS, split_axis=0, concat_axis=0, tiled=True)  36.8 us
    dot_general x1, matrix products, body(): d_act = jnp.dot(d_all, w_two.T, preferred_element_type=jnp.float32)  34.7 us
    dot_general x1, matrix products, body(): hidden = jnp.dot(rows_all, w_one.T, preferred_element_type=jnp.float32)  25.6 us
    add x6, other arithmetic, adam_update(): polyak_decay * average_state + (1.0 - polyak_decay) * weight_new  21.1 us
    ppermute x2, starting transfers between devices, swap_cores(): return lax.ppermute(value, 'c', [(0, 1), (1, 0)])  19.7 us
  transfers between devices with their start and end apart: 14, of which 3 were waited for; matrix products, arithmetic and copies ran while one was open for 35% of the time, Pallas kernels for 7%

profile of v2, /device:TPU:0, one launch (start us, length us, event | category | flops | bytes accessed | tf_op | source)
XLA Modules:
  0.0 666.5 jit_solution(738579439797036710)
XLA Ops:
  4.5 44.6 %gather_weights.1 = (bf16[5,768,768]{2,1,0:T(8,128)(2,1)}, f32[8,768]{1,0:T(8,128)S(1)}, f32[8,768]{1,0:T(8,128)S(1)}) custom-call(f32[5,24,768]{2,1,0:T(8,128)S(1)} %copy-done.1, f32[8,768]{1,0:T(8,128)S(1)} %scatter.9.tail_ref), custom_call_target="tpu_custom_call" | custom-call | tf_op jit(solution)/shard_map/gather_weights/pallas_call | solution.py:309
  53.0 10.6 %collective-permute-start = (bf16[2,384,768]{2,1,0:T(8,128)(2,1)}, bf16[2,384,768]{2,1,0:T(8,128)(2,1)}, u32[]{:S(2)}, u32[]{:S(2)}) collective-permute-start(bf16[2,384,768]{2,1,0:T(8,128)(2,1)} %fusion.74), channel_id=1, source_target_pairs={{0,0},{1,8},{4,4},{5,12},{8,16},{9,24},{12,20},{13,28},{16,1},{17,... | collective-permute-start | bytes 3538952 | tf_op jit(solution)/shard_map/ppermute | solution.py:665
  128.1 10.5 %all-to-all-done = f32[8,3,272]{2,1,0:T(4,128)S(1)} async-done(((f32[8,3,272]{2,1,0:T(4,128)}), f32[8,3,272]{2,1,0:T(4,128)S(1)}, u32[]{:S(2)}, u32[]{:S(2)}) %all-to-all-start) | async-done | bytes 26144 | tf_op jit(solution)/shard_map/all_to_all | solution.py:683
  149.5 19.7 %collective-permute-start.4 = (bf16[2,4,384,768]{3,2,1,0:T(8,128)(2,1)}, bf16[2,4,384,768]{3,2,1,0:T(8,128)(2,1)}, u32[]{:S(2)}, u32[]{:S(2)}) collective-permute-start(bf16[2,4,384,768]{3,2,1,0:T(8,128)(2,1)} %copy.195), channel_id=1, source_target_pairs={{0,1},{1,0},{2,3},{3,2},{4,5},{5,4},{6,7},{7,6},{8,9},{9,8},{10,11... | collective-permute-start | bytes 14155784 | tf_op jit(solution)/shard_map/ppermute | solution.py:656
  188.7 10.2 %all-to-all-done.1 = bf16[8,272,768]{2,1,0:T(8,128)(2,1)} async-done(((bf16[8,272,768]{2,1,0:T(8,128)(2,1)}), bf16[8,272,768]{2,1,0:T(8,128)(2,1)}, u32[]{:S(2)}, u32[]{:S(2)}) %all-to-all-start.1) | async-done | bytes 3342368 | tf_op jit(solution)/shard_map/all_to_all | solution.py:683
  198.9 25.6 %multiply_convert_fusion = (bf16[2176,3072]{1,0:T(8,128)(2,1)}, f32[2176,3072]{1,0:T(8,128)}) fusion(bf16[2176,768]{1,0:T(8,128)(2,1)} %bitcast.12, bf16[3072,768]{1,0:T(8,128)(2,1)} %bitcast.236), kind=kOutput, calls=%fused_computation.11 | convolution fusion | flops 10327818240 | bytes 48168960 | tf_op jit(solution)/shard_map/dot_general | solution.py:800
  224.5 15.2 %convolution_convert_fusion.3 = bf16[2176,768]{1,0:T(8,128)(2,1)S(1)} fusion(bf16[2176,3072]{1,0:T(8,128)(2,1)} %get-tuple-element.170, bf16[3072,768]{1,0:T(8,128)(2,1)} %bitcast.238), kind=kOutput, calls=%fused_computation.43 | convolution fusion | flops 10269327360 | bytes 21430272 | tf_op jit(solution)/shard_map/dot_general | solution.py:802
  242.4 41.8 %head_step.1 = (f32[576,768]{1,0:T(8,128)}, f32[8,16,768]{2,1,0:T(8,128)}, f32[16,768]{1,0:T(8,128)}, f32[8,768]{1,0:T(8,128)}, f32[8,128]{1,0:T(8,128)}, /*index=5*/f32[8,768]{1,0:T(8,128)}) custom-call(f32[8,16,768]{2,1,0:T(8,128)} %pad.24.part_ref, f32[16,768]{1,0:T(8,128)} %pad.25.own_ref, f32[1,768]{1,0:T(1,128)} %broadcast_in_dim.74.imp_ref, ...), custom_call_target="tpu_custom_call" | custom-call | tf_op jit(solution)/shard_map/head_step/pallas_call | solution.py:608
  284.2 8.1 %multiply_convert_fusion.2 = (bf16[8,272,768]{2,1,0:T(8,128)(2,1)S(1)}, f32[8,272]{1,0:T(8,128)S(1)}) fusion(f32[8,272]{1,0:T(8,128)S(1)} %bitcast.269, bf16[8,272,768]{2,1,0:T(8,128)(2,1)S(1)} %bitcast.244, f32[8,16,768]{2,1,0:T(8,128)} %get-tuple-element.71, f32[8,272]{1,0:T(8,128)S(1)} %bitcast.271, f32[8,272]{1,0:T(8,128)S(1)} %bitcast.273, ...), kind=kOutput, calls=%fused_computation.35 | convolution fusion | flops 249054080 | bytes 7112752 | tf_op jit(solution)/shard_map/dsi,diw->dsw/dot_general | solution.py:837
  292.4 15.6 %fusion.20 = bf16[1,3072,768]{2,1,0:T(8,128)(2,1)S(1)} fusion(bf16[2176,3072]{1,0:T(8,128)(2,1)} %get-tuple-element.170, bf16[2176,768]{1,0:T(8,128)(2,1)S(1)} %bitcast.279), kind=kOutput, calls=%fused_computation.55 | convolution fusion | flops 10270015488 | bytes 21430272 | tf_op jit(solution)/shard_map/dot_general | solution.py:846
  308.0 34.7 %fusion.6 = bf16[2176,3072]{1,0:T(8,128)(2,1)} fusion(f32[2176,3072]{1,0:T(8,128)} %get-tuple-element.171, bf16[2176,768]{1,0:T(8,128)(2,1)} %bitcast.280, bf16[3072,768]{1,0:T(8,128)(2,1)} %bitcast.239), kind=kOutput, calls=%fused_computation.10 | convolution fusion | flops 10401349632 | bytes 48168960 | tf_op jit(solution)/shard_map/dot_general | solution.py:840
  342.7 15.6 %fusion.19 = bf16[1,3072,768]{2,1,0:T(8,128)(2,1)S(1)} fusion(bf16[2176,3072]{1,0:T(8,128)(2,1)} %fusion.6, bf16[2176,768]{1,0:T(8,128)(2,1)} %bitcast.12), kind=kOutput, calls=%fused_computation.54 | convolution fusion | flops 10270015488 | bytes 21430272 | tf_op jit(solution)/shard_map/dot_general | solution.py:847
  365.8 16.2 %convolution_convert_fusion.2 = bf16[2176,768]{1,0:T(8,128)(2,1)} fusion(bf16[2176,3072]{1,0:T(8,128)(2,1)} %fusion.6, bf16[3072,768]{1,0:T(8,128)(2,1)} %bitcast.237), kind=kOutput, calls=%fused_computation.42 | convolution fusion | flops 10269327360 | bytes 21430272 | tf_op jit(solution)/shard_map/dot_general | solution.py:842
  406.0 6.2 gather_fusion.1
  428.9 10.3 %collective-permute-start.8 = (bf16[2,384,768]{2,1,0:T(8,128)(2,1)}, bf16[2,384,768]{2,1,0:T(8,128)(2,1)}, u32[]{:S(2)}, u32[]{:S(2)}) collective-permute-start(bf16[2,384,768]{2,1,0:T(8,128)(2,1)} %get-tuple-element.132), channel_id=1, source_target_pairs={{0,0},{8,1},{4,4},{12,5},{16,8},{24,9},{20,12},{28,13},{1,16},{9,1... | collective-permute-start | bytes 3538952 | tf_op jit(solution)/shard_map/ppermute | solution.py:675
  439.7 16.0 %all-to-all-done.2 = bf16[8,272,768]{2,1,0:T(8,128)(2,1)} async-done(((bf16[8,272,768]{2,1,0:T(8,128)(2,1)}), bf16[8,272,768]{2,1,0:T(8,128)(2,1)}, u32[]{:S(2)}, u32[]{:S(2)}) %all-to-all-start.2) | async-done | bytes 3342368 | tf_op jit(solution)/shard_map/all_to_all | solution.py:683
  455.7 6.3 fusion.26
  478.4 7.9 %multiply_reduce_fusion = (f32[4,12,256]{2,1,0:T(8,128)S(1)}, f32[4,12,256,256]{2,3,1,0:T(8,128)S(1)}) fusion(f32[4,12,256]{2,1,0:T(8,128)S(1)} %log_add_fusion, f32[4,12,256,256]{2,3,1,0:T(8,128)} %copy-done.6, pred[4,256,256]{1,2,0:T(8,128)(4,1)S(1)} %copy-done.39, bf16[4,256,12,64]{1,0,3,2:T(4,128)(2,1)S(1)} %copy-done.31, ...), kind=kOutput, calls=%fused_computation.15 | convolution fusion | flops 418369536 | bytes 28672000 | tf_op jit(solution)/shard_map/rqhd,rkhd->rhqk/dot_general | solution.py:111
  486.4 7.2 %multiply_convert_fusion.1 = bf16[4,12,256,256]{2,3,1,0:T(8,128)(2,1)S(1)} fusion(f32[4,12,256,256]{2,3,1,0:T(8,128)S(1)} %get-tuple-element.174, f32[4,12,256]{2,1,0:T(8,128)S(1)} %get-tuple-element.173, f32[4,12,256]{2,1,0:T(8,128)S(1)} %log_add_fusion, f32[4,12,256,256]{2,3,1,0:T(8,128)} %copy-done.6, pred[4,256,256]{1,2,0:T(8,128)(4,1)S(1)} %copy-done.39), kind=kLoop, calls=%fused_computation.14 | loop fusion | flops 18874368 | bytes 31817728 | tf_op jit(solution)/shard_map/convert_element_type | solution.py:118
  525.4 8.6 %fusion.150 = (f32[768]{0:T(1024)S(1)}, f32[1024,768]{1,0:T(8,128)}) fusion(bf16[5,768,768]{2,1,0:T(8,128)(2,1)} %get-tuple-element.65, bf16[1,1024,768]{2,1,0:T(8,128)(2,1)S(1)} %copy.215, bf16[1,1024,768]{2,1,0:T(8,128)(2,1)} %copy.214, bf16[1,1024,768]{2,1,0:T(8,128)(2,1)} %copy.213), kind=kOutput, calls=%fused_computation.294 | convolution fusion | flops 3629382912 | bytes 11406336 | tf_op jit(solution)/shard_map/kte,kde->td/dot_general | solution.py:878
  560.1 6.2 fusion.13.g_ref
  566.3 44.7 %scatter_dense.1 = f32[144,768]{1,0:T(8,128)S(1)} custom-call(bf16[2,4,2,2,144,768]{5,4,3,2,1,0:T(8,128)(2,1)} %fusion.13.g_ref), custom_call_target="tpu_custom_call" | custom-call | tf_op jit(solution)/shard_map/scatter_dense/pallas_call | solution.py:408
  624.3 11.6 %share_sums.1 = f32[8,128]{1,0:T(8,128)} custom-call(f32[8,128]{1,0:T(8,128)} %iota.57.in_ref), custom_call_target="tpu_custom_call" | custom-call | tf_op jit(solution)/shard_map/share_sums/pallas_call | solution.py:456
  639.4 8.0 %multiply_add_fusion.4 = (f32[576,768]{1,0:T(8,128)}, f32[576,768]{1,0:T(8,128)}, f32[576,768]{1,0:T(8,128)}, f32[576,768]{1,0:T(8,128)}) fusion(f32[576,768]{1,0:T(8,128)} %param.65, f32[576,768]{1,0:T(8,128)} %head_ref.1, f32[576,768]{1,0:T(8,128)} %get-tuple-element.75, f32[]{:T(128)S(6)} %min.3, f32[576,768]{1,0:T(8,128)} %param.63, f32[576,768]{1,0:T(8,128)} %param.64), kind=kLoop, calls=%fused_computation.108 | loop fusion | flops 8404992 | bytes 15925252 | tf_op jit(solution)/shard_map/add | solution.py:75
  (420 shorter events, 250.3 us)
Async XLA Ops:
  0.7 69.2 %copy-start = (bf16[1024,768]{1,0:T(8,128)(2,1)S(1)}, bf16[1024,768]{1,0:T(8,128)(2,1)}, u32[]{:S(2)}) copy-start(bf16[1024,768]{1,0:T(8,128)(2,1)} %param.36) | copy-start | bytes 4718596
  49.1 22.7 %copy-start.5 = (f32[8,768]{1,0:T(8,128)}, f32[8,768]{1,0:T(8,128)S(1)}, u32[]{:S(2)}) copy-start(f32[8,768]{1,0:T(8,128)S(1)} %get-tuple-element.66.gain_ref) | copy-start | bytes 73732
  49.1 60.1 %copy-start.3 = (f32[8,768]{1,0:T(8,128)}, f32[8,768]{1,0:T(8,128)S(1)}, u32[]{:S(2)}) copy-start(f32[8,768]{1,0:T(8,128)S(1)} %get-tuple-element.67) | copy-start | bytes 73732
  51.7 18.1 %copy-start.115 = (bf16[5,768,768]{2,1,0:T(8,128)(2,1)S(1)}, bf16[5,768,768]{2,1,0:T(8,128)(2,1)}, u32[]{:S(2)}) copy-start(bf16[5,768,768]{2,1,0:T(8,128)(2,1)} %get-tuple-element.65) | copy-start | bytes 17694724
  53.0 90.3 %collective-permute-start = (bf16[2,384,768]{2,1,0:T(8,128)(2,1)}, bf16[2,384,768]{2,1,0:T(8,128)(2,1)}, u32[]{:S(2)}, u32[]{:S(2)}) collective-permute-start(bf16[2,384,768]{2,1,0:T(8,128)(2,1)} %fusion.74), channel_id=1, source_target_pairs={{0,0},{1,8},{4,4},{5,12},{8,16},{9,24},{12,20},{13,28},{16,1},{17,... | collective-permute-start | bytes 3538952 | tf_op jit(solution)/shard_map/ppermute | solution.py:665
  63.6 79.7 %collective-permute-start.2 = (bf16[2,384,768]{2,1,0:T(8,128)(2,1)}, bf16[2,384,768]{2,1,0:T(8,128)(2,1)}, u32[]{:S(2)}, u32[]{:S(2)}) collective-permute-start(bf16[2,384,768]{2,1,0:T(8,128)(2,1)} %fusion.74), channel_id=1, source_target_pairs={{0,16},{1,24},{4,20},{5,28},{8,0},{9,8},{12,4},{13,12},{16,17},{17... | collective-permute-start | bytes 3538952 | tf_op jit(solution)/shard_map/ppermute | solution.py:665
  64.8 78.5 %collective-permute-start.1 = (bf16[2,384,768]{2,1,0:T(8,128)(2,1)}, bf16[2,384,768]{2,1,0:T(8,128)(2,1)}, u32[]{:S(2)}, u32[]{:S(2)}) collective-permute-start(bf16[2,384,768]{2,1,0:T(8,128)(2,1)} %fusion.72), channel_id=1, source_target_pairs={{0,4},{1,12},{4,16},{5,24},{8,20},{9,28},{12,0},{13,8},{16,5},{17,... | collective-permute-start | bytes 3538952 | tf_op jit(solution)/shard_map/ppermute | solution.py:665
  66.8 76.5 %collective-permute-start.3 = (bf16[2,384,768]{2,1,0:T(8,128)(2,1)}, bf16[2,384,768]{2,1,0:T(8,128)(2,1)}, u32[]{:S(2)}, u32[]{:S(2)}) collective-permute-start(bf16[2,384,768]{2,1,0:T(8,128)(2,1)} %fusion.72), channel_id=1, source_target_pairs={{0,20},{1,28},{4,0},{5,8},{8,4},{9,12},{12,16},{13,24},{16,21},{17... | collective-permute-start | bytes 3538952 | tf_op jit(solution)/shard_map/ppermute | solution.py:665
  69.8 103.0 %copy-start.72 = (f32[4,256]{1,0:T(4,128)}, f32[4,256]{1,0:T(4,128)S(1)}, u32[]{:S(2)}) copy-start(f32[4,256]{1,0:T(4,128)S(1)} %get-tuple-element.154) | copy-start | bytes 12292
  71.8 36.8 %copy-start.74 = (f32[768]{0:T(1024)}, f32[768]{0:T(1024)S(1)}, u32[]{:S(2)}) copy-start(f32[768]{0:T(1024)S(1)} %get-tuple-element.86) | copy-start | bytes 9220
  86.1 86.6 %copy-start.64 = (s32[4,256]{1,0:T(4,128)}, s32[4,256]{1,0:T(4,128)S(1)}, u32[]{:S(2)}) copy-start(s32[4,256]{1,0:T(4,128)S(1)} %convert_reduce_fusion) | copy-start | bytes 12292
  108.4 64.4 %copy-start.91 = (f32[4,3]{1,0:T(4,128)}, f32[4,3]{1,0:T(4,128)S(1)}, u32[]{:S(2)}) copy-start(f32[4,3]{1,0:T(4,128)S(1)} %broadcast_maximum_fusion) | copy-start | bytes 148
  109.2 18.9 %copy-start.18 = (bf16[1024,768]{0,1:T(8,128)(2,1)}, bf16[1024,768]{0,1:T(8,128)(2,1)S(1)}, u32[]{:S(2)}) copy-start(bf16[1024,768]{0,1:T(8,128)(2,1)S(1)} %add_convert_fusion.2) | copy-start | bytes 4718596
  118.8 19.9 %all-to-all-start = ((f32[8,3,272]{2,1,0:T(4,128)}), f32[8,3,272]{2,1,0:T(4,128)S(1)}, u32[]{:S(2)}, u32[]{:S(2)}) async-start(f32[8,3,272]{2,1,0:T(4,128)} %maximum_bitcast_fusion.1), calls=%async_computation | async-start | bytes 98304 | tf_op jit(solution)/shard_map/all_to_all | solution.py:683
  138.6 60.3 %all-to-all-start.1 = ((bf16[8,272,768]{2,1,0:T(8,128)(2,1)}), bf16[8,272,768]{2,1,0:T(8,128)(2,1)}, u32[]{:S(2)}, u32[]{:S(2)}) async-start(bf16[8,272,768]{2,1,0:T(8,128)(2,1)} %bitcast.242), calls=%async_computation.1 | async-start | bytes 6684672 | tf_op jit(solution)/shard_map/all_to_all | solution.py:683
  149.5 31.2 %collective-permute-start.4 = (bf16[2,4,384,768]{3,2,1,0:T(8,128)(2,1)}, bf16[2,4,384,768]{3,2,1,0:T(8,128)(2,1)}, u32[]{:S(2)}, u32[]{:S(2)}) collective-permute-start(bf16[2,4,384,768]{3,2,1,0:T(8,128)(2,1)} %copy.195), channel_id=1, source_target_pairs={{0,1},{1,0},{2,3},{3,2},{4,5},{5,4},{6,7},{7,6},{8,9},{9,8},{10,11... | collective-permute-start | bytes 14155784 | tf_op jit(solution)/shard_map/ppermute | solution.py:656
  308.0 50.3 %copy-start.16 = (bf16[1,3072,768]{2,1,0:T(8,128)(2,1)}, bf16[1,3072,768]{2,1,0:T(8,128)(2,1)S(1)}, u32[]{:S(2)}) copy-start(bf16[1,3072,768]{2,1,0:T(8,128)(2,1)S(1)} %fusion.20) | copy-start | bytes 14155780
  361.9 57.5 %collective-permute-start.5 = (bf16[2,1536,768]{2,1,0:T(8,128)(2,1)}, bf16[2,1536,768]{2,1,0:T(8,128)(2,1)}, u32[]{:S(2)}, u32[]{:S(2)}) collective-permute-start(bf16[2,1536,768]{2,1,0:T(8,128)(2,1)} %pad_maximum_fusion.1), channel_id=1, source_target_pairs={{0,1},{1,0},{2,3},{3,2},{4,5},{5,4},{6,7},{7,6},{8,9},{9,8},{10,11... | collective-permute-start | bytes 14155784 | tf_op jit(solution)/shard_map/ppermute | solution.py:656
  362.5 19.6 %all-to-all-start.3 = ((f32[8,1,272]{2,1,0:T(1,128)}), f32[8,1,272]{2,1,0:T(1,128)S(1)}, u32[]{:S(2)}, u32[]{:S(2)}) async-start(f32[8,1,272]{2,1,0:T(1,128)} %all_to_all.18), calls=%async_computation.3 | async-start | bytes 24576 | tf_op jit(solution)/shard_map/all_to_all | solution.py:683
  382.1 73.6 %all-to-all-start.2 = ((bf16[8,272,768]{2,1,0:T(8,128)(2,1)}), bf16[8,272,768]{2,1,0:T(8,128)(2,1)}, u32[]{:S(2)}, u32[]{:S(2)}) async-start(bf16[8,272,768]{2,1,0:T(8,128)(2,1)} %bitcast.241), calls=%async_computation.2 | async-start | bytes 6684672 | tf_op jit(solution)/shard_map/all_to_all | solution.py:683
  426.0 188.9 %collective-permute-start.6 = (bf16[2,384,768]{2,1,0:T(8,128)(2,1)}, bf16[2,384,768]{2,1,0:T(8,128)(2,1)}, u32[]{:S(2)}, u32[]{:S(2)}) collective-permute-start(bf16[2,384,768]{2,1,0:T(8,128)(2,1)} %get-tuple-element.134), channel_id=1, source_target_pairs={{4,0},{12,1},{16,4},{24,5},{20,8},{28,9},{0,12},{8,13},{5,16},{13,... | collective-permute-start | bytes 3538952 | tf_op jit(solution)/shard_map/ppermute | solution.py:675
  428.9 186.0 %collective-permute-start.7 = (bf16[2,384,768]{2,1,0:T(8,128)(2,1)}, bf16[2,384,768]{2,1,0:T(8,128)(2,1)}, u32[]{:S(2)}, u32[]{:S(2)}) collective-permute-start(bf16[2,384,768]{2,1,0:T(8,128)(2,1)} %get-tuple-element.133), channel_id=1, source_target_pairs={{20,0},{28,1},{0,4},{8,5},{4,8},{12,9},{16,12},{24,13},{21,16},{29... | collective-permute-start | bytes 3538952 | tf_op jit(solution)/shard_map/ppermute | solution.py:675
  428.9 186.0 %collective-permute-start.8 = (bf16[2,384,768]{2,1,0:T(8,128)(2,1)}, bf16[2,384,768]{2,1,0:T(8,128)(2,1)}, u32[]{:S(2)}, u32[]{:S(2)}) collective-permute-start(bf16[2,384,768]{2,1,0:T(8,128)(2,1)} %get-tuple-element.132), channel_id=1, source_target_pairs={{0,0},{8,1},{4,4},{12,5},{16,8},{24,9},{20,12},{28,13},{1,16},{9,1... | collective-permute-start | bytes 3538952 | tf_op jit(solution)/shard_map/ppermute | solution.py:675
  439.2 175.7 %collective-permute-start.9 = (bf16[2,384,768]{2,1,0:T(8,128)(2,1)}, bf16[2,384,768]{2,1,0:T(8,128)(2,1)}, u32[]{:S(2)}, u32[]{:S(2)}) collective-permute-start(bf16[2,384,768]{2,1,0:T(8,128)(2,1)} %get-tuple-element.135), channel_id=1, source_target_pairs={{16,0},{24,1},{20,4},{28,5},{0,8},{8,9},{4,12},{12,13},{17,16},{25... | collective-permute-start | bytes 3538952 | tf_op jit(solution)/shard_map/ppermute | solution.py:675
  (111 other events, 649.2 us)

commit v3 on v2

--- a/solution.py
+++ b/solution.py
@@ -37,32 +37,6 @@
     return centre * lax.rsqrt(spread + eps_norm) * gain + shift
 
 
-def softmax_rows(logits):
-    top_val = jnp.max(logits, -1, keepdims=True)
-    powers = jnp.exp(logits - top_val)
-    return powers / jnp.sum(powers, -1, keepdims=True)
-
-
-def route(pick_ids, valid_flat, rank_ids, n_experts, capacity, padded):
-    columns = jnp.arange(n_experts, dtype=jnp.int32)
-    first_hot = (pick_ids[:, 0:1] == columns[None, :]).astype(jnp.float32) * valid_flat[:, None]
-    second_hot = (pick_ids[:, 1:2] == columns[None, :]).astype(jnp.float32) * valid_flat[:, None]
-    before = (rank_ids[None, :] < rank_ids[:, None]).astype(jnp.bfloat16)
-    hot = jnp.concatenate([first_hot, second_hot], 1)
-    ahead = jnp.dot(before, hot.astype(jnp.bfloat16), preferred_element_type=jnp.float32)
-    first_pos = jnp.sum(first_hot * ahead[:, :n_experts], 1)
-    second_pos = jnp.sum(second_hot * (ahead[:, n_experts:] + jnp.sum(first_hot, 0)[None, :]), 1)
-    first_kept = valid_flat * (first_pos < capacity).astype(jnp.float32)
-    second_kept = valid_flat * (second_pos < capacity).astype(jnp.float32)
-    first_slot = jnp.where(
-        first_kept > 0, pick_ids[:, 0] * padded + first_pos.astype(jnp.int32), -1
-    )
-    second_slot = jnp.where(
-        second_kept > 0, pick_ids[:, 1] * padded + second_pos.astype(jnp.int32), -1
-    )
-    return (first_slot, second_slot, first_kept, second_kept)
-
-
 def adam_update(weight, first_state, second_state, average_state, gradient, factor, step_rate):
     clipped = gradient * factor
     first_new = beta_first * first_state + (1.0 - beta_first) * clipped
@@ -84,24 +58,6 @@
         "rqhd,rkhd->rhqk", shaped[0], shaped[1], preferred_element_type=jnp.float32
     ) * head_dim ** (-0.5)
     return (shaped, jnp.where(allow_mask[:, None], scores, mask_fill), head_dim ** (-0.5))
-
-
-def attention_forward(proj_qkv, allow_mask, n_heads):
-    shaped, masked, unused_scale = split_heads(proj_qkv, allow_mask, n_heads)
-    top_val = jnp.max(masked, -1, keepdims=True)
-    powers = jnp.exp(masked - top_val)
-    totals = jnp.sum(powers, -1, keepdims=True)
-    att_probs = powers / totals
-    output = jnp.einsum(
-        "rhqk,rkhd->rqhd",
-        att_probs.astype(jnp.bfloat16),
-        shaped[2],
-        preferred_element_type=jnp.float32,
-    )
-    return (
-        output.astype(jnp.bfloat16).reshape(proj_qkv.shape[1], proj_qkv.shape[2]),
-        top_val + jnp.log(totals),
-    )
 
 
 def attention_backward(proj_qkv, allow_mask, log_total, d_output, n_heads):
@@ -215,7 +171,10 @@
     return peers + [at.sibling()]
 
 
-def gather_kernel(sizes, rows, mats, dense_ref, tail_ref, w_ref, gain_ref, router_ref, land, *sems):
+def gather_kernel(
+    sizes, rows, mats, routing, dense_ref, tail_ref, pick_ref, rank_ref, mask_ref, length_ref,
+    w_ref, gain_ref, router_ref, col_ref, land, *sems
+):
     at = Place(sizes)
     Z, Y, X = at.Z, at.Y, at.X
     depth = land.shape[4]
@@ -276,6 +235,8 @@
                 part = land.at[at.c, z, at.x, at.y]
                 send(part, part, z_out.at[z], z_in.at[z], at.at(z=z)).wait_recv()
             one(order[step])
+        if step == 0:
+            col_ref[...] = route_math(*routing, pick_ref, rank_ref, mask_ref, length_ref)
         if 0 <= step - 1 < Z:
             two(order[step - 1])
         if 0 <= step - 2 < Z:
@@ -299,7 +260,7 @@
     router_ref[...] = jnp.concatenate([tail[:, 128 : 128 + rows] for tail in tails], 1)
 
 
-def gather_weights(sizes, dense, tail):
+def gather_weights(sizes, routing, dense, tail, picks, ranks, slot_mask, lengths):
     mats, rows, width = dense.shape
     count = tail.shape[0]
     depth = round_up(mats * rows + count, 16)
@@ -307,21 +268,22 @@
     dma = pltpu.SemaphoreType.DMA
     by_y, by_x = dma((Z, Y)), dma((Z, X))
     return pl.pallas_call(
-        functools.partial(gather_kernel, sizes, rows, mats),
+        functools.partial(gather_kernel, sizes, rows, mats, routing),
         out_shape=(
             jax.ShapeDtypeStruct((mats, width, width), jnp.bfloat16),
             jax.ShapeDtypeStruct((8, width), jnp.float32),
             jax.ShapeDtypeStruct((count, width), jnp.float32),
+            jax.ShapeDtypeStruct((picks.shape[0], 128), jnp.float32),
         ),
-        in_specs=[whole()] * 2,
-        out_specs=(whole(),) * 3,
+        in_specs=[whole()] * 6,
+        out_specs=(whole(),) * 4,
         scratch_shapes=[VMEM((2, Z, X, Y, depth, width), jnp.bfloat16), dma((Z,)), dma((Z,))]
         + [by_y, by_y, by_x, by_x, by_x, by_x, by_y, by_y, dma((Z,)), dma((Z,))],
         compiler_params=pltpu.CompilerParams(
             collective_id=1, has_side_effects=True, vmem_limit_bytes=48 * MIB
         ),
         name="gather_weights",
-    )(dense, tail)
+    )(dense, tail, picks, ranks, slot_mask, lengths)
 
 
 def scatter_kernel(sizes, g_ref, out_ref, hold, sib, got_xa, got_yb, got_ya, got_xb, got_z, *sems):
@@ -537,7 +499,7 @@
     a_three = scaled * gain + shift
     row = lax.broadcasted_iota(jnp.int32, (IMAGE_PAD, width), 0)
     block = jnp.where(row < images, a_three, 0.0)
-    pieces = split_three(imp_ref[...])
+    pieces = split_three(imp_ref[0:1])
     for index, piece in enumerate(pieces):
         block = jnp.where(row == images + index, piece.astype(jnp.float32), block)
     rows[at.c, at.chip] = block.astype(jnp.bfloat16)
@@ -637,6 +599,352 @@
     )(part, own, imp, gains, head, label)
 
 
+def route_math(per_image, n_experts, capacity, padded, pick_ref, rank_ref, mask_ref, length_ref):
+    rows_here, span = mask_ref.shape
+    tokens = rows_here * span
+    valid = mask_ref[...].astype(jnp.float32)
+    lengths = length_ref[...]
+    position = lax.broadcasted_iota(jnp.int32, (rows_here, span), 1)
+    segment = jnp.zeros((rows_here, span), jnp.int32)
+    bound = jnp.zeros((rows_here, 1), jnp.int32)
+    for image in range(per_image):
+        bound = bound + lengths[:, image : image + 1]
+        segment = segment + jnp.where(position >= bound, 1, 0)
+    pool = jnp.zeros_like(valid)
+    for image in range(per_image):
+        member = jnp.where(segment == image, valid, 0.0)
+        pool = pool + member / jnp.maximum(jnp.sum(member, 1, keepdims=True), 1.0)
+    line = lax.broadcasted_iota(jnp.int32, (rows_here, span), 0)
+    image = (segment + per_image * line).astype(jnp.float32)
+
+    def flat(value):
+        return jnp.concatenate([value[i : i + 1] for i in range(rows_here)], 1)
+
+    rank_row = rank_ref[...].astype(jnp.float32)
+    table = jnp.concatenate([flat(valid), flat(pool), flat(image), rank_row], 0)
+    table = jnp.concatenate([table, jnp.zeros((124, tokens), jnp.float32)], 0).T
+    valid_col, pool_col, image_col, rank_col = (table[:, i : i + 1] for i in range(4))
+    picks = pick_ref[...]
+    pick_one, pick_two = picks[:, 0:1], picks[:, 1:2]
+    lane = lax.broadcasted_iota(jnp.int32, (tokens, 128), 1)
+    in_first, in_second = lane < n_experts, (lane >= n_experts) & (lane < 2 * n_experts)
+    hot = jnp.where(in_first & (pick_one == lane), valid_col, 0.0)
+    hot = hot + jnp.where(in_second & (pick_two == lane - n_experts), valid_col, 0.0)
+    shifted = jnp.where(in_second & (pick_one == lane - n_experts), valid_col, 0.0)
+    before = jnp.where(rank_row < rank_col, 1.0, 0.0).astype(jnp.bfloat16)
+    ahead = dot_f32(before, hot.astype(jnp.bfloat16), NN) + jnp.sum(shifted, 0, keepdims=True)
+    counted = hot * ahead
+    pos_one = jnp.sum(jnp.where(in_first, counted, 0.0), 1, keepdims=True)
+    pos_two = jnp.sum(jnp.where(in_second, counted, 0.0), 1, keepdims=True)
+
+    def place(pick, pos):
+        kept = (valid_col > 0.0) & (pos < capacity)
+        return jnp.where(kept, pick.astype(jnp.float32) * padded + pos, -1.0)
+
+    columns = (
+        place(pick_one, pos_one),
+        place(pick_two, pos_two),
+        valid_col,
+        pool_col,
+        image_col,
+        pick_one.astype(jnp.float32),
+        pick_two.astype(jnp.float32),
+    )
+    result = jnp.zeros((tokens, 128), jnp.float32)
+    for index, column in enumerate(columns):
+        result = jnp.where(lane == index, column, result)
+    return result
+
+
+def lane_mask(shape, left):
+    lane = lax.broadcasted_iota(jnp.int32, shape, 1)
+    return lane < 64 if left else lane >= 64
+
+
+def allowed_slots(lengths, row, images, valid_row, span):
+    query = lax.broadcasted_iota(jnp.int32, (span, span), 0)
+    key = lax.broadcasted_iota(jnp.int32, (span, span), 1)
+    bound = 0
+    query_seg, key_seg = jnp.zeros((span, span), jnp.int32), jnp.zeros((span, span), jnp.int32)
+    for image in range(images):
+        bound = bound + lengths[row, image]
+        query_seg = query_seg + jnp.where(query >= bound, 1, 0)
+        key_seg = key_seg + jnp.where(key >= bound, 1, 0)
+    return (query_seg == key_seg) & ((valid_row > 0) | (query == key))
+
+
+def dense_forward_kernel(
+    n_experts, images, length_ref, mask_ref, patch_ref, w_ref, gain_ref, router_ref, col_ref,
+    x_zero_ref, a_one_ref, qkv_ref, att_ref, x_one_ref, a_two_ref, prob_ref, lse_ref, pool_ref, imp_ref
+):
+    row = pl.program_id(0)
+    span, width = patch_ref.shape
+    x_zero = dot_f32(patch_ref[...], w_ref[0], NN)
+    x_zero_ref[...] = x_zero
+    a_one = (norm_parts(x_zero)[0] * gain_ref[0:1] + gain_ref[3:4]).astype(jnp.bfloat16)
+    a_one_ref[...] = a_one
+    for part in range(3):
+        qkv_ref[:, part * width : (part + 1) * width] = dot_f32(a_one, w_ref[1 + part], NN).astype(
+            jnp.bfloat16
+        )
+    open_to = allowed_slots(length_ref, row, images, mask_ref[0], span)
+    lane = lax.broadcasted_iota(jnp.int32, (span, 128), 1)
+    logs = jnp.zeros((span, 128), jnp.float32)
+    for pair in range(width // 128):
+        query, key, value = (
+            qkv_ref[:, part * width + pair * 128 : part * width + (pair + 1) * 128]
+            for part in range(3)
+        )
+        outs = []
+        for side in range(2):
+            held = jnp.where((lane < 64) == (side == 0), query, jnp.zeros_like(query))
+            scores = jnp.where(open_to, dot_f32(held, key, NT) * 64**-0.5, mask_fill)
+            top = jnp.max(scores, 1, keepdims=True)
+            powers = jnp.exp(scores - top)
+            total = jnp.sum(powers, 1, keepdims=True)
+            probs = (powers * (1.0 / total)).astype(jnp.bfloat16)
+            outs.append(dot_f32(probs, value, NN))
+            logs = jnp.where(lane == 2 * pair + side, top + jnp.log(total), logs)
+        att_ref[:, pair * 128 : (pair + 1) * 128] = jnp.where(lane < 64, outs[0], outs[1]).astype(
+            jnp.bfloat16
+        )
+    lse_ref[...] = logs
+    x_one = x_zero + dot_f32(att_ref[...], w_ref[4], NN)
+    x_one_ref[...] = x_one
+    a_two = (norm_parts(x_one)[0] * gain_ref[1:2] + gain_ref[4:5]).astype(jnp.bfloat16)
+    a_two_ref[...] = a_two
+    routers = router_ref[...].astype(jnp.bfloat16)
+    if routers.shape[0] < 128:
+        routers = jnp.concatenate(
+            [routers, jnp.zeros((128 - routers.shape[0], width), jnp.bfloat16)], 0
+        )
+    logits = jnp.where(lane < n_experts, dot_f32(a_two, routers, NT), mask_fill)
+    powers = jnp.exp(logits - jnp.max(logits, 1, keepdims=True))
+    probs = powers / jnp.sum(powers, 1, keepdims=True)
+    prob_ref[...] = probs
+
+    @pl.when(row == 0)
+    def _():
+        pool_ref[...] = jnp.zeros_like(pool_ref)
+        imp_ref[...] = jnp.zeros_like(imp_ref)
+
+    valid, pool, image = col_ref[:, 2:3], col_ref[:, 3:4], col_ref[:, 4:5]
+    imp_ref[0:1, 0:128] += jnp.sum(probs * valid, 0, keepdims=True)
+    line = lax.broadcasted_iota(jnp.int32, pool_ref.shape, 0)
+    for index in range(images):
+        number = row * images + index
+        weight = jnp.where(image == number.astype(jnp.float32), pool, 0.0)
+        pooled = jnp.sum(x_one * weight, 0, keepdims=True)
+        pool_ref[...] = jnp.where(line == number, pooled, pool_ref[...])
+
+
+def dense_forward(n_experts, lengths, slot_mask, patches, weights, gains, routers, columns):
+    rows_here, span = slot_mask.shape
+    tokens, width = patches.shape
+    f32, half = jnp.float32, jnp.bfloat16
+
+    def block(wide):
+        return pl.BlockSpec((span, wide), lambda i: (i, 0))
+
+    def out(wide, kind):
+        return jax.ShapeDtypeStruct((tokens, wide), kind)
+
+    def fixed(shape):
+        return pl.BlockSpec(shape, lambda i: (0, 0))
+
+    return pl.pallas_call(
+        functools.partial(dense_forward_kernel, n_experts, lengths.shape[1]),
+        grid=(rows_here,),
+        out_shape=(
+            out(width, f32), out(width, half), out(3 * width, half), out(width, half),
+            out(width, f32), out(width, half), out(128, f32), out(128, f32),
+            jax.ShapeDtypeStruct((IMAGE_PAD, width), f32), jax.ShapeDtypeStruct((8, width), f32),
+        ),
+        in_specs=[
+            whole(pltpu.SMEM), pl.BlockSpec((1, 1, span), lambda i: (i, 0, 0)), block(width),
+            whole(), whole(), whole(), block(128),
+        ],
+        out_specs=(
+            block(width), block(width), block(3 * width), block(width), block(width), block(width),
+            block(128), block(128), fixed((IMAGE_PAD, width)), fixed((8, width)),
+        ),
+        compiler_params=pltpu.CompilerParams(vmem_limit_bytes=48 * MIB),
+        name="dense_forward",
+    )(lengths, slot_mask[:, None, :], patches, weights, gains, routers, columns)
+
+
+def dispatch_kernel(
+    sizes, n_experts, padded, a_two_ref, prob_ref, col_ref, rows_ref, detail_ref,
+    send_rows, send_detail, places, own_sem, r_out, r_in, m_out, m_in
+):
+    at = Place(sizes)
+    tokens = a_two_ref.shape[0]
+    team = others(at.member, n_experts)
+    greet([at.of_member(member) for member in team])
+    columns = col_ref[...]
+    places[...] = columns.T[:8]
+    lane = lax.broadcasted_iota(jnp.int32, (tokens, 128), 1)
+    kind, expert = lax.div(lane, n_experts), lax.rem(lane, n_experts).astype(jnp.float32)
+    slot_lane = lax.broadcasted_iota(jnp.int32, (tokens, send_detail.shape[2]), 1).astype(jnp.float32)
+    pool, image = columns[:, 3:4], columns[:, 4:5]
+    details = None
+    for choice in range(2):
+        slot, pick = columns[:, choice : choice + 1], columns[:, 5 + choice : 6 + choice]
+        hot = (expert == pick) & (slot >= 0.0)
+        gate = jnp.sum(jnp.where(hot & (kind == 0), prob_ref[...], 0.0), 1, keepdims=True)
+        values = jnp.zeros((tokens, 128), jnp.float32)
+        pieces = [*split_three(gate), *split_three(pool), image]
+        for index, piece in enumerate(pieces):
+            values = jnp.where(kind == index, piece.astype(jnp.float32), values)
+        values = jnp.where(hot, values, 0.0).astype(jnp.bfloat16)
+        spot = jnp.where(slot >= 0.0, slot - pick * padded, -1.0)
+        chosen = jnp.where(spot == slot_lane, 1.0, 0.0).astype(jnp.bfloat16)
+        found = dot_f32(values, chosen, TN)
+        details = found if details is None else details + found
+    n = n_experts
+    gates = details[0:n] + details[n : 2 * n] + details[2 * n : 3 * n]
+    pools = details[3 * n : 4 * n] + details[4 * n : 5 * n] + details[5 * n : 6 * n]
+    images = details[6 * n : 7 * n]
+    for index in range(n):
+        for spot, value in enumerate((gates, pools, images)):
+            send_detail[index, spot : spot + 1] = value[index : index + 1]
+        send_detail[index, 3:8] = jnp.zeros((5, send_detail.shape[2]), jnp.float32)
+
+    def rows_of(member):
+        slots = lax.broadcasted_iota(jnp.int32, (padded, tokens), 0) + member * padded
+        slots = slots.astype(jnp.float32)
+        match = (slots == places[0:1]) | (slots == places[1:2])
+        match = jnp.where(match, 1.0, 0.0).astype(jnp.bfloat16)
+        send_rows[member] = dot_f32(match, a_two_ref[...], NN).astype(jnp.bfloat16)
+
+    def row_copy(member, source):
+        return send(
+            send_rows.at[member], rows_ref.at[source], r_out.at[member], r_in.at[source], at.of_member(member)
+        )
+
+    def detail_copy(member, source):
+        return send(
+            send_detail.at[member], detail_ref.at[source], m_out.at[member], m_in.at[source], at.of_member(member)
+        )
+
+    def step(index, carry):
+        member = lax.rem(at.member + index, n_experts)
+        rows_of(member)
+        row_copy(member, at.member).start()
+        detail_copy(member, at.member).start()
+        return carry
+
+    lax.fori_loop(1, n_experts, step, 0)
+    rows_of(at.member)
+    keep_rows = pltpu.make_async_copy(send_rows.at[at.member], rows_ref.at[at.member], own_sem.at[0])
+    keep_detail = pltpu.make_async_copy(send_detail.at[at.member], detail_ref.at[at.member], own_sem.at[1])
+    keep_rows.start()
+    keep_detail.start()
+    for member in team:
+        row_copy(member, member).wait_recv()
+        detail_copy(member, member).wait_recv()
+    for member in team:
+        row_copy(member, at.member).wait_send()
+        detail_copy(member, at.member).wait_send()
+    keep_rows.wait()
+    keep_detail.wait()
+
+
+def dispatch(sizes, n_experts, padded, a_two, probs, columns):
+    tokens, width = a_two.shape
+    lanes = round_up(padded, 128)
+    dma = pltpu.SemaphoreType.DMA
+    each = dma((n_experts,))
+    return pl.pallas_call(
+        functools.partial(dispatch_kernel, sizes, n_experts, padded),
+        out_shape=(
+            jax.ShapeDtypeStruct((n_experts, padded, width), jnp.bfloat16),
+            jax.ShapeDtypeStruct((n_experts, 8, lanes), jnp.float32),
+        ),
+        in_specs=[whole()] * 3,
+        out_specs=(whole(ANY), whole(ANY)),
+        scratch_shapes=[
+            VMEM((n_experts, padded, width), jnp.bfloat16),
+            VMEM((n_experts, 8, lanes), jnp.float32),
+            VMEM((8, tokens), jnp.float32),
+            dma((2,)), each, each, each, each,
+        ],
+        compiler_params=pltpu.CompilerParams(
+            collective_id=5, has_side_effects=True, vmem_limit_bytes=48 * MIB
+        ),
+        name="dispatch",
+    )(a_two, probs, columns)
+
+
+def image_hot(detail, padded):
+    image = detail[2:3, :padded]
+    line = lax.broadcasted_iota(jnp.int32, (IMAGE_PAD, padded), 0).astype(jnp.float32)
+    return line == image
+
+
+def expert_forward_kernel(
+    padded, rows_ref, detail_ref, own_ref, other_ref, act_ref, slope_ref, y_ref, part_ref
+):
+    many, unused, width = rows_ref.shape
+    rows = rows_ref[...].reshape(many * padded, width)
+    half = own_ref.shape[1]
+    step = 384
+    total = None
+    for index, ref in enumerate((own_ref, other_ref)):
+        for start in range(0, half, step):
+            hidden = dot_f32(rows, ref[0, start : start + step], NT)
+            square = hidden * hidden
+            curve = jnp.tanh(0.7978845608 * hidden * (1.0 + 0.044715 * square))
+            upper = 0.5 * (1.0 + curve)
+            act = (hidden * upper).astype(jnp.bfloat16)
+            slope = upper + 0.5 * hidden * (1.0 - curve * curve) * (
+                0.7978845608 + 3.0 * 0.7978845608 * 0.044715 * square
+            )
+            spot = index * half + start
+            act_ref[:, spot : spot + step] = act
+            slope_ref[:, spot : spot + step] = slope.astype(jnp.bfloat16)
+            found = dot_f32(act, ref[1, start : start + step], NN)
+            total = found if total is None else total + found
+    result = total.astype(jnp.bfloat16)
+    y_ref[...] = result.reshape(many, padded, width)
+    for source in range(many):
+        detail = detail_ref[source]
+        weight = detail[0:1, :padded] * detail[1:2, :padded]
+        weights = jnp.where(image_hot(detail, padded), weight, 0.0)
+        pieces = jnp.concatenate(split_three(weights), 0)
+        sums = dot_f32(pieces, result[source * padded : (source + 1) * padded], NN)
+        part_ref[source] = (
+            sums[:IMAGE_PAD] + sums[IMAGE_PAD : 2 * IMAGE_PAD] + sums[2 * IMAGE_PAD :]
+        )
+
+
+def expert_forward(rows, details, own_half, other_half):
+    sources, padded, width = rows.shape
+    hidden = 2 * own_half.shape[1]
+    many = max(1, 576 // padded)
+    lanes = details.shape[2]
+    half = jnp.bfloat16
+
+    def by_source(*shape):
+        return pl.BlockSpec((many, *shape), lambda i: (i, 0, 0))
+
+    flat = pl.BlockSpec((many * padded, hidden), lambda i: (i, 0))
+    return pl.pallas_call(
+        functools.partial(expert_forward_kernel, padded),
+        grid=(sources // many,),
+        out_shape=(
+            jax.ShapeDtypeStruct((sources * padded, hidden), half),
+            jax.ShapeDtypeStruct((sources * padded, hidden), half),
+            jax.ShapeDtypeStruct((sources, padded, width), half),
+            jax.ShapeDtypeStruct((sources, IMAGE_PAD, width), jnp.float32),
+        ),
+        in_specs=[by_source(padded, width), by_source(8, lanes), whole(), whole()],
+        out_specs=(flat, flat, by_source(padded, width), by_source(IMAGE_PAD, width)),
+        compiler_params=pltpu.CompilerParams(vmem_limit_bytes=56 * MIB),
+        name="expert_forward",
+    )(rows, details, own_half, other_half)
+
+
 def shard_moves(n_blocks):
     span = 2 * n_blocks
     moves = []
@@ -722,23 +1030,37 @@
     tail = jnp.zeros((n_tail, dense_weights.shape[2]), jnp.float32)
     tail = tail.at[:6, :rows_own].set(norm_params)
     tail = tail.at[:n_experts, 128 : 128 + rows_own].set(router_weights.T)
-    layer_b, gain_rows, router_t = gather_weights(sizes, dense_weights, tail)
+    rows_here, n_slots_row = slot_mask.shape
+    tokens, model_width = patches.shape
+    n_images = lengths.shape[0] * lengths.shape[1]
+    capacity = (21 * tokens * TOP + 20 * n_experts - 1) // (20 * n_experts)
+    padded = round_up(capacity, 16)
+    n_slots = n_experts * padded
+    layer_b, gain_rows, router_t, columns = gather_weights(
+        sizes,
+        (lengths.shape[1], n_experts, capacity, padded),
+        dense_weights,
+        tail,
+        expert_picks,
+        priority_rank,
+        slot_mask,
+        lengths,
+    )
     router_b = router_t[:n_experts].T.astype(jnp.bfloat16)
     expert_in_now, expert_out_now, layer_b = lax.optimization_barrier((expert_in, expert_out, layer_b))
     own_chunks = fetch_experts(expert_in_now, expert_out_now, n_blocks)
-    own_half = jnp.stack(own_chunks, 1)
+    own_half = jnp.concatenate(own_chunks, 1)
     other_half = swap_cores(own_half)
     w_one = jnp.concatenate([own_half[0], other_half[0]], 0)
     w_two = jnp.concatenate([own_half[1], other_half[1]], 0)
-    rows_here, n_slots_row = slot_mask.shape
-    tokens = rows_here * n_slots_row
-    model_width = layer_b.shape[2]
-    n_images = lengths.shape[0] * lengths.shape[1]
-    capacity = (21 * tokens * TOP + 20 * n_experts - 1) // (20 * n_experts)
-    padded = (capacity + 15) // 16 * 16
-    n_slots = n_experts * padded
-    w_one = w_one.reshape(-1, model_width)
-    w_two = w_two.reshape(-1, model_width)
+    x_zero, a_one, qkv, att_out, x_one, a_two, router_probs, logs, pooled, part_importance = (
+        dense_forward(
+            n_experts, lengths, slot_mask, patches, layer_b, gain_rows, router_t, columns
+        )
+    )
+    arrived, details = dispatch(sizes, n_experts, padded, a_two, router_probs, columns)
+    activated, slope, result, part_pooled = expert_forward(arrived, details, own_half, other_half)
+
     valid = slot_mask.astype(jnp.float32)
     positions = jnp.arange(n_slots_row, dtype=jnp.int32)
     bounds = jnp.cumsum(lengths, 1)
@@ -752,71 +1074,33 @@
     ).astype(jnp.float32) * valid[:, None, :]
     pooling = member / jnp.maximum(jnp.sum(member, -1, keepdims=True), 1.0)
     valid_flat = valid.reshape(tokens)
-    pool_flat = jnp.sum(pooling, 1).reshape(tokens)
-    image_flat = (segment + jnp.arange(rows_here)[:, None] * lengths.shape[1]).reshape(tokens)
-    slot_one, slot_two, kept_one, kept_two = route(
-        expert_picks, valid_flat, priority_rank[0], n_experts, capacity, padded
-    )
-    x_zero = jnp.dot(patches, layer_b[0], preferred_element_type=jnp.float32)
-    a_one = layer_norm(x_zero, gain_rows[0], gain_rows[3]).astype(jnp.bfloat16)
-    proj_qkv = jnp.einsum(
-        "td,kde->kte", a_one, layer_b[1:4], preferred_element_type=jnp.float32
-    ).astype(jnp.bfloat16)
-    att_out, log_total = attention_forward(proj_qkv, allowed, HEADS)
-    x_one = x_zero + jnp.dot(att_out, layer_b[4], preferred_element_type=jnp.float32)
-    a_two = layer_norm(x_one, gain_rows[1], gain_rows[4]).astype(jnp.bfloat16)
-    router_probs = softmax_rows(jnp.dot(a_two, router_b, preferred_element_type=jnp.float32))
-    part_importance = jnp.sum(router_probs * valid_flat[:, None], 0)
+    slot_one, slot_two = columns[:, 0].astype(jnp.int32), columns[:, 1].astype(jnp.int32)
+    kept_one = (slot_one >= 0).astype(jnp.float32)
+    kept_two = (slot_two >= 0).astype(jnp.float32)
+    router_probs = router_probs[:, :n_experts]
+    proj_qkv = qkv.reshape(tokens, 3, model_width).transpose(1, 0, 2)
+    log_total = logs[:, :HEADS].reshape(rows_here, n_slots_row, HEADS).transpose(0, 2, 1)[..., None]
     pick_one = expert_picks[:, 0]
     pick_two = expert_picks[:, 1]
-    columns = jnp.arange(n_experts, dtype=jnp.int32)
-    hot_one = (pick_one[:, None] == columns[None]).astype(jnp.float32)
-    hot_two = (pick_two[:, None] == columns[None]).astype(jnp.float32)
-    gate_one = jnp.sum(router_probs * hot_one, 1) * kept_one
-    gate_two = jnp.sum(router_probs * hot_two, 1) * kept_two
+    ids = jnp.arange(n_experts, dtype=jnp.int32)
+    hot_one = (pick_one[:, None] == ids[None]).astype(jnp.float32)
+    hot_two = (pick_two[:, None] == ids[None]).astype(jnp.float32)
     slot_ids = jnp.arange(n_slots, dtype=jnp.int32)
-    match_one = slot_one[None, :] == slot_ids[:, None]
-    match_two = slot_two[None, :] == slot_ids[:, None]
-    match = (match_one | match_two).astype(jnp.bfloat16)
-    send_rows = (
-        jnp.dot(match, a_two, preferred_element_type=jnp.float32)
-        .astype(jnp.bfloat16)
-        .reshape(n_experts, padded, model_width)
-    )
-    held = jnp.where(match_one | match_two, 1.0, 0.0)
-    slot_gate = jnp.sum(
-        jnp.where(match_one, gate_one[None], 0.0) + jnp.where(match_two, gate_two[None], 0.0), 1
-    )
-    slot_pool = jnp.sum(held * pool_flat[None], 1)
-    slot_image = jnp.sum(held * image_flat.astype(jnp.float32)[None], 1)
-    details = jnp.stack([slot_gate, slot_pool, slot_image]).reshape(3, n_experts, padded)
-    arrived = to_members(send_rows)
-    details = to_members(details.transpose(1, 0, 2))
-    got_gate, got_pool, got_image = details[:, 0], details[:, 1], details[:, 2]
-    image_hot = (
+    match = (
+        (slot_one[None, :] == slot_ids[:, None]) | (slot_two[None, :] == slot_ids[:, None])
+    ).astype(jnp.bfloat16)
+    got_gate, got_pool, got_image = (details[:, i, :padded] for i in range(3))
+    image_hots = (
         got_image[:, :, None] == jnp.arange(n_images).astype(jnp.float32)[None, None]
     ).astype(jnp.float32) * got_pool[:, :, None]
     rows_all = arrived.reshape(n_slots, model_width)
-    hidden = jnp.dot(rows_all, w_one.T, preferred_element_type=jnp.float32)
-    activated = jax.nn.gelu(hidden).astype(jnp.bfloat16)
-    result = jnp.dot(activated, w_two, preferred_element_type=jnp.float32).astype(jnp.bfloat16)
-    result = result.reshape(n_experts, padded, model_width).astype(jnp.float32)
-    part_pooled = jnp.einsum(
-        "dsi,dsw->diw", image_hot * got_gate[:, :, None], result, precision=high_prec
-    )
-    pooled = jnp.einsum(
-        "ris,rsd->rid",
-        pooling,
-        x_one.reshape(rows_here, n_slots_row, model_width),
-        precision=high_prec,
-    ).reshape(-1, model_width)
-    pad_rows = ((0, IMAGE_PAD - n_images), (0, 0))
+    result = result.astype(jnp.float32)
     g_head, d_pooled_all, d_pooled, g_norm_three, local_loss, importance = head_step(
         sizes,
         n_images,
-        jnp.pad(part_pooled, ((0, 0), *pad_rows)),
-        jnp.pad(pooled, pad_rows),
-        jnp.pad(part_importance, (0, model_width - n_experts))[None],
+        part_pooled,
+        pooled,
+        part_importance,
         gain_rows,
         head_weights,
         class_labels,
@@ -834,11 +1118,11 @@
     d_two = jnp.einsum(
         "ris,rid->rsd", pooling, d_pooled.reshape(rows_here, -1, model_width), precision=high_prec
     ).reshape(tokens, model_width)
-    d_two_slots = jnp.einsum("dsi,diw->dsw", image_hot, d_pooled_all, precision=high_prec)
+    d_two_slots = jnp.einsum("dsi,diw->dsw", image_hots, d_pooled_all, precision=high_prec)
     slot_d_gate = jnp.sum(d_two_slots * result, -1)
     d_all = (d_two_slots * got_gate[:, :, None]).astype(jnp.bfloat16).reshape(n_slots, model_width)
     d_act = jnp.dot(d_all, w_two.T, preferred_element_type=jnp.float32)
-    d_hidden = jax.vjp(jax.nn.gelu, hidden)[1](d_act)[0].astype(jnp.bfloat16)
+    d_hidden = (d_act * slope.astype(jnp.float32)).astype(jnp.bfloat16)
     d_inputs = jnp.dot(d_hidden, w_one, preferred_element_type=jnp.float32).astype(jnp.bfloat16)
     d_back = to_members(d_inputs.reshape(n_experts, padded, model_width))
     d_back = d_back.reshape(n_slots, model_width)

time: 673 us -> 720 us (1.070)
  Pallas kernels: 143 us -> 267 us
  matrix products: 211 us -> 130 us
  other arithmetic: 93.8 us -> 76.7 us
  starting transfers between devices: 65.7 us -> 77.8 us
  waiting for transfers between devices: 36.8 us -> 48.4 us
    pallas_call x1 -> x4, Pallas kernels: 44.6 us -> 167 us  [the longest x1 54.7 us: dispatch(): pl.pallas_call(functools.partial(dispatch_kernel, sizes, n_experts, padde...]
    dot_general x12 -> x1, matrix products: 74.2 us -> 8.75 us  [body(): jnp.einsum('dsi,diw->dsw', image_hots, d_pooled_all, precision=high_prec)]
    ppermute x4, waiting for transfers between devices: 0.01 us -> 48.3 us  [fetch_experts(): lax.ppermute(ordered[step % 2], ('g', 'r', 'c'), pairs)]
    all_to_all x4 -> x2, waiting for transfers between devices: 36.8 us -> 0.01 us  [to_members(): lax.all_to_all(value, MEMBERS, split_axis=0, concat_axis=0, tiled=True)]
    ppermute x2, starting transfers between devices: 19.7 us -> 48.9 us  [swap_cores(): return lax.ppermute(value, 'c', [(0, 1), (1, 0)])]
    dot_general x1, matrix products: 34.7 us -> 18.5 us  [body(): d_act = jnp.dot(d_all, w_two.T, preferred_element_type=jnp.float32)]
    reduce_sum x6 -> x0, other arithmetic: 13.6 us -> none  [the longest x1 5.91 us: body(): jnp.sum(jnp.where(match_one, gate_one[None], 0.0) + jnp.where(match_two,...]
    ppermute x4, starting transfers between devices: 15.6 us -> 6.65 us  [fetch_experts(): lax.ppermute(ordered[step % 2], ('g', 'r', 'c'), pairs)]
  transfers between devices with their start and end apart: 14 -> 12, of which waited for: 3 -> 3; matrix products, arithmetic and copies ran while one was open for 35% -> 26% of each run, Pallas kernels for 7% -> 17%
where the time goes in v3:
time: 720 us; the launch traced here: 714 us
  Pallas kernels  267 us (37%)
  matrix products  130 us (18%)
  local copies, waits for them, and re-layouts  101 us (14%)
  starting transfers between devices  77.8 us (11%)
  other arithmetic  76.7 us (11%)
  waiting for transfers between devices  48.4 us (7%)
  between operations  13.9 us (2%)
    pallas_call x1, Pallas kernels, dispatch(): pl.pallas_call(functools.partial(dispatch_kernel, sizes, n_experts, padde...  54.7 us
    ppermute x2, starting transfers between devices, swap_cores(): return lax.ppermute(value, 'c', [(0, 1), (1, 0)])  48.9 us
    ppermute x4, waiting for transfers between devices, fetch_experts(): lax.ppermute(ordered[step % 2], ('g', 'r', 'c'), pairs)  48.3 us
    pallas_call x1, Pallas kernels, scatter_dense(): pl.pallas_call(functools.partial(scatter_kernel, sizes), out_shape=jax.Sh...  45.8 us
    pallas_call x1, Pallas kernels, gather_weights(): pl.pallas_call(functools.partial(gather_kernel, sizes, rows, mats, routin...  44.7 us
    pallas_call x1, Pallas kernels, head_step(): pl.pallas_call(functools.partial(head_kernel, sizes, images), out_shape=(...  43.8 us
    pallas_call x1, Pallas kernels, expert_forward(): pl.pallas_call(functools.partial(expert_forward_kernel, padded), grid=(so...  43.6 us
    pallas_call x1, Pallas kernels, dense_forward(): pl.pallas_call(functools.partial(dense_forward_kernel, n_experts, lengths...  24.2 us
  transfers between devices with their start and end apart: 12, of which 3 were waited for; matrix products, arithmetic and copies ran while one was open for 26% of the time, Pallas kernels for 17%

profile of v3, /device:TPU:0, one launch (start us, length us, event | category | flops | bytes accessed | tf_op | source)
XLA Modules:
  0.0 714.0 jit_solution(1496225985528797695)
XLA Ops:
  7.4 44.7 %gather_weights.1 = (bf16[5,768,768]{2,1,0:T(8,128)(2,1)}, f32[8,768]{1,0:T(8,128)S(1)}, f32[8,768]{1,0:T(8,128)S(1)}, f32[1024,128]{1,0:T(8,128)S(1)}) custom-call(f32[5,24,768]{2,1,0:T(8,128)S(1)} %copy-done.3, f32[8,768]{1,0:T(8,128)S(1)} %scatter.9.tail_ref, s32[1024,2]{1,0:T(8,128)S(1)} %copy.132.pick_ref, s32[1,1024]{1,0:T(1,128)S(1)} %copy-done.13, ...), custom_call_target="tpu_custom_call" | custom-call | tf_op jit(solution)/shard_map/gather_weights/pallas_call | solution.py:270
  62.9 15.6 %collective-permute-done.1 = bf16[2,384,768]{2,1,0:T(8,128)(2,1)S(1)} collective-permute-done((bf16[2,384,768]{2,1,0:T(8,128)(2,1)S(1)}, bf16[2,384,768]{2,1,0:T(8,128)(2,1)S(1)}, u32[]{:S(2)}, u32[]{:S(2)}) %collective-permute-start.1) | collective-permute-done | bytes 1179680 | tf_op jit(solution)/shard_map/ppermute | solution.py:973
  79.6 8.5 %collective-permute-done.2 = bf16[2,384,768]{2,1,0:T(8,128)(2,1)S(1)} collective-permute-done((bf16[2,384,768]{2,1,0:T(8,128)(2,1)S(1)}, bf16[2,384,768]{2,1,0:T(8,128)(2,1)S(1)}, u32[]{:S(2)}, u32[]{:S(2)}) %collective-permute-start.2) | collective-permute-done | bytes 1179680 | tf_op jit(solution)/shard_map/ppermute | solution.py:973
  89.3 24.2 %collective-permute-done.3 = bf16[2,384,768]{2,1,0:T(8,128)(2,1)S(1)} collective-permute-done((bf16[2,384,768]{2,1,0:T(8,128)(2,1)S(1)}, bf16[2,384,768]{2,1,0:T(8,128)(2,1)S(1)}, u32[]{:S(2)}, u32[]{:S(2)}) %collective-permute-start.3) | collective-permute-done | bytes 1179680 | tf_op jit(solution)/shard_map/ppermute | solution.py:973
  114.6 48.9 %collective-permute-start.4 = (bf16[2,1536,768]{2,1,0:T(8,128)(2,1)}, bf16[2,1536,768]{2,1,0:T(8,128)(2,1)}, u32[]{:S(2)}, u32[]{:S(2)}) collective-permute-start(bf16[2,1536,768]{2,1,0:T(8,128)(2,1)} %constant_dynamic-update-slice_fusion.own_ref), channel_id=1, source_target_pairs={{0,1},{1,0},{2,3},{3,2},{4,5},{5,4},{6,7},{7,6},{8,9},{9,8},{10,11... | collective-permute-start | bytes 14155784 | tf_op jit(solution)/shard_map/ppermute | solution.py:964
  163.7 24.2 %dense_forward.1 = (f32[1024,768]{1,0:T(8,128)}, bf16[1024,768]{1,0:T(8,128)(2,1)S(1)}, bf16[1024,2304]{1,0:T(8,128)(2,1)}, bf16[1024,768]{1,0:T(8,128)(2,1)S(1)...) custom-call(s32[4,3]{1,0:T(4,128)S(1)} %copy-done.12, ...), custom_call_target="tpu_custom_call" | custom-call | tf_op jit(solution)/shard_map/dense_forward/pallas_call | solution.py:755
  192.8 54.7 %dispatch.1 = (bf16[8,272,768]{2,1,0:T(8,128)(2,1)S(1)}, f32[8,8,384]{2,1,0:T(8,128)S(1)}) custom-call(bf16[1024,768]{1,0:T(8,128)(2,1)S(1)} %copy-done.1, f32[1024,128]{1,0:T(8,128)S(1)} %get-tuple-element.87.prob_ref, f32[1024,128]{1,0:T(8,128)S(1)} %get-tuple-element.85.col_ref), custom_call_target="tpu_custom_call" | custom-call | tf_op jit(solution)/shard_map/dispatch/pallas_call | solution.py:858
  253.6 6.7 copy.133
  280.1 43.6 %expert_forward.1 = (bf16[2176,3072]{1,0:T(8,128)(2,1)}, bf16[2176,3072]{1,0:T(8,128)(2,1)}, bf16[8,272,768]{2,1,0:T(8,128)(2,1)}, f32[8,16,768]{2,1,0:T(8,128)}) custom-call(bf16[8,272,768]{2,1,0:T(8,128)(2,1)} %copy-done, f32[8,8,384]{2,1,0:T(8,128)} %copy-done.5, bf16[2,1536,768]{2,1,0:T(8,128)(2,1)} %constant_dynamic-update-slice_fusion.own_ref, ...), custom_call_target="tpu_custom_call" | custom-call | tf_op jit(solution)/shard_map/expert_forward/pallas_call | solution.py:932
  323.8 43.8 %head_step.1 = (f32[576,768]{1,0:T(8,128)}, f32[8,16,768]{2,1,0:T(8,128)}, f32[16,768]{1,0:T(8,128)}, f32[8,768]{1,0:T(8,128)}, f32[8,128]{1,0:T(8,128)}, /*index=5*/f32[8,768]{1,0:T(8,128)}) custom-call(f32[8,16,768]{2,1,0:T(8,128)} %get-tuple-element.92.part_ref, f32[16,768]{1,0:T(8,128)} %copy-done.9, f32[8,768]{1,0:T(8,128)} %copy-done.10, ...), custom_call_target="tpu_custom_call" | custom-call | tf_op jit(solution)/shard_map/head_step/pallas_call | solution.py:570
  367.6 8.8 %multiply_convert_fusion.2 = (bf16[8,272,768]{2,1,0:T(8,128)(2,1)S(1)}, f32[8,272]{1,0:T(8,128)S(1)}) fusion(f32[8,272]{1,0:T(8,128)S(1)} %get-tuple-element.188, bf16[8,272,768]{2,1,0:T(8,128)(2,1)} %get-tuple-element.100, f32[8,16,768]{2,1,0:T(8,128)} %get-tuple-element.98, f32[8,272]{1,0:T(8,128)S(1)} %get-tuple-element.189, f32[8,272]{1,0:T(8,128)S(1)} %bitcast.167, ...), kind=kOutput, calls=%fused_computation.17 | convolution fusion | flops 249054080 | bytes 7112752 | tf_op jit(solution)/shard_map/dsi,diw->dsw/dot_general | solution.py:1121
  376.4 17.3 %fusion.20 = bf16[1,3072,768]{2,1,0:T(8,128)(2,1)} fusion(bf16[2176,3072]{1,0:T(8,128)(2,1)} %get-tuple-element.108, bf16[2176,768]{1,0:T(8,128)(2,1)S(1)} %bitcast.168), kind=kOutput, calls=%fused_computation.40 | convolution fusion | flops 10270015488 | bytes 21430272 | tf_op jit(solution)/shard_map/dot_general | solution.py:1130
  398.5 18.5 %multiply_convert_fusion = bf16[2176,3072]{1,0:T(8,128)(2,1)} fusion(bf16[2176,3072]{1,0:T(8,128)(2,1)} %get-tuple-element.99, bf16[2176,768]{1,0:T(8,128)(2,1)} %bitcast.169, bf16[1536,768]{1,0:T(8,128)(2,1)} %get-tuple-element.164, bf16[1536,768]{1,0:T(8,128)(2,1)} %get-tuple-element.162), kind=kOutput, calls=%fused_computation.2 | convolution fusion | flops 10297147392 | bytes 34799616 | tf_op jit(solution)/shard_map/dot_general | solution.py:1124
  417.0 15.6 %fusion.19 = bf16[1,3072,768]{2,1,0:T(8,128)(2,1)S(1)} fusion(bf16[2176,3072]{1,0:T(8,128)(2,1)} %multiply_convert_fusion, bf16[2176,768]{1,0:T(8,128)(2,1)} %bitcast.145), kind=kOutput, calls=%fused_computation.39 | convolution fusion | flops 10270015488 | bytes 21430272 | tf_op jit(solution)/shard_map/dot_general | solution.py:1131
  440.4 16.2 %convolution_convert_fusion.2 = bf16[2176,768]{1,0:T(8,128)(2,1)} fusion(bf16[2176,3072]{1,0:T(8,128)(2,1)} %multiply_convert_fusion, bf16[1536,768]{1,0:T(8,128)(2,1)} %get-tuple-element.163, bf16[1536,768]{1,0:T(8,128)(2,1)} %get-tuple-element.161), kind=kOutput, calls=%fused_computation.27 | convolution fusion | flops 10278764544 | bytes 21430272 | tf_op jit(solution)/shard_map/dot_general | solution.py:1126
  468.0 6.4 fusion.45
  515.6 10.3 %collective-permute-start.8 = (bf16[2,384,768]{2,1,0:T(8,128)(2,1)}, bf16[2,384,768]{2,1,0:T(8,128)(2,1)}, u32[]{:S(2)}, u32[]{:S(2)}) collective-permute-start(bf16[2,384,768]{2,1,0:T(8,128)(2,1)} %get-tuple-element.154), channel_id=1, source_target_pairs={{0,0},{8,1},{4,4},{12,5},{16,8},{24,9},{20,12},{28,13},{1,16},{9,1... | collective-permute-start | bytes 3538952 | tf_op jit(solution)/shard_map/ppermute | solution.py:983
  526.3 6.5 fusion.2
  546.3 7.2 %multiply_reduce_fusion = (f32[4,12,256]{2,1,0:T(8,128)S(1)}, f32[4,12,256,256]{2,3,1,0:T(8,128)S(1)}) fusion(f32[4,12,256,256]{2,3,1,0:T(8,128)} %fusion.45, f32[4,12,256]{2,1,0:T(8,128)S(1)} %copy.137, pred[4,256,256]{1,2,0:T(8,128)(4,1)S(1)} %or_and_fusion, bf16[4,256,12,64]{1,0,3,2:T(4,128)(2,1)S(1)} %copy-done.31, bf16[4,256,12,64]{1,0,3,2:T(4,128)(2,1)S(1)} %reshape.346), kind=kOutput, calls=%fused_computation.6 | convolution fusion | flops 418369536 | bytes 28672000 | tf_op jit(solution)/shard_map/rqhd,rkhd->rhqk/dot_general | solution.py:67
  553.5 7.1 multiply_convert_fusion.1
  586.1 7.8 %multiply_reduce_fusion.3 = (f32[1024]{0:T(1024)S(1)}, f32[768]{0:T(1024)S(1)}, f32[768]{0:T(1024)S(1)}, f32[1024,768,1]{1,0,2:T(8,128)S(1)}) fusion(f32[1024,768]{1,0:T(8,128)S(1)} %copy-done.19, f32[1024]{0:T(1024)S(1)} %broadcast_multiply_fusion, f32[768]{0:T(1024)S(1)} %get-tuple-element.118, f32[1024]{0:T(1024)S(1)} %copy-done.54, ...), kind=kOutput, calls=%fused_computation.54 | convolution fusion | flops 3634886144 | bytes 14570496 | tf_op jit(solution)/shard_map/kte,kde->td/dot_general | solution.py:1162
  615.1 45.8 %scatter_dense.1 = f32[144,768]{1,0:T(8,128)S(1)} custom-call(bf16[2,4,2,2,144,768]{5,4,3,2,1,0:T(8,128)(2,1)} %fusion.4.g_ref), custom_call_target="tpu_custom_call" | custom-call | tf_op jit(solution)/shard_map/scatter_dense/pallas_call | solution.py:370
  674.6 9.8 %share_sums.1 = f32[8,128]{1,0:T(8,128)} custom-call(f32[8,128]{1,0:T(8,128)} %iota.50.in_ref), custom_call_target="tpu_custom_call" | custom-call | tf_op jit(solution)/shard_map/share_sums/pallas_call | solution.py:418
  687.1 8.0 %multiply_add_fusion.4 = (f32[576,768]{1,0:T(8,128)}, f32[576,768]{1,0:T(8,128)}, f32[576,768]{1,0:T(8,128)}, f32[576,768]{1,0:T(8,128)}) fusion(f32[576,768]{1,0:T(8,128)} %param.65, f32[576,768]{1,0:T(8,128)} %head_ref.1, f32[576,768]{1,0:T(8,128)} %get-tuple-element.109, f32[]{:T(128)S(6)} %min.3, f32[576,768]{1,0:T(8,128)} %param.63, f32[576,768]{1,0:T(8,128)} %param.64), kind=kLoop, calls=%fused_computation.86 | loop fusion | flops 8404992 | bytes 15925252 | tf_op jit(solution)/shard_map/add | solution.py:49
  (277 shorter events, 199.8 us)
Async XLA Ops:
  52.2 111.5 %copy-start.6 = (f32[8,768]{1,0:T(8,128)}, f32[8,768]{1,0:T(8,128)S(1)}, u32[]{:S(2)}) copy-start(f32[8,768]{1,0:T(8,128)S(1)} %get-tuple-element.83.gain_ref) | copy-start | bytes 73732
  55.1 6.7 collective-permute-start
  55.8 22.7 %collective-permute-start.1 = (bf16[2,384,768]{2,1,0:T(8,128)(2,1)S(1)}, bf16[2,384,768]{2,1,0:T(8,128)(2,1)S(1)}, u32[]{:S(2)}, u32[]{:S(2)}) collective-permute-start(bf16[2,384,768]{2,1,0:T(8,128)(2,1)S(1)} %get-tuple-element.169), channel_id=1, source_target_pairs={{0,4},{1,12},{4,16},{5,24},{8,20},{9,28},{12,0},{13,8},{16,5},{17,... | collective-permute-start | bytes 3538952 | tf_op jit(solution)/shard_map/ppermute | solution.py:973
  57.8 30.3 %collective-permute-start.2 = (bf16[2,384,768]{2,1,0:T(8,128)(2,1)S(1)}, bf16[2,384,768]{2,1,0:T(8,128)(2,1)S(1)}, u32[]{:S(2)}, u32[]{:S(2)}) collective-permute-start(bf16[2,384,768]{2,1,0:T(8,128)(2,1)S(1)} %get-tuple-element.170), channel_id=1, source_target_pairs={{0,16},{1,24},{4,20},{5,28},{8,0},{9,8},{12,4},{13,12},{16,17},{17... | collective-permute-start | bytes 3538952 | tf_op jit(solution)/shard_map/ppermute | solution.py:973
  61.7 51.8 %collective-permute-start.3 = (bf16[2,384,768]{2,1,0:T(8,128)(2,1)S(1)}, bf16[2,384,768]{2,1,0:T(8,128)(2,1)S(1)}, u32[]{:S(2)}, u32[]{:S(2)}) collective-permute-start(bf16[2,384,768]{2,1,0:T(8,128)(2,1)S(1)} %get-tuple-element.169), channel_id=1, source_target_pairs={{0,20},{1,28},{4,0},{5,8},{8,4},{9,12},{12,16},{13,24},{16,21},{17... | collective-permute-start | bytes 3538952 | tf_op jit(solution)/shard_map/ppermute | solution.py:973
  79.6 84.0 %copy-start.12 = (s32[4,3]{1,0:T(4,128)S(1)}, s32[4,3]{1,0:T(4,128)}, u32[]{:S(2)}) copy-start(s32[4,3]{1,0:T(4,128)} %length_ref.3) | copy-start | bytes 148
  114.6 165.6 %collective-permute-start.4 = (bf16[2,1536,768]{2,1,0:T(8,128)(2,1)}, bf16[2,1536,768]{2,1,0:T(8,128)(2,1)}, u32[]{:S(2)}, u32[]{:S(2)}) collective-permute-start(bf16[2,1536,768]{2,1,0:T(8,128)(2,1)} %constant_dynamic-update-slice_fusion.own_ref), channel_id=1, source_target_pairs={{0,1},{1,0},{2,3},{3,2},{4,5},{5,4},{6,7},{7,6},{8,9},{9,8},{10,11... | collective-permute-start | bytes 14155784 | tf_op jit(solution)/shard_map/ppermute | solution.py:964
  163.7 85.6 %copy-start.8 = (s32[4,256]{1,0:T(4,128)S(1)}, s32[4,256]{1,0:T(4,128)}, u32[]{:S(2)}) copy-start(s32[4,256]{1,0:T(4,128)} %mask_ref.1) | copy-start | bytes 12292
  270.1 197.9 %copy-start.20 = (bf16[4,256,12,64]{1,0,3,2:T(4,128)(2,1)}, bf16[4,256,12,64]{1,0,3,2:T(4,128)(2,1)S(1)}, u32[]{:S(2)}) copy-start(bf16[4,256,12,64]{1,0,3,2:T(4,128)(2,1)S(1)} %squeeze.59) | copy-start | bytes 4718596
  376.4 17.3 %copy-start.64 = (bf16[8,272,768]{2,1,0:T(8,128)(2,1)}, bf16[8,272,768]{2,1,0:T(8,128)(2,1)S(1)}, u32[]{:S(2)}) copy-start(bf16[8,272,768]{2,1,0:T(8,128)(2,1)S(1)} %get-tuple-element.150) | copy-start | bytes 10027012
  417.0 15.6 %copy-start.22 = (bf16[1,3072,768]{2,1,0:T(8,128)(2,1)S(1)}, bf16[1,3072,768]{2,1,0:T(8,128)(2,1)}, u32[]{:S(2)}) copy-start(bf16[1,3072,768]{2,1,0:T(8,128)(2,1)} %fusion.20) | copy-start | bytes 14155780
  436.2 69.9 %collective-permute-start.5 = (bf16[2,1536,768]{2,1,0:T(8,128)(2,1)}, bf16[2,1536,768]{2,1,0:T(8,128)(2,1)}, u32[]{:S(2)}, u32[]{:S(2)}) collective-permute-start(bf16[2,1536,768]{2,1,0:T(8,128)(2,1)} %pad_maximum_fusion.1), channel_id=1, source_target_pairs={{0,1},{1,0},{2,3},{3,2},{4,5},{5,4},{6,7},{7,6},{8,9},{9,8},{10,11... | collective-permute-start | bytes 14155784 | tf_op jit(solution)/shard_map/ppermute | solution.py:964
  436.8 19.8 %all-to-all-start.1 = ((f32[8,1,272]{2,1,0:T(1,128)}), f32[8,1,272]{2,1,0:T(1,128)S(1)}, u32[]{:S(2)}, u32[]{:S(2)}) async-start(f32[8,1,272]{2,1,0:T(1,128)} %all_to_all.10), calls=%async_computation.1 | async-start | bytes 24576 | tf_op jit(solution)/shard_map/all_to_all | solution.py:991
  456.6 69.7 %all-to-all-start = ((bf16[8,272,768]{2,1,0:T(8,128)(2,1)}), bf16[8,272,768]{2,1,0:T(8,128)(2,1)}, u32[]{:S(2)}, u32[]{:S(2)}) async-start(bf16[8,272,768]{2,1,0:T(8,128)(2,1)} %bitcast.153), calls=%async_computation | async-start | bytes 6684672 | tf_op jit(solution)/shard_map/all_to_all | solution.py:991
  468.0 10.2 %copy-start.51 = (f32[16,768]{1,0:T(8,128)S(1)}, f32[16,768]{1,0:T(8,128)}, u32[]{:S(2)}) copy-start(f32[16,768]{1,0:T(8,128)} %get-tuple-element.103) | copy-start | bytes 147460
  512.6 152.1 %collective-permute-start.6 = (bf16[2,384,768]{2,1,0:T(8,128)(2,1)}, bf16[2,384,768]{2,1,0:T(8,128)(2,1)}, u32[]{:S(2)}, u32[]{:S(2)}) collective-permute-start(bf16[2,384,768]{2,1,0:T(8,128)(2,1)} %get-tuple-element.156), channel_id=1, source_target_pairs={{4,0},{12,1},{16,4},{24,5},{20,8},{28,9},{0,12},{8,13},{5,16},{13,... | collective-permute-start | bytes 3538952 | tf_op jit(solution)/shard_map/ppermute | solution.py:983
  515.6 149.2 %collective-permute-start.7 = (bf16[2,384,768]{2,1,0:T(8,128)(2,1)}, bf16[2,384,768]{2,1,0:T(8,128)(2,1)}, u32[]{:S(2)}, u32[]{:S(2)}) collective-permute-start(bf16[2,384,768]{2,1,0:T(8,128)(2,1)} %get-tuple-element.155), channel_id=1, source_target_pairs={{20,0},{28,1},{0,4},{8,5},{4,8},{12,9},{16,12},{24,13},{21,16},{29... | collective-permute-start | bytes 3538952 | tf_op jit(solution)/shard_map/ppermute | solution.py:983
  515.6 149.2 %collective-permute-start.8 = (bf16[2,384,768]{2,1,0:T(8,128)(2,1)}, bf16[2,384,768]{2,1,0:T(8,128)(2,1)}, u32[]{:S(2)}, u32[]{:S(2)}) collective-permute-start(bf16[2,384,768]{2,1,0:T(8,128)(2,1)} %get-tuple-element.154), channel_id=1, source_target_pairs={{0,0},{8,1},{4,4},{12,5},{16,8},{24,9},{20,12},{28,13},{1,16},{9,1... | collective-permute-start | bytes 3538952 | tf_op jit(solution)/shard_map/ppermute | solution.py:983
  525.9 138.9 %collective-permute-start.9 = (bf16[2,384,768]{2,1,0:T(8,128)(2,1)}, bf16[2,384,768]{2,1,0:T(8,128)(2,1)}, u32[]{:S(2)}, u32[]{:S(2)}) collective-permute-start(bf16[2,384,768]{2,1,0:T(8,128)(2,1)} %get-tuple-element.157), channel_id=1, source_target_pairs={{16,0},{24,1},{20,4},{28,5},{0,8},{8,9},{4,12},{12,13},{17,16},{25... | collective-permute-start | bytes 3538952 | tf_op jit(solution)/shard_map/ppermute | solution.py:983
  553.5 8.1 %copy-start.21 = (bf16[4,256,12,64]{1,0,3,2:T(4,128)(2,1)S(1)}, bf16[4,256,12,64]{1,0,3,2:T(4,128)(2,1)}, u32[]{:S(2)}) copy-start(bf16[4,256,12,64]{1,0,3,2:T(4,128)(2,1)} %copy-done.20) | copy-start | bytes 4718596
  687.1 8.1 %copy-start.28 = (f32[1,384,768]{2,1,0:T(8,128)S(1)}, f32[1,384,768]{2,1,0:T(8,128)}, u32[]{:S(2)}) copy-start(f32[1,384,768]{2,1,0:T(8,128)} %copy-done.27) | copy-start | bytes 3538948
  687.1 8.1 %copy-start.30 = (f32[1,384,768]{2,1,0:T(8,128)S(1)}, f32[1,384,768]{2,1,0:T(8,128)}, u32[]{:S(2)}) copy-start(f32[1,384,768]{2,1,0:T(8,128)} %copy-done.29) | copy-start | bytes 3538948
  687.1 8.4 %copy-start.37 = (f32[2,384,768]{2,1,0:T(8,128)S(1)}, f32[2,384,768]{2,1,0:T(8,128)}, u32[]{:S(2)}) copy-start(f32[2,384,768]{2,1,0:T(8,128)} %param.59) | copy-start | bytes 7077892
  687.1 9.6 %copy-start.38 = (f32[2,384,768]{2,1,0:T(8,128)S(1)}, f32[2,384,768]{2,1,0:T(8,128)}, u32[]{:S(2)}) copy-start(f32[2,384,768]{2,1,0:T(8,128)} %param.60) | copy-start | bytes 7077892
  (56 other events, 216.7 us)

commit v4 on v3

--- a/solution.py
+++ b/solution.py
@@ -31,12 +31,6 @@
 MEMBERS = ("x", "r")
 
 
-def layer_norm(values, gain, shift):
-    centre = values - jnp.mean(values, -1, keepdims=True)
-    spread = jnp.mean(centre * centre, -1, keepdims=True)
-    return centre * lax.rsqrt(spread + eps_norm) * gain + shift
-
-
 def adam_update(weight, first_state, second_state, average_state, gradient, factor, step_rate):
     clipped = gradient * factor
     first_new = beta_first * first_state + (1.0 - beta_first) * clipped
@@ -50,46 +44,14 @@
     return (weight_new, first_new, second_new, average_new)
 
 
-def split_heads(proj_qkv, allow_mask, n_heads):
-    n_rows, n_slots_row = (allow_mask.shape[0], allow_mask.shape[1])
-    head_dim = proj_qkv.shape[-1] // n_heads
-    shaped = proj_qkv.reshape(3, n_rows, n_slots_row, n_heads, head_dim)
-    scores = jnp.einsum(
-        "rqhd,rkhd->rhqk", shaped[0], shaped[1], preferred_element_type=jnp.float32
-    ) * head_dim ** (-0.5)
-    return (shaped, jnp.where(allow_mask[:, None], scores, mask_fill), head_dim ** (-0.5))
-
-
-def attention_backward(proj_qkv, allow_mask, log_total, d_output, n_heads):
-    shaped, masked, score_scale = split_heads(proj_qkv, allow_mask, n_heads)
-    att_probs = jnp.exp(masked - log_total)
-    grad_out = d_output.reshape(shaped.shape[1:])
-    d_probs = jnp.einsum("rqhd,rkhd->rhqk", grad_out, shaped[2], preferred_element_type=jnp.float32)
-    d_values = jnp.einsum(
-        "rhqk,rqhd->rkhd",
-        att_probs.astype(jnp.bfloat16),
-        grad_out,
-        preferred_element_type=jnp.float32,
-    )
-    d_scores = (att_probs * (d_probs - jnp.sum(att_probs * d_probs, -1, keepdims=True))).astype(
-        jnp.bfloat16
-    )
-    d_query = (
-        jnp.einsum("rhqk,rkhd->rqhd", d_scores, shaped[1], preferred_element_type=jnp.float32)
-        * score_scale
-    )
-    d_keys = (
-        jnp.einsum("rhqk,rqhd->rkhd", d_scores, shaped[0], preferred_element_type=jnp.float32)
-        * score_scale
-    )
-    stacked = jnp.stack([d_query, d_keys, d_values]).astype(jnp.bfloat16)
-    return stacked.reshape(proj_qkv.shape)
-
-
 MESH_ID = pl.DeviceIdType.MESH
 VMEM = pltpu.VMEM
 ANY = pl.ANY
 MIB = 1 << 20
+
+
+def cost(microseconds):
+    return pl.CostEstimate(flops=int(microseconds * 1.15e9), bytes_accessed=0, transcendentals=0)
 
 
 def whole(space=None):
@@ -282,6 +244,7 @@
         compiler_params=pltpu.CompilerParams(
             collective_id=1, has_side_effects=True, vmem_limit_bytes=48 * MIB
         ),
+        cost_estimate=cost(44),
         name="gather_weights",
     )(dense, tail, picks, ranks, slot_mask, lengths)
 
@@ -385,6 +348,7 @@
         compiler_params=pltpu.CompilerParams(
             collective_id=2, has_side_effects=True, vmem_limit_bytes=48 * MIB
         ),
+        cost_estimate=cost(45),
         name="scatter_dense",
     )(blocks)
 
@@ -422,6 +386,7 @@
         out_specs=whole(),
         scratch_shapes=[VMEM((count, *values.shape), jnp.float32), dma((count,)), dma((count,))],
         compiler_params=pltpu.CompilerParams(collective_id=3, has_side_effects=True),
+        cost_estimate=cost(10),
         name="share_sums",
     )(values)
 
@@ -595,6 +560,7 @@
         compiler_params=pltpu.CompilerParams(
             collective_id=4, has_side_effects=True, vmem_limit_bytes=56 * MIB
         ),
+        cost_estimate=cost(42),
         name="head_step",
     )(part, own, imp, gains, head, label)
 
@@ -769,6 +735,7 @@
             block(128), block(128), fixed((IMAGE_PAD, width)), fixed((8, width)),
         ),
         compiler_params=pltpu.CompilerParams(vmem_limit_bytes=48 * MIB),
+        cost_estimate=cost(25),
         name="dense_forward",
     )(lengths, slot_mask[:, None, :], patches, weights, gains, routers, columns)
 
@@ -872,6 +839,7 @@
         compiler_params=pltpu.CompilerParams(
             collective_id=5, has_side_effects=True, vmem_limit_bytes=48 * MIB
         ),
+        cost_estimate=cost(50),
         name="dispatch",
     )(a_two, probs, columns)
 
@@ -887,24 +855,24 @@
 ):
     many, unused, width = rows_ref.shape
     rows = rows_ref[...].reshape(many * padded, width)
-    half = own_ref.shape[1]
-    step = 384
+    chunks, unused, part = act_ref.shape
+    half = chunks // 2
     total = None
-    for index, ref in enumerate((own_ref, other_ref)):
-        for start in range(0, half, step):
-            hidden = dot_f32(rows, ref[0, start : start + step], NT)
-            square = hidden * hidden
-            curve = jnp.tanh(0.7978845608 * hidden * (1.0 + 0.044715 * square))
-            upper = 0.5 * (1.0 + curve)
-            act = (hidden * upper).astype(jnp.bfloat16)
-            slope = upper + 0.5 * hidden * (1.0 - curve * curve) * (
-                0.7978845608 + 3.0 * 0.7978845608 * 0.044715 * square
-            )
-            spot = index * half + start
-            act_ref[:, spot : spot + step] = act
-            slope_ref[:, spot : spot + step] = slope.astype(jnp.bfloat16)
-            found = dot_f32(act, ref[1, start : start + step], NN)
-            total = found if total is None else total + found
+    for index in range(chunks):
+        ref, start = (own_ref, index * part) if index < half else (other_ref, (index - half) * part)
+        hidden = dot_f32(rows, ref[0, start : start + part], NT)
+        square = hidden * hidden
+        curve = jnp.tanh(hidden * (0.7978845608 + 0.7978845608 * 0.044715 * square))
+        upper = 0.5 + 0.5 * curve
+        gelu = hidden * upper
+        act = gelu.astype(jnp.bfloat16)
+        slope = upper + gelu * (1.0 - upper) * (
+            2.0 * 0.7978845608 + 6.0 * 0.7978845608 * 0.044715 * square
+        )
+        act_ref[index] = act
+        slope_ref[index] = slope.astype(jnp.bfloat16)
+        found = dot_f32(act, ref[1, start : start + part], NN)
+        total = found if total is None else total + found
     result = total.astype(jnp.bfloat16)
     y_ref[...] = result.reshape(many, padded, width)
     for source in range(many):
@@ -918,9 +886,9 @@
         )
 
 
-def expert_forward(rows, details, own_half, other_half):
+def expert_forward(rows, details, own_half, other_half, chunks):
     sources, padded, width = rows.shape
-    hidden = 2 * own_half.shape[1]
+    part = 2 * own_half.shape[1] // chunks
     many = max(1, 576 // padded)
     lanes = details.shape[2]
     half = jnp.bfloat16
@@ -928,21 +896,378 @@
     def by_source(*shape):
         return pl.BlockSpec((many, *shape), lambda i: (i, 0, 0))
 
-    flat = pl.BlockSpec((many * padded, hidden), lambda i: (i, 0))
+    flat = pl.BlockSpec((chunks, many * padded, part), lambda i: (0, i, 0))
     return pl.pallas_call(
         functools.partial(expert_forward_kernel, padded),
         grid=(sources // many,),
         out_shape=(
-            jax.ShapeDtypeStruct((sources * padded, hidden), half),
-            jax.ShapeDtypeStruct((sources * padded, hidden), half),
+            jax.ShapeDtypeStruct((chunks, sources * padded, part), half),
+            jax.ShapeDtypeStruct((chunks, sources * padded, part), half),
             jax.ShapeDtypeStruct((sources, padded, width), half),
             jax.ShapeDtypeStruct((sources, IMAGE_PAD, width), jnp.float32),
         ),
         in_specs=[by_source(padded, width), by_source(8, lanes), whole(), whole()],
         out_specs=(flat, flat, by_source(padded, width), by_source(IMAGE_PAD, width)),
         compiler_params=pltpu.CompilerParams(vmem_limit_bytes=56 * MIB),
+        cost_estimate=cost(40),
         name="expert_forward",
     )(rows, details, own_half, other_half)
+
+
+def expert_backward_kernel(
+    sizes, padded, rows_ref, detail_ref, pool_ref, y_ref, slope_ref, act_ref, own_ref, other_ref, *refs
+):
+    at = Place(sizes)
+    sources, unused, width = rows_ref.shape
+    chunks, unused, part = slope_ref.shape
+    half = chunks // 2
+    back_ref, gate_ref, *outs = refs[: 2 + half]
+    d_hidden, d_rows, send_rows, send_gate, send_grad, got_grad = refs[2 + half : 8 + half]
+    own_sem, r_out, r_in, m_out, m_in, g_out, g_in, g_keep = refs[8 + half :]
+    many = y_ref.shape[0]
+    rounds = sources // many
+    step = pl.program_id(0)
+    team = others(at.member, sources)
+
+    def row_copy(member, source):
+        return send(
+            send_rows.at[member], back_ref.at[source], r_out.at[member], r_in.at[source], at.of_member(member)
+        )
+
+    def gate_copy(member, source):
+        return send(
+            send_gate.at[member], gate_ref.at[source], m_out.at[member], m_in.at[source], at.of_member(member)
+        )
+
+    def keep_copies():
+        return (
+            pltpu.make_async_copy(send_rows.at[at.member], back_ref.at[at.member], own_sem.at[0]),
+            pltpu.make_async_copy(send_gate.at[at.member], gate_ref.at[at.member], own_sem.at[1]),
+        )
+
+    def grad_copy(index):
+        return send(
+            send_grad.at[index], got_grad.at[index], g_out.at[index], g_in.at[index], at.sibling()
+        )
+
+    def out_copy(index):
+        return pltpu.make_async_copy(got_grad.at[index], outs[index], g_keep.at[index])
+
+    @pl.when(step == 0)
+    def _():
+        greet([at.of_member(member) for member in team] + [at.sibling()])
+
+    @pl.when(step < rounds)
+    def _():
+        block = lax.rem(lax.div(at.member, many) + 1 + step, rounds)
+        d_out = []
+        for index in range(many):
+            source = block * many + index
+            detail = detail_ref[source]
+            hot = image_hot(detail, padded)
+            hots = jnp.where(hot, 1.0, 0.0).astype(jnp.bfloat16)
+            pools = jnp.concatenate(split_three(pool_ref[source]), 0)
+            wide = dot_f32(jnp.concatenate([hots] * 3, 0), pools, TN)
+            lanes = detail.shape[1]
+            upright = jnp.concatenate([detail, jnp.zeros((120, lanes), jnp.float32)], 0).T
+            gate, pool = upright[:padded, 0:1], upright[:padded, 1:2]
+            d_out.append((gate * (pool * wide)).astype(jnp.bfloat16))
+            along = dot_f32(pools, y_ref[index], NT)
+            along = along[:IMAGE_PAD] + along[IMAGE_PAD : 2 * IMAGE_PAD] + along[2 * IMAGE_PAD :]
+            d_gate = jnp.sum(jnp.where(hot, along, 0.0), 0, keepdims=True) * detail[1:2, :padded]
+            send_gate[source] = jnp.zeros(detail.shape, jnp.float32)
+            send_gate[source, 0:1, :padded] = d_gate
+        d_out = jnp.concatenate(d_out, 0)
+        count = many * padded
+        span = pl.ds(pl.multiple_of(block * count, 16), count)
+        d_rows[span] = d_out
+        total = None
+        for index in range(chunks):
+            ref, start = (own_ref, index * part) if index < half else (other_ref, (index - half) * part)
+            d_act = dot_f32(d_out, ref[1, start : start + part], NT)
+            d_hid = (d_act * slope_ref[index].astype(jnp.float32)).astype(jnp.bfloat16)
+            d_hidden[index, span] = d_hid
+            found = dot_f32(d_hid, ref[0, start : start + part], NN)
+            total = found if total is None else total + found
+        total = total.astype(jnp.bfloat16)
+        for index in range(many):
+            source = block * many + index
+            send_rows[source] = total[index * padded : (index + 1) * padded]
+
+            @pl.when(source != at.member)
+            def _():
+                row_copy(source, at.member).start()
+                gate_copy(source, at.member).start()
+
+            @pl.when(source == at.member)
+            def _():
+                for copy in keep_copies():
+                    copy.start()
+
+    @pl.when(step >= rounds)
+    def _():
+        index = step - rounds
+        chunk = lax.rem(index + half, chunks)
+        rows = rows_ref[...].reshape(sources * padded, width)
+        g_one = dot_f32(d_hidden[chunk], rows, TN)
+        g_two = dot_f32(act_ref[0], d_rows[...], TN)
+
+        @pl.when(index < half)
+        def _():
+            send_grad[index, 0] = g_one.astype(jnp.bfloat16)
+            send_grad[index, 1] = g_two.astype(jnp.bfloat16)
+            grad_copy(index).start()
+
+        @pl.when(index >= half)
+        def _():
+            spot = index - half
+            grad_copy(spot).wait_recv()
+            got_grad[spot, 0] = (got_grad[spot, 0].astype(jnp.float32) + g_one).astype(jnp.bfloat16)
+            got_grad[spot, 1] = (got_grad[spot, 1].astype(jnp.float32) + g_two).astype(jnp.bfloat16)
+
+        for spot in range(half):
+
+            @pl.when(index == spot + half)
+            def _():
+                out_copy(spot).start()
+
+    @pl.when(step == rounds + chunks - 1)
+    def _():
+        for member in team:
+            row_copy(member, member).wait_recv()
+            gate_copy(member, member).wait_recv()
+        for member in team:
+            row_copy(member, at.member).wait_send()
+            gate_copy(member, at.member).wait_send()
+        for copy in keep_copies():
+            copy.wait()
+        for spot in range(half):
+            grad_copy(spot).wait_send()
+            out_copy(spot).wait()
+
+
+def expert_backward(sizes, rows, details, pools, results, slopes, acts, own_half, other_half):
+    sources, padded, width = rows.shape
+    chunks, count, part = acts.shape
+    many = max(1, 576 // padded)
+    rounds, half = sources // many, chunks // 2
+    lanes = details.shape[2]
+    kind = jnp.bfloat16
+    dma = pltpu.SemaphoreType.DMA
+    each, parts = dma((sources,)), dma((half,))
+
+    def block_of(step):
+        member = lax.axis_index("x") * QUAD + lax.axis_index("r")
+        return lax.rem(lax.div(member, many) + 1 + jnp.minimum(step, rounds - 1), rounds)
+
+    def chunk_of(step):
+        return lax.rem(jnp.maximum(step - rounds, 0) + half, chunks)
+
+    return pl.pallas_call(
+        functools.partial(expert_backward_kernel, sizes, padded),
+        grid=(rounds + chunks,),
+        out_shape=(
+            jax.ShapeDtypeStruct((sources, padded, width), kind),
+            jax.ShapeDtypeStruct((sources, 8, lanes), jnp.float32),
+        )
+        + (jax.ShapeDtypeStruct((2, part, width), kind),) * half,
+        in_specs=[
+            whole(), whole(), whole(),
+            pl.BlockSpec((many, padded, width), lambda i: (block_of(i), 0, 0)),
+            pl.BlockSpec((chunks, many * padded, part), lambda i: (0, block_of(i), 0)),
+            pl.BlockSpec((1, count, part), lambda i: (chunk_of(i), 0, 0)),
+            whole(), whole(),
+        ],
+        out_specs=(whole(ANY),) * (2 + half),
+        scratch_shapes=[
+            VMEM((chunks, count, part), kind),
+            VMEM((count, width), kind),
+            VMEM((sources, padded, width), kind),
+            VMEM((sources, 8, lanes), jnp.float32),
+            VMEM((half, 2, part, width), kind),
+            VMEM((half, 2, part, width), kind),
+            dma((2,)), each, each, each, each, parts, parts, parts,
+        ],
+        compiler_params=pltpu.CompilerParams(
+            collective_id=6, has_side_effects=True, vmem_limit_bytes=62 * MIB
+        ),
+        cost_estimate=cost(65),
+        name="expert_backward",
+    )(rows, details, pools, results, slopes, acts, own_half, other_half)
+
+
+def dense_backward_kernel(
+    sizes, n_experts, images, padded, length_ref, mask_ref, patch_ref, x_zero_ref, a_one_ref, qkv_ref, att_ref,
+    x_one_ref, a_two_ref, prob_ref, lse_ref, col_ref, w_ref, gain_ref, router_ref, back_ref, gate_ref,
+    pool_ref, imp_ref, third_ref, out_ref, grads, g_router, g_norm, d_qkv
+):
+    row = pl.program_id(0)
+    span, width = patch_ref.shape
+    mats, rows = grads.shape[0], width // (8 * sizes["g"] * sizes["x"])
+
+    @pl.when(row == 0)
+    def _():
+        grads[...] = jnp.zeros_like(grads)
+        g_router[...] = jnp.zeros_like(g_router)
+        g_norm[...] = third_ref[...]
+
+    columns = col_ref[...]
+    slot_one, slot_two = columns[:, 0:1], columns[:, 1:2]
+    count = n_experts * padded
+    slot = lax.broadcasted_iota(jnp.int32, (span, count), 1).astype(jnp.float32)
+    match = jnp.where((slot == slot_one) | (slot == slot_two), 1.0, 0.0).astype(jnp.bfloat16)
+    d_a_two = dot_f32(match, back_ref[...].reshape(count, width), NN)
+    lanes = gate_ref.shape[2]
+    spot = lax.broadcasted_iota(jnp.int32, (span, lanes), 1)
+    inside = spot < padded
+    spot = spot.astype(jnp.float32)
+    found_one, found_two = jnp.zeros((span, lanes), jnp.float32), jnp.zeros((span, lanes), jnp.float32)
+    for expert in range(n_experts):
+        line = jnp.broadcast_to(gate_ref[expert, 0:1], (span, lanes))
+        found_one = jnp.where(inside & (spot == slot_one - expert * padded), line, found_one)
+        found_two = jnp.where(inside & (spot == slot_two - expert * padded), line, found_two)
+    d_gate_one = jnp.sum(found_one, 1, keepdims=True)
+    d_gate_two = jnp.sum(found_two, 1, keepdims=True)
+    lane = lax.broadcasted_iota(jnp.int32, (span, 128), 1)
+    number = lane.astype(jnp.float32)
+    valid, pool, image = columns[:, 2:3], columns[:, 3:4], columns[:, 4:5]
+    head = lax.broadcasted_iota(jnp.int32, (1, 128), 1) < n_experts
+    importance = imp_ref[0:1, 0:128]
+    centre = jnp.sum(jnp.where(head, importance, 0.0), 1, keepdims=True) / n_experts
+    away = jnp.where(head, importance - centre, 0.0)
+    spread = jnp.sum(away * away, 1, keepdims=True) / n_experts
+    d_imp = aux_weight * (
+        2.0 * away / (n_experts * centre * centre)
+        - 2.0 * spread / (n_experts * centre * centre * centre)
+    )
+    d_probs = valid * d_imp
+    d_probs = d_probs + jnp.where(number == columns[:, 5:6], d_gate_one, 0.0)
+    d_probs = d_probs + jnp.where(number == columns[:, 6:7], d_gate_two, 0.0)
+    probs = prob_ref[...]
+    d_router = (probs * (d_probs - jnp.sum(probs * d_probs, 1, keepdims=True))).astype(jnp.bfloat16)
+    g_router[...] += dot_f32(d_router, a_two_ref[...], TN)
+    routers = router_ref[...].astype(jnp.bfloat16)
+    if routers.shape[0] < 128:
+        routers = jnp.concatenate(
+            [routers, jnp.zeros((128 - routers.shape[0], width), jnp.bfloat16)], 0
+        )
+    d_a_two = d_a_two + dot_f32(d_router, routers, NN)
+    scaled, scale = norm_parts(x_one_ref[...])
+    g_norm[1:2] += jnp.sum(d_a_two * scaled, 0, keepdims=True)
+    g_norm[4:5] += jnp.sum(d_a_two, 0, keepdims=True)
+    d_x_one = norm_back(d_a_two, scaled, scale, gain_ref[1:2])
+    for index in range(images):
+        place = row * images + index
+        weight = jnp.where(image == place.astype(jnp.float32), pool, 0.0)
+        d_x_one = d_x_one + weight * pool_ref[pl.ds(place, 1)]
+    d_att = d_x_one.astype(jnp.bfloat16)
+    grads[4] += dot_f32(att_ref[...], d_att, TN)
+    d_out = dot_f32(d_att, w_ref[4], NT).astype(jnp.bfloat16)
+    open_to = allowed_slots(length_ref, row, images, mask_ref[0], span)
+    logs = lse_ref[...]
+    for pair in range(width // 128):
+        query, key, value = (
+            qkv_ref[:, part * width + pair * 128 : part * width + (pair + 1) * 128]
+            for part in range(3)
+        )
+        d_pair = d_out[:, pair * 128 : (pair + 1) * 128]
+        found = []
+        for side in range(2):
+            left = (lane < 64) == (side == 0)
+            held = jnp.where(left, query, jnp.zeros_like(query))
+            scores = jnp.where(open_to, dot_f32(held, key, NT) * 64**-0.5, mask_fill)
+            total = logs[:, 2 * pair + side : 2 * pair + side + 1]
+            chance = jnp.exp(scores - total)
+            d_held = jnp.where(left, d_pair, jnp.zeros_like(d_pair))
+            d_chance = dot_f32(d_held, value, NT)
+            d_value = dot_f32(chance.astype(jnp.bfloat16), d_pair, TN)
+            d_scores = chance * (d_chance - jnp.sum(chance * d_chance, 1, keepdims=True))
+            d_scores = d_scores.astype(jnp.bfloat16)
+            d_query = dot_f32(d_scores, key, NN) * 64**-0.5
+            d_key = dot_f32(d_scores, query, TN) * 64**-0.5
+            found.append((d_query, d_key, d_value))
+        for part in range(3):
+            d_qkv[:, part * width + pair * 128 : part * width + (pair + 1) * 128] = jnp.where(
+                lane < 64, found[0][part], found[1][part]
+            ).astype(jnp.bfloat16)
+    d_a_one = None
+    for part in range(3):
+        piece = d_qkv[:, part * width : (part + 1) * width]
+        grads[1 + part] += dot_f32(a_one_ref[...], piece, TN)
+        found = dot_f32(piece, w_ref[1 + part], NT)
+        d_a_one = found if d_a_one is None else d_a_one + found
+    scaled, scale = norm_parts(x_zero_ref[...])
+    g_norm[0:1] += jnp.sum(d_a_one * scaled, 0, keepdims=True)
+    g_norm[3:4] += jnp.sum(d_a_one, 0, keepdims=True)
+    d_x_zero = norm_back(d_a_one, scaled, scale, gain_ref[0:1]) + d_x_one
+    grads[0] += dot_f32(patch_ref[...], d_x_zero.astype(jnp.bfloat16), TN)
+
+    @pl.when(row == pl.num_programs(0) - 1)
+    def _():
+        Z, Y, X = QUAD, sizes["g"], sizes["x"]
+        tall = max(8, n_experts)
+        norms = g_norm[...]
+        if tall > 8:
+            norms = jnp.concatenate([norms, jnp.zeros((tall - 8, width), jnp.float32)], 0)
+        router_grads = g_router[:tall]
+        depth = out_ref.shape[4]
+        device = 0
+        for z in range(Z):
+            for y in range(Y):
+                for x in range(X):
+                    for c in range(2):
+                        spot = slice(device * rows, (device + 1) * rows)
+                        blank = jnp.zeros((tall, 128 - rows), jnp.float32)
+                        tail = [norms[:, spot], blank, router_grads[:, spot], blank]
+                        tail.append(jnp.zeros((tall, width - 256), jnp.float32))
+                        pieces = [grads[mat, spot] for mat in range(mats)]
+                        pieces.append(jnp.concatenate(tail, 1))
+                        left = depth - mats * rows - tall
+                        if left:
+                            pieces.append(jnp.zeros((left, width), jnp.float32))
+                        out_ref[c, z, x, y] = jnp.concatenate(pieces, 0).astype(jnp.bfloat16)
+                        device += 1
+
+
+def dense_backward(
+    sizes, n_experts, padded, rows_own, lengths, slot_mask, patches, kept, columns, weights, gains, routers, back,
+    gates, pooled, importance, third
+):
+    rows_here, span = slot_mask.shape
+    tokens, width = patches.shape
+    mats = weights.shape[0]
+    depth = round_up(mats * rows_own + max(8, n_experts), 16)
+    x_zero, a_one, qkv, att, x_one, a_two, probs, logs = kept
+
+    def block(wide):
+        return pl.BlockSpec((span, wide), lambda i: (i, 0))
+
+    return pl.pallas_call(
+        functools.partial(dense_backward_kernel, sizes, n_experts, lengths.shape[1], padded),
+        grid=(rows_here,),
+        out_shape=jax.ShapeDtypeStruct(
+            (2, QUAD, sizes["x"], sizes["g"], depth, width), jnp.bfloat16
+        ),
+        in_specs=[
+            whole(pltpu.SMEM), pl.BlockSpec((1, 1, span), lambda i: (i, 0, 0)), block(width),
+            block(width), block(width), block(3 * width), block(width), block(width), block(width),
+            block(128), block(128), block(128),
+        ]
+        + [whole()] * 8,
+        out_specs=whole(),
+        scratch_shapes=[
+            VMEM((mats, width, width), jnp.float32),
+            VMEM((128, width), jnp.float32),
+            VMEM((8, width), jnp.float32),
+            VMEM((span, 3 * width), jnp.bfloat16),
+        ],
+        compiler_params=pltpu.CompilerParams(vmem_limit_bytes=60 * MIB),
+        cost_estimate=cost(50),
+        name="dense_backward",
+    )(
+        lengths, slot_mask[:, None, :], patches, x_zero, a_one, qkv, att, x_one, a_two, probs, logs, columns,
+        weights, gains, routers, back, gates, pooled, importance, third,
+    )
 
 
 def shard_moves(n_blocks):
@@ -985,10 +1310,6 @@
         sums[step % 2] = back if sums[step % 2] is None else sums[step % 2] + back
     zero, one = jnp.where(odd, sums[1], sums[0]), jnp.where(odd, sums[0], sums[1])
     return jnp.stack([zero[0], one[0]]), jnp.stack([zero[1], one[1]])
-
-
-def to_members(value):
-    return lax.all_to_all(value, MEMBERS, split_axis=0, concat_axis=0, tiled=True)
 
 
 def body(
@@ -1035,7 +1356,6 @@
     n_images = lengths.shape[0] * lengths.shape[1]
     capacity = (21 * tokens * TOP + 20 * n_experts - 1) // (20 * n_experts)
     padded = round_up(capacity, 16)
-    n_slots = n_experts * padded
     layer_b, gain_rows, router_t, columns = gather_weights(
         sizes,
         (lengths.shape[1], n_experts, capacity, padded),
@@ -1046,56 +1366,20 @@
         slot_mask,
         lengths,
     )
-    router_b = router_t[:n_experts].T.astype(jnp.bfloat16)
     expert_in_now, expert_out_now, layer_b = lax.optimization_barrier((expert_in, expert_out, layer_b))
     own_chunks = fetch_experts(expert_in_now, expert_out_now, n_blocks)
     own_half = jnp.concatenate(own_chunks, 1)
     other_half = swap_cores(own_half)
-    w_one = jnp.concatenate([own_half[0], other_half[0]], 0)
-    w_two = jnp.concatenate([own_half[1], other_half[1]], 0)
     x_zero, a_one, qkv, att_out, x_one, a_two, router_probs, logs, pooled, part_importance = (
         dense_forward(
             n_experts, lengths, slot_mask, patches, layer_b, gain_rows, router_t, columns
         )
     )
     arrived, details = dispatch(sizes, n_experts, padded, a_two, router_probs, columns)
-    activated, slope, result, part_pooled = expert_forward(arrived, details, own_half, other_half)
-
-    valid = slot_mask.astype(jnp.float32)
-    positions = jnp.arange(n_slots_row, dtype=jnp.int32)
-    bounds = jnp.cumsum(lengths, 1)
-    segment = jnp.sum((positions[None, :, None] >= bounds[:, None, :]).astype(jnp.int32), -1)
-    diagonal = positions[:, None] == positions[None, :]
-    allowed = (segment[:, :, None] == segment[:, None, :]) & (
-        (valid[:, None, :] > 0) | diagonal[None]
-    )
-    member = (
-        segment[:, None, :] == jnp.arange(lengths.shape[1], dtype=jnp.int32)[None, :, None]
-    ).astype(jnp.float32) * valid[:, None, :]
-    pooling = member / jnp.maximum(jnp.sum(member, -1, keepdims=True), 1.0)
-    valid_flat = valid.reshape(tokens)
-    slot_one, slot_two = columns[:, 0].astype(jnp.int32), columns[:, 1].astype(jnp.int32)
-    kept_one = (slot_one >= 0).astype(jnp.float32)
-    kept_two = (slot_two >= 0).astype(jnp.float32)
-    router_probs = router_probs[:, :n_experts]
-    proj_qkv = qkv.reshape(tokens, 3, model_width).transpose(1, 0, 2)
-    log_total = logs[:, :HEADS].reshape(rows_here, n_slots_row, HEADS).transpose(0, 2, 1)[..., None]
-    pick_one = expert_picks[:, 0]
-    pick_two = expert_picks[:, 1]
-    ids = jnp.arange(n_experts, dtype=jnp.int32)
-    hot_one = (pick_one[:, None] == ids[None]).astype(jnp.float32)
-    hot_two = (pick_two[:, None] == ids[None]).astype(jnp.float32)
-    slot_ids = jnp.arange(n_slots, dtype=jnp.int32)
-    match = (
-        (slot_one[None, :] == slot_ids[:, None]) | (slot_two[None, :] == slot_ids[:, None])
-    ).astype(jnp.bfloat16)
-    got_gate, got_pool, got_image = (details[:, i, :padded] for i in range(3))
-    image_hots = (
-        got_image[:, :, None] == jnp.arange(n_images).astype(jnp.float32)[None, None]
-    ).astype(jnp.float32) * got_pool[:, :, None]
-    rows_all = arrived.reshape(n_slots, model_width)
-    result = result.astype(jnp.float32)
-    g_head, d_pooled_all, d_pooled, g_norm_three, local_loss, importance = head_step(
+    activated, slope, result, part_pooled = expert_forward(
+        arrived, details, own_half, other_half, 4 * n_blocks
+    )
+    g_head, d_pooled_all, d_pooled, g_norm_three, local_loss, total_importance = head_step(
         sizes,
         n_images,
         part_pooled,
@@ -1105,85 +1389,38 @@
         head_weights,
         class_labels,
     )
-    importance = importance[0, :n_experts]
+    d_back, back_gate, *grads = expert_backward(
+        sizes, arrived, details, d_pooled_all, result, slope, activated, own_half, other_half
+    )
+    g_one, g_two = return_experts(grads, n_blocks)
+    blocks = dense_backward(
+        sizes,
+        n_experts,
+        padded,
+        rows_own,
+        lengths,
+        slot_mask,
+        patches,
+        (x_zero, a_one, qkv, att_out, x_one, a_two, router_probs, logs),
+        columns,
+        layer_b,
+        gain_rows,
+        router_t,
+        d_back,
+        back_gate,
+        d_pooled,
+        total_importance,
+        g_norm_three,
+    )
+    reduced = scatter_dense(sizes, blocks)
+    n_dense = dense_weights.shape[0] * rows_own
+    g_layers = reduced[:n_dense].reshape(-1, rows_own, model_width)
+    g_norms = reduced[n_dense : n_dense + 6, :rows_own]
+    g_router = reduced[n_dense : n_dense + n_experts, 128 : 128 + rows_own].T
+    importance = total_importance[0, :n_experts]
     local_loss = local_loss[0, 0]
-    d_pooled_all = d_pooled_all[:, :n_images]
-    d_pooled = d_pooled[:n_images]
     centre = jnp.mean(importance)
     spread = jnp.mean((importance - centre) ** 2)
-    d_imp = aux_weight * (
-        2.0 * (importance - centre) / (n_experts * centre * centre)
-        - 2.0 * spread / (n_experts * centre * centre * centre)
-    )
-    d_two = jnp.einsum(
-        "ris,rid->rsd", pooling, d_pooled.reshape(rows_here, -1, model_width), precision=high_prec
-    ).reshape(tokens, model_width)
-    d_two_slots = jnp.einsum("dsi,diw->dsw", image_hots, d_pooled_all, precision=high_prec)
-    slot_d_gate = jnp.sum(d_two_slots * result, -1)
-    d_all = (d_two_slots * got_gate[:, :, None]).astype(jnp.bfloat16).reshape(n_slots, model_width)
-    d_act = jnp.dot(d_all, w_two.T, preferred_element_type=jnp.float32)
-    d_hidden = (d_act * slope.astype(jnp.float32)).astype(jnp.bfloat16)
-    d_inputs = jnp.dot(d_hidden, w_one, preferred_element_type=jnp.float32).astype(jnp.bfloat16)
-    d_back = to_members(d_inputs.reshape(n_experts, padded, model_width))
-    d_back = d_back.reshape(n_slots, model_width)
-    back_gate = to_members(slot_d_gate).reshape(n_slots)
-    g_two = jnp.dot(activated.T, d_all, preferred_element_type=jnp.float32)
-    g_one = jnp.dot(d_hidden.T, rows_all, preferred_element_type=jnp.float32)
-    half = g_one.shape[0] // 2
-    grads = jnp.stack([g_one, g_two], 0).astype(jnp.bfloat16)
-    summed = grads[:, :half].astype(jnp.float32) + swap_cores(grads[:, half:]).astype(jnp.float32)
-    summed = summed.astype(jnp.bfloat16).reshape(2, 2 * n_blocks, -1, model_width)
-    g_one, g_two = return_experts([summed[:, i] for i in range(2 * n_blocks)], n_blocks)
-    d_gate_one = kept_one * jnp.take(back_gate, jnp.maximum(slot_one, 0), axis=0)
-    d_gate_two = kept_two * jnp.take(back_gate, jnp.maximum(slot_two, 0), axis=0)
-    d_a_two = lax.dot_general(
-        match, d_back, (((0,), (0,)), ((), ())), preferred_element_type=jnp.float32
-    )
-    d_probs = (
-        hot_one * d_gate_one[:, None]
-        + hot_two * d_gate_two[:, None]
-        + valid_flat[:, None] * d_imp[None, :]
-    )
-    d_router = (
-        router_probs * (d_probs - jnp.sum(router_probs * d_probs, 1, keepdims=True))
-    ).astype(jnp.bfloat16)
-    g_router = jnp.dot(a_two.T, d_router, preferred_element_type=jnp.float32)
-    d_a_two = d_a_two + jnp.dot(d_router, router_b.T, preferred_element_type=jnp.float32)
-    unused_out, norm_back = jax.vjp(layer_norm, x_one, gain_rows[1], gain_rows[4])
-    d_x_one, g_gain_two, g_shift_two = norm_back(d_a_two)
-    d_x_one = d_x_one + d_two
-    d_att_b = d_x_one.astype(jnp.bfloat16)
-    g_out_proj = jnp.dot(att_out.T, d_att_b, preferred_element_type=jnp.float32)
-    d_att_out = jnp.dot(d_att_b, layer_b[4].T, preferred_element_type=jnp.float32).astype(
-        jnp.bfloat16
-    )
-    d_qkv = attention_backward(proj_qkv, allowed, log_total, d_att_out, HEADS)
-    g_qkv = jnp.einsum("td,kte->kde", a_one, d_qkv, preferred_element_type=jnp.float32)
-    d_a_one = jnp.einsum("kte,kde->td", d_qkv, layer_b[1:4], preferred_element_type=jnp.float32)
-    unused_out, norm_back = jax.vjp(layer_norm, x_zero, gain_rows[0], gain_rows[3])
-    d_x_zero, g_gain_one, g_shift_one = norm_back(d_a_one)
-    d_x_zero = (d_x_zero + d_x_one).astype(jnp.bfloat16)
-    g_embed = jnp.dot(patches.T, d_x_zero, preferred_element_type=jnp.float32)
-    g_layers = jnp.concatenate([g_embed[None], g_qkv, g_out_proj[None]], 0)
-    zero = jnp.zeros_like(g_gain_one)
-    g_norms = g_norm_three[:6] + jnp.stack(
-        [g_gain_one, g_gain_two, zero, g_shift_one, g_shift_two, zero]
-    )
-    def spread_rows(value):
-        value = value.reshape(value.shape[0], QUAD, n_blocks, sizes["x"], 2, rows_own, -1)
-        return value.transpose(4, 1, 3, 2, 0, 5, 6)
-
-    blocks = spread_rows(g_layers.astype(jnp.bfloat16))
-    blocks = blocks.reshape(*blocks.shape[:4], -1, model_width)
-    small = jnp.concatenate([g_norms, g_router.T], 0).astype(jnp.bfloat16)
-    small = spread_rows(small[..., None])[..., 0]
-    n_dense, n_small = blocks.shape[4], small.shape[4]
-    depth = round_up(n_dense + n_small, 16)
-    small = jnp.pad(small, ((0, 0),) * 4 + ((0, depth - n_dense - n_small), (0, model_width - rows_own)))
-    reduced = scatter_dense(sizes, jnp.concatenate([blocks, small], 4))
-    g_layers = reduced[:n_dense].reshape(-1, rows_own, model_width)
-    g_norms = reduced[n_dense : n_dense + 6, :rows_own]
-    g_router = reduced[n_dense + 6 : n_dense + n_small, :rows_own].T
     squares = (
         jnp.sum(g_layers * g_layers) + jnp.sum(g_router * g_router) + jnp.sum(g_norms * g_norms)
     )

time: 720 us -> 580 us (0.81)
  Pallas kernels: 267 us -> 413 us
  matrix products: 130 us -> 0 us
  local copies, waits for them, and re-layouts: 101 us -> 19.4 us
  other arithmetic: 76.7 us -> 37 us
  waiting for transfers between devices: 48.4 us -> 21.9 us
    dot_general x19 -> x0, matrix products: 130 us -> none  [the longest x1 18.5 us: body(): d_act = jnp.dot(d_all, w_two.T, preferred_element_type=jnp.float32)]
    pallas_call x0 -> x2, Pallas kernels: none -> 128 us  [the longest x1 72 us: expert_backward(): pl.pallas_call(functools.partial(expert_backward_kernel, sizes, padded),...]
    ppermute x4, waiting for transfers between devices: 48.3 us -> 21.9 us  [fetch_experts(): lax.ppermute(ordered[step % 2], ('g', 'r', 'c'), pairs)]
    squeeze x6 -> x0, local copies, waits for them, and re-layouts: 21.5 us -> none  [the longest x2 9.72 us: body(): w_one = jnp.concatenate([own_half[0], other_half[0]], 0)]
    pallas_call x1, Pallas kernels: 45.8 us -> 62.7 us  [scatter_dense(): pl.pallas_call(functools.partial(scatter_kernel, sizes), out_shape=jax.Sh...]
    another operation x9 -> x0, local copies, waits for them, and re-layouts: 13 us -> none  [the longest x6 12.9 us: attention_backward(): stacked = jnp.stack([d_query, d_keys, d_values]).astype(jnp.bfloat16)]
    gather x2 -> x0, local copies, waits for them, and re-layouts: 12.3 us -> none  [the longest x1 6.15 us: body(): jnp.take(back_gate, jnp.maximum(slot_one, 0), axis=0)]
    reduce_sum x8 -> x0, other arithmetic: 12.3 us -> none  [the longest x4 7.34 us: layer_norm(): centre = values - jnp.mean(values, -1, keepdims=True)]
  transfers between devices with their start and end apart: 12 -> 9, of which waited for: 3 -> 2; matrix products, arithmetic and copies ran while one was open for 26% -> 2% of each run, Pallas kernels for 17% -> 34%
where the time goes in v4:
time: 580 us; the launch traced here: 575 us
  Pallas kernels  413 us (71%)
  starting transfers between devices  72.6 us (13%)
  other arithmetic  37 us (6%)
  waiting for transfers between devices  21.9 us (4%)
  local copies, waits for them, and re-layouts  19.4 us (3%)
  between operations  11.8 us (2%)
    pallas_call x1, Pallas kernels, expert_backward(): pl.pallas_call(functools.partial(expert_backward_kernel, sizes, padded),...  72 us
    pallas_call x1, Pallas kernels, scatter_dense(): pl.pallas_call(functools.partial(scatter_kernel, sizes), out_shape=jax.Sh...  62.7 us
    pallas_call x1, Pallas kernels, dense_backward(): pl.pallas_call(functools.partial(dense_backward_kernel, sizes, n_experts,...  56.2 us
    pallas_call x1, Pallas kernels, dispatch(): pl.pallas_call(functools.partial(dispatch_kernel, sizes, n_experts, padde...  54 us
    ppermute x1, starting transfers between devices, swap_cores(): return lax.ppermute(value, 'c', [(0, 1), (1, 0)])  50.6 us
    pallas_call x1, Pallas kernels, gather_weights(): pl.pallas_call(functools.partial(gather_kernel, sizes, rows, mats, routin...  44.7 us
    pallas_call x1, Pallas kernels, head_step(): pl.pallas_call(functools.partial(head_kernel, sizes, images), out_shape=(...  44 us
    pallas_call x1, Pallas kernels, expert_forward(): pl.pallas_call(functools.partial(expert_forward_kernel, padded), grid=(so...  43.1 us
  transfers between devices with their start and end apart: 9, of which 2 were waited for; matrix products, arithmetic and copies ran while one was open for 2% of the time, Pallas kernels for 34%

profile of v4, /device:TPU:0, one launch (start us, length us, event | category | flops | bytes accessed | tf_op | source)
XLA Modules:
  0.0 575.3 jit_solution(7841114973533359875)
XLA Ops:
  7.4 44.7 %gather_weights.1 = (bf16[5,768,768]{2,1,0:T(8,128)(2,1)}, f32[8,768]{1,0:T(8,128)S(1)}, f32[8,768]{1,0:T(8,128)S(1)}, f32[1024,128]{1,0:T(8,128)S(1)}) custom-call(f32[5,24,768]{2,1,0:T(8,128)S(1)} %copy-done, f32[8,768]{1,0:T(8,128)S(1)} %scatter.9.tail_ref, s32[1024,2]{1,0:T(8,128)S(1)} %copy.57.pick_ref, s32[1,1024]{1,0:T(1,128)S(1)} %copy-done.5, ...), custom_call_target="tpu_custom_call" | custom-call | flops 50600001536 | tf_op jit(solution)/shard_map/gather_weights/pallas_call | solution.py:232
  52.2 2.1 convert_bitcast_fusion
  55.3 4.2 collective-permute-start.2
  59.5 2.0 collective-permute-start.1
  61.8 24.0 %dense_forward.1 = (f32[1024,768]{1,0:T(8,128)}, bf16[1024,768]{1,0:T(8,128)(2,1)S(1)}, bf16[1024,2304]{1,0:T(8,128)(2,1)}, bf16[1024,768]{1,0:T(8,128)(2,1)S(1)...) custom-call(s32[4,3]{1,0:T(4,128)S(1)} %copy-done.7, ...), custom_call_target="tpu_custom_call" | custom-call | flops 28750000128 | tf_op jit(solution)/shard_map/dense_forward/pallas_call | solution.py:721
  87.1 12.6 %collective-permute-done.1 = bf16[2,384,768]{2,1,0:T(8,128)(2,1)S(1)} collective-permute-done((bf16[2,384,768]{2,1,0:T(8,128)(2,1)S(1)}, bf16[2,384,768]{2,1,0:T(8,128)(2,1)S(1)}, u32[]{:S(2)}, u32[]{:S(2)}) %collective-permute-start.1) | collective-permute-done | bytes 1179680 | tf_op jit(solution)/shard_map/ppermute | solution.py:1298
  101.9 9.3 %collective-permute-done.3 = bf16[2,384,768]{2,1,0:T(8,128)(2,1)S(1)} collective-permute-done((bf16[2,384,768]{2,1,0:T(8,128)(2,1)S(1)}, bf16[2,384,768]{2,1,0:T(8,128)(2,1)S(1)}, u32[]{:S(2)}, u32[]{:S(2)}) %collective-permute-start.3) | collective-permute-done | bytes 1179680 | tf_op jit(solution)/shard_map/ppermute | solution.py:1298
  112.4 50.6 %collective-permute-start.4 = (bf16[2,1536,768]{2,1,0:T(8,128)(2,1)}, bf16[2,1536,768]{2,1,0:T(8,128)(2,1)}, u32[]{:S(2)}, u32[]{:S(2)}) collective-permute-start(bf16[2,1536,768]{2,1,0:T(8,128)(2,1)} %constant_dynamic-update-slice_fusion.own_ref), channel_id=1, source_target_pairs={{0,1},{1,0},{2,3},{3,2},{4,5},{5,4},{6,7},{7,6},{8,9},{9,8},{10,11... | collective-permute-start | bytes 14155784 | tf_op jit(solution)/shard_map/ppermute | solution.py:1289
  163.0 54.0 %dispatch.1 = (bf16[8,272,768]{2,1,0:T(8,128)(2,1)S(1)}, f32[8,8,384]{2,1,0:T(8,128)S(1)}) custom-call(bf16[1024,768]{1,0:T(8,128)(2,1)S(1)} %copy-done.10, f32[1024,128]{1,0:T(8,128)S(1)} %get-tuple-element.92.prob_ref, f32[1024,128]{1,0:T(8,128)S(1)} %get-tuple-element.90.col_ref), custom_call_target="tpu_custom_call" | custom-call | flops 57500000256 | tf_op jit(solution)/shard_map/dispatch/pallas_call | solution.py:825
  217.1 1.8 copy-done.11
  219.5 43.1 %expert_forward.1 = (bf16[8,2176,384]{2,1,0:T(8,128)(2,1)}, bf16[8,2176,384]{2,1,0:T(8,128)(2,1)}, bf16[8,272,768]{2,1,0:T(8,128)(2,1)}, f32[8,16,768]{2,1,0:T(8,128)}) custom-call(bf16[8,272,768]{2,1,0:T(8,128)(2,1)} %copy-done.11, f32[8,8,384]{2,1,0:T(8,128)} %copy-done.16, bf16[2,1536,768]{2,1,0:T(8,128)(2,1)} %constant_dynamic-update-slice_fusion.own_ref, ...), custom_call_target="tpu_custom_call" | custom-call | flops 46000001024 | tf_op jit(solution)/shard_map/expert_forward/pallas_call | solution.py:900
  262.5 44.0 %head_step.1 = (f32[576,768]{1,0:T(8,128)}, f32[8,16,768]{2,1,0:T(8,128)}, f32[16,768]{1,0:T(8,128)}, f32[8,768]{1,0:T(8,128)}, f32[8,128]{1,0:T(8,128)}, /*index=5*/f32[8,768]{1,0:T(8,128)}) custom-call(f32[8,16,768]{2,1,0:T(8,128)} %get-tuple-element.97.part_ref, f32[16,768]{1,0:T(8,128)} %copy-done.15, f32[8,768]{1,0:T(8,128)} %copy-done.19, ...), custom_call_target="tpu_custom_call" | custom-call | flops 48299999232 | tf_op jit(solution)/shard_map/head_step/pallas_call | solution.py:535
  306.5 72.0 %expert_backward.1 = (bf16[8,272,768]{2,1,0:T(8,128)(2,1)}, f32[8,8,384]{2,1,0:T(8,128)}, bf16[2,384,768]{2,1,0:T(8,128)(2,1)}, bf16[2,384,768]{2,1,0:T(8,128)(2...) custom-call(bf16[8,272,768]{2,1,0:T(8,128)(2,1)} %copy-done.11, f32[8,8,384]{2,1,0:T(8,128)} %copy-done.16, ...), custom_call_target="tpu_custom_call" | custom-call | flops 74750001152 | tf_op jit(solution)/shard_map/expert_backward/pallas_call | solution.py:1066
  378.6 1.4 collective-permute-start.6
  380.2 2.9 collective-permute-start.8
  383.0 10.4 %collective-permute-start.7 = (bf16[2,384,768]{2,1,0:T(8,128)(2,1)}, bf16[2,384,768]{2,1,0:T(8,128)(2,1)}, u32[]{:S(2)}, u32[]{:S(2)}) collective-permute-start(bf16[2,384,768]{2,1,0:T(8,128)(2,1)} %get-tuple-element.118), channel_id=1, source_target_pairs={{0,0},{8,1},{4,4},{12,5},{16,8},{24,9},{20,12},{28,13},{1,16},{9,1... | collective-permute-start | bytes 3538952 | tf_op jit(solution)/shard_map/ppermute | solution.py:1308
  393.4 56.2 %dense_backward.1.g_ref = bf16[2,4,2,2,128,768]{5,4,3,2,1,0:T(8,128)(2,1)} custom-call(s32[4,3]{1,0:T(4,128)} %length_ref.5, s32[4,1,256]{2,1,0:T(1,128)} %copy-done.4, bf16[1024,768]{1,0:T(8,128)(2,1)} %patch_ref.3, f32[1024,768]{1,0:T(8,128)} %get-tuple-element.101.x_zero_ref, bf16[1024,768]{1,0:T(8,128)(2,1)} %copy-done.8, ...), custom_call_target="tpu_custom_call" | custom-call | flops 57500000256 | tf_op jit(solution)/shard_map/dense_backward/pallas_call | solution.py:1245
  449.6 62.7 %scatter_dense.1 = f32[128,768]{1,0:T(8,128)S(1)} custom-call(bf16[2,4,2,2,128,768]{5,4,3,2,1,0:T(8,128)(2,1)} %dense_backward.1.g_ref), custom_call_target="tpu_custom_call" | custom-call | flops 51749998592 | tf_op jit(solution)/shard_map/scatter_dense/pallas_call | solution.py:333
  520.6 1.8 multiply_reduce_fusion.6
  524.2 2.6 fusion.3
  534.1 11.8 %share_sums.1 = f32[8,128]{1,0:T(8,128)} custom-call(f32[8,128]{1,0:T(8,128)} %iota.15.in_ref), custom_call_target="tpu_custom_call" | custom-call | flops 11500000256 | tf_op jit(solution)/shard_map/share_sums/pallas_call | solution.py:382
  549.9 8.6 %multiply_add_fusion.2 = (f32[2,384,768]{2,1,0:T(8,128)}, f32[2,384,768]{2,1,0:T(8,128)}, f32[2,384,768]{2,1,0:T(8,128)}, f32[2,384,768]{2,1,0:T(8,128)}) fusion(f32[2,384,768]{2,1,0:T(8,128)} %param.55, f32[2,384,768]{2,1,0:T(8,128)} %param.52, f32[]{:T(128)S(6)} %min.3, f32[1,384,768]{2,1,0:T(8,128)} %copy-done.20, f32[1,384,768]{2,1,0:T(8,128)} %copy-done.21, ...), kind=kLoop, calls=%fused_computation.12 | loop fusion | flops 11796480 | bytes 21233668 | tf_op jit(solution)/shard_map/add | solution.py:43
  560.4 5.7 multiply_add_fusion
  567.2 4.1 multiply_add_fusion.4
  (125 shorter events, 31.0 us)
Async XLA Ops:
  7.4 44.7 %copy-start.22 = (f32[2,384,768]{2,1,0:T(8,128)S(1)}, f32[2,384,768]{2,1,0:T(8,128)}, u32[]{:S(2)}) copy-start(f32[2,384,768]{2,1,0:T(8,128)} %param.52) | copy-start | bytes 7077892
  52.2 110.9 %copy-start.12 = (f32[1024,128]{1,0:T(8,128)}, f32[1024,128]{1,0:T(8,128)S(1)}, u32[]{:S(2)}) copy-start(f32[1024,128]{1,0:T(8,128)S(1)} %get-tuple-element.90.col_ref) | copy-start | bytes 1572868
  54.6 31.3 %collective-permute-start = (bf16[2,384,768]{2,1,0:T(8,128)(2,1)S(1)}, bf16[2,384,768]{2,1,0:T(8,128)(2,1)S(1)}, u32[]{:S(2)}, u32[]{:S(2)}) collective-permute-start(bf16[2,384,768]{2,1,0:T(8,128)(2,1)S(1)} %get-tuple-element.154), channel_id=1, source_target_pairs={{0,0},{1,8},{4,4},{5,12},{8,16},{9,24},{12,20},{13,28},{16,1},{17,... | collective-permute-start | bytes 3538952 | tf_op jit(solution)/shard_map/ppermute | solution.py:1298
  55.3 45.5 %collective-permute-start.2 = (bf16[2,384,768]{2,1,0:T(8,128)(2,1)S(1)}, bf16[2,384,768]{2,1,0:T(8,128)(2,1)S(1)}, u32[]{:S(2)}, u32[]{:S(2)}) collective-permute-start(bf16[2,384,768]{2,1,0:T(8,128)(2,1)S(1)} %get-tuple-element.154), channel_id=1, source_target_pairs={{0,16},{1,24},{4,20},{5,28},{8,0},{9,8},{12,4},{13,12},{16,17},{17... | collective-permute-start | bytes 3538952 | tf_op jit(solution)/shard_map/ppermute | solution.py:1298
  59.5 40.2 %collective-permute-start.1 = (bf16[2,384,768]{2,1,0:T(8,128)(2,1)S(1)}, bf16[2,384,768]{2,1,0:T(8,128)(2,1)S(1)}, u32[]{:S(2)}, u32[]{:S(2)}) collective-permute-start(bf16[2,384,768]{2,1,0:T(8,128)(2,1)S(1)} %get-tuple-element.153), channel_id=1, source_target_pairs={{0,4},{1,12},{4,16},{5,24},{8,20},{9,28},{12,0},{13,8},{16,5},{17,... | collective-permute-start | bytes 3538952 | tf_op jit(solution)/shard_map/ppermute | solution.py:1298
  61.5 49.8 %collective-permute-start.3 = (bf16[2,384,768]{2,1,0:T(8,128)(2,1)S(1)}, bf16[2,384,768]{2,1,0:T(8,128)(2,1)S(1)}, u32[]{:S(2)}, u32[]{:S(2)}) collective-permute-start(bf16[2,384,768]{2,1,0:T(8,128)(2,1)S(1)} %get-tuple-element.153), channel_id=1, source_target_pairs={{0,20},{1,28},{4,0},{5,8},{8,4},{9,12},{12,16},{13,24},{16,21},{17... | collective-permute-start | bytes 3538952 | tf_op jit(solution)/shard_map/ppermute | solution.py:1298
  61.8 24.1 %copy-start.4 = (s32[4,1,256]{2,1,0:T(1,128)}, s32[4,1,256]{2,1,0:T(1,128)S(1)}, u32[]{:S(2)}) copy-start(s32[4,1,256]{2,1,0:T(1,128)S(1)} %broadcast_in_dim.13.mask_ref) | copy-start | bytes 12292
  85.8 16.0 %copy-start.8 = (bf16[1024,768]{1,0:T(8,128)(2,1)}, bf16[1024,768]{1,0:T(8,128)(2,1)S(1)}, u32[]{:S(2)}) copy-start(bf16[1024,768]{1,0:T(8,128)(2,1)S(1)} %get-tuple-element.102.a_one_ref) | copy-start | bytes 4718596
  85.8 16.0 %copy-start.9 = (bf16[1024,768]{1,0:T(8,128)(2,1)}, bf16[1024,768]{1,0:T(8,128)(2,1)S(1)}, u32[]{:S(2)}) copy-start(bf16[1024,768]{1,0:T(8,128)(2,1)S(1)} %get-tuple-element.104.att_ref) | copy-start | bytes 4718596
  85.9 16.0 %copy-start.14 = (f32[1024,128]{1,0:T(8,128)}, f32[1024,128]{1,0:T(8,128)S(1)}, u32[]{:S(2)}) copy-start(f32[1024,128]{1,0:T(8,128)S(1)} %get-tuple-element.106.lse_ref) | copy-start | bytes 1572868
  85.9 16.0 %copy-start.15 = (f32[16,768]{1,0:T(8,128)}, f32[16,768]{1,0:T(8,128)S(1)}, u32[]{:S(2)}) copy-start(f32[16,768]{1,0:T(8,128)S(1)} %get-tuple-element.98.own_ref) | copy-start | bytes 147460
  85.9 16.0 %copy-start.19 = (f32[8,768]{1,0:T(8,128)}, f32[8,768]{1,0:T(8,128)S(1)}, u32[]{:S(2)}) copy-start(f32[8,768]{1,0:T(8,128)S(1)} %get-tuple-element.99.imp_ref) | copy-start | bytes 73732
  85.9 77.1 %copy-start.13 = (f32[1024,128]{1,0:T(8,128)}, f32[1024,128]{1,0:T(8,128)S(1)}, u32[]{:S(2)}) copy-start(f32[1024,128]{1,0:T(8,128)S(1)} %get-tuple-element.92.prob_ref) | copy-start | bytes 1572868
  100.8 62.2 %copy-start.10 = (bf16[1024,768]{1,0:T(8,128)(2,1)S(1)}, bf16[1024,768]{1,0:T(8,128)(2,1)}, u32[]{:S(2)}) copy-start(bf16[1024,768]{1,0:T(8,128)(2,1)} %get-tuple-element.91.a_two_ref) | copy-start | bytes 4718596
  112.4 107.1 %collective-permute-start.4 = (bf16[2,1536,768]{2,1,0:T(8,128)(2,1)}, bf16[2,1536,768]{2,1,0:T(8,128)(2,1)}, u32[]{:S(2)}, u32[]{:S(2)}) collective-permute-start(bf16[2,1536,768]{2,1,0:T(8,128)(2,1)} %constant_dynamic-update-slice_fusion.own_ref), channel_id=1, source_target_pairs={{0,1},{1,0},{2,3},{3,2},{4,5},{5,4},{6,7},{7,6},{8,9},{9,8},{10,11... | collective-permute-start | bytes 14155784 | tf_op jit(solution)/shard_map/ppermute | solution.py:1289
  378.6 145.6 %collective-permute-start.6 = (bf16[2,384,768]{2,1,0:T(8,128)(2,1)}, bf16[2,384,768]{2,1,0:T(8,128)(2,1)S(1)}, u32[]{:S(2)}, u32[]{:S(2)}) collective-permute-start(bf16[2,384,768]{2,1,0:T(8,128)(2,1)} %get-tuple-element.117), channel_id=1, source_target_pairs={{20,0},{28,1},{0,4},{8,5},{4,8},{12,9},{16,12},{24,13},{21,16},{29... | collective-permute-start | bytes 3538952 | tf_op jit(solution)/shard_map/ppermute | solution.py:1308
  380.0 144.2 %collective-permute-start.5 = (bf16[2,384,768]{2,1,0:T(8,128)(2,1)}, bf16[2,384,768]{2,1,0:T(8,128)(2,1)}, u32[]{:S(2)}, u32[]{:S(2)}) collective-permute-start(bf16[2,384,768]{2,1,0:T(8,128)(2,1)} %get-tuple-element.116), channel_id=1, source_target_pairs={{4,0},{12,1},{16,4},{24,5},{20,8},{28,9},{0,12},{8,13},{5,16},{13,... | collective-permute-start | bytes 3538952 | tf_op jit(solution)/shard_map/ppermute | solution.py:1308
  380.2 144.0 %collective-permute-start.8 = (bf16[2,384,768]{2,1,0:T(8,128)(2,1)}, bf16[2,384,768]{2,1,0:T(8,128)(2,1)}, u32[]{:S(2)}, u32[]{:S(2)}) collective-permute-start(bf16[2,384,768]{2,1,0:T(8,128)(2,1)} %get-tuple-element.119), channel_id=1, source_target_pairs={{16,0},{24,1},{20,4},{28,5},{0,8},{8,9},{4,12},{12,13},{17,16},{25... | collective-permute-start | bytes 3538952 | tf_op jit(solution)/shard_map/ppermute | solution.py:1308
  383.0 141.2 %collective-permute-start.7 = (bf16[2,384,768]{2,1,0:T(8,128)(2,1)}, bf16[2,384,768]{2,1,0:T(8,128)(2,1)}, u32[]{:S(2)}, u32[]{:S(2)}) collective-permute-start(bf16[2,384,768]{2,1,0:T(8,128)(2,1)} %get-tuple-element.118), channel_id=1, source_target_pairs={{0,0},{8,1},{4,4},{12,5},{16,8},{24,9},{20,12},{28,13},{1,16},{9,1... | collective-permute-start | bytes 3538952 | tf_op jit(solution)/shard_map/ppermute | solution.py:1308
  449.6 73.5 %copy-start.24 = (f32[576,768]{1,0:T(8,128)S(1)}, f32[576,768]{1,0:T(8,128)}, u32[]{:S(2)}) copy-start(f32[576,768]{1,0:T(8,128)} %get-tuple-element.120) | copy-start | bytes 5308420
  534.1 15.2 %copy-start.36 = (f32[6,24]{1,0:T(8,128)S(1)}, f32[6,24]{1,0:T(8,128)}, u32[]{:S(2)}) copy-start(f32[6,24]{1,0:T(8,128)} %param.48) | copy-start | bytes 1732
  534.1 15.1 %copy-start.41 = (f32[6,24]{1,0:T(8,128)S(1)}, f32[6,24]{1,0:T(8,128)}, u32[]{:S(2)}) copy-start(f32[6,24]{1,0:T(8,128)} %param.51) | copy-start | bytes 1732
  534.1 15.1 %copy-start.42 = (f32[6,24]{1,0:T(8,128)S(1)}, f32[6,24]{1,0:T(8,128)}, u32[]{:S(2)}) copy-start(f32[6,24]{1,0:T(8,128)} %param.49) | copy-start | bytes 1732
  534.1 15.1 %copy-start.43 = (f32[6,24]{1,0:T(8,128)S(1)}, f32[6,24]{1,0:T(8,128)}, u32[]{:S(2)}) copy-start(f32[6,24]{1,0:T(8,128)} %param.50) | copy-start | bytes 1732
  (29 other events, 183.6 us)

commit v5 on v4

--- a/solution.py
+++ b/solution.py
@@ -391,6 +391,7 @@
     )(values)
 
 
+EARLY = 1
 IMAGE_PAD = 16
 
 
@@ -850,77 +851,143 @@
     return line == image
 
 
-def expert_forward_kernel(
-    padded, rows_ref, detail_ref, own_ref, other_ref, act_ref, slope_ref, y_ref, part_ref
-):
+TILE = 32
+
+
+def tiles(count):
+    return [slice(start, min(start + TILE, count)) for start in range(0, count, TILE)]
+
+
+def expert_forward_kernel(sizes, padded, rows_ref, detail_ref, *refs):
+    at = Place(sizes)
+    half = len(refs) - 11
+    chunks = refs[:half]
+    act_ref, slope_ref, y_ref, part_ref, other_ref = refs[half : half + 5]
+    weights, total, own_sem, s_out, s_in, keep_sem = refs[half + 5 :]
     many, unused, width = rows_ref.shape
-    rows = rows_ref[...].reshape(many * padded, width)
-    chunks, unused, part = act_ref.shape
-    half = chunks // 2
-    total = None
-    for index in range(chunks):
-        ref, start = (own_ref, index * part) if index < half else (other_ref, (index - half) * part)
-        hidden = dot_f32(rows, ref[0, start : start + part], NT)
-        square = hidden * hidden
-        curve = jnp.tanh(hidden * (0.7978845608 + 0.7978845608 * 0.044715 * square))
-        upper = 0.5 + 0.5 * curve
-        gelu = hidden * upper
-        act = gelu.astype(jnp.bfloat16)
-        slope = upper + gelu * (1.0 - upper) * (
-            2.0 * 0.7978845608 + 6.0 * 0.7978845608 * 0.044715 * square
+    count = many * padded
+    turn, block = pl.program_id(0), pl.program_id(1)
+
+    def own_copy(index):
+        return pltpu.make_async_copy(chunks[index], weights.at[0, index], own_sem.at[index])
+
+    def swap_copy(index):
+        return send(
+            chunks[index], weights.at[1, index], s_out.at[index], s_in.at[index], at.sibling()
         )
-        act_ref[index] = act
-        slope_ref[index] = slope.astype(jnp.bfloat16)
-        found = dot_f32(act, ref[1, start : start + part], NN)
-        total = found if total is None else total + found
-    result = total.astype(jnp.bfloat16)
-    y_ref[...] = result.reshape(many, padded, width)
-    for source in range(many):
-        detail = detail_ref[source]
-        weight = detail[0:1, :padded] * detail[1:2, :padded]
-        weights = jnp.where(image_hot(detail, padded), weight, 0.0)
-        pieces = jnp.concatenate(split_three(weights), 0)
-        sums = dot_f32(pieces, result[source * padded : (source + 1) * padded], NN)
-        part_ref[source] = (
-            sums[:IMAGE_PAD] + sums[IMAGE_PAD : 2 * IMAGE_PAD] + sums[2 * IMAGE_PAD :]
-        )
-
-
-def expert_forward(rows, details, own_half, other_half, chunks):
+
+    def keep_copy():
+        return pltpu.make_async_copy(weights.at[1], other_ref, keep_sem.at[0])
+
+    @pl.when((turn == 0) & (block == 0))
+    def _():
+        for index in range(half):
+            own_copy(index).start()
+        greet([at.sibling()])
+        for index in range(half):
+            swap_copy(index).start()
+        for index in range(half):
+            own_copy(index).wait()
+
+    @pl.when((turn == 1) & (block == 0))
+    def _():
+        for index in range(half):
+            swap_copy(index).wait_recv()
+        keep_copy().start()
+
+    rows = rows_ref[...].reshape(count, width)
+    for index in range(half):
+        hidden_all = dot_f32(rows, weights[turn, index, 0], NT)
+        for spot in tiles(count):
+            hidden = hidden_all[spot]
+            square = hidden * hidden
+            curve = jnp.tanh(hidden * (0.7978845608 + 0.7978845608 * 0.044715 * square))
+            upper = 0.5 + 0.5 * curve
+            gelu = hidden * upper
+            slope = upper + gelu * (1.0 - upper) * (
+                2.0 * 0.7978845608 + 6.0 * 0.7978845608 * 0.044715 * square
+            )
+            act_ref[index, spot] = gelu.astype(jnp.bfloat16)
+            slope_ref[index, spot] = slope.astype(jnp.bfloat16)
+    acts = jnp.concatenate([act_ref[index] for index in range(half)], 1)
+    ends = jnp.concatenate([weights[turn, index, 1] for index in range(half)], 0)
+    found = dot_f32(acts, ends, NN)
+    span = pl.ds(pl.multiple_of(block * count, 16), count)
+
+    @pl.when(turn == 0)
+    def _():
+        total[span] = found
+
+    @pl.when(turn == 1)
+    def _():
+        result = (total[span] + found).astype(jnp.bfloat16)
+        y_ref[...] = result.reshape(many, padded, width)
+        for source in range(many):
+            detail = detail_ref[source]
+            weight = detail[0:1, :padded] * detail[1:2, :padded]
+            shares = jnp.where(image_hot(detail, padded), weight, 0.0)
+            pieces = jnp.concatenate(split_three(shares), 0)
+            sums = dot_f32(pieces, result[source * padded : (source + 1) * padded], NN)
+            part_ref[source] = (
+                sums[:IMAGE_PAD] + sums[IMAGE_PAD : 2 * IMAGE_PAD] + sums[2 * IMAGE_PAD :]
+            )
+
+    @pl.when((turn == 1) & (block == pl.num_programs(1) - 1))
+    def _():
+        for index in range(half):
+            swap_copy(index).wait_send()
+        keep_copy().wait()
+
+
+def expert_forward(sizes, rows, details, chunks):
     sources, padded, width = rows.shape
-    part = 2 * own_half.shape[1] // chunks
+    half = len(chunks)
+    part = chunks[0].shape[1]
     many = max(1, 576 // padded)
     lanes = details.shape[2]
-    half = jnp.bfloat16
+    kind = jnp.bfloat16
+    dma = pltpu.SemaphoreType.DMA
 
     def by_source(*shape):
-        return pl.BlockSpec((many, *shape), lambda i: (i, 0, 0))
-
-    flat = pl.BlockSpec((chunks, many * padded, part), lambda i: (0, i, 0))
+        return pl.BlockSpec((many, *shape), lambda t, i: (i, 0, 0))
+
+    def late(*shape):
+        return pl.BlockSpec((many, *shape), lambda t, i: (i * t, 0, 0))
+
+    flat = pl.BlockSpec((half, many * padded, part), lambda t, i: (t, i, 0))
     return pl.pallas_call(
-        functools.partial(expert_forward_kernel, padded),
-        grid=(sources // many,),
+        functools.partial(expert_forward_kernel, sizes, padded),
+        grid=(2, sources // many),
         out_shape=(
-            jax.ShapeDtypeStruct((chunks, sources * padded, part), half),
-            jax.ShapeDtypeStruct((chunks, sources * padded, part), half),
-            jax.ShapeDtypeStruct((sources, padded, width), half),
+            jax.ShapeDtypeStruct((2 * half, sources * padded, part), kind),
+            jax.ShapeDtypeStruct((2 * half, sources * padded, part), kind),
+            jax.ShapeDtypeStruct((sources, padded, width), kind),
             jax.ShapeDtypeStruct((sources, IMAGE_PAD, width), jnp.float32),
+            jax.ShapeDtypeStruct((half, 2, part, width), kind),
         ),
-        in_specs=[by_source(padded, width), by_source(8, lanes), whole(), whole()],
-        out_specs=(flat, flat, by_source(padded, width), by_source(IMAGE_PAD, width)),
-        compiler_params=pltpu.CompilerParams(vmem_limit_bytes=56 * MIB),
+        in_specs=[by_source(padded, width), by_source(8, lanes)] + [whole(ANY)] * half,
+        out_specs=(flat, flat, late(padded, width), late(IMAGE_PAD, width), whole(ANY)),
+        scratch_shapes=[
+            VMEM((2, half, 2, part, width), kind),
+            VMEM((sources * padded, width), jnp.float32),
+            dma((half,)), dma((half,)), dma((half,)), dma((1,)),
+        ],
+        compiler_params=pltpu.CompilerParams(
+            collective_id=7, has_side_effects=True, vmem_limit_bytes=56 * MIB
+        ),
         cost_estimate=cost(40),
         name="expert_forward",
-    )(rows, details, own_half, other_half)
+    )(rows, details, *chunks)
 
 
 def expert_backward_kernel(
-    sizes, padded, rows_ref, detail_ref, pool_ref, y_ref, slope_ref, act_ref, own_ref, other_ref, *refs
+    sizes, padded, rows_ref, detail_ref, pool_ref, y_ref, slope_ref, act_ref, other_ref, *refs
 ):
     at = Place(sizes)
     sources, unused, width = rows_ref.shape
     chunks, unused, part = slope_ref.shape
     half = chunks // 2
+    own_refs, refs = refs[:half], refs[half:]
     back_ref, gate_ref, *outs = refs[: 2 + half]
     d_hidden, d_rows, send_rows, send_gate, send_grad, got_grad = refs[2 + half : 8 + half]
     own_sem, r_out, r_in, m_out, m_in, g_out, g_in, g_keep = refs[8 + half :]
@@ -981,14 +1048,20 @@
         count = many * padded
         span = pl.ds(pl.multiple_of(block * count, 16), count)
         d_rows[span] = d_out
-        total = None
+
+        def weight(index, which):
+            return own_refs[index][which] if index < half else other_ref[index - half, which]
+
         for index in range(chunks):
-            ref, start = (own_ref, index * part) if index < half else (other_ref, (index - half) * part)
-            d_act = dot_f32(d_out, ref[1, start : start + part], NT)
-            d_hid = (d_act * slope_ref[index].astype(jnp.float32)).astype(jnp.bfloat16)
-            d_hidden[index, span] = d_hid
-            found = dot_f32(d_hid, ref[0, start : start + part], NN)
-            total = found if total is None else total + found
+            d_act = dot_f32(d_out, weight(index, 1), NT)
+            for spot in tiles(count):
+                rows_now = pl.ds(pl.multiple_of(block * count + spot.start, 16), spot.stop - spot.start)
+                d_hidden[index, rows_now] = (
+                    d_act[spot] * slope_ref[index, spot].astype(jnp.float32)
+                ).astype(jnp.bfloat16)
+        d_hids = jnp.concatenate([d_hidden[index, span] for index in range(chunks)], 1)
+        starts = jnp.concatenate([weight(index, 0) for index in range(chunks)], 0)
+        total = dot_f32(d_hids, starts, NN)
         total = total.astype(jnp.bfloat16)
         for index in range(many):
             source = block * many + index
@@ -1046,10 +1119,10 @@
             out_copy(spot).wait()
 
 
-def expert_backward(sizes, rows, details, pools, results, slopes, acts, own_half, other_half):
+def expert_backward(sizes, rows, details, pools, results, slopes, acts, chunks_own, other):
     sources, padded, width = rows.shape
     chunks, count, part = acts.shape
-    many = max(1, 576 // padded)
+    many = max(1, (288 if part % 128 else 576) // padded)
     rounds, half = sources // many, chunks // 2
     lanes = details.shape[2]
     kind = jnp.bfloat16
@@ -1076,8 +1149,8 @@
             pl.BlockSpec((many, padded, width), lambda i: (block_of(i), 0, 0)),
             pl.BlockSpec((chunks, many * padded, part), lambda i: (0, block_of(i), 0)),
             pl.BlockSpec((1, count, part), lambda i: (chunk_of(i), 0, 0)),
-            whole(), whole(),
-        ],
+        ]
+        + [whole()] * (1 + half),
         out_specs=(whole(ANY),) * (2 + half),
         scratch_shapes=[
             VMEM((chunks, count, part), kind),
@@ -1093,7 +1166,7 @@
         ),
         cost_estimate=cost(65),
         name="expert_backward",
-    )(rows, details, pools, results, slopes, acts, own_half, other_half)
+    )(rows, details, pools, results, slopes, acts, other, *chunks_own)
 
 
 def dense_backward_kernel(
@@ -1285,19 +1358,16 @@
     return moves
 
 
-def swap_cores(value):
-    return lax.ppermute(value, "c", [(0, 1), (1, 0)])
-
-
-def fetch_experts(expert_in, expert_out, n_blocks):
+def order_shards(expert_in, expert_out):
     place = lax.axis_index("g") * QUAD + lax.axis_index("r")
     odd = lax.rem(place, 2) == 1
     both = jnp.stack([expert_in, expert_out], 1).astype(jnp.bfloat16)
-    ordered = [jnp.where(odd, both[1], both[0]), jnp.where(odd, both[0], both[1])]
-    return [
-        lax.ppermute(ordered[step % 2], ("g", "r", "c"), pairs)
-        for step, pairs in enumerate(shard_moves(n_blocks))
-    ]
+    return [jnp.where(odd, both[1], both[0]), jnp.where(odd, both[0], both[1])]
+
+
+def fetch_experts(shards, n_blocks, steps):
+    moves = shard_moves(n_blocks)
+    return [lax.ppermute(shards[step % 2], ("g", "r", "c"), moves[step]) for step in steps]
 
 
 def return_experts(parts, n_blocks):
@@ -1356,6 +1426,8 @@
     n_images = lengths.shape[0] * lengths.shape[1]
     capacity = (21 * tokens * TOP + 20 * n_experts - 1) // (20 * n_experts)
     padded = round_up(capacity, 16)
+    shards = order_shards(expert_in, expert_out)
+    own_chunks = fetch_experts(shards, n_blocks, range(EARLY))
     layer_b, gain_rows, router_t, columns = gather_weights(
         sizes,
         (lengths.shape[1], n_experts, capacity, padded),
@@ -1366,18 +1438,16 @@
         slot_mask,
         lengths,
     )
-    expert_in_now, expert_out_now, layer_b = lax.optimization_barrier((expert_in, expert_out, layer_b))
-    own_chunks = fetch_experts(expert_in_now, expert_out_now, n_blocks)
-    own_half = jnp.concatenate(own_chunks, 1)
-    other_half = swap_cores(own_half)
+    shards, layer_b = lax.optimization_barrier((shards, layer_b))
+    own_chunks += fetch_experts(shards, n_blocks, range(EARLY, 2 * n_blocks))
     x_zero, a_one, qkv, att_out, x_one, a_two, router_probs, logs, pooled, part_importance = (
         dense_forward(
             n_experts, lengths, slot_mask, patches, layer_b, gain_rows, router_t, columns
         )
     )
     arrived, details = dispatch(sizes, n_experts, padded, a_two, router_probs, columns)
-    activated, slope, result, part_pooled = expert_forward(
-        arrived, details, own_half, other_half, 4 * n_blocks
+    activated, slope, result, part_pooled, other_chunks = expert_forward(
+        sizes, arrived, details, own_chunks
     )
     g_head, d_pooled_all, d_pooled, g_norm_three, local_loss, total_importance = head_step(
         sizes,
@@ -1390,7 +1460,7 @@
         class_labels,
     )
     d_back, back_gate, *grads = expert_backward(
-        sizes, arrived, details, d_pooled_all, result, slope, activated, own_half, other_half
+        sizes, arrived, details, d_pooled_all, result, slope, activated, own_chunks, other_chunks
     )
     g_one, g_two = return_experts(grads, n_blocks)
     blocks = dense_backward(

time: 580 us -> 537 us (0.926)
  starting transfers between devices: 72.6 us -> 24.2 us
  Pallas kernels: 413 us -> 442 us
  waiting for transfers between devices: 21.9 us -> 0.02 us
    ppermute x5 -> x4, starting transfers between devices: 57.8 us -> 9.02 us  [fetch_experts(): lax.ppermute(shards[step % 2], ('g', 'r', 'c'), moves[step])]
    ppermute x5 -> x4, waiting for transfers between devices: 21.9 us -> 0.01 us  [fetch_experts(): lax.ppermute(shards[step % 2], ('g', 'r', 'c'), moves[step])]
    pallas_call x1, Pallas kernels: 44.7 us -> 63.3 us  [gather_weights(): pl.pallas_call(functools.partial(gather_kernel, sizes, rows, mats, routin...]
    pallas_call x1, Pallas kernels: 54 us -> 64.4 us  [dispatch(): pl.pallas_call(functools.partial(dispatch_kernel, sizes, n_experts, padde...]
    pallas_call x1, Pallas kernels: 44 us -> 51.4 us  [head_step(): pl.pallas_call(functools.partial(head_kernel, sizes, images), out_shape=(...]
    pallas_call x1, Pallas kernels: 72 us -> 65.7 us  [expert_backward(): pl.pallas_call(functools.partial(expert_backward_kernel, sizes, padded),...]
    unnamed x92 -> x95, local copies, waits for them, and re-layouts: 14.1 us -> 13.9 us
  transfers between devices with their start and end apart: 9 -> 8, of which waited for: 2 -> 0; matrix products, arithmetic and copies ran while one was open for 2% -> 2% of each run, Pallas kernels for 34% -> 51%
where the time goes in v5:
time: 537 us; the launch traced here: 532 us
  Pallas kernels  442 us (82%)
  other arithmetic  36.8 us (7%)
  starting transfers between devices  24.2 us (5%)
  local copies, waits for them, and re-layouts  17.6 us (3%)
  between operations  11.6 us (2%)
    pallas_call x1, Pallas kernels, expert_backward(): pl.pallas_call(functools.partial(expert_backward_kernel, sizes, padded),...  65.7 us
    pallas_call x1, Pallas kernels, dispatch(): pl.pallas_call(functools.partial(dispatch_kernel, sizes, n_experts, padde...  64.4 us
    pallas_call x1, Pallas kernels, gather_weights(): pl.pallas_call(functools.partial(gather_kernel, sizes, rows, mats, routin...  63.3 us
    pallas_call x1, Pallas kernels, scatter_dense(): pl.pallas_call(functools.partial(scatter_kernel, sizes), out_shape=jax.Sh...  63 us
    pallas_call x1, Pallas kernels, dense_backward(): pl.pallas_call(functools.partial(dense_backward_kernel, sizes, n_experts,...  56.1 us
    pallas_call x1, Pallas kernels, head_step(): pl.pallas_call(functools.partial(head_kernel, sizes, images), out_shape=(...  51.4 us
    pallas_call x1, Pallas kernels, expert_forward(): pl.pallas_call(functools.partial(expert_forward_kernel, sizes, padded), g...  43.7 us
    pallas_call x1, Pallas kernels, dense_forward(): pl.pallas_call(functools.partial(dense_forward_kernel, n_experts, lengths...  24 us
  transfers between devices with their start and end apart: 8, of which 0 were waited for; matrix products, arithmetic and copies ran while one was open for 2% of the time, Pallas kernels for 51%

profile of v5, /device:TPU:0, one launch (start us, length us, event | category | flops | bytes accessed | tf_op | source)
XLA Modules:
  0.0 532.5 jit_solution(18057707124588527181)
XLA Ops:
  0.7 2.6 convert_bitcast_fusion
  3.7 1.7 collective-permute-start
  7.2 63.3 %gather_weights.1 = (bf16[5,768,768]{2,1,0:T(8,128)(2,1)}, f32[8,768]{1,0:T(8,128)S(1)}, f32[8,768]{1,0:T(8,128)S(1)}, f32[1024,128]{1,0:T(8,128)S(1)}) custom-call(f32[5,24,768]{2,1,0:T(8,128)S(1)} %copy-done, f32[8,768]{1,0:T(8,128)S(1)} %scatter.9.tail_ref, s32[1024,2]{1,0:T(8,128)S(1)} %copy.57.pick_ref, s32[1,1024]{1,0:T(1,128)S(1)} %copy-done.4, ...), custom_call_target="tpu_custom_call" | custom-call | flops 50600001536 | tf_op jit(solution)/shard_map/gather_weights/pallas_call | solution.py:232
  70.6 1.5 collective-permute-start.1
  72.1 5.5 %collective-permute-start.3 = (bf16[2,384,768]{2,1,0:T(8,128)(2,1)S(1)}, bf16[2,384,768]{2,1,0:T(8,128)(2,1)S(1)}, u32[]{:S(2)}, u32[]{:S(2)}) collective-permute-start(bf16[2,384,768]{2,1,0:T(8,128)(2,1)S(1)} %get-tuple-element.96), channel_id=1, source_target_pairs={{0,20},{1,28},{4,0},{5,8},{8,4},{9,12},{12,16},{13,24},{16,21},{17... | collective-permute-start | bytes 3538952 | tf_op jit(solution)/shard_map/ppermute | solution.py:1370
  77.9 24.0 %dense_forward.1 = (f32[1024,768]{1,0:T(8,128)}, bf16[1024,768]{1,0:T(8,128)(2,1)S(1)}, bf16[1024,2304]{1,0:T(8,128)(2,1)}, bf16[1024,768]{1,0:T(8,128)(2,1)S(1)...) custom-call(s32[4,3]{1,0:T(4,128)S(1)} %copy-done.5, ...), custom_call_target="tpu_custom_call" | custom-call | flops 28750000128 | tf_op jit(solution)/shard_map/dense_forward/pallas_call | solution.py:722
  105.7 1.6 copy-done.8
  107.3 64.4 %dispatch.1 = (bf16[8,272,768]{2,1,0:T(8,128)(2,1)S(1)}, f32[8,8,384]{2,1,0:T(8,128)S(1)}) custom-call(bf16[1024,768]{1,0:T(8,128)(2,1)S(1)} %copy-done.8, f32[1024,128]{1,0:T(8,128)S(1)} %get-tuple-element.93.prob_ref, f32[1024,128]{1,0:T(8,128)S(1)} %get-tuple-element.91.col_ref), custom_call_target="tpu_custom_call" | custom-call | flops 57500000256 | tf_op jit(solution)/shard_map/dispatch/pallas_call | solution.py:826
  171.7 1.7 copy-done.9
  175.8 43.7 %expert_forward.1 = (bf16[8,2176,384]{2,1,0:T(8,128)(2,1)}, bf16[8,2176,384]{2,1,0:T(8,128)(2,1)}, bf16[8,272,768]{2,1,0:T(8,128)(2,1)}, f32[8,16,768]{2,1,0:T(8,128)}, bf16[4,2,384,768]{3,2,1,0:T(8,128)(2,1)}) custom-call(bf16[8,272,768]{2,1,0:T(8,128)(2,1)} %copy-done.9, f32[8,8,384]{2,1,0:T(8,128)} %copy-done.14, ...), custom_call_target="tpu_custom_call" | custom-call | flops 46000001024 | tf_op jit(solution)/shard_map/expert_forward/pallas_call | solution.py:958
  219.5 51.4 %head_step.1 = (f32[576,768]{1,0:T(8,128)}, f32[8,16,768]{2,1,0:T(8,128)}, f32[16,768]{1,0:T(8,128)}, f32[8,768]{1,0:T(8,128)}, f32[8,128]{1,0:T(8,128)}, /*index=5*/f32[8,768]{1,0:T(8,128)}) custom-call(f32[8,16,768]{2,1,0:T(8,128)} %get-tuple-element.98.part_ref, f32[16,768]{1,0:T(8,128)} %copy-done.13, f32[8,768]{1,0:T(8,128)} %copy-done.17, ...), custom_call_target="tpu_custom_call" | custom-call | flops 48299999232 | tf_op jit(solution)/shard_map/head_step/pallas_call | solution.py:536
  270.9 65.7 %expert_backward.1 = (bf16[8,272,768]{2,1,0:T(8,128)(2,1)}, f32[8,8,384]{2,1,0:T(8,128)}, bf16[2,384,768]{2,1,0:T(8,128)(2,1)}, bf16[2,384,768]{2,1,0:T(8,128)(2...) custom-call(bf16[8,272,768]{2,1,0:T(8,128)(2,1)} %copy-done.9, f32[8,8,384]{2,1,0:T(8,128)} %copy-done.14, ...), custom_call_target="tpu_custom_call" | custom-call | flops 74750001152 | tf_op jit(solution)/shard_map/expert_backward/pallas_call | solution.py:1139
  336.6 1.8 collective-permute-start.5
  338.4 3.1 collective-permute-start.7
  341.5 10.3 %collective-permute-start.6 = (bf16[2,384,768]{2,1,0:T(8,128)(2,1)}, bf16[2,384,768]{2,1,0:T(8,128)(2,1)}, u32[]{:S(2)}, u32[]{:S(2)}) collective-permute-start(bf16[2,384,768]{2,1,0:T(8,128)(2,1)} %get-tuple-element.120), channel_id=1, source_target_pairs={{0,0},{8,1},{4,4},{12,5},{16,8},{24,9},{20,12},{28,13},{1,16},{9,1... | collective-permute-start | bytes 3538952 | tf_op jit(solution)/shard_map/ppermute | solution.py:1378
  351.8 56.1 %dense_backward.1.g_ref = bf16[2,4,2,2,128,768]{5,4,3,2,1,0:T(8,128)(2,1)} custom-call(s32[4,3]{1,0:T(4,128)} %length_ref.5, s32[4,1,256]{2,1,0:T(1,128)} %copy-done.3, bf16[1024,768]{1,0:T(8,128)(2,1)} %patch_ref.3, f32[1024,768]{1,0:T(8,128)} %get-tuple-element.102.x_zero_ref, bf16[1024,768]{1,0:T(8,128)(2,1)} %copy-done.6, ...), custom_call_target="tpu_custom_call" | custom-call | flops 57500000256 | tf_op jit(solution)/shard_map/dense_backward/pallas_call | solution.py:1318
  408.0 63.0 %scatter_dense.1 = f32[128,768]{1,0:T(8,128)S(1)} custom-call(bf16[2,4,2,2,128,768]{5,4,3,2,1,0:T(8,128)(2,1)} %dense_backward.1.g_ref), custom_call_target="tpu_custom_call" | custom-call | flops 51749998592 | tf_op jit(solution)/shard_map/scatter_dense/pallas_call | solution.py:333
  479.2 1.8 multiply_reduce_fusion.6
  482.8 2.6 fusion.3
  492.7 10.5 %share_sums.1 = f32[8,128]{1,0:T(8,128)} custom-call(f32[8,128]{1,0:T(8,128)} %iota.15.in_ref), custom_call_target="tpu_custom_call" | custom-call | flops 11500000256 | tf_op jit(solution)/shard_map/share_sums/pallas_call | solution.py:382
  507.3 8.6 %multiply_add_fusion.2 = (f32[2,384,768]{2,1,0:T(8,128)}, f32[2,384,768]{2,1,0:T(8,128)}, f32[2,384,768]{2,1,0:T(8,128)}, f32[2,384,768]{2,1,0:T(8,128)}) fusion(f32[2,384,768]{2,1,0:T(8,128)} %param.55, f32[2,384,768]{2,1,0:T(8,128)} %param.52, f32[]{:T(128)S(6)} %min.3, f32[1,384,768]{2,1,0:T(8,128)} %copy-done.18, f32[1,384,768]{2,1,0:T(8,128)} %copy-done.19, ...), kind=kLoop, calls=%fused_computation.12 | loop fusion | flops 11796480 | bytes 21233668 | tf_op jit(solution)/shard_map/add | solution.py:43
  517.7 5.7 %multiply_add_fusion = (f32[2,384,768]{2,1,0:T(8,128)}, f32[2,384,768]{2,1,0:T(8,128)}, f32[2,384,768]{2,1,0:T(8,128)}, f32[2,384,768]{2,1,0:T(8,128)}) fusion(f32[2,384,768]{2,1,0:T(8,128)S(1)} %copy-done.23, f32[2,384,768]{2,1,0:T(8,128)S(1)} %copy-done.20, f32[]{:T(128)S(6)} %min.3, f32[1,384,768]{2,1,0:T(8,128)S(1)} %get-tuple-element.153, ...), kind=kLoop, calls=%fused_computation.9 | loop fusion | flops 11796480 | bytes 21233668 | tf_op jit(solution)/shard_map/add | solution.py:43
  524.6 4.1 multiply_add_fusion.4
  528.7 1.3 multiply_add_fusion.6
  (125 shorter events, 24.8 us)
Async XLA Ops:
  3.7 170.3 %collective-permute-start = (bf16[2,384,768]{2,1,0:T(8,128)(2,1)S(1)}, bf16[2,384,768]{2,1,0:T(8,128)(2,1)}, u32[]{:S(2)}, u32[]{:S(2)}) collective-permute-start(bf16[2,384,768]{2,1,0:T(8,128)(2,1)S(1)} %get-tuple-element.97), channel_id=1, source_target_pairs={{0,0},{1,8},{4,4},{5,12},{8,16},{9,24},{12,20},{13,28},{16,1},{17,... | collective-permute-start | bytes 3538952 | tf_op jit(solution)/shard_map/ppermute | solution.py:1370
  70.5 31.4 %copy-start.15 = (f32[8,768]{1,0:T(8,128)}, f32[8,768]{1,0:T(8,128)S(1)}, u32[]{:S(2)}) copy-start(f32[8,768]{1,0:T(8,128)S(1)} %get-tuple-element.89.gain_ref) | copy-start | bytes 73732
  70.5 31.4 %copy-start.16 = (f32[8,768]{1,0:T(8,128)}, f32[8,768]{1,0:T(8,128)S(1)}, u32[]{:S(2)}) copy-start(f32[8,768]{1,0:T(8,128)S(1)} %get-tuple-element.90.router_ref) | copy-start | bytes 73732
  70.6 35.1 %copy-start.10 = (f32[1024,128]{1,0:T(8,128)}, f32[1024,128]{1,0:T(8,128)S(1)}, u32[]{:S(2)}) copy-start(f32[1024,128]{1,0:T(8,128)S(1)} %get-tuple-element.91.col_ref) | copy-start | bytes 1572868
  70.6 103.4 %collective-permute-start.1 = (bf16[2,384,768]{2,1,0:T(8,128)(2,1)S(1)}, bf16[2,384,768]{2,1,0:T(8,128)(2,1)S(1)}, u32[]{:S(2)}, u32[]{:S(2)}) collective-permute-start(bf16[2,384,768]{2,1,0:T(8,128)(2,1)S(1)} %get-tuple-element.96), channel_id=1, source_target_pairs={{0,4},{1,12},{4,16},{5,24},{8,20},{9,28},{12,0},{13,8},{16,5},{17,... | collective-permute-start | bytes 3538952 | tf_op jit(solution)/shard_map/ppermute | solution.py:1370
  72.1 101.9 %collective-permute-start.3 = (bf16[2,384,768]{2,1,0:T(8,128)(2,1)S(1)}, bf16[2,384,768]{2,1,0:T(8,128)(2,1)S(1)}, u32[]{:S(2)}, u32[]{:S(2)}) collective-permute-start(bf16[2,384,768]{2,1,0:T(8,128)(2,1)S(1)} %get-tuple-element.96), channel_id=1, source_target_pairs={{0,20},{1,28},{4,0},{5,8},{8,4},{9,12},{12,16},{13,24},{16,21},{17... | collective-permute-start | bytes 3538952 | tf_op jit(solution)/shard_map/ppermute | solution.py:1370
  77.6 96.4 %collective-permute-start.2 = (bf16[2,384,768]{2,1,0:T(8,128)(2,1)S(1)}, bf16[2,384,768]{2,1,0:T(8,128)(2,1)S(1)}, u32[]{:S(2)}, u32[]{:S(2)}) collective-permute-start(bf16[2,384,768]{2,1,0:T(8,128)(2,1)S(1)} %get-tuple-element.97), channel_id=1, source_target_pairs={{0,16},{1,24},{4,20},{5,28},{8,0},{9,8},{12,4},{13,12},{16,17},{17... | collective-permute-start | bytes 3538952 | tf_op jit(solution)/shard_map/ppermute | solution.py:1370
  77.9 24.0 %copy-start.3 = (s32[4,1,256]{2,1,0:T(1,128)}, s32[4,1,256]{2,1,0:T(1,128)S(1)}, u32[]{:S(2)}) copy-start(s32[4,1,256]{2,1,0:T(1,128)S(1)} %broadcast_in_dim.13.mask_ref) | copy-start | bytes 12292
  105.7 66.0 %copy-start.11 = (f32[1024,128]{1,0:T(8,128)}, f32[1024,128]{1,0:T(8,128)S(1)}, u32[]{:S(2)}) copy-start(f32[1024,128]{1,0:T(8,128)S(1)} %get-tuple-element.93.prob_ref) | copy-start | bytes 1572868
  105.7 66.0 %copy-start.17 = (f32[8,768]{1,0:T(8,128)}, f32[8,768]{1,0:T(8,128)S(1)}, u32[]{:S(2)}) copy-start(f32[8,768]{1,0:T(8,128)S(1)} %get-tuple-element.100.imp_ref) | copy-start | bytes 73732
  336.6 146.1 %collective-permute-start.5 = (bf16[2,384,768]{2,1,0:T(8,128)(2,1)}, bf16[2,384,768]{2,1,0:T(8,128)(2,1)S(1)}, u32[]{:S(2)}, u32[]{:S(2)}) collective-permute-start(bf16[2,384,768]{2,1,0:T(8,128)(2,1)} %get-tuple-element.119), channel_id=1, source_target_pairs={{20,0},{28,1},{0,4},{8,5},{4,8},{12,9},{16,12},{24,13},{21,16},{29... | collective-permute-start | bytes 3538952 | tf_op jit(solution)/shard_map/ppermute | solution.py:1378
  338.4 144.4 %collective-permute-start.4 = (bf16[2,384,768]{2,1,0:T(8,128)(2,1)}, bf16[2,384,768]{2,1,0:T(8,128)(2,1)}, u32[]{:S(2)}, u32[]{:S(2)}) collective-permute-start(bf16[2,384,768]{2,1,0:T(8,128)(2,1)} %get-tuple-element.118), channel_id=1, source_target_pairs={{4,0},{12,1},{16,4},{24,5},{20,8},{28,9},{0,12},{8,13},{5,16},{13,... | collective-permute-start | bytes 3538952 | tf_op jit(solution)/shard_map/ppermute | solution.py:1378
  338.4 144.4 %collective-permute-start.7 = (bf16[2,384,768]{2,1,0:T(8,128)(2,1)}, bf16[2,384,768]{2,1,0:T(8,128)(2,1)}, u32[]{:S(2)}, u32[]{:S(2)}) collective-permute-start(bf16[2,384,768]{2,1,0:T(8,128)(2,1)} %get-tuple-element.121), channel_id=1, source_target_pairs={{16,0},{24,1},{20,4},{28,5},{0,8},{8,9},{4,12},{12,13},{17,16},{25... | collective-permute-start | bytes 3538952 | tf_op jit(solution)/shard_map/ppermute | solution.py:1378
  341.5 141.3 %collective-permute-start.6 = (bf16[2,384,768]{2,1,0:T(8,128)(2,1)}, bf16[2,384,768]{2,1,0:T(8,128)(2,1)}, u32[]{:S(2)}, u32[]{:S(2)}) collective-permute-start(bf16[2,384,768]{2,1,0:T(8,128)(2,1)} %get-tuple-element.120), channel_id=1, source_target_pairs={{0,0},{8,1},{4,4},{12,5},{16,8},{24,9},{20,12},{28,13},{1,16},{9,1... | collective-permute-start | bytes 3538952 | tf_op jit(solution)/shard_map/ppermute | solution.py:1378
  408.0 73.8 %copy-start.21 = (f32[576,768]{1,0:T(8,128)S(1)}, f32[576,768]{1,0:T(8,128)}, u32[]{:S(2)}) copy-start(f32[576,768]{1,0:T(8,128)} %get-tuple-element.122) | copy-start | bytes 5308420
  492.7 13.3 %copy-start.36 = (f32[24,8]{0,1:T(8,128)S(1)}, f32[24,8]{0,1:T(8,128)}, u32[]{:S(2)}) copy-start(f32[24,8]{0,1:T(8,128)} %param.44) | copy-start | bytes 2308
  492.7 13.3 %copy-start.38 = (f32[24,8]{0,1:T(8,128)S(1)}, f32[24,8]{0,1:T(8,128)}, u32[]{:S(2)}) copy-start(f32[24,8]{0,1:T(8,128)} %param.47) | copy-start | bytes 2308
  492.7 13.3 %copy-start.39 = (f32[24,8]{0,1:T(8,128)S(1)}, f32[24,8]{0,1:T(8,128)}, u32[]{:S(2)}) copy-start(f32[24,8]{0,1:T(8,128)} %param.45) | copy-start | bytes 2308
  492.7 13.3 %copy-start.40 = (f32[24,8]{0,1:T(8,128)S(1)}, f32[24,8]{0,1:T(8,128)}, u32[]{:S(2)}) copy-start(f32[24,8]{0,1:T(8,128)} %param.46) | copy-start | bytes 2308
  492.7 13.9 %copy-start.34 = (f32[6,24]{1,0:T(8,128)S(1)}, f32[6,24]{1,0:T(8,128)}, u32[]{:S(2)}) copy-start(f32[6,24]{1,0:T(8,128)} %param.48) | copy-start | bytes 1732
  492.7 13.9 %copy-start.41 = (f32[6,24]{1,0:T(8,128)S(1)}, f32[6,24]{1,0:T(8,128)}, u32[]{:S(2)}) copy-start(f32[6,24]{1,0:T(8,128)} %param.51) | copy-start | bytes 1732
  492.7 13.9 %copy-start.42 = (f32[6,24]{1,0:T(8,128)S(1)}, f32[6,24]{1,0:T(8,128)}, u32[]{:S(2)}) copy-start(f32[6,24]{1,0:T(8,128)} %param.49) | copy-start | bytes 1732
  492.7 13.9 %copy-start.43 = (f32[6,24]{1,0:T(8,128)S(1)}, f32[6,24]{1,0:T(8,128)}, u32[]{:S(2)}) copy-start(f32[6,24]{1,0:T(8,128)} %param.50) | copy-start | bytes 1732
  507.2 10.5 %copy-start.25 = (f32[2,384,768]{2,1,0:T(8,128)S(1)}, f32[2,384,768]{2,1,0:T(8,128)}, u32[]{:S(2)}) copy-start(f32[2,384,768]{2,1,0:T(8,128)} %param.58) | copy-start | bytes 7077892
  (31 other events, 111.1 us)

commit v6 on v5

--- a/solution.py
+++ b/solution.py
@@ -249,7 +249,11 @@
     )(dense, tail, picks, ranks, slot_mask, lengths)
 
 
-def scatter_kernel(sizes, g_ref, out_ref, hold, sib, got_xa, got_yb, got_ya, got_xb, got_z, *sems):
+def total_square(value):
+    return jnp.sum(jnp.sum(value * value, 0, keepdims=True), 1, keepdims=True)
+
+
+def scatter_kernel(sizes, g_ref, out_ref, square_ref, hold, sib, got_xa, got_yb, got_ya, got_xb, got_z, *sems):
     at = Place(sizes)
     Z, Y, X = at.Z, at.Y, at.X
     depth = g_ref.shape[4]
@@ -320,6 +324,7 @@
     for z in order[:-1]:
         send(got_z.at[z], got_z.at[z], z_out.at[z], z_in.at[z], at.at(z=z)).wait_recv()
         out_ref[...] += wide(got_z[z])
+    square_ref[...] = jnp.broadcast_to(total_square(out_ref[...]), square_ref.shape)
     for copy in started:
         copy.wait_send()
 
@@ -332,9 +337,12 @@
     half = jnp.bfloat16
     return pl.pallas_call(
         functools.partial(scatter_kernel, sizes),
-        out_shape=jax.ShapeDtypeStruct((depth, width), jnp.float32),
+        out_shape=(
+            jax.ShapeDtypeStruct((depth, width), jnp.float32),
+            jax.ShapeDtypeStruct((8, 128), jnp.float32),
+        ),
         in_specs=[whole()],
-        out_specs=whole(),
+        out_specs=(whole(), whole()),
         scratch_shapes=[
             VMEM((Z, X, Y, depth, width), half),
             VMEM((Z, X, Y, depth, width), half),
@@ -353,8 +361,11 @@
     )(blocks)
 
 
-def sums_kernel(sizes, in_ref, out_ref, land, out_sem, in_sem):
+def finish_kernel(sizes, n_experts, head_ref, dense_ref, imp_ref, *refs):
     at = Place(sizes)
+    many = len(refs) - 7
+    parts = refs[:many]
+    first_ref, second_ref, out_ref, land, own, out_sem, in_sem = refs[many:]
     count = 2 * at.chips
     me = at.chip * 2 + at.c
     ids = others(me, count)
@@ -365,33 +376,65 @@
         return spot
 
     greet([peer(device) for device in ids])
-    land[me] = in_ref[...]
-    copies = [send(in_ref, land.at[me], out_sem.at[d], in_sem.at[me], peer(d)) for d in ids]
+    place = lax.rem(at.g * QUAD + at.r, 2)
+    square = dense_ref[0:1, 0:1] + head_ref[1:2, 0:1]
+    for parity in range(2):
+        expert = place if parity == 0 else 1 - place
+        for index, ref in enumerate((first_ref, second_ref)):
+            total = None
+            for step in range(parity, many, 2):
+                found = parts[step][index].astype(jnp.float32)
+                total = found if total is None else total + found
+            ref[expert] = total
+            square = square + total_square(total)
+    line = lax.broadcasted_iota(jnp.int32, own.shape, 0)
+    own[...] = jnp.where(line == 0, head_ref[0:1, 0:1], jnp.where(line == 1, square, 0.0))
+    land[me] = own[...]
+    copies = [send(own, land.at[me], out_sem.at[d], in_sem.at[me], peer(d)) for d in ids]
     for copy in copies:
         copy.start()
+    importance = imp_ref[0:1, 0:128]
+    head = lax.broadcasted_iota(jnp.int32, (1, 128), 1) < n_experts
+    centre = jnp.sum(jnp.where(head, importance, 0.0), 1, keepdims=True) / n_experts
+    away = jnp.where(head, importance - centre, 0.0)
+    spread = jnp.sum(away * away, 1, keepdims=True) / n_experts
+    balance = aux_weight * spread / (centre * centre)
     for d in ids:
         send(land.at[d], land.at[d], out_sem.at[d], in_sem.at[d], peer(d)).wait_recv()
-    out_ref[...] = jnp.sum(land[...], 0)
+    sums = jnp.sum(land[...], 0)
+    norm = jnp.sqrt(sums[1:2, 0:1])
+    factor = jnp.minimum(1.0, clip_limit / norm)
+    loss = sums[0:1, 0:1] + balance
+    out_ref[...] = jnp.where(line == 0, loss, jnp.where(line == 1, norm, factor))
     for copy in copies:
         copy.wait_send()
 
 
-def share_sums(sizes, values):
-    count = sizes["g"] * QUAD * sizes["x"] * 2
+def finish(sizes, n_experts, parts, head_sums, dense_sums, importance):
+    devices = sizes["g"] * QUAD * sizes["x"] * 2
+    unused, rows, width = parts[0].shape
     dma = pltpu.SemaphoreType.DMA
+    grads = jax.ShapeDtypeStruct((2, rows, width), jnp.float32)
     return pl.pallas_call(
-        functools.partial(sums_kernel, sizes),
-        out_shape=jax.ShapeDtypeStruct(values.shape, jnp.float32),
-        in_specs=[whole()],
-        out_specs=whole(),
-        scratch_shapes=[VMEM((count, *values.shape), jnp.float32), dma((count,)), dma((count,))],
-        compiler_params=pltpu.CompilerParams(collective_id=3, has_side_effects=True),
+        functools.partial(finish_kernel, sizes, n_experts),
+        out_shape=(grads, grads, jax.ShapeDtypeStruct((8, 128), jnp.float32)),
+        in_specs=[whole()] * (3 + len(parts)),
+        out_specs=(whole(),) * 3,
+        scratch_shapes=[
+            VMEM((devices, 8, 128), jnp.float32),
+            VMEM((8, 128), jnp.float32),
+            dma((devices,)),
+            dma((devices,)),
+        ],
+        compiler_params=pltpu.CompilerParams(
+            collective_id=3, has_side_effects=True, vmem_limit_bytes=48 * MIB
+        ),
         cost_estimate=cost(10),
-        name="share_sums",
-    )(values)
-
-
-EARLY = 1
+        name="finish",
+    )(head_sums, dense_sums, importance, *parts)
+
+
+EARLY = 0
 IMAGE_PAD = 16
 
 
@@ -490,13 +533,15 @@
     loss = jnp.maximum(logits, 0.0) + jnp.log1p(power) - target * logits
     loss = jnp.sum(jnp.where(image < images, loss, 0.0), 1, keepdims=True)
     loss = jnp.sum(loss, 0, keepdims=True) / count
-    sums_ref[...] = jnp.broadcast_to(loss, sums_ref.shape)
     chance = jnp.where(logits >= 0.0, 1.0, power) / (1.0 + power)
     d_logits[...] = jnp.where(image < images, (chance - target) / count, 0.0).astype(jnp.bfloat16)
     partial = dot_f32(d_logits[...], head_b[...], TN)
     d_rows[...] = partial.reshape(d_rows.shape).astype(jnp.bfloat16)
     begin(send(d_rows.at[1 - at.c], d_sib, s_out.at[1], s_in.at[1], at.sibling()))
-    g_head_ref[...] = dot_f32(d_logits[...], gathered, NN)
+    g_head = dot_f32(d_logits[...], gathered, NN)
+    g_head_ref[...] = g_head
+    line = lax.broadcasted_iota(jnp.int32, sums_ref.shape, 0)
+    sums_ref[...] = jnp.where(line == 0, loss, jnp.where(line == 1, total_square(g_head), 0.0))
     send(d_sib, d_sib, s_out.at[1], s_in.at[1], at.sibling()).wait_recv()
     d_sum[...] = (d_rows[at.c].astype(jnp.float32) + d_sib[...].astype(jnp.float32)).astype(jnp.bfloat16)
     for chip in same_core:
@@ -1371,15 +1416,10 @@
 
 
 def return_experts(parts, n_blocks):
-    place = lax.axis_index("g") * QUAD + lax.axis_index("r")
-    odd = lax.rem(place, 2) == 1
-    sums = [None, None]
-    for step, pairs in enumerate(shard_moves(n_blocks)):
-        back = lax.ppermute(parts[step], ("g", "r", "c"), [(dst, src) for src, dst in pairs])
-        back = back.astype(jnp.float32)
-        sums[step % 2] = back if sums[step % 2] is None else sums[step % 2] + back
-    zero, one = jnp.where(odd, sums[1], sums[0]), jnp.where(odd, sums[0], sums[1])
-    return jnp.stack([zero[0], one[0]]), jnp.stack([zero[1], one[1]])
+    return [
+        lax.ppermute(part, ("g", "r", "c"), [(dst, src) for src, dst in pairs])
+        for part, pairs in zip(parts, shard_moves(n_blocks))
+    ]
 
 
 def body(
@@ -1449,7 +1489,7 @@
     activated, slope, result, part_pooled, other_chunks = expert_forward(
         sizes, arrived, details, own_chunks
     )
-    g_head, d_pooled_all, d_pooled, g_norm_three, local_loss, total_importance = head_step(
+    g_head, d_pooled_all, d_pooled, g_norm_three, head_sums, total_importance = head_step(
         sizes,
         n_images,
         part_pooled,
@@ -1462,7 +1502,7 @@
     d_back, back_gate, *grads = expert_backward(
         sizes, arrived, details, d_pooled_all, result, slope, activated, own_chunks, other_chunks
     )
-    g_one, g_two = return_experts(grads, n_blocks)
+    parts = return_experts(grads, n_blocks)
     blocks = dense_backward(
         sizes,
         n_experts,
@@ -1482,25 +1522,16 @@
         total_importance,
         g_norm_three,
     )
-    reduced = scatter_dense(sizes, blocks)
+    reduced, dense_sums = scatter_dense(sizes, blocks)
+    g_one, g_two, totals = finish(
+        sizes, n_experts, parts, head_sums, dense_sums, total_importance
+    )
     n_dense = dense_weights.shape[0] * rows_own
     g_layers = reduced[:n_dense].reshape(-1, rows_own, model_width)
     g_norms = reduced[n_dense : n_dense + 6, :rows_own]
     g_router = reduced[n_dense : n_dense + n_experts, 128 : 128 + rows_own].T
     importance = total_importance[0, :n_experts]
-    local_loss = local_loss[0, 0]
-    centre = jnp.mean(importance)
-    spread = jnp.mean((importance - centre) ** 2)
-    squares = (
-        jnp.sum(g_layers * g_layers) + jnp.sum(g_router * g_router) + jnp.sum(g_norms * g_norms)
-    )
-    squares = squares + jnp.sum(g_one * g_one) + jnp.sum(g_two * g_two) + jnp.sum(g_head * g_head)
-    line = lax.broadcasted_iota(jnp.int32, (8, 128), 0)
-    all_sums = share_sums(sizes, jnp.where(line == 0, local_loss, squares))
-    loss_sum, square_sum = all_sums[0, 0], all_sums[1, 0]
-    grad_norm = jnp.sqrt(square_sum)
-    factor = jnp.minimum(1.0, clip_limit / grad_norm)
-    loss_value = loss_sum + aux_weight * spread / (centre * centre)
+    loss_value, grad_norm, factor = totals[0, 0], totals[1, 0], totals[2, 0]
     dense_out = adam_update(
         dense_weights, dense_first, dense_second, dense_average, g_layers, factor, base_rate
     )

time: 537 us -> 518 us (0.965)
  between operations: 11.6 us -> 1.43 us
  waiting for transfers between devices: 0.02 us -> 6.91 us
  starting transfers between devices: 24.2 us -> 18.5 us
    pallas_call x1, Pallas kernels: 63.3 us -> 44.7 us  [gather_weights(): pl.pallas_call(functools.partial(gather_kernel, sizes, rows, mats, routin...]
    pallas_call x1, Pallas kernels: 43.7 us -> 53.9 us  [expert_forward(): pl.pallas_call(functools.partial(expert_forward_kernel, sizes, padded), g...]
    reduce_sum x8 -> x0, other arithmetic: 8.44 us -> none  [the longest x1 1.79 us: body(): spread = jnp.mean((importance - centre) ** 2)]
    add x6, other arithmetic: 20.9 us -> 28.3 us  [adam_update(): polyak_decay * average_state + (1.0 - polyak_decay) * weight_new]
    ppermute x4, waiting for transfers between devices: 0.01 us -> 6.9 us  [return_experts(): lax.ppermute(part, ('g', 'r', 'c'), [(dst, src) for src, dst in pairs])]
    pallas_call x1, Pallas kernels: 64.4 us -> 70 us  [dispatch(): pl.pallas_call(functools.partial(dispatch_kernel, sizes, n_experts, padde...]
    ppermute x4, starting transfers between devices: 15.2 us -> 9.58 us  [return_experts(): lax.ppermute(part, ('g', 'r', 'c'), [(dst, src) for src, dst in pairs])]
    unnamed x95 -> x87, local copies, waits for them, and re-layouts: 13.9 us -> 11.5 us
  transfers between devices with their start and end apart: 8 -> 8, of which waited for: 0 -> 1; matrix products, arithmetic and copies ran while one was open for 2% -> 0% of each run, Pallas kernels for 51% -> 41%
where the time goes in v6:
time: 518 us; the launch traced here: 513 us
  Pallas kernels  439 us (85%)
  other arithmetic  34.1 us (7%)
  starting transfers between devices  18.5 us (4%)
  local copies, waits for them, and re-layouts  13.5 us (3%)
  waiting for transfers between devices  6.91 us (1%)
    pallas_call x1, Pallas kernels, dispatch(): pl.pallas_call(functools.partial(dispatch_kernel, sizes, n_experts, padde...  70 us
    pallas_call x1, Pallas kernels, expert_backward(): pl.pallas_call(functools.partial(expert_backward_kernel, sizes, padded),...  65.7 us
    pallas_call x1, Pallas kernels, scatter_dense(): pl.pallas_call(functools.partial(scatter_kernel, sizes), out_shape=(jax.S...  59.3 us
    pallas_call x1, Pallas kernels, dense_backward(): pl.pallas_call(functools.partial(dense_backward_kernel, sizes, n_experts,...  56.1 us
    pallas_call x1, Pallas kernels, expert_forward(): pl.pallas_call(functools.partial(expert_forward_kernel, sizes, padded), g...  53.9 us
    pallas_call x1, Pallas kernels, head_step(): pl.pallas_call(functools.partial(head_kernel, sizes, images), out_shape=(...  47.2 us
    pallas_call x1, Pallas kernels, gather_weights(): pl.pallas_call(functools.partial(gather_kernel, sizes, rows, mats, routin...  44.7 us
    add x6, other arithmetic, adam_update(): polyak_decay * average_state + (1.0 - polyak_decay) * weight_new  28.3 us
  transfers between devices with their start and end apart: 8, of which 1 were waited for; matrix products, arithmetic and copies ran while one was open for 0% of the time, Pallas kernels for 41%

profile of v6, /device:TPU:0, one launch (start us, length us, event | category | flops | bytes accessed | tf_op | source)
XLA Modules:
  0.0 513.5 jit_solution(14094881987749698530)
XLA Ops:
  2.2 1.3 select_bitcast_fusion.2
  4.3 2.6 convert_bitcast_fusion
  8.1 44.7 %gather_weights.1 = (bf16[5,768,768]{2,1,0:T(8,128)(2,1)}, f32[8,768]{1,0:T(8,128)S(1)}, f32[8,768]{1,0:T(8,128)S(1)}, f32[1024,128]{1,0:T(8,128)S(1)}) custom-call(f32[5,24,768]{2,1,0:T(8,128)S(1)} %copy-done, f32[8,768]{1,0:T(8,128)S(1)} %scatter.9.tail_ref, s32[1024,2]{1,0:T(8,128)S(1)} %copy.57.pick_ref, s32[1,1024]{1,0:T(1,128)S(1)} %copy-done.4, ...), custom_call_target="tpu_custom_call" | custom-call | flops 50600001536 | tf_op jit(solution)/shard_map/gather_weights/pallas_call | solution.py:232
  52.9 1.6 collective-permute-start.2
  55.2 6.5 %collective-permute-start.3 = (bf16[2,384,768]{2,1,0:T(8,128)(2,1)S(1)}, bf16[2,384,768]{2,1,0:T(8,128)(2,1)S(1)}, u32[]{:S(2)}, u32[]{:S(2)}) collective-permute-start(bf16[2,384,768]{2,1,0:T(8,128)(2,1)S(1)} %get-tuple-element.102), channel_id=1, source_target_pairs={{0,20},{1,28},{4,0},{5,8},{8,4},{9,12},{12,16},{13,24},{16,21},{17... | collective-permute-start | bytes 3538952 | tf_op jit(solution)/shard_map/ppermute | solution.py:1415
  61.9 24.0 %dense_forward.1 = (f32[1024,768]{1,0:T(8,128)}, bf16[1024,768]{1,0:T(8,128)(2,1)S(1)}, bf16[1024,2304]{1,0:T(8,128)(2,1)}, bf16[1024,768]{1,0:T(8,128)(2,1)S(1)...) custom-call(s32[4,3]{1,0:T(4,128)S(1)} %copy-done.5, ...), custom_call_target="tpu_custom_call" | custom-call | flops 28750000128 | tf_op jit(solution)/shard_map/dense_forward/pallas_call | solution.py:767
  89.6 1.6 copy-done.9
  91.2 70.0 %dispatch.1 = (bf16[8,272,768]{2,1,0:T(8,128)(2,1)S(1)}, f32[8,8,384]{2,1,0:T(8,128)S(1)}) custom-call(bf16[1024,768]{1,0:T(8,128)(2,1)S(1)} %copy-done.9, f32[1024,128]{1,0:T(8,128)S(1)} %get-tuple-element.98.prob_ref, f32[1024,128]{1,0:T(8,128)S(1)} %get-tuple-element.96.col_ref), custom_call_target="tpu_custom_call" | custom-call | flops 57500000256 | tf_op jit(solution)/shard_map/dispatch/pallas_call | solution.py:871
  161.3 1.7 copy-done.10
  165.8 53.9 %expert_forward.1 = (bf16[8,2176,384]{2,1,0:T(8,128)(2,1)}, bf16[8,2176,384]{2,1,0:T(8,128)(2,1)}, bf16[8,272,768]{2,1,0:T(8,128)(2,1)}, f32[8,16,768]{2,1,0:T(8,128)}, bf16[4,2,384,768]{3,2,1,0:T(8,128)(2,1)}) custom-call(bf16[8,272,768]{2,1,0:T(8,128)(2,1)} %copy-done.10, f32[8,8,384]{2,1,0:T(8,128)} %copy-done.15, bf16[2,384,768]{2,1,0:T(8,128)(2,1)} %copy-done.40, ...), custom_call_target="tpu_custom_call" | custom-call | flops 46000001024 | tf_op jit(solution)/shard_map/expert_forward/pallas_call | solution.py:1003
  219.7 47.2 %head_step.1 = (f32[576,768]{1,0:T(8,128)}, f32[8,16,768]{2,1,0:T(8,128)}, f32[16,768]{1,0:T(8,128)}, f32[8,768]{1,0:T(8,128)}, f32[8,128]{1,0:T(8,128)}, /*index=5*/f32[8,768]{1,0:T(8,128)}) custom-call(f32[8,16,768]{2,1,0:T(8,128)} %get-tuple-element.103.part_ref, f32[16,768]{1,0:T(8,128)} %copy-done.14, f32[8,768]{1,0:T(8,128)} %copy-done.19, ...), custom_call_target="tpu_custom_call" | custom-call | flops 48299999232 | tf_op jit(solution)/shard_map/head_step/pallas_call | solution.py:581
  266.9 65.7 %expert_backward.1 = (bf16[8,272,768]{2,1,0:T(8,128)(2,1)}, f32[8,8,384]{2,1,0:T(8,128)}, bf16[2,384,768]{2,1,0:T(8,128)(2,1)}, bf16[2,384,768]{2,1,0:T(8,128)(2...) custom-call(bf16[8,272,768]{2,1,0:T(8,128)(2,1)} %copy-done.10, f32[8,8,384]{2,1,0:T(8,128)} %copy-done.15, ...), custom_call_target="tpu_custom_call" | custom-call | flops 74750001152 | tf_op jit(solution)/shard_map/expert_backward/pallas_call | solution.py:1184
  332.5 1.9 collective-permute-start.4
  334.5 1.6 collective-permute-start.5
  336.1 3.0 collective-permute-start.6
  339.1 3.0 collective-permute-start.7
  342.1 56.1 %dense_backward.1.g_ref = bf16[2,4,2,2,128,768]{5,4,3,2,1,0:T(8,128)(2,1)} custom-call(s32[4,3]{1,0:T(4,128)} %length_ref.5, s32[4,1,256]{2,1,0:T(1,128)} %copy-done.3, bf16[1024,768]{1,0:T(8,128)(2,1)} %patch_ref.3, f32[1024,768]{1,0:T(8,128)} %get-tuple-element.107.x_zero_ref, bf16[1024,768]{1,0:T(8,128)(2,1)} %copy-done.7, ...), custom_call_target="tpu_custom_call" | custom-call | flops 57500000256 | tf_op jit(solution)/shard_map/dense_backward/pallas_call | solution.py:1363
  398.2 59.3 %scatter_dense.1 = (f32[128,768]{1,0:T(8,128)S(1)}, f32[8,128]{1,0:T(8,128)S(1)}) custom-call(bf16[2,4,2,2,128,768]{5,4,3,2,1,0:T(8,128)(2,1)} %dense_backward.1.g_ref), custom_call_target="tpu_custom_call" | custom-call | flops 51749998592 | tf_op jit(solution)/shard_map/scatter_dense/pallas_call | solution.py:338
  458.1 6.9 %collective-permute-done.7.refs_3_ = bf16[2,384,768]{2,1,0:T(8,128)(2,1)} collective-permute-done((bf16[2,384,768]{2,1,0:T(8,128)(2,1)}, bf16[2,384,768]{2,1,0:T(8,128)(2,1)}, u32[]{:S(2)}, u32[]{:S(2)}) %collective-permute-start.7) | collective-permute-done | bytes 1179680 | tf_op jit(solution)/shard_map/ppermute | solution.py:1420
  465.1 18.1 %finish.1 = (f32[2,384,768]{2,1,0:T(8,128)}, f32[2,384,768]{2,1,0:T(8,128)}, f32[8,128]{1,0:T(8,128)S(1)}) custom-call(f32[8,128]{1,0:T(8,128)S(1)} %copy-done.16, f32[8,128]{1,0:T(8,128)S(1)} %get-tuple-element.123.dense_ref, f32[8,768]{1,0:T(8,128)S(1)} %copy-done.6, bf16[2,384,768]{2,1,0:T(8,128)(2,1)S(1)} %collective-permute-done.4.refs_0_, ...), custom_call_target="tpu_custom_call" | custom-call | flops 11500000256 | tf_op jit(solution)/shard_map/finish/pallas_call | solution.py:418
  487.3 1.3 multiply_add_fusion.6
  488.7 7.7 %multiply_add_fusion.4 = (f32[576,768]{1,0:T(8,128)}, f32[576,768]{1,0:T(8,128)}, f32[576,768]{1,0:T(8,128)}, f32[576,768]{1,0:T(8,128)}) fusion(f32[576,768]{1,0:T(8,128)S(1)} %copy-done.27, f32[576,768]{1,0:T(8,128)S(1)} %copy-done.26, f32[576,768]{1,0:T(8,128)} %get-tuple-element.132, f32[]{:T(128)} %bitcast.8, f32[576,768]{1,0:T(8,128)} %param.61, ...), kind=kLoop, calls=%fused_computation.14 | loop fusion | flops 8404992 | bytes 15925252 | tf_op jit(solution)/shard_map/add | solution.py:43
  496.4 8.0 %multiply_add_fusion = (f32[2,384,768]{2,1,0:T(8,128)}, f32[2,384,768]{2,1,0:T(8,128)}, f32[2,384,768]{2,1,0:T(8,128)}, f32[2,384,768]{2,1,0:T(8,128)}) fusion(f32[2,384,768]{2,1,0:T(8,128)S(1)} %copy-done.22, f32[2,384,768]{2,1,0:T(8,128)S(1)} %copy-done.20, f32[2,384,768]{2,1,0:T(8,128)} %get-tuple-element.131, f32[]{:T(128)} %bitcast.8, ...), kind=kLoop, calls=%fused_computation.7 | loop fusion | flops 11206656 | bytes 21233668 | tf_op jit(solution)/shard_map/add | solution.py:43
  504.4 8.9 %multiply_add_fusion.2 = (f32[2,384,768]{2,1,0:T(8,128)}, f32[2,384,768]{2,1,0:T(8,128)}, f32[2,384,768]{2,1,0:T(8,128)}, f32[2,384,768]{2,1,0:T(8,128)}) fusion(f32[2,384,768]{2,1,0:T(8,128)S(1)} %copy-done.25, f32[2,384,768]{2,1,0:T(8,128)S(1)} %copy-done.21, f32[2,384,768]{2,1,0:T(8,128)} %get-tuple-element.130, f32[]{:T(128)} %bitcast.8, ...), kind=kLoop, calls=%fused_computation.10 | loop fusion | flops 11206656 | bytes 21233668 | tf_op jit(solution)/shard_map/add | solution.py:43
  (104 shorter events, 15.5 us)
Async XLA Ops:
  52.9 33.1 %copy-start.17 = (f32[8,768]{1,0:T(8,128)}, f32[8,768]{1,0:T(8,128)S(1)}, u32[]{:S(2)}) copy-start(f32[8,768]{1,0:T(8,128)S(1)} %get-tuple-element.94.gain_ref) | copy-start | bytes 73732
  52.9 33.0 %copy-start.18 = (f32[8,768]{1,0:T(8,128)}, f32[8,768]{1,0:T(8,128)S(1)}, u32[]{:S(2)}) copy-start(f32[8,768]{1,0:T(8,128)S(1)} %get-tuple-element.95.router_ref) | copy-start | bytes 73732
  52.9 36.8 %copy-start.11 = (f32[1024,128]{1,0:T(8,128)}, f32[1024,128]{1,0:T(8,128)S(1)}, u32[]{:S(2)}) copy-start(f32[1024,128]{1,0:T(8,128)S(1)} %get-tuple-element.96.col_ref) | copy-start | bytes 1572868
  52.9 110.7 %collective-permute-start.2 = (bf16[2,384,768]{2,1,0:T(8,128)(2,1)S(1)}, bf16[2,384,768]{2,1,0:T(8,128)(2,1)S(1)}, u32[]{:S(2)}, u32[]{:S(2)}) collective-permute-start(bf16[2,384,768]{2,1,0:T(8,128)(2,1)S(1)} %get-tuple-element.101), channel_id=1, source_target_pairs={{0,16},{1,24},{4,20},{5,28},{8,0},{9,8},{12,4},{13,12},{16,17},{17... | collective-permute-start | bytes 3538952 | tf_op jit(solution)/shard_map/ppermute | solution.py:1415
  54.5 109.2 %collective-permute-start = (bf16[2,384,768]{2,1,0:T(8,128)(2,1)S(1)}, bf16[2,384,768]{2,1,0:T(8,128)(2,1)S(1)}, u32[]{:S(2)}, u32[]{:S(2)}) collective-permute-start(bf16[2,384,768]{2,1,0:T(8,128)(2,1)S(1)} %get-tuple-element.101), channel_id=1, source_target_pairs={{0,0},{1,8},{4,4},{5,12},{8,16},{9,24},{12,20},{13,28},{16,1},{17,... | collective-permute-start | bytes 3538952 | tf_op jit(solution)/shard_map/ppermute | solution.py:1415
  55.2 108.5 %collective-permute-start.3 = (bf16[2,384,768]{2,1,0:T(8,128)(2,1)S(1)}, bf16[2,384,768]{2,1,0:T(8,128)(2,1)S(1)}, u32[]{:S(2)}, u32[]{:S(2)}) collective-permute-start(bf16[2,384,768]{2,1,0:T(8,128)(2,1)S(1)} %get-tuple-element.102), channel_id=1, source_target_pairs={{0,20},{1,28},{4,0},{5,8},{8,4},{9,12},{12,16},{13,24},{16,21},{17... | collective-permute-start | bytes 3538952 | tf_op jit(solution)/shard_map/ppermute | solution.py:1415
  61.7 102.0 %collective-permute-start.1 = (bf16[2,384,768]{2,1,0:T(8,128)(2,1)S(1)}, bf16[2,384,768]{2,1,0:T(8,128)(2,1)S(1)}, u32[]{:S(2)}, u32[]{:S(2)}) collective-permute-start(bf16[2,384,768]{2,1,0:T(8,128)(2,1)S(1)} %get-tuple-element.102), channel_id=1, source_target_pairs={{0,4},{1,12},{4,16},{5,24},{8,20},{9,28},{12,0},{13,8},{16,5},{17,... | collective-permute-start | bytes 3538952 | tf_op jit(solution)/shard_map/ppermute | solution.py:1415
  61.9 24.0 %copy-start.3 = (s32[4,1,256]{2,1,0:T(1,128)}, s32[4,1,256]{2,1,0:T(1,128)S(1)}, u32[]{:S(2)}) copy-start(s32[4,1,256]{2,1,0:T(1,128)S(1)} %broadcast_in_dim.2.mask_ref) | copy-start | bytes 12292
  89.6 71.7 %copy-start.12 = (f32[1024,128]{1,0:T(8,128)}, f32[1024,128]{1,0:T(8,128)S(1)}, u32[]{:S(2)}) copy-start(f32[1024,128]{1,0:T(8,128)S(1)} %get-tuple-element.98.prob_ref) | copy-start | bytes 1572868
  89.6 71.7 %copy-start.19 = (f32[8,768]{1,0:T(8,128)}, f32[8,768]{1,0:T(8,128)S(1)}, u32[]{:S(2)}) copy-start(f32[8,768]{1,0:T(8,128)S(1)} %get-tuple-element.105.imp_ref) | copy-start | bytes 73732
  332.5 125.5 %collective-permute-start.4 = (bf16[2,384,768]{2,1,0:T(8,128)(2,1)}, bf16[2,384,768]{2,1,0:T(8,128)(2,1)S(1)}, u32[]{:S(2)}, u32[]{:S(2)}) collective-permute-start(bf16[2,384,768]{2,1,0:T(8,128)(2,1)} %get-tuple-element.124), channel_id=1, source_target_pairs={{0,0},{8,1},{4,4},{12,5},{16,8},{24,9},{20,12},{28,13},{1,16},{9,1... | collective-permute-start | bytes 3538952 | tf_op jit(solution)/shard_map/ppermute | solution.py:1420
  334.5 123.6 %collective-permute-start.5 = (bf16[2,384,768]{2,1,0:T(8,128)(2,1)}, bf16[2,384,768]{2,1,0:T(8,128)(2,1)S(1)}, u32[]{:S(2)}, u32[]{:S(2)}) collective-permute-start(bf16[2,384,768]{2,1,0:T(8,128)(2,1)} %get-tuple-element.125), channel_id=1, source_target_pairs={{4,0},{12,1},{16,4},{24,5},{20,8},{28,9},{0,12},{8,13},{5,16},{13,... | collective-permute-start | bytes 3538952 | tf_op jit(solution)/shard_map/ppermute | solution.py:1420
  336.1 122.0 %collective-permute-start.6 = (bf16[2,384,768]{2,1,0:T(8,128)(2,1)}, bf16[2,384,768]{2,1,0:T(8,128)(2,1)S(1)}, u32[]{:S(2)}, u32[]{:S(2)}) collective-permute-start(bf16[2,384,768]{2,1,0:T(8,128)(2,1)} %get-tuple-element.126), channel_id=1, source_target_pairs={{16,0},{24,1},{20,4},{28,5},{0,8},{8,9},{4,12},{12,13},{17,16},{25... | collective-permute-start | bytes 3538952 | tf_op jit(solution)/shard_map/ppermute | solution.py:1420
  339.1 125.9 %collective-permute-start.7 = (bf16[2,384,768]{2,1,0:T(8,128)(2,1)}, bf16[2,384,768]{2,1,0:T(8,128)(2,1)}, u32[]{:S(2)}, u32[]{:S(2)}) collective-permute-start(bf16[2,384,768]{2,1,0:T(8,128)(2,1)} %get-tuple-element.127), channel_id=1, source_target_pairs={{20,0},{28,1},{0,4},{8,5},{4,8},{12,9},{16,12},{24,13},{21,16},{29... | collective-permute-start | bytes 3538952 | tf_op jit(solution)/shard_map/ppermute | solution.py:1420
  398.2 59.3 %copy-start.6 = (f32[8,768]{1,0:T(8,128)S(1)}, f32[8,768]{1,0:T(8,128)}, u32[]{:S(2)}) copy-start(f32[8,768]{1,0:T(8,128)} %get-tuple-element.121.imp_ref) | copy-start | bytes 73732
  398.2 66.7 %copy-start.16 = (f32[8,128]{1,0:T(8,128)S(1)}, f32[8,128]{1,0:T(8,128)}, u32[]{:S(2)}) copy-start(f32[8,128]{1,0:T(8,128)} %get-tuple-element.106.head_ref) | copy-start | bytes 12292
  465.0 21.0 %copy-start.32 = (f32[24,8]{0,1:T(8,128)S(1)}, f32[24,8]{0,1:T(8,128)}, u32[]{:S(2)}) copy-start(f32[24,8]{0,1:T(8,128)} %param.44) | copy-start | bytes 2308
  465.0 21.0 %copy-start.36 = (f32[24,8]{0,1:T(8,128)S(1)}, f32[24,8]{0,1:T(8,128)}, u32[]{:S(2)}) copy-start(f32[24,8]{0,1:T(8,128)} %param.47) | copy-start | bytes 2308
  465.0 21.0 %copy-start.37 = (f32[24,8]{0,1:T(8,128)S(1)}, f32[24,8]{0,1:T(8,128)}, u32[]{:S(2)}) copy-start(f32[24,8]{0,1:T(8,128)} %param.45) | copy-start | bytes 2308
  465.0 21.0 %copy-start.38 = (f32[24,8]{0,1:T(8,128)S(1)}, f32[24,8]{0,1:T(8,128)}, u32[]{:S(2)}) copy-start(f32[24,8]{0,1:T(8,128)} %param.46) | copy-start | bytes 2308
  465.1 22.2 %copy-start.1 = (f32[5,24,768]{2,1,0:T(8,128)S(1)}, f32[5,24,768]{2,1,0:T(8,128)}, u32[]{:S(2)}) copy-start(f32[5,24,768]{2,1,0:T(8,128)} %dense_ref.1) | copy-start | bytes 1105924
  465.1 22.2 %copy-start.28 = (f32[5,24,768]{2,1,0:T(8,128)S(1)}, f32[5,24,768]{2,1,0:T(8,128)}, u32[]{:S(2)}) copy-start(f32[5,24,768]{2,1,0:T(8,128)} %param.43) | copy-start | bytes 1105924
  465.1 22.2 %copy-start.29 = (f32[5,24,768]{2,1,0:T(8,128)S(1)}, f32[5,24,768]{2,1,0:T(8,128)}, u32[]{:S(2)}) copy-start(f32[5,24,768]{2,1,0:T(8,128)} %param.41) | copy-start | bytes 1105924
  465.1 22.2 %copy-start.30 = (f32[5,24,768]{2,1,0:T(8,128)S(1)}, f32[5,24,768]{2,1,0:T(8,128)}, u32[]{:S(2)}) copy-start(f32[5,24,768]{2,1,0:T(8,128)} %param.42) | copy-start | bytes 1105924
  (27 other events, 154.7 us)

commit v7 on v6

--- a/solution.py
+++ b/solution.py
@@ -354,7 +354,7 @@
         ]
         + [by_z, by_z, by_x, by_x, by_y, by_y, by_y, by_y, by_x, by_x, by_z, by_z],
         compiler_params=pltpu.CompilerParams(
-            collective_id=2, has_side_effects=True, vmem_limit_bytes=48 * MIB
+            collective_id=2, has_side_effects=True, vmem_limit_bytes=28 * MIB
         ),
         cost_estimate=cost(45),
         name="scatter_dense",
@@ -427,14 +427,13 @@
             dma((devices,)),
         ],
         compiler_params=pltpu.CompilerParams(
-            collective_id=3, has_side_effects=True, vmem_limit_bytes=48 * MIB
+            collective_id=3, has_side_effects=True, vmem_limit_bytes=20 * MIB
         ),
         cost_estimate=cost(10),
         name="finish",
     )(head_sums, dense_sums, importance, *parts)
 
 
-EARLY = 0
 IMAGE_PAD = 16
 
 
@@ -668,11 +667,6 @@
     return result
 
 
-def lane_mask(shape, left):
-    lane = lax.broadcasted_iota(jnp.int32, shape, 1)
-    return lane < 64 if left else lane >= 64
-
-
 def allowed_slots(lengths, row, images, valid_row, span):
     query = lax.broadcasted_iota(jnp.int32, (span, span), 0)
     key = lax.broadcasted_iota(jnp.int32, (span, span), 1)
@@ -685,115 +679,174 @@
     return (query_seg == key_seg) & ((valid_row > 0) | (query == key))
 
 
-def dense_forward_kernel(
-    n_experts, images, length_ref, mask_ref, patch_ref, w_ref, gain_ref, router_ref, col_ref,
-    x_zero_ref, a_one_ref, qkv_ref, att_ref, x_one_ref, a_two_ref, prob_ref, lse_ref, pool_ref, imp_ref
+TILE = 32
+
+
+def tiles(count):
+    return [slice(start, min(start + TILE, count)) for start in range(0, count, TILE)]
+
+
+class Team:
+    def __init__(self, at):
+        self.at, self.span = at, 2 * at.G
+        self.spot = at.g * QUAD + at.r
+
+    def target(self, step):
+        at = self.at
+        chosen = lax.rem(self.spot + step, self.span)
+        block, index = lax.div(chosen, 2), lax.rem(chosen, 2)
+        core = lax.div(self.spot, self.span)
+        r = 2 * at.c + index
+        own = (block == at.g) & (r == at.r) & (core == at.c)
+        return {"g": block, "r": r, "x": at.x, "c": core}, index, own
+
+    def source(self, step):
+        at = self.at
+        chosen = at.g * 2 + lax.rem(at.r, 2)
+        spot = at.c * self.span + lax.rem(chosen - step + self.span, self.span)
+        device = {"g": lax.div(spot, QUAD), "r": lax.rem(spot, QUAD), "x": at.x, "c": lax.div(at.r, 2)}
+        return device, lax.rem(at.r, 2)
+
+    def peers(self):
+        at = self.at
+        count = 2 * at.G * QUAD
+        me = self.spot * 2 + at.c
+        line = []
+        for device in others(me, count):
+            spot = lax.div(device, 2)
+            line.append(
+                {"g": lax.div(spot, QUAD), "r": lax.rem(spot, QUAD), "x": at.x, "c": lax.rem(device, 2)}
+            )
+        for x in others(at.x, at.X):
+            line += [{"g": at.g, "r": r, "x": x, "c": at.c} for r in range(QUAD)]
+        return line
+
+
+def image_hot(detail, padded):
+    image = detail[2:3, :padded]
+    line = lax.broadcasted_iota(jnp.int32, (IMAGE_PAD, padded), 0).astype(jnp.float32)
+    return line == image
+
+
+def forward_kernel(
+    sizes, n_experts, images, padded,
+    length_ref, mask_ref, patch_ref, w_ref, gain_ref, router_ref, col_ref, shard_ref,
+    x_zero_out, a_one_out, qkv_out, att_out, x_one_out, a_two_out, prob_ref, lse_ref, pool_ref, imp_ref,
+    rows_out, detail_out, act_out, slope_out, y_out, part_ref, weight_out,
+    x_zero_buf, a_one_buf, qkv_buf, att_buf, x_one_buf, a_two_ref, weights, send_rows, send_detail, places,
+    rows_in, detail_in, total, act_buf, slope_buf, dense_sem, keep_sem, own_sem,
+    w_out, w_in, s_out, s_in, r_out, r_in, m_out, m_in, act_sem, slope_sem
 ):
-    row = pl.program_id(0)
-    span, width = patch_ref.shape
-    x_zero = dot_f32(patch_ref[...], w_ref[0], NN)
-    x_zero_ref[...] = x_zero
-    a_one = (norm_parts(x_zero)[0] * gain_ref[0:1] + gain_ref[3:4]).astype(jnp.bfloat16)
-    a_one_ref[...] = a_one
-    for part in range(3):
-        qkv_ref[:, part * width : (part + 1) * width] = dot_f32(a_one, w_ref[1 + part], NN).astype(
-            jnp.bfloat16
+    at = Place(sizes)
+    team = Team(at)
+    half = weights.shape[1]
+    span, width = mask_ref.shape[2], patch_ref.shape[1]
+    rows_here = mask_ref.shape[0]
+    tokens = rows_here * span
+    greet(team.peers())
+
+    def shard_copy(step):
+        device, index, own = team.target(step)
+        return send(
+            shard_ref.at[index], weights.at[0, step], w_out.at[step], w_in.at[step], device
         )
-    open_to = allowed_slots(length_ref, row, images, mask_ref[0], span)
-    lane = lax.broadcasted_iota(jnp.int32, (span, 128), 1)
-    logs = jnp.zeros((span, 128), jnp.float32)
-    for pair in range(width // 128):
-        query, key, value = (
-            qkv_ref[:, part * width + pair * 128 : part * width + (pair + 1) * 128]
-            for part in range(3)
-        )
-        outs = []
-        for side in range(2):
-            held = jnp.where((lane < 64) == (side == 0), query, jnp.zeros_like(query))
-            scores = jnp.where(open_to, dot_f32(held, key, NT) * 64**-0.5, mask_fill)
-            top = jnp.max(scores, 1, keepdims=True)
-            powers = jnp.exp(scores - top)
-            total = jnp.sum(powers, 1, keepdims=True)
-            probs = (powers * (1.0 / total)).astype(jnp.bfloat16)
-            outs.append(dot_f32(probs, value, NN))
-            logs = jnp.where(lane == 2 * pair + side, top + jnp.log(total), logs)
-        att_ref[:, pair * 128 : (pair + 1) * 128] = jnp.where(lane < 64, outs[0], outs[1]).astype(
-            jnp.bfloat16
-        )
-    lse_ref[...] = logs
-    x_one = x_zero + dot_f32(att_ref[...], w_ref[4], NN)
-    x_one_ref[...] = x_one
-    a_two = (norm_parts(x_one)[0] * gain_ref[1:2] + gain_ref[4:5]).astype(jnp.bfloat16)
-    a_two_ref[...] = a_two
+
+    def shard_own(step):
+        device, index, own = team.target(step)
+        return pltpu.make_async_copy(shard_ref.at[index], weights.at[0, step], w_in.at[step])
+
+    for step in range(half):
+        own = team.target(step)[2]
+
+        @pl.when(own)
+        def _():
+            shard_own(step).start()
+
+        @pl.when(jnp.logical_not(own))
+        def _():
+            shard_copy(step).start()
+
+    dense = (
+        (x_zero_buf, x_zero_out), (a_one_buf, a_one_out), (qkv_buf, qkv_out), (att_buf, att_out), (x_one_buf, x_one_out),
+    )
+
+    def dense_copies(row):
+        slot = lax.rem(row, 2)
+        here = pl.ds(pl.multiple_of(row * span, 16), span)
+        return [
+            pltpu.make_async_copy(buf.at[slot], out.at[here], dense_sem.at[index, slot])
+            for index, (buf, out) in enumerate(dense)
+        ]
+
+    pool_ref[...] = jnp.zeros_like(pool_ref)
+    imp_ref[...] = jnp.zeros_like(imp_ref)
     routers = router_ref[...].astype(jnp.bfloat16)
     if routers.shape[0] < 128:
         routers = jnp.concatenate(
             [routers, jnp.zeros((128 - routers.shape[0], width), jnp.bfloat16)], 0
         )
-    logits = jnp.where(lane < n_experts, dot_f32(a_two, routers, NT), mask_fill)
-    powers = jnp.exp(logits - jnp.max(logits, 1, keepdims=True))
-    probs = powers / jnp.sum(powers, 1, keepdims=True)
-    prob_ref[...] = probs
-
-    @pl.when(row == 0)
-    def _():
-        pool_ref[...] = jnp.zeros_like(pool_ref)
-        imp_ref[...] = jnp.zeros_like(imp_ref)
-
-    valid, pool, image = col_ref[:, 2:3], col_ref[:, 3:4], col_ref[:, 4:5]
-    imp_ref[0:1, 0:128] += jnp.sum(probs * valid, 0, keepdims=True)
-    line = lax.broadcasted_iota(jnp.int32, pool_ref.shape, 0)
-    for index in range(images):
-        number = row * images + index
-        weight = jnp.where(image == number.astype(jnp.float32), pool, 0.0)
-        pooled = jnp.sum(x_one * weight, 0, keepdims=True)
-        pool_ref[...] = jnp.where(line == number, pooled, pool_ref[...])
-
-
-def dense_forward(n_experts, lengths, slot_mask, patches, weights, gains, routers, columns):
-    rows_here, span = slot_mask.shape
-    tokens, width = patches.shape
-    f32, half = jnp.float32, jnp.bfloat16
-
-    def block(wide):
-        return pl.BlockSpec((span, wide), lambda i: (i, 0))
-
-    def out(wide, kind):
-        return jax.ShapeDtypeStruct((tokens, wide), kind)
-
-    def fixed(shape):
-        return pl.BlockSpec(shape, lambda i: (0, 0))
-
-    return pl.pallas_call(
-        functools.partial(dense_forward_kernel, n_experts, lengths.shape[1]),
-        grid=(rows_here,),
-        out_shape=(
-            out(width, f32), out(width, half), out(3 * width, half), out(width, half),
-            out(width, f32), out(width, half), out(128, f32), out(128, f32),
-            jax.ShapeDtypeStruct((IMAGE_PAD, width), f32), jax.ShapeDtypeStruct((8, width), f32),
-        ),
-        in_specs=[
-            whole(pltpu.SMEM), pl.BlockSpec((1, 1, span), lambda i: (i, 0, 0)), block(width),
-            whole(), whole(), whole(), block(128),
-        ],
-        out_specs=(
-            block(width), block(width), block(3 * width), block(width), block(width), block(width),
-            block(128), block(128), fixed((IMAGE_PAD, width)), fixed((8, width)),
-        ),
-        compiler_params=pltpu.CompilerParams(vmem_limit_bytes=48 * MIB),
-        cost_estimate=cost(25),
-        name="dense_forward",
-    )(lengths, slot_mask[:, None, :], patches, weights, gains, routers, columns)
-
-
-def dispatch_kernel(
-    sizes, n_experts, padded, a_two_ref, prob_ref, col_ref, rows_ref, detail_ref,
-    send_rows, send_detail, places, own_sem, r_out, r_in, m_out, m_in
-):
-    at = Place(sizes)
-    tokens = a_two_ref.shape[0]
-    team = others(at.member, n_experts)
-    greet([at.of_member(member) for member in team])
+    lane = lax.broadcasted_iota(jnp.int32, (span, 128), 1)
+
+    def dense_row(row, carry):
+        @pl.when(row >= 2)
+        def _():
+            for copy in dense_copies(row - 2):
+                copy.wait()
+
+        slot = lax.rem(row, 2)
+        here = pl.ds(pl.multiple_of(row * span, 16), span)
+        x_zero = dot_f32(patch_ref[here], w_ref[0], NN)
+        x_zero_buf[slot] = x_zero
+        a_one = (norm_parts(x_zero)[0] * gain_ref[0:1] + gain_ref[3:4]).astype(jnp.bfloat16)
+        a_one_buf[slot] = a_one
+        for part in range(3):
+            qkv_buf[slot, :, part * width : (part + 1) * width] = dot_f32(
+                a_one, w_ref[1 + part], NN
+            ).astype(jnp.bfloat16)
+        open_to = allowed_slots(length_ref, row, images, mask_ref[row], span)
+        logs = jnp.zeros((span, 128), jnp.float32)
+        for pair in range(width // 128):
+            query, key, value = (
+                qkv_buf[slot, :, part * width + pair * 128 : part * width + (pair + 1) * 128]
+                for part in range(3)
+            )
+            outs = []
+            for side in range(2):
+                held = jnp.where((lane < 64) == (side == 0), query, jnp.zeros_like(query))
+                scores = jnp.where(open_to, dot_f32(held, key, NT) * 64**-0.5, mask_fill)
+                top = jnp.max(scores, 1, keepdims=True)
+                powers = jnp.exp(scores - top)
+                whole_sum = jnp.sum(powers, 1, keepdims=True)
+                probs = (powers * (1.0 / whole_sum)).astype(jnp.bfloat16)
+                outs.append(dot_f32(probs, value, NN))
+                logs = jnp.where(lane == 2 * pair + side, top + jnp.log(whole_sum), logs)
+            att_buf[slot, :, pair * 128 : (pair + 1) * 128] = jnp.where(
+                lane < 64, outs[0], outs[1]
+            ).astype(jnp.bfloat16)
+        lse_ref[here] = logs
+        x_one = x_zero + dot_f32(att_buf[slot], w_ref[4], NN)
+        x_one_buf[slot] = x_one
+        a_two = (norm_parts(x_one)[0] * gain_ref[1:2] + gain_ref[4:5]).astype(jnp.bfloat16)
+        a_two_ref[here] = a_two
+        logits = jnp.where(lane < n_experts, dot_f32(a_two, routers, NT), mask_fill)
+        powers = jnp.exp(logits - jnp.max(logits, 1, keepdims=True))
+        probs = powers / jnp.sum(powers, 1, keepdims=True)
+        prob_ref[here] = probs
+        columns = col_ref[here]
+        valid, pool, image = columns[:, 2:3], columns[:, 3:4], columns[:, 4:5]
+        imp_ref[0:1, 0:128] += jnp.sum(probs * valid, 0, keepdims=True)
+        line = lax.broadcasted_iota(jnp.int32, pool_ref.shape, 0)
+        for index in range(images):
+            number = row * images + index
+            weight = jnp.where(image == number.astype(jnp.float32), pool, 0.0)
+            pooled = jnp.sum(x_one * weight, 0, keepdims=True)
+            pool_ref[...] = jnp.where(line == number, pooled, pool_ref[...])
+        for copy in dense_copies(row):
+            copy.start()
+        return carry
+
+    lax.fori_loop(0, rows_here, dense_row, 0)
+
     columns = col_ref[...]
     places[...] = columns.T[:8]
     lane = lax.broadcasted_iota(jnp.int32, (tokens, 128), 1)
@@ -817,9 +870,9 @@
     n = n_experts
     gates = details[0:n] + details[n : 2 * n] + details[2 * n : 3 * n]
     pools = details[3 * n : 4 * n] + details[4 * n : 5 * n] + details[5 * n : 6 * n]
-    images = details[6 * n : 7 * n]
+    numbers = details[6 * n : 7 * n]
     for index in range(n):
-        for spot, value in enumerate((gates, pools, images)):
+        for spot, value in enumerate((gates, pools, numbers)):
             send_detail[index, spot : spot + 1] = value[index : index + 1]
         send_detail[index, 3:8] = jnp.zeros((5, send_detail.shape[2]), jnp.float32)
 
@@ -828,211 +881,222 @@
         slots = slots.astype(jnp.float32)
         match = (slots == places[0:1]) | (slots == places[1:2])
         match = jnp.where(match, 1.0, 0.0).astype(jnp.bfloat16)
-        send_rows[member] = dot_f32(match, a_two_ref[...], NN).astype(jnp.bfloat16)
+        return dot_f32(match, a_two_ref[...], NN).astype(jnp.bfloat16)
 
     def row_copy(member, source):
         return send(
-            send_rows.at[member], rows_ref.at[source], r_out.at[member], r_in.at[source], at.of_member(member)
+            send_rows.at[member], rows_in.at[source], r_out.at[member], r_in.at[source], at.of_member(member)
         )
 
     def detail_copy(member, source):
         return send(
-            send_detail.at[member], detail_ref.at[source], m_out.at[member], m_in.at[source], at.of_member(member)
+            send_detail.at[member], detail_in.at[source], m_out.at[member], m_in.at[source], at.of_member(member)
         )
 
-    def step(index, carry):
+    def dispatch_step(index, carry):
         member = lax.rem(at.member + index, n_experts)
-        rows_of(member)
+        send_rows[member] = rows_of(member)
         row_copy(member, at.member).start()
         detail_copy(member, at.member).start()
         return carry
 
-    lax.fori_loop(1, n_experts, step, 0)
-    rows_of(at.member)
-    keep_rows = pltpu.make_async_copy(send_rows.at[at.member], rows_ref.at[at.member], own_sem.at[0])
-    keep_detail = pltpu.make_async_copy(send_detail.at[at.member], detail_ref.at[at.member], own_sem.at[1])
-    keep_rows.start()
-    keep_detail.start()
-    for member in team:
-        row_copy(member, member).wait_recv()
-        detail_copy(member, member).wait_recv()
-    for member in team:
-        row_copy(member, at.member).wait_send()
-        detail_copy(member, at.member).wait_send()
-    keep_rows.wait()
-    keep_detail.wait()
-
-
-def dispatch(sizes, n_experts, padded, a_two, probs, columns):
-    tokens, width = a_two.shape
+    lax.fori_loop(1, n_experts, dispatch_step, 0)
+    rows_in[at.member] = rows_of(at.member)
+    detail_in[at.member] = send_detail[at.member]
+    a_two_copy = pltpu.make_async_copy(a_two_ref, a_two_out, keep_sem.at[0])
+    a_two_copy.start()
+    for row in range(max(rows_here - 2, 0), rows_here):
+        for copy in dense_copies(row):
+            copy.wait()
+
+    def swap_copy(index):
+        return send(
+            weights.at[0, index], weights.at[1, index], s_out.at[index], s_in.at[index], at.sibling()
+        )
+
+    for step in range(half):
+        device, index, own = team.target(step)
+
+        @pl.when(own)
+        def _():
+            shard_own(step).wait()
+
+        @pl.when(jnp.logical_not(own))
+        def _():
+            shard_copy(step).wait_recv()
+
+        swap_copy(step).start()
+
+    many = act_buf.shape[2] // padded
+    count = many * padded
+    rounds = n_experts // many
+    part = act_buf.shape[3]
+
+    def hidden_copies(index):
+        slot, turn = lax.rem(index, 2), lax.div(index, rounds)
+        block = block_of(index)
+        here = pl.ds(pl.multiple_of(block * count, 16), count)
+        there = pl.ds(turn * half, half)
+        return (
+            pltpu.make_async_copy(act_buf.at[slot], act_out.at[there, here], act_sem.at[slot]),
+            pltpu.make_async_copy(slope_buf.at[slot], slope_out.at[there, here], slope_sem.at[slot]),
+        )
+
+    def block_of(index):
+        return lax.rem(lax.div(at.member, many) + index, rounds)
+
+    def expert_step(index, carry):
+        slot, turn = lax.rem(index, 2), lax.div(index, rounds)
+        block = block_of(index)
+
+        @pl.when(turn == 0)
+        def _():
+            for spot in range(many):
+                source = block * many + spot
+
+                @pl.when(source != at.member)
+                def _():
+                    row_copy(source, source).wait_recv()
+                    detail_copy(source, source).wait_recv()
+
+        @pl.when(index == rounds)
+        def _():
+            for step in range(half):
+                swap_copy(step).wait_recv()
+
+        @pl.when(index >= 2)
+        def _():
+            for copy in hidden_copies(index - 2):
+                copy.wait()
+
+        rows = rows_in[pl.ds(block * many, many)].reshape(count, width)
+        for chunk in range(half):
+            hidden_all = dot_f32(rows, weights[turn, chunk, 0], NT)
+            for spot in tiles(count):
+                hidden = hidden_all[spot]
+                square = hidden * hidden
+                curve = jnp.tanh(hidden * (0.7978845608 + 0.7978845608 * 0.044715 * square))
+                upper = 0.5 + 0.5 * curve
+                gelu = hidden * upper
+                slope = upper + gelu * (1.0 - upper) * (
+                    2.0 * 0.7978845608 + 6.0 * 0.7978845608 * 0.044715 * square
+                )
+                act_buf[slot, chunk, spot] = gelu.astype(jnp.bfloat16)
+                slope_buf[slot, chunk, spot] = slope.astype(jnp.bfloat16)
+        for copy in hidden_copies(index):
+            copy.start()
+        acts = jnp.concatenate([act_buf[slot, chunk] for chunk in range(half)], 1)
+        ends = jnp.concatenate([weights[turn, chunk, 1] for chunk in range(half)], 0)
+        found = dot_f32(acts, ends, NN)
+        here = pl.ds(pl.multiple_of(block * count, 16), count)
+
+        @pl.when(turn == 0)
+        def _():
+            total[here] = found
+
+        @pl.when(turn == 1)
+        def _():
+            result = (total[here] + found).astype(jnp.bfloat16)
+            for spot in range(many):
+                source = block * many + spot
+                mine = result[spot * padded : (spot + 1) * padded]
+                send_rows[source] = mine
+                detail = detail_in[source]
+                weight = detail[0:1, :padded] * detail[1:2, :padded]
+                shares = jnp.where(image_hot(detail, padded), weight, 0.0)
+                pieces = jnp.concatenate(split_three(shares), 0)
+                sums = dot_f32(pieces, mine, NN)
+                part_ref[source] = (
+                    sums[:IMAGE_PAD] + sums[IMAGE_PAD : 2 * IMAGE_PAD] + sums[2 * IMAGE_PAD :]
+                )
+
+        @pl.when(index == rounds - 1)
+        def _():
+            for member in others(at.member, n_experts):
+                row_copy(member, at.member).wait_send()
+                detail_copy(member, at.member).wait_send()
+
+        return carry
+
+    lax.fori_loop(0, 2 * rounds, expert_step, 0)
+    keeps = [
+        pltpu.make_async_copy(rows_in, rows_out, keep_sem.at[1]),
+        pltpu.make_async_copy(detail_in, detail_out, keep_sem.at[2]),
+        pltpu.make_async_copy(send_rows, y_out, keep_sem.at[3]),
+        pltpu.make_async_copy(weights, weight_out, keep_sem.at[4]),
+    ]
+    for copy in keeps:
+        copy.start()
+    for index in range(2 * rounds - 2, 2 * rounds):
+        for copy in hidden_copies(index):
+            copy.wait()
+    for step in range(half):
+        own = team.target(step)[2]
+        swap_copy(step).wait_send()
+
+        @pl.when(jnp.logical_not(own))
+        def _():
+            shard_copy(step).wait_send()
+
+    a_two_copy.wait()
+    for copy in keeps:
+        copy.wait()
+
+
+def forward(sizes, n_experts, padded, lengths, slot_mask, patches, weights, gains, routers, columns, shards):
+    rows_here, span = slot_mask.shape
+    tokens, width = patches.shape
+    part = shards.shape[2]
+    half = 2 * sizes["g"]
     lanes = round_up(padded, 128)
+    many = max(1, 576 // padded)
+    count = n_experts * padded
+    f32, kind = jnp.float32, jnp.bfloat16
     dma = pltpu.SemaphoreType.DMA
-    each = dma((n_experts,))
+    each, parts, two = dma((n_experts,)), dma((half,)), dma((2,))
+
+    def out(wide, dtype):
+        return jax.ShapeDtypeStruct((tokens, wide), dtype)
+
+    hidden = jax.ShapeDtypeStruct((2 * half, count, part), kind)
+    rows = (n_experts, padded, width)
     return pl.pallas_call(
-        functools.partial(dispatch_kernel, sizes, n_experts, padded),
+        functools.partial(forward_kernel, sizes, n_experts, lengths.shape[1], padded),
         out_shape=(
-            jax.ShapeDtypeStruct((n_experts, padded, width), jnp.bfloat16),
-            jax.ShapeDtypeStruct((n_experts, 8, lanes), jnp.float32),
+            out(width, f32), out(width, kind), out(3 * width, kind), out(width, kind), out(width, f32),
+            out(width, kind), out(128, f32), out(128, f32),
+            jax.ShapeDtypeStruct((IMAGE_PAD, width), f32), jax.ShapeDtypeStruct((8, width), f32),
+            jax.ShapeDtypeStruct(rows, kind), jax.ShapeDtypeStruct((n_experts, 8, lanes), f32),
+            hidden, hidden, jax.ShapeDtypeStruct(rows, kind),
+            jax.ShapeDtypeStruct((n_experts, IMAGE_PAD, width), f32),
+            jax.ShapeDtypeStruct((2, half, 2, part, width), kind),
         ),
-        in_specs=[whole()] * 3,
-        out_specs=(whole(ANY), whole(ANY)),
+        in_specs=[whole(pltpu.SMEM)] + [whole()] * 6 + [whole(ANY)],
+        out_specs=(whole(ANY),) * 6 + (whole(),) * 4 + (whole(ANY),) * 5 + (whole(), whole(ANY)),
         scratch_shapes=[
-            VMEM((n_experts, padded, width), jnp.bfloat16),
-            VMEM((n_experts, 8, lanes), jnp.float32),
-            VMEM((8, tokens), jnp.float32),
-            dma((2,)), each, each, each, each,
+            VMEM((2, span, width), f32), VMEM((2, span, width), kind), VMEM((2, span, 3 * width), kind),
+            VMEM((2, span, width), kind), VMEM((2, span, width), f32), VMEM((tokens, width), kind),
+            VMEM((2, half, 2, part, width), kind), VMEM(rows, kind), VMEM((n_experts, 8, lanes), f32),
+            VMEM((8, tokens), f32), VMEM(rows, kind), VMEM((n_experts, 8, lanes), f32),
+            VMEM((count, width), f32), VMEM((2, half, many * padded, part), kind),
+            VMEM((2, half, many * padded, part), kind), dma((5, 2)), dma((5,)), two,
+            parts, parts, parts, parts, each, each, each, each, two, two,
         ],
         compiler_params=pltpu.CompilerParams(
-            collective_id=5, has_side_effects=True, vmem_limit_bytes=48 * MIB
+            collective_id=5, has_side_effects=True, vmem_limit_bytes=60 * MIB
         ),
-        cost_estimate=cost(50),
-        name="dispatch",
-    )(a_two, probs, columns)
-
-
-def image_hot(detail, padded):
-    image = detail[2:3, :padded]
-    line = lax.broadcasted_iota(jnp.int32, (IMAGE_PAD, padded), 0).astype(jnp.float32)
-    return line == image
-
-
-TILE = 32
-
-
-def tiles(count):
-    return [slice(start, min(start + TILE, count)) for start in range(0, count, TILE)]
-
-
-def expert_forward_kernel(sizes, padded, rows_ref, detail_ref, *refs):
-    at = Place(sizes)
-    half = len(refs) - 11
-    chunks = refs[:half]
-    act_ref, slope_ref, y_ref, part_ref, other_ref = refs[half : half + 5]
-    weights, total, own_sem, s_out, s_in, keep_sem = refs[half + 5 :]
-    many, unused, width = rows_ref.shape
-    count = many * padded
-    turn, block = pl.program_id(0), pl.program_id(1)
-
-    def own_copy(index):
-        return pltpu.make_async_copy(chunks[index], weights.at[0, index], own_sem.at[index])
-
-    def swap_copy(index):
-        return send(
-            chunks[index], weights.at[1, index], s_out.at[index], s_in.at[index], at.sibling()
-        )
-
-    def keep_copy():
-        return pltpu.make_async_copy(weights.at[1], other_ref, keep_sem.at[0])
-
-    @pl.when((turn == 0) & (block == 0))
-    def _():
-        for index in range(half):
-            own_copy(index).start()
-        greet([at.sibling()])
-        for index in range(half):
-            swap_copy(index).start()
-        for index in range(half):
-            own_copy(index).wait()
-
-    @pl.when((turn == 1) & (block == 0))
-    def _():
-        for index in range(half):
-            swap_copy(index).wait_recv()
-        keep_copy().start()
-
-    rows = rows_ref[...].reshape(count, width)
-    for index in range(half):
-        hidden_all = dot_f32(rows, weights[turn, index, 0], NT)
-        for spot in tiles(count):
-            hidden = hidden_all[spot]
-            square = hidden * hidden
-            curve = jnp.tanh(hidden * (0.7978845608 + 0.7978845608 * 0.044715 * square))
-            upper = 0.5 + 0.5 * curve
-            gelu = hidden * upper
-            slope = upper + gelu * (1.0 - upper) * (
-                2.0 * 0.7978845608 + 6.0 * 0.7978845608 * 0.044715 * square
-            )
-            act_ref[index, spot] = gelu.astype(jnp.bfloat16)
-            slope_ref[index, spot] = slope.astype(jnp.bfloat16)
-    acts = jnp.concatenate([act_ref[index] for index in range(half)], 1)
-    ends = jnp.concatenate([weights[turn, index, 1] for index in range(half)], 0)
-    found = dot_f32(acts, ends, NN)
-    span = pl.ds(pl.multiple_of(block * count, 16), count)
-
-    @pl.when(turn == 0)
-    def _():
-        total[span] = found
-
-    @pl.when(turn == 1)
-    def _():
-        result = (total[span] + found).astype(jnp.bfloat16)
-        y_ref[...] = result.reshape(many, padded, width)
-        for source in range(many):
-            detail = detail_ref[source]
-            weight = detail[0:1, :padded] * detail[1:2, :padded]
-            shares = jnp.where(image_hot(detail, padded), weight, 0.0)
-            pieces = jnp.concatenate(split_three(shares), 0)
-            sums = dot_f32(pieces, result[source * padded : (source + 1) * padded], NN)
-            part_ref[source] = (
-                sums[:IMAGE_PAD] + sums[IMAGE_PAD : 2 * IMAGE_PAD] + sums[2 * IMAGE_PAD :]
-            )
-
-    @pl.when((turn == 1) & (block == pl.num_programs(1) - 1))
-    def _():
-        for index in range(half):
-            swap_copy(index).wait_send()
-        keep_copy().wait()
-
-
-def expert_forward(sizes, rows, details, chunks):
-    sources, padded, width = rows.shape
-    half = len(chunks)
-    part = chunks[0].shape[1]
-    many = max(1, 576 // padded)
-    lanes = details.shape[2]
-    kind = jnp.bfloat16
-    dma = pltpu.SemaphoreType.DMA
-
-    def by_source(*shape):
-        return pl.BlockSpec((many, *shape), lambda t, i: (i, 0, 0))
-
-    def late(*shape):
-        return pl.BlockSpec((many, *shape), lambda t, i: (i * t, 0, 0))
-
-    flat = pl.BlockSpec((half, many * padded, part), lambda t, i: (t, i, 0))
-    return pl.pallas_call(
-        functools.partial(expert_forward_kernel, sizes, padded),
-        grid=(2, sources // many),
-        out_shape=(
-            jax.ShapeDtypeStruct((2 * half, sources * padded, part), kind),
-            jax.ShapeDtypeStruct((2 * half, sources * padded, part), kind),
-            jax.ShapeDtypeStruct((sources, padded, width), kind),
-            jax.ShapeDtypeStruct((sources, IMAGE_PAD, width), jnp.float32),
-            jax.ShapeDtypeStruct((half, 2, part, width), kind),
-        ),
-        in_specs=[by_source(padded, width), by_source(8, lanes)] + [whole(ANY)] * half,
-        out_specs=(flat, flat, late(padded, width), late(IMAGE_PAD, width), whole(ANY)),
-        scratch_shapes=[
-            VMEM((2, half, 2, part, width), kind),
-            VMEM((sources * padded, width), jnp.float32),
-            dma((half,)), dma((half,)), dma((half,)), dma((1,)),
-        ],
-        compiler_params=pltpu.CompilerParams(
-            collective_id=7, has_side_effects=True, vmem_limit_bytes=56 * MIB
-        ),
-        cost_estimate=cost(40),
-        name="expert_forward",
-    )(rows, details, *chunks)
+        cost_estimate=cost(120),
+        name="forward",
+    )(lengths, slot_mask[:, None, :], patches, weights, gains, routers, columns, shards)
 
 
 def expert_backward_kernel(
-    sizes, padded, rows_ref, detail_ref, pool_ref, y_ref, slope_ref, act_ref, other_ref, *refs
+    sizes, padded, rows_ref, detail_ref, pool_ref, y_ref, slope_ref, act_ref, weight_ref, *refs
 ):
     at = Place(sizes)
     sources, unused, width = rows_ref.shape
     chunks, unused, part = slope_ref.shape
     half = chunks // 2
-    own_refs, refs = refs[:half], refs[half:]
     back_ref, gate_ref, *outs = refs[: 2 + half]
     d_hidden, d_rows, send_rows, send_gate, send_grad, got_grad = refs[2 + half : 8 + half]
     own_sem, r_out, r_in, m_out, m_in, g_out, g_in, g_keep = refs[8 + half :]
@@ -1095,7 +1159,7 @@
         d_rows[span] = d_out
 
         def weight(index, which):
-            return own_refs[index][which] if index < half else other_ref[index - half, which]
+            return weight_ref[index // half, index % half, which]
 
         for index in range(chunks):
             d_act = dot_f32(d_out, weight(index, 1), NT)
@@ -1164,7 +1228,7 @@
             out_copy(spot).wait()
 
 
-def expert_backward(sizes, rows, details, pools, results, slopes, acts, chunks_own, other):
+def expert_backward(sizes, rows, details, pools, results, slopes, acts, weights):
     sources, padded, width = rows.shape
     chunks, count, part = acts.shape
     many = max(1, (288 if part % 128 else 576) // padded)
@@ -1195,7 +1259,7 @@
             pl.BlockSpec((chunks, many * padded, part), lambda i: (0, block_of(i), 0)),
             pl.BlockSpec((1, count, part), lambda i: (chunk_of(i), 0, 0)),
         ]
-        + [whole()] * (1 + half),
+        + [whole()],
         out_specs=(whole(ANY),) * (2 + half),
         scratch_shapes=[
             VMEM((chunks, count, part), kind),
@@ -1211,7 +1275,7 @@
         ),
         cost_estimate=cost(65),
         name="expert_backward",
-    )(rows, details, pools, results, slopes, acts, other, *chunks_own)
+    )(rows, details, pools, results, slopes, acts, weights)
 
 
 def dense_backward_kernel(
@@ -1403,18 +1467,6 @@
     return moves
 
 
-def order_shards(expert_in, expert_out):
-    place = lax.axis_index("g") * QUAD + lax.axis_index("r")
-    odd = lax.rem(place, 2) == 1
-    both = jnp.stack([expert_in, expert_out], 1).astype(jnp.bfloat16)
-    return [jnp.where(odd, both[1], both[0]), jnp.where(odd, both[0], both[1])]
-
-
-def fetch_experts(shards, n_blocks, steps):
-    moves = shard_moves(n_blocks)
-    return [lax.ppermute(shards[step % 2], ("g", "r", "c"), moves[step]) for step in steps]
-
-
 def return_experts(parts, n_blocks):
     return [
         lax.ppermute(part, ("g", "r", "c"), [(dst, src) for src, dst in pairs])
@@ -1466,8 +1518,6 @@
     n_images = lengths.shape[0] * lengths.shape[1]
     capacity = (21 * tokens * TOP + 20 * n_experts - 1) // (20 * n_experts)
     padded = round_up(capacity, 16)
-    shards = order_shards(expert_in, expert_out)
-    own_chunks = fetch_experts(shards, n_blocks, range(EARLY))
     layer_b, gain_rows, router_t, columns = gather_weights(
         sizes,
         (lengths.shape[1], n_experts, capacity, padded),
@@ -1478,16 +1528,12 @@
         slot_mask,
         lengths,
     )
-    shards, layer_b = lax.optimization_barrier((shards, layer_b))
-    own_chunks += fetch_experts(shards, n_blocks, range(EARLY, 2 * n_blocks))
-    x_zero, a_one, qkv, att_out, x_one, a_two, router_probs, logs, pooled, part_importance = (
-        dense_forward(
-            n_experts, lengths, slot_mask, patches, layer_b, gain_rows, router_t, columns
-        )
-    )
-    arrived, details = dispatch(sizes, n_experts, padded, a_two, router_probs, columns)
-    activated, slope, result, part_pooled, other_chunks = expert_forward(
-        sizes, arrived, details, own_chunks
+    shards = jnp.stack([expert_in, expert_out], 1).astype(jnp.bfloat16)
+    (
+        x_zero, a_one, qkv, att_out, x_one, a_two, router_probs, logs, pooled, part_importance,
+        arrived, details, activated, slope, result, part_pooled, expert_weights
+    ) = forward(
+        sizes, n_experts, padded, lengths, slot_mask, patches, layer_b, gain_rows, router_t, columns, shards
     )
     g_head, d_pooled_all, d_pooled, g_norm_three, head_sums, total_importance = head_step(
         sizes,
@@ -1500,7 +1546,7 @@
         class_labels,
     )
     d_back, back_gate, *grads = expert_backward(
-        sizes, arrived, details, d_pooled_all, result, slope, activated, own_chunks, other_chunks
+        sizes, arrived, details, d_pooled_all, result, slope, activated, expert_weights
     )
     parts = return_experts(grads, n_blocks)
     blocks = dense_backward(

time: 518 us -> 515 us (level)
  starting transfers between devices: 18.5 us -> 9.65 us
  Pallas kernels: 439 us -> 447 us
    ppermute x4 -> x0, starting transfers between devices: 8.96 us -> none  [fetch_experts(): lax.ppermute(shards[step % 2], ('g', 'r', 'c'), moves[step])]
    pallas_call x1, Pallas kernels: 47.2 us -> 55.6 us  [head_step(): pl.pallas_call(functools.partial(head_kernel, sizes, images), out_shape=(...]
    unnamed x87 -> x63, local copies, waits for them, and re-layouts: 11.5 us -> 5.84 us
    pallas_call x3 -> x1, Pallas kernels: 148 us -> 152 us  [forward(): pl.pallas_call(functools.partial(forward_kernel, sizes, n_experts, length...]
  transfers between devices with their start and end apart: 8 -> 4, of which waited for: 1 -> 1; matrix products, arithmetic and copies ran while one was open for 0% -> 0% of each run, Pallas kernels for 41% -> 22%
where the time goes in v7:
time: 515 us; the launch traced here: 506 us
  Pallas kernels  447 us (87%)
  other arithmetic  31.7 us (6%)
  starting transfers between devices  9.65 us (2%)
  local copies, waits for them, and re-layouts  8.95 us (2%)
  waiting for transfers between devices  6.99 us (1%)
    pallas_call x1, Pallas kernels, forward(): pl.pallas_call(functools.partial(forward_kernel, sizes, n_experts, length...  152 us
    pallas_call x1, Pallas kernels, expert_backward(): pl.pallas_call(functools.partial(expert_backward_kernel, sizes, padded),...  66.1 us
    pallas_call x1, Pallas kernels, scatter_dense(): pl.pallas_call(functools.partial(scatter_kernel, sizes), out_shape=(jax.S...  56.4 us
    pallas_call x1, Pallas kernels, dense_backward(): pl.pallas_call(functools.partial(dense_backward_kernel, sizes, n_experts,...  56.2 us
    pallas_call x1, Pallas kernels, head_step(): pl.pallas_call(functools.partial(head_kernel, sizes, images), out_shape=(...  55.6 us
    pallas_call x1, Pallas kernels, gather_weights(): pl.pallas_call(functools.partial(gather_kernel, sizes, rows, mats, routin...  44.7 us
    add x6, other arithmetic, adam_update(): polyak_decay * average_state + (1.0 - polyak_decay) * weight_new  24.7 us
    pallas_call x1, Pallas kernels, finish(): pl.pallas_call(functools.partial(finish_kernel, sizes, n_experts), out_sh...  16 us
  transfers between devices with their start and end apart: 4, of which 1 were waited for; matrix products, arithmetic and copies ran while one was open for 0% of the time, Pallas kernels for 22%

profile of v7, /device:TPU:0, one launch (start us, length us, event | category | flops | bytes accessed | tf_op | source)
XLA Modules:
  0.0 506.3 jit_solution(2921309321002543837)
XLA Ops:
  1.3 1.3 broadcast_in_dim.2.mask_ref
  2.6 0.9 copy.57.pick_ref
  3.5 1.3 select_bitcast_fusion
  5.5 2.6 convert_bitcast_fusion
  8.2 1.6 pad_maximum_fusion.shard_ref
  10.0 44.7 %gather_weights.1 = (bf16[5,768,768]{2,1,0:T(8,128)(2,1)}, f32[8,768]{1,0:T(8,128)S(1)}, f32[8,768]{1,0:T(8,128)S(1)}, f32[1024,128]{1,0:T(8,128)S(1)}) custom-call(f32[5,24,768]{2,1,0:T(8,128)S(1)} %copy-done, f32[8,768]{1,0:T(8,128)S(1)} %scatter.9.tail_ref, s32[1024,2]{1,0:T(8,128)S(1)} %copy.57.pick_ref, s32[1,1024]{1,0:T(1,128)S(1)} %copy-done.3, ...), custom_call_target="tpu_custom_call" | custom-call | flops 50600001536 | tf_op jit(solution)/shard_map/gather_weights/pallas_call | solution.py:232
  56.7 152.5 %forward.1 = (f32[1024,768]{1,0:T(8,128)}, bf16[1024,768]{1,0:T(8,128)(2,1)}, bf16[1024,2304]{1,0:T(8,128)(2,1)}, bf16[1024,768]{1,0:T(8,128)(2,1)}, f32[1024,76...) custom-call(s32[4,3]{1,0:T(4,128)} %length_ref.5, ...), custom_call_target="tpu_custom_call" | custom-call | flops 138000007168 | tf_op jit(solution)/shard_map/forward/pallas_call | solution.py:1063
  209.2 55.6 %head_step.1 = (f32[576,768]{1,0:T(8,128)}, f32[8,16,768]{2,1,0:T(8,128)}, f32[16,768]{1,0:T(8,128)}, f32[8,768]{1,0:T(8,128)}, f32[8,128]{1,0:T(8,128)}, /*index=5*/f32[8,768]{1,0:T(8,128)}) custom-call(f32[8,16,768]{2,1,0:T(8,128)} %get-tuple-element.93.part_ref, f32[16,768]{1,0:T(8,128)} %get-tuple-element.94.own_ref, ...), custom_call_target="tpu_custom_call" | custom-call | flops 48299999232 | tf_op jit(solution)/shard_map/head_step/pallas_call | solution.py:580
  264.8 66.1 %expert_backward.1 = (bf16[8,272,768]{2,1,0:T(8,128)(2,1)}, f32[8,8,384]{2,1,0:T(8,128)}, bf16[2,384,768]{2,1,0:T(8,128)(2,1)}, bf16[2,384,768]{2,1,0:T(8,128)(2...) custom-call(bf16[8,272,768]{2,1,0:T(8,128)(2,1)} %get-tuple-element.105.rows_ref, ...), custom_call_target="tpu_custom_call" | custom-call | flops 74750001152 | tf_op jit(solution)/shard_map/expert_backward/pallas_call | solution.py:1248
  330.9 1.9 collective-permute-start
  332.8 1.4 collective-permute-start.1
  334.3 3.5 collective-permute-start.2
  337.7 2.8 collective-permute-start.3
  340.6 56.2 %dense_backward.1.g_ref = bf16[2,4,2,2,128,768]{5,4,3,2,1,0:T(8,128)(2,1)} custom-call(s32[4,3]{1,0:T(4,128)} %length_ref.5, s32[4,1,256]{2,1,0:T(1,128)} %broadcast_in_dim.2.mask_ref, bf16[1024,768]{1,0:T(8,128)(2,1)} %patch_ref.3, f32[1024,768]{1,0:T(8,128)} %get-tuple-element.97.x_zero_ref, bf16[1024,768]{1,0:T(8,128)(2,1)} %get-tuple-element.98.a_one_ref, ...), custom_call_target="tpu_custom_call" | custom-call | flops 57500000256 | tf_op jit(solution)/shard_map/dense_backward/pallas_call | solution.py:1427
  396.8 2.8 copy-done.6
  399.6 56.4 %scatter_dense.1 = (f32[128,768]{1,0:T(8,128)S(1)}, f32[8,128]{1,0:T(8,128)S(1)}) custom-call(bf16[2,4,2,2,128,768]{5,4,3,2,1,0:T(8,128)(2,1)S(1)} %copy-done.6), custom_call_target="tpu_custom_call" | custom-call | flops 51749998592 | tf_op jit(solution)/shard_map/scatter_dense/pallas_call | solution.py:338
  456.5 7.0 %collective-permute-done.3.refs_3_ = bf16[2,384,768]{2,1,0:T(8,128)(2,1)} collective-permute-done((bf16[2,384,768]{2,1,0:T(8,128)(2,1)}, bf16[2,384,768]{2,1,0:T(8,128)(2,1)}, u32[]{:S(2)}, u32[]{:S(2)}) %collective-permute-start.3) | collective-permute-done | bytes 1179680 | tf_op jit(solution)/shard_map/ppermute | solution.py:1472
  463.7 16.0 %finish.1 = (f32[2,384,768]{2,1,0:T(8,128)S(1)}, f32[2,384,768]{2,1,0:T(8,128)S(1)}, f32[8,128]{1,0:T(8,128)S(1)}) custom-call(f32[8,128]{1,0:T(8,128)S(1)} %copy-done.8, f32[8,128]{1,0:T(8,128)S(1)} %get-tuple-element.117.dense_ref, f32[8,768]{1,0:T(8,128)S(1)} %copy-done.5, bf16[2,384,768]{2,1,0:T(8,128)(2,1)S(1)} %collective-permute-done.refs_0_, ...), custom_call_target="tpu_custom_call" | custom-call | flops 11500000256 | tf_op jit(solution)/shard_map/finish/pallas_call | solution.py:418
  481.0 1.2 multiply_add_fusion.8
  482.2 1.2 multiply_add_fusion.10
  483.4 1.3 multiply_add_fusion.6
  484.8 4.7 multiply_add_fusion.4
  489.6 7.5 %multiply_add_fusion = (f32[2,384,768]{2,1,0:T(8,128)}, f32[2,384,768]{2,1,0:T(8,128)}, f32[2,384,768]{2,1,0:T(8,128)}, f32[2,384,768]{2,1,0:T(8,128)}) fusion(f32[2,384,768]{2,1,0:T(8,128)S(1)} %copy-done.13, f32[2,384,768]{2,1,0:T(8,128)S(1)} %copy-done.11, f32[2,384,768]{2,1,0:T(8,128)S(1)} %get-tuple-element.125, f32[]{:T(128)} %bitcast.6, ...), kind=kLoop, calls=%fused_computation.6 | loop fusion | flops 11206656 | bytes 21233668 | tf_op jit(solution)/shard_map/add | solution.py:43
  497.1 8.8 %multiply_add_fusion.2 = (f32[2,384,768]{2,1,0:T(8,128)}, f32[2,384,768]{2,1,0:T(8,128)}, f32[2,384,768]{2,1,0:T(8,128)}, f32[2,384,768]{2,1,0:T(8,128)}) fusion(f32[2,384,768]{2,1,0:T(8,128)} %param.55, f32[2,384,768]{2,1,0:T(8,128)S(1)} %copy-done.12, f32[2,384,768]{2,1,0:T(8,128)S(1)} %get-tuple-element.124, f32[]{:T(128)} %bitcast.6, ...), kind=kLoop, calls=%fused_computation.9 | loop fusion | flops 11206656 | bytes 21233668 | tf_op jit(solution)/shard_map/add | solution.py:43
  (70 shorter events, 5.5 us)
Async XLA Ops:
  330.9 125.6 %collective-permute-start = (bf16[2,384,768]{2,1,0:T(8,128)(2,1)}, bf16[2,384,768]{2,1,0:T(8,128)(2,1)S(1)}, u32[]{:S(2)}, u32[]{:S(2)}) collective-permute-start(bf16[2,384,768]{2,1,0:T(8,128)(2,1)} %get-tuple-element.118), channel_id=1, source_target_pairs={{0,0},{8,1},{4,4},{12,5},{16,8},{24,9},{20,12},{28,13},{1,16},{9,1... | collective-permute-start | bytes 3538952 | tf_op jit(solution)/shard_map/ppermute | solution.py:1472
  332.8 123.7 %collective-permute-start.1 = (bf16[2,384,768]{2,1,0:T(8,128)(2,1)}, bf16[2,384,768]{2,1,0:T(8,128)(2,1)S(1)}, u32[]{:S(2)}, u32[]{:S(2)}) collective-permute-start(bf16[2,384,768]{2,1,0:T(8,128)(2,1)} %get-tuple-element.119), channel_id=1, source_target_pairs={{4,0},{12,1},{16,4},{24,5},{20,8},{28,9},{0,12},{8,13},{5,16},{13,... | collective-permute-start | bytes 3538952 | tf_op jit(solution)/shard_map/ppermute | solution.py:1472
  334.3 122.3 %collective-permute-start.2 = (bf16[2,384,768]{2,1,0:T(8,128)(2,1)}, bf16[2,384,768]{2,1,0:T(8,128)(2,1)S(1)}, u32[]{:S(2)}, u32[]{:S(2)}) collective-permute-start(bf16[2,384,768]{2,1,0:T(8,128)(2,1)} %get-tuple-element.120), channel_id=1, source_target_pairs={{16,0},{24,1},{20,4},{28,5},{0,8},{8,9},{4,12},{12,13},{17,16},{25... | collective-permute-start | bytes 3538952 | tf_op jit(solution)/shard_map/ppermute | solution.py:1472
  337.7 125.8 %collective-permute-start.3 = (bf16[2,384,768]{2,1,0:T(8,128)(2,1)}, bf16[2,384,768]{2,1,0:T(8,128)(2,1)}, u32[]{:S(2)}, u32[]{:S(2)}) collective-permute-start(bf16[2,384,768]{2,1,0:T(8,128)(2,1)} %get-tuple-element.121), channel_id=1, source_target_pairs={{20,0},{28,1},{0,4},{8,5},{4,8},{12,9},{16,12},{24,13},{21,16},{29... | collective-permute-start | bytes 3538952 | tf_op jit(solution)/shard_map/ppermute | solution.py:1472
  399.6 56.4 %copy-start.5 = (f32[8,768]{1,0:T(8,128)S(1)}, f32[8,768]{1,0:T(8,128)}, u32[]{:S(2)}) copy-start(f32[8,768]{1,0:T(8,128)} %get-tuple-element.115.imp_ref) | copy-start | bytes 73732
  399.6 63.9 %copy-start.8 = (f32[8,128]{1,0:T(8,128)S(1)}, f32[8,128]{1,0:T(8,128)}, u32[]{:S(2)}) copy-start(f32[8,128]{1,0:T(8,128)} %get-tuple-element.96.head_ref) | copy-start | bytes 12292
  463.5 17.5 %copy-start.23 = (f32[6,24]{1,0:T(8,128)S(1)}, f32[6,24]{1,0:T(8,128)}, u32[]{:S(2)}) copy-start(f32[6,24]{1,0:T(8,128)} %param.48) | copy-start | bytes 1732
  463.5 17.5 %copy-start.25 = (f32[6,24]{1,0:T(8,128)S(1)}, f32[6,24]{1,0:T(8,128)}, u32[]{:S(2)}) copy-start(f32[6,24]{1,0:T(8,128)} %param.51) | copy-start | bytes 1732
  463.5 17.5 %copy-start.26 = (f32[6,24]{1,0:T(8,128)S(1)}, f32[6,24]{1,0:T(8,128)}, u32[]{:S(2)}) copy-start(f32[6,24]{1,0:T(8,128)} %param.49) | copy-start | bytes 1732
  463.5 17.5 %copy-start.27 = (f32[6,24]{1,0:T(8,128)S(1)}, f32[6,24]{1,0:T(8,128)}, u32[]{:S(2)}) copy-start(f32[6,24]{1,0:T(8,128)} %param.50) | copy-start | bytes 1732
  463.5 18.7 %copy-start.24 = (f32[24,8]{0,1:T(8,128)S(1)}, f32[24,8]{0,1:T(8,128)}, u32[]{:S(2)}) copy-start(f32[24,8]{0,1:T(8,128)} %param.44) | copy-start | bytes 2308
  463.5 18.7 %copy-start.28 = (f32[24,8]{0,1:T(8,128)S(1)}, f32[24,8]{0,1:T(8,128)}, u32[]{:S(2)}) copy-start(f32[24,8]{0,1:T(8,128)} %param.47) | copy-start | bytes 2308
  463.5 18.7 %copy-start.29 = (f32[24,8]{0,1:T(8,128)S(1)}, f32[24,8]{0,1:T(8,128)}, u32[]{:S(2)}) copy-start(f32[24,8]{0,1:T(8,128)} %param.45) | copy-start | bytes 2308
  463.6 18.7 %copy-start.30 = (f32[24,8]{0,1:T(8,128)S(1)}, f32[24,8]{0,1:T(8,128)}, u32[]{:S(2)}) copy-start(f32[24,8]{0,1:T(8,128)} %param.46) | copy-start | bytes 2308
  463.6 19.8 %copy-start.1 = (f32[5,24,768]{2,1,0:T(8,128)S(1)}, f32[5,24,768]{2,1,0:T(8,128)}, u32[]{:S(2)}) copy-start(f32[5,24,768]{2,1,0:T(8,128)} %dense_ref.1) | copy-start | bytes 1105924
  463.6 19.8 %copy-start.20 = (f32[5,24,768]{2,1,0:T(8,128)S(1)}, f32[5,24,768]{2,1,0:T(8,128)}, u32[]{:S(2)}) copy-start(f32[5,24,768]{2,1,0:T(8,128)} %param.43) | copy-start | bytes 1105924
  463.6 19.8 %copy-start.21 = (f32[5,24,768]{2,1,0:T(8,128)S(1)}, f32[5,24,768]{2,1,0:T(8,128)}, u32[]{:S(2)}) copy-start(f32[5,24,768]{2,1,0:T(8,128)} %param.41) | copy-start | bytes 1105924
  463.6 19.8 %copy-start.22 = (f32[5,24,768]{2,1,0:T(8,128)S(1)}, f32[5,24,768]{2,1,0:T(8,128)}, u32[]{:S(2)}) copy-start(f32[5,24,768]{2,1,0:T(8,128)} %param.42) | copy-start | bytes 1105924
  463.6 21.2 %copy-start.17 = (f32[576,768]{1,0:T(8,128)S(1)}, f32[576,768]{1,0:T(8,128)}, u32[]{:S(2)}) copy-start(f32[576,768]{1,0:T(8,128)} %param.61) | copy-start | bytes 5308420
  463.6 21.2 %copy-start.18 = (f32[576,768]{1,0:T(8,128)S(1)}, f32[576,768]{1,0:T(8,128)}, u32[]{:S(2)}) copy-start(f32[576,768]{1,0:T(8,128)} %param.62) | copy-start | bytes 5308420
  463.6 21.1 %copy-start.19 = (f32[576,768]{1,0:T(8,128)S(1)}, f32[576,768]{1,0:T(8,128)}, u32[]{:S(2)}) copy-start(f32[576,768]{1,0:T(8,128)} %get-tuple-element.126) | copy-start | bytes 5308420
  479.6 5.2 %copy-start.15 = (f32[576,768]{1,0:T(8,128)S(1)}, f32[576,768]{1,0:T(8,128)}, u32[]{:S(2)}) copy-start(f32[576,768]{1,0:T(8,128)} %head_ref.1) | copy-start | bytes 5308420
  479.6 5.2 %copy-start.16 = (f32[576,768]{1,0:T(8,128)S(1)}, f32[576,768]{1,0:T(8,128)}, u32[]{:S(2)}) copy-start(f32[576,768]{1,0:T(8,128)} %param.63) | copy-start | bytes 5308420
  489.6 7.5 %copy-start.12 = (f32[2,384,768]{2,1,0:T(8,128)S(1)}, f32[2,384,768]{2,1,0:T(8,128)}, u32[]{:S(2)}) copy-start(f32[2,384,768]{2,1,0:T(8,128)} %param.52) | copy-start | bytes 7077892
  (11 other events, 26.1 us)

commit v8 on v7

--- a/solution.py
+++ b/solution.py
@@ -740,31 +740,57 @@
     at = Place(sizes)
     team = Team(at)
     half = weights.shape[1]
+    early, middle = half // 2, half * 3 // 4
     span, width = mask_ref.shape[2], patch_ref.shape[1]
     rows_here = mask_ref.shape[0]
     tokens = rows_here * span
     greet(team.peers())
 
+    def spot_of(step, side=0):
+        return step // early, side * early + step % early
+
+    def swap_copy(step):
+        return send(
+            weights.at[spot_of(step)], weights.at[spot_of(step, 1)], s_out.at[step], s_in.at[step], at.sibling()
+        )
+
     def shard_copy(step):
         device, index, own = team.target(step)
         return send(
-            shard_ref.at[index], weights.at[0, step], w_out.at[step], w_in.at[step], device
+            shard_ref.at[index], weights.at[spot_of(step)], w_out.at[step], w_in.at[step], device
         )
 
     def shard_own(step):
         device, index, own = team.target(step)
-        return pltpu.make_async_copy(shard_ref.at[index], weights.at[0, step], w_in.at[step])
-
-    for step in range(half):
-        own = team.target(step)[2]
-
-        @pl.when(own)
-        def _():
-            shard_own(step).start()
-
-        @pl.when(jnp.logical_not(own))
-        def _():
-            shard_copy(step).start()
+        return pltpu.make_async_copy(shard_ref.at[index], weights.at[spot_of(step)], w_in.at[step])
+
+    def shard_starts(steps):
+        for step in steps:
+            own = team.target(step)[2]
+
+            @pl.when(own)
+            def _():
+                shard_own(step).start()
+
+            @pl.when(jnp.logical_not(own))
+            def _():
+                shard_copy(step).start()
+
+    def shard_waits(steps):
+        for step in steps:
+            own = team.target(step)[2]
+
+            @pl.when(own)
+            def _():
+                shard_own(step).wait()
+
+            @pl.when(jnp.logical_not(own))
+            def _():
+                shard_copy(step).wait_recv()
+
+            swap_copy(step).start()
+
+    shard_starts(range(early))
 
     dense = (
         (x_zero_buf, x_zero_out), (a_one_buf, a_one_out), (qkv_buf, qkv_out), (att_buf, att_out), (x_one_buf, x_one_out),
@@ -901,6 +927,7 @@
         return carry
 
     lax.fori_loop(1, n_experts, dispatch_step, 0)
+    shard_starts(range(early, middle))
     rows_in[at.member] = rows_of(at.member)
     detail_in[at.member] = send_detail[at.member]
     a_two_copy = pltpu.make_async_copy(a_two_ref, a_two_out, keep_sem.at[0])
@@ -909,23 +936,9 @@
         for copy in dense_copies(row):
             copy.wait()
 
-    def swap_copy(index):
-        return send(
-            weights.at[0, index], weights.at[1, index], s_out.at[index], s_in.at[index], at.sibling()
-        )
-
-    for step in range(half):
-        device, index, own = team.target(step)
-
-        @pl.when(own)
-        def _():
-            shard_own(step).wait()
-
-        @pl.when(jnp.logical_not(own))
-        def _():
-            shard_copy(step).wait_recv()
-
-        swap_copy(step).start()
+    shard_waits(range(early))
+    for step in range(early):
+        swap_copy(step).wait_recv()
 
     many = act_buf.shape[2] // padded
     count = many * padded
@@ -959,10 +972,13 @@
                     row_copy(source, source).wait_recv()
                     detail_copy(source, source).wait_recv()
 
+        @pl.when(index == 0)
+        def _():
+            shard_starts(range(middle, half))
+
         @pl.when(index == rounds)
         def _():
-            for step in range(half):
-                swap_copy(step).wait_recv()
+            shard_waits(range(early, half))
 
         @pl.when(index >= 2)
         def _():
@@ -971,6 +987,13 @@
 
         rows = rows_in[pl.ds(block * many, many)].reshape(count, width)
         for chunk in range(half):
+            if chunk == early:
+
+                @pl.when(index == rounds)
+                def _():
+                    for step in range(early, half):
+                        swap_copy(step).wait_recv()
+
             hidden_all = dot_f32(rows, weights[turn, chunk, 0], NT)
             for spot in tiles(count):
                 hidden = hidden_all[spot]
@@ -1090,6 +1113,13 @@
     )(lengths, slot_mask[:, None, :], patches, weights, gains, routers, columns, shards)
 
 
+def chunk_at(index, half):
+    early = half // 2
+    step = lax.rem(index, half)
+    side = jnp.where(index < half, early, 0)
+    return lax.div(step, early) * half + side + lax.rem(step, early)
+
+
 def expert_backward_kernel(
     sizes, padded, rows_ref, detail_ref, pool_ref, y_ref, slope_ref, act_ref, weight_ref, *refs
 ):
@@ -1189,7 +1219,7 @@
     @pl.when(step >= rounds)
     def _():
         index = step - rounds
-        chunk = lax.rem(index + half, chunks)
+        chunk = chunk_at(index, half)
         rows = rows_ref[...].reshape(sources * padded, width)
         g_one = dot_f32(d_hidden[chunk], rows, TN)
         g_two = dot_f32(act_ref[0], d_rows[...], TN)
@@ -1243,7 +1273,7 @@
         return lax.rem(lax.div(member, many) + 1 + jnp.minimum(step, rounds - 1), rounds)
 
     def chunk_of(step):
-        return lax.rem(jnp.maximum(step - rounds, 0) + half, chunks)
+        return chunk_at(jnp.maximum(step - rounds, 0), half)
 
     return pl.pallas_call(
         functools.partial(expert_backward_kernel, sizes, padded),

time: 515 us -> 513 us (level)
    pallas_call x1, Pallas kernels: 55.6 us -> 49 us  [head_step(): pl.pallas_call(functools.partial(head_kernel, sizes, images), out_shape=(...]
where the time goes in v8:
time: 513 us; the launch traced here: 504 us
  Pallas kernels  446 us (87%)
  other arithmetic  31.7 us (6%)
  starting transfers between devices  9.05 us (2%)
  local copies, waits for them, and re-layouts  8.95 us (2%)
  waiting for transfers between devices  6.9 us (1%)
    pallas_call x1, Pallas kernels, forward(): pl.pallas_call(functools.partial(forward_kernel, sizes, n_experts, length...  158 us
    pallas_call x1, Pallas kernels, expert_backward(): pl.pallas_call(functools.partial(expert_backward_kernel, sizes, padded),...  66 us
    pallas_call x1, Pallas kernels, scatter_dense(): pl.pallas_call(functools.partial(scatter_kernel, sizes), out_shape=(jax.S...  56.4 us
    pallas_call x1, Pallas kernels, dense_backward(): pl.pallas_call(functools.partial(dense_backward_kernel, sizes, n_experts,...  56.2 us
    pallas_call x1, Pallas kernels, head_step(): pl.pallas_call(functools.partial(head_kernel, sizes, images), out_shape=(...  49 us
    pallas_call x1, Pallas kernels, gather_weights(): pl.pallas_call(functools.partial(gather_kernel, sizes, rows, mats, routin...  44.7 us
    add x6, other arithmetic, adam_update(): polyak_decay * average_state + (1.0 - polyak_decay) * weight_new  24.7 us
    pallas_call x1, Pallas kernels, finish(): pl.pallas_call(functools.partial(finish_kernel, sizes, n_experts), out_sh...  15.9 us
  transfers between devices with their start and end apart: 4, of which 1 were waited for; matrix products, arithmetic and copies ran while one was open for 0% of the time, Pallas kernels for 22%

profile of v8, /device:TPU:0, one launch (start us, length us, event | category | flops | bytes accessed | tf_op | source)
XLA Modules:
  0.0 504.0 jit_solution(2713867296482401166)
XLA Ops:
  1.3 1.3 broadcast_in_dim.2.mask_ref
  2.6 0.9 copy.57.pick_ref
  3.5 1.3 select_bitcast_fusion
  5.5 2.6 convert_bitcast_fusion
  8.2 1.6 pad_maximum_fusion.shard_ref
  10.0 44.7 %gather_weights.1 = (bf16[5,768,768]{2,1,0:T(8,128)(2,1)}, f32[8,768]{1,0:T(8,128)S(1)}, f32[8,768]{1,0:T(8,128)S(1)}, f32[1024,128]{1,0:T(8,128)S(1)}) custom-call(f32[5,24,768]{2,1,0:T(8,128)S(1)} %copy-done, f32[8,768]{1,0:T(8,128)S(1)} %scatter.9.tail_ref, s32[1024,2]{1,0:T(8,128)S(1)} %copy.57.pick_ref, s32[1,1024]{1,0:T(1,128)S(1)} %copy-done.3, ...), custom_call_target="tpu_custom_call" | custom-call | flops 50600001536 | tf_op jit(solution)/shard_map/gather_weights/pallas_call | solution.py:232
  56.7 157.6 %forward.1 = (f32[1024,768]{1,0:T(8,128)}, bf16[1024,768]{1,0:T(8,128)(2,1)}, bf16[1024,2304]{1,0:T(8,128)(2,1)}, bf16[1024,768]{1,0:T(8,128)(2,1)}, f32[1024,76...) custom-call(s32[4,3]{1,0:T(4,128)} %length_ref.5, ...), custom_call_target="tpu_custom_call" | custom-call | flops 138000007168 | tf_op jit(solution)/shard_map/forward/pallas_call | solution.py:1086
  214.3 49.0 %head_step.1 = (f32[576,768]{1,0:T(8,128)}, f32[8,16,768]{2,1,0:T(8,128)}, f32[16,768]{1,0:T(8,128)}, f32[8,768]{1,0:T(8,128)}, f32[8,128]{1,0:T(8,128)}, /*index=5*/f32[8,768]{1,0:T(8,128)}) custom-call(f32[8,16,768]{2,1,0:T(8,128)} %get-tuple-element.93.part_ref, f32[16,768]{1,0:T(8,128)} %get-tuple-element.94.own_ref, ...), custom_call_target="tpu_custom_call" | custom-call | flops 48299999232 | tf_op jit(solution)/shard_map/head_step/pallas_call | solution.py:580
  263.3 66.0 %expert_backward.1 = (bf16[8,272,768]{2,1,0:T(8,128)(2,1)}, f32[8,8,384]{2,1,0:T(8,128)}, bf16[2,384,768]{2,1,0:T(8,128)(2,1)}, bf16[2,384,768]{2,1,0:T(8,128)(2...) custom-call(bf16[8,272,768]{2,1,0:T(8,128)(2,1)} %get-tuple-element.105.rows_ref, ...), custom_call_target="tpu_custom_call" | custom-call | flops 74750001152 | tf_op jit(solution)/shard_map/expert_backward/pallas_call | solution.py:1278
  329.3 1.9 collective-permute-start
  331.2 1.6 collective-permute-start.1
  332.8 2.4 collective-permute-start.2
  335.2 3.1 collective-permute-start.3
  338.4 56.2 %dense_backward.1.g_ref = bf16[2,4,2,2,128,768]{5,4,3,2,1,0:T(8,128)(2,1)} custom-call(s32[4,3]{1,0:T(4,128)} %length_ref.5, s32[4,1,256]{2,1,0:T(1,128)} %broadcast_in_dim.2.mask_ref, bf16[1024,768]{1,0:T(8,128)(2,1)} %patch_ref.3, f32[1024,768]{1,0:T(8,128)} %get-tuple-element.97.x_zero_ref, bf16[1024,768]{1,0:T(8,128)(2,1)} %get-tuple-element.98.a_one_ref, ...), custom_call_target="tpu_custom_call" | custom-call | flops 57500000256 | tf_op jit(solution)/shard_map/dense_backward/pallas_call | solution.py:1457
  394.6 2.8 copy-done.6
  397.4 56.4 %scatter_dense.1 = (f32[128,768]{1,0:T(8,128)S(1)}, f32[8,128]{1,0:T(8,128)S(1)}) custom-call(bf16[2,4,2,2,128,768]{5,4,3,2,1,0:T(8,128)(2,1)S(1)} %copy-done.6), custom_call_target="tpu_custom_call" | custom-call | flops 51749998592 | tf_op jit(solution)/shard_map/scatter_dense/pallas_call | solution.py:338
  454.3 6.9 %collective-permute-done.3.refs_3_ = bf16[2,384,768]{2,1,0:T(8,128)(2,1)} collective-permute-done((bf16[2,384,768]{2,1,0:T(8,128)(2,1)}, bf16[2,384,768]{2,1,0:T(8,128)(2,1)}, u32[]{:S(2)}, u32[]{:S(2)}) %collective-permute-start.3) | collective-permute-done | bytes 1179680 | tf_op jit(solution)/shard_map/ppermute | solution.py:1502
  461.4 15.9 %finish.1 = (f32[2,384,768]{2,1,0:T(8,128)S(1)}, f32[2,384,768]{2,1,0:T(8,128)S(1)}, f32[8,128]{1,0:T(8,128)S(1)}) custom-call(f32[8,128]{1,0:T(8,128)S(1)} %copy-done.8, f32[8,128]{1,0:T(8,128)S(1)} %get-tuple-element.117.dense_ref, f32[8,768]{1,0:T(8,128)S(1)} %copy-done.5, bf16[2,384,768]{2,1,0:T(8,128)(2,1)S(1)} %collective-permute-done.refs_0_, ...), custom_call_target="tpu_custom_call" | custom-call | flops 11500000256 | tf_op jit(solution)/shard_map/finish/pallas_call | solution.py:418
  478.7 1.2 multiply_add_fusion.8
  479.9 1.2 multiply_add_fusion.10
  481.1 1.3 multiply_add_fusion.6
  482.5 4.7 multiply_add_fusion.4
  487.3 7.5 %multiply_add_fusion = (f32[2,384,768]{2,1,0:T(8,128)}, f32[2,384,768]{2,1,0:T(8,128)}, f32[2,384,768]{2,1,0:T(8,128)}, f32[2,384,768]{2,1,0:T(8,128)}) fusion(f32[2,384,768]{2,1,0:T(8,128)S(1)} %copy-done.13, f32[2,384,768]{2,1,0:T(8,128)S(1)} %copy-done.11, f32[2,384,768]{2,1,0:T(8,128)S(1)} %get-tuple-element.125, f32[]{:T(128)} %bitcast.6, ...), kind=kLoop, calls=%fused_computation.6 | loop fusion | flops 11206656 | bytes 21233668 | tf_op jit(solution)/shard_map/add | solution.py:43
  494.8 8.8 %multiply_add_fusion.2 = (f32[2,384,768]{2,1,0:T(8,128)}, f32[2,384,768]{2,1,0:T(8,128)}, f32[2,384,768]{2,1,0:T(8,128)}, f32[2,384,768]{2,1,0:T(8,128)}) fusion(f32[2,384,768]{2,1,0:T(8,128)} %param.55, f32[2,384,768]{2,1,0:T(8,128)S(1)} %copy-done.12, f32[2,384,768]{2,1,0:T(8,128)S(1)} %get-tuple-element.124, f32[]{:T(128)} %bitcast.6, ...), kind=kLoop, calls=%fused_computation.9 | loop fusion | flops 11206656 | bytes 21233668 | tf_op jit(solution)/shard_map/add | solution.py:43
  (70 shorter events, 5.5 us)
Async XLA Ops:
  329.3 125.0 %collective-permute-start = (bf16[2,384,768]{2,1,0:T(8,128)(2,1)}, bf16[2,384,768]{2,1,0:T(8,128)(2,1)S(1)}, u32[]{:S(2)}, u32[]{:S(2)}) collective-permute-start(bf16[2,384,768]{2,1,0:T(8,128)(2,1)} %get-tuple-element.118), channel_id=1, source_target_pairs={{0,0},{8,1},{4,4},{12,5},{16,8},{24,9},{20,12},{28,13},{1,16},{9,1... | collective-permute-start | bytes 3538952 | tf_op jit(solution)/shard_map/ppermute | solution.py:1502
  331.2 123.1 %collective-permute-start.1 = (bf16[2,384,768]{2,1,0:T(8,128)(2,1)}, bf16[2,384,768]{2,1,0:T(8,128)(2,1)S(1)}, u32[]{:S(2)}, u32[]{:S(2)}) collective-permute-start(bf16[2,384,768]{2,1,0:T(8,128)(2,1)} %get-tuple-element.119), channel_id=1, source_target_pairs={{4,0},{12,1},{16,4},{24,5},{20,8},{28,9},{0,12},{8,13},{5,16},{13,... | collective-permute-start | bytes 3538952 | tf_op jit(solution)/shard_map/ppermute | solution.py:1502
  332.8 121.5 %collective-permute-start.2 = (bf16[2,384,768]{2,1,0:T(8,128)(2,1)}, bf16[2,384,768]{2,1,0:T(8,128)(2,1)S(1)}, u32[]{:S(2)}, u32[]{:S(2)}) collective-permute-start(bf16[2,384,768]{2,1,0:T(8,128)(2,1)} %get-tuple-element.120), channel_id=1, source_target_pairs={{16,0},{24,1},{20,4},{28,5},{0,8},{8,9},{4,12},{12,13},{17,16},{25... | collective-permute-start | bytes 3538952 | tf_op jit(solution)/shard_map/ppermute | solution.py:1502
  335.2 126.0 %collective-permute-start.3 = (bf16[2,384,768]{2,1,0:T(8,128)(2,1)}, bf16[2,384,768]{2,1,0:T(8,128)(2,1)}, u32[]{:S(2)}, u32[]{:S(2)}) collective-permute-start(bf16[2,384,768]{2,1,0:T(8,128)(2,1)} %get-tuple-element.121), channel_id=1, source_target_pairs={{20,0},{28,1},{0,4},{8,5},{4,8},{12,9},{16,12},{24,13},{21,16},{29... | collective-permute-start | bytes 3538952 | tf_op jit(solution)/shard_map/ppermute | solution.py:1502
  397.4 56.4 %copy-start.5 = (f32[8,768]{1,0:T(8,128)S(1)}, f32[8,768]{1,0:T(8,128)}, u32[]{:S(2)}) copy-start(f32[8,768]{1,0:T(8,128)} %get-tuple-element.115.imp_ref) | copy-start | bytes 73732
  397.4 63.8 %copy-start.8 = (f32[8,128]{1,0:T(8,128)S(1)}, f32[8,128]{1,0:T(8,128)}, u32[]{:S(2)}) copy-start(f32[8,128]{1,0:T(8,128)} %get-tuple-element.96.head_ref) | copy-start | bytes 12292
  461.2 17.5 %copy-start.23 = (f32[6,24]{1,0:T(8,128)S(1)}, f32[6,24]{1,0:T(8,128)}, u32[]{:S(2)}) copy-start(f32[6,24]{1,0:T(8,128)} %param.48) | copy-start | bytes 1732
  461.2 17.5 %copy-start.25 = (f32[6,24]{1,0:T(8,128)S(1)}, f32[6,24]{1,0:T(8,128)}, u32[]{:S(2)}) copy-start(f32[6,24]{1,0:T(8,128)} %param.51) | copy-start | bytes 1732
  461.2 17.5 %copy-start.26 = (f32[6,24]{1,0:T(8,128)S(1)}, f32[6,24]{1,0:T(8,128)}, u32[]{:S(2)}) copy-start(f32[6,24]{1,0:T(8,128)} %param.49) | copy-start | bytes 1732
  461.2 17.5 %copy-start.27 = (f32[6,24]{1,0:T(8,128)S(1)}, f32[6,24]{1,0:T(8,128)}, u32[]{:S(2)}) copy-start(f32[6,24]{1,0:T(8,128)} %param.50) | copy-start | bytes 1732
  461.2 18.7 %copy-start.24 = (f32[24,8]{0,1:T(8,128)S(1)}, f32[24,8]{0,1:T(8,128)}, u32[]{:S(2)}) copy-start(f32[24,8]{0,1:T(8,128)} %param.44) | copy-start | bytes 2308
  461.2 18.7 %copy-start.28 = (f32[24,8]{0,1:T(8,128)S(1)}, f32[24,8]{0,1:T(8,128)}, u32[]{:S(2)}) copy-start(f32[24,8]{0,1:T(8,128)} %param.47) | copy-start | bytes 2308
  461.3 18.6 %copy-start.29 = (f32[24,8]{0,1:T(8,128)S(1)}, f32[24,8]{0,1:T(8,128)}, u32[]{:S(2)}) copy-start(f32[24,8]{0,1:T(8,128)} %param.45) | copy-start | bytes 2308
  461.3 18.6 %copy-start.30 = (f32[24,8]{0,1:T(8,128)S(1)}, f32[24,8]{0,1:T(8,128)}, u32[]{:S(2)}) copy-start(f32[24,8]{0,1:T(8,128)} %param.46) | copy-start | bytes 2308
  461.3 19.8 %copy-start.1 = (f32[5,24,768]{2,1,0:T(8,128)S(1)}, f32[5,24,768]{2,1,0:T(8,128)}, u32[]{:S(2)}) copy-start(f32[5,24,768]{2,1,0:T(8,128)} %dense_ref.1) | copy-start | bytes 1105924
  461.3 19.8 %copy-start.20 = (f32[5,24,768]{2,1,0:T(8,128)S(1)}, f32[5,24,768]{2,1,0:T(8,128)}, u32[]{:S(2)}) copy-start(f32[5,24,768]{2,1,0:T(8,128)} %param.43) | copy-start | bytes 1105924
  461.3 19.8 %copy-start.21 = (f32[5,24,768]{2,1,0:T(8,128)S(1)}, f32[5,24,768]{2,1,0:T(8,128)}, u32[]{:S(2)}) copy-start(f32[5,24,768]{2,1,0:T(8,128)} %param.41) | copy-start | bytes 1105924
  461.3 19.8 %copy-start.22 = (f32[5,24,768]{2,1,0:T(8,128)S(1)}, f32[5,24,768]{2,1,0:T(8,128)}, u32[]{:S(2)}) copy-start(f32[5,24,768]{2,1,0:T(8,128)} %param.42) | copy-start | bytes 1105924
  461.3 21.1 %copy-start.17 = (f32[576,768]{1,0:T(8,128)S(1)}, f32[576,768]{1,0:T(8,128)}, u32[]{:S(2)}) copy-start(f32[576,768]{1,0:T(8,128)} %param.61) | copy-start | bytes 5308420
  461.3 21.1 %copy-start.18 = (f32[576,768]{1,0:T(8,128)S(1)}, f32[576,768]{1,0:T(8,128)}, u32[]{:S(2)}) copy-start(f32[576,768]{1,0:T(8,128)} %param.62) | copy-start | bytes 5308420
  461.4 21.1 %copy-start.19 = (f32[576,768]{1,0:T(8,128)S(1)}, f32[576,768]{1,0:T(8,128)}, u32[]{:S(2)}) copy-start(f32[576,768]{1,0:T(8,128)} %get-tuple-element.126) | copy-start | bytes 5308420
  477.3 5.2 %copy-start.15 = (f32[576,768]{1,0:T(8,128)S(1)}, f32[576,768]{1,0:T(8,128)}, u32[]{:S(2)}) copy-start(f32[576,768]{1,0:T(8,128)} %head_ref.1) | copy-start | bytes 5308420
  477.3 5.2 %copy-start.16 = (f32[576,768]{1,0:T(8,128)S(1)}, f32[576,768]{1,0:T(8,128)}, u32[]{:S(2)}) copy-start(f32[576,768]{1,0:T(8,128)} %param.63) | copy-start | bytes 5308420
  487.2 7.5 %copy-start.12 = (f32[2,384,768]{2,1,0:T(8,128)S(1)}, f32[2,384,768]{2,1,0:T(8,128)}, u32[]{:S(2)}) copy-start(f32[2,384,768]{2,1,0:T(8,128)} %param.52) | copy-start | bytes 7077892
  (11 other events, 26.1 us)

commit v9 on v8

--- a/solution.py
+++ b/solution.py
@@ -133,23 +133,13 @@
     return peers + [at.sibling()]
 
 
-def gather_kernel(
-    sizes, rows, mats, routing, dense_ref, tail_ref, pick_ref, rank_ref, mask_ref, length_ref,
-    w_ref, gain_ref, router_ref, col_ref, land, *sems
-):
-    at = Place(sizes)
+def gather_dense(at, rows, mats, count, land, sems, started, beside, idle):
     Z, Y, X = at.Z, at.Y, at.X
     depth = land.shape[4]
     cut = depth // 2 // 16 * 16
     first, second = pl.ds(0, cut), pl.ds(cut, depth - cut)
     z_out, z_in, ya_out, ya_in, xb_out, xb_in, xa_out, xa_in, yb_out, yb_in, c_out, c_in = sems
-    block = jnp.concatenate([dense_ref[...].reshape(mats * rows, -1), tail_ref[...]], 0)
-    if block.shape[0] < depth:
-        block = jnp.pad(block, ((0, depth - block.shape[0]), (0, 0)))
     mine = land.at[at.c, at.z, at.x, at.y]
-    mine[...] = block.astype(jnp.bfloat16)
-    greet(grid_peers(at))
-    started = []
 
     def begin(copy):
         copy.start()
@@ -198,7 +188,9 @@
                 send(part, part, z_out.at[z], z_in.at[z], at.at(z=z)).wait_recv()
             one(order[step])
         if step == 0:
-            col_ref[...] = route_math(*routing, pick_ref, rank_ref, mask_ref, length_ref)
+            beside()
+        if step == Z - 1:
+            idle()
         if 0 <= step - 1 < Z:
             two(order[step - 1])
         if 0 <= step - 2 < Z:
@@ -206,9 +198,10 @@
     for z in order:
         plane = land.at[1 - at.c, z]
         send(plane, plane, c_out.at[z], c_in.at[z], at.sibling()).wait_recv()
-    for copy in started:
-        copy.wait_send()
-    chips = [(z, y, x) for z in range(Z) for y in range(Y) for x in range(X)]
+
+
+def assemble_dense(at, rows, mats, count, land, w_ref, gain_ref, router_ref):
+    chips = [(z, y, x) for z in range(at.Z) for y in range(at.Y) for x in range(at.X)]
     cores = [(c, z, x, y) for z, y, x in chips for c in range(2)]
     group = 16 // math.gcd(16, rows)
     for start in range(0, len(cores), group):
@@ -216,37 +209,10 @@
             w_ref[mat, start * rows : (start + group) * rows] = jnp.concatenate(
                 [land[spot][mat * rows : (mat + 1) * rows] for spot in cores[start : start + group]], 0
             )
-    base, count = mats * rows, tail_ref.shape[0]
+    base = mats * rows
     tails = [land[spot][base : base + count].astype(jnp.float32) for spot in cores]
     gain_ref[...] = jnp.concatenate([tail[:8, :rows] for tail in tails], 1)
     router_ref[...] = jnp.concatenate([tail[:, 128 : 128 + rows] for tail in tails], 1)
-
-
-def gather_weights(sizes, routing, dense, tail, picks, ranks, slot_mask, lengths):
-    mats, rows, width = dense.shape
-    count = tail.shape[0]
-    depth = round_up(mats * rows + count, 16)
-    Z, Y, X = QUAD, sizes["g"], sizes["x"]
-    dma = pltpu.SemaphoreType.DMA
-    by_y, by_x = dma((Z, Y)), dma((Z, X))
-    return pl.pallas_call(
-        functools.partial(gather_kernel, sizes, rows, mats, routing),
-        out_shape=(
-            jax.ShapeDtypeStruct((mats, width, width), jnp.bfloat16),
-            jax.ShapeDtypeStruct((8, width), jnp.float32),
-            jax.ShapeDtypeStruct((count, width), jnp.float32),
-            jax.ShapeDtypeStruct((picks.shape[0], 128), jnp.float32),
-        ),
-        in_specs=[whole()] * 6,
-        out_specs=(whole(),) * 4,
-        scratch_shapes=[VMEM((2, Z, X, Y, depth, width), jnp.bfloat16), dma((Z,)), dma((Z,))]
-        + [by_y, by_y, by_x, by_x, by_x, by_x, by_y, by_y, dma((Z,)), dma((Z,))],
-        compiler_params=pltpu.CompilerParams(
-            collective_id=1, has_side_effects=True, vmem_limit_bytes=48 * MIB
-        ),
-        cost_estimate=cost(44),
-        name="gather_weights",
-    )(dense, tail, picks, ranks, slot_mask, lengths)
 
 
 def total_square(value):
@@ -382,7 +348,7 @@
         expert = place if parity == 0 else 1 - place
         for index, ref in enumerate((first_ref, second_ref)):
             total = None
-            for step in range(parity, many, 2):
+            for step in range(parity * many // 2, (parity + 1) * many // 2):
                 found = parts[step][index].astype(jnp.float32)
                 total = found if total is None else total + found
             ref[expert] = total
@@ -632,16 +598,18 @@
         return jnp.concatenate([value[i : i + 1] for i in range(rows_here)], 1)
 
     rank_row = rank_ref[...].astype(jnp.float32)
-    table = jnp.concatenate([flat(valid), flat(pool), flat(image), rank_row], 0)
-    table = jnp.concatenate([table, jnp.zeros((124, tokens), jnp.float32)], 0).T
-    valid_col, pool_col, image_col, rank_col = (table[:, i : i + 1] for i in range(4))
-    picks = pick_ref[...]
-    pick_one, pick_two = picks[:, 0:1], picks[:, 1:2]
+    picks = pick_ref[...].astype(jnp.float32)
+    table = jnp.concatenate([flat(valid), flat(pool), flat(image), rank_row, picks], 0)
+    table = jnp.concatenate([table, jnp.zeros((122, tokens), jnp.float32)], 0).T
+    valid_col, pool_col, image_col, rank_col, pick_one, pick_two = (
+        table[:, i : i + 1] for i in range(6)
+    )
     lane = lax.broadcasted_iota(jnp.int32, (tokens, 128), 1)
     in_first, in_second = lane < n_experts, (lane >= n_experts) & (lane < 2 * n_experts)
-    hot = jnp.where(in_first & (pick_one == lane), valid_col, 0.0)
-    hot = hot + jnp.where(in_second & (pick_two == lane - n_experts), valid_col, 0.0)
-    shifted = jnp.where(in_second & (pick_one == lane - n_experts), valid_col, 0.0)
+    number = lane.astype(jnp.float32)
+    hot = jnp.where(in_first & (pick_one == number), valid_col, 0.0)
+    hot = hot + jnp.where(in_second & (pick_two == number - n_experts), valid_col, 0.0)
+    shifted = jnp.where(in_second & (pick_one == number - n_experts), valid_col, 0.0)
     before = jnp.where(rank_row < rank_col, 1.0, 0.0).astype(jnp.bfloat16)
     ahead = dot_f32(before, hot.astype(jnp.bfloat16), NN) + jnp.sum(shifted, 0, keepdims=True)
     counted = hot * ahead
@@ -650,7 +618,7 @@
 
     def place(pick, pos):
         kept = (valid_col > 0.0) & (pos < capacity)
-        return jnp.where(kept, pick.astype(jnp.float32) * padded + pos, -1.0)
+        return jnp.where(kept, pick * padded + pos, -1.0)
 
     columns = (
         place(pick_one, pos_one),
@@ -658,8 +626,8 @@
         valid_col,
         pool_col,
         image_col,
-        pick_one.astype(jnp.float32),
-        pick_two.astype(jnp.float32),
+        pick_one,
+        pick_two,
     )
     result = jnp.zeros((tokens, 128), jnp.float32)
     for index, column in enumerate(columns):
@@ -686,6 +654,10 @@
     return [slice(start, min(start + TILE, count)) for start in range(0, count, TILE)]
 
 
+def step_order(blocks):
+    return [*range(0, 2 * blocks, 2), *range(1, 2 * blocks, 2)]
+
+
 class Team:
     def __init__(self, at):
         self.at, self.span = at, 2 * at.G
@@ -693,19 +665,12 @@
 
     def target(self, step):
         at = self.at
-        chosen = lax.rem(self.spot + step, self.span)
+        chosen = lax.rem(self.spot + step_order(at.G)[step], self.span)
         block, index = lax.div(chosen, 2), lax.rem(chosen, 2)
         core = lax.div(self.spot, self.span)
         r = 2 * at.c + index
         own = (block == at.g) & (r == at.r) & (core == at.c)
         return {"g": block, "r": r, "x": at.x, "c": core}, index, own
-
-    def source(self, step):
-        at = self.at
-        chosen = at.g * 2 + lax.rem(at.r, 2)
-        spot = at.c * self.span + lax.rem(chosen - step + self.span, self.span)
-        device = {"g": lax.div(spot, QUAD), "r": lax.rem(spot, QUAD), "x": at.x, "c": lax.div(at.r, 2)}
-        return device, lax.rem(at.r, 2)
 
     def peers(self):
         at = self.at
@@ -730,21 +695,49 @@
 
 def forward_kernel(
     sizes, n_experts, images, padded,
-    length_ref, mask_ref, patch_ref, w_ref, gain_ref, router_ref, col_ref, shard_ref,
-    x_zero_out, a_one_out, qkv_out, att_out, x_one_out, a_two_out, prob_ref, lse_ref, pool_ref, imp_ref,
+    length_ref, lengths_ref, mask_ref, pick_ref, rank_ref, patch_ref, dense_ref, norm_ref, routing_ref, in_ref, out_ref,
+    w_keep, gain_ref, router_ref, col_ref, x_zero_out, a_one_out, qkv_out, att_out, x_one_out, a_two_out, prob_ref, lse_ref, pool_ref, imp_ref,
     rows_out, detail_out, act_out, slope_out, y_out, part_ref, weight_out,
-    x_zero_buf, a_one_buf, qkv_buf, att_buf, x_one_buf, a_two_ref, weights, send_rows, send_detail, places,
+    land, w_ref, shard_ref, x_zero_buf, a_one_buf, qkv_buf, att_buf, x_one_buf, a_two_ref, weights, send_rows, send_detail, places,
     rows_in, detail_in, total, act_buf, slope_buf, dense_sem, keep_sem, own_sem,
-    w_out, w_in, s_out, s_in, r_out, r_in, m_out, m_in, act_sem, slope_sem
+    w_out, w_in, s_out, s_in, r_out, r_in, m_out, m_in, act_sem, slope_sem, cast_sem, *gather_sems
 ):
     at = Place(sizes)
     team = Team(at)
     half = weights.shape[1]
-    early, middle = half // 2, half * 3 // 4
-    span, width = mask_ref.shape[2], patch_ref.shape[1]
-    rows_here = mask_ref.shape[0]
+    early = half // 2
+    rows_here, span = mask_ref.shape
+    width = patch_ref.shape[1]
     tokens = rows_here * span
-    greet(team.peers())
+    mats, rows_own, unused = dense_ref.shape
+    tall = router_ref.shape[0]
+    capacity = (21 * tokens * TOP + 20 * n_experts - 1) // (20 * n_experts)
+
+    part_rows = shard_ref.shape[2]
+    casts = [
+        pltpu.make_async_copy(ref.at[expert], total.at[pl.ds((index * 2 + expert) * part_rows, part_rows)], cast_sem.at[index, expert])
+        for index, ref in enumerate((in_ref, out_ref))
+        for expert in range(2)
+    ]
+    for copy in casts:
+        copy.start()
+    depth = land.shape[4]
+    routing = routing_ref[...]
+    routing = jnp.concatenate([routing, jnp.zeros((rows_own, 128 - n_experts), jnp.float32)], 1)
+    routing = jnp.concatenate([routing, jnp.zeros((128 - rows_own, 128), jnp.float32)], 0).T
+    norms = norm_ref[...]
+    norms = jnp.concatenate([norms, jnp.zeros((norms.shape[0], 128 - rows_own), jnp.float32)], 1)
+    norms = jnp.concatenate([norms, jnp.zeros((tall - norms.shape[0], 128), jnp.float32)], 0)
+    tail = jnp.concatenate(
+        [norms, routing[:tall], jnp.zeros((tall, width - 256), jnp.float32)], 1
+    )
+    block = jnp.concatenate([dense_ref[...].reshape(mats * rows_own, width), tail], 0)
+    if block.shape[0] < depth:
+        block = jnp.concatenate(
+            [block, jnp.zeros((depth - block.shape[0], width), jnp.float32)], 0
+        )
+    land[at.c, at.z, at.x, at.y] = block.astype(jnp.bfloat16)
+    greet(team.peers() + grid_peers(at))
 
     def spot_of(step, side=0):
         return step // early, side * early + step % early
@@ -790,19 +783,42 @@
 
             swap_copy(step).start()
 
-    shard_starts(range(early))
+    def beside_gather():
+        col_ref[...] = route_math(
+            images, n_experts, capacity, padded, pick_ref, rank_ref, mask_ref, lengths_ref
+        )
+        for copy in casts:
+            copy.wait()
+        for index in range(2):
+            for expert in range(2):
+                here = pl.ds((index * 2 + expert) * part_rows, part_rows)
+                shard_ref[expert, index] = total[here].astype(jnp.bfloat16)
+
+    gathers = []
+    gather_dense(
+        at, rows_own, mats, tall, land, gather_sems, gathers, beside_gather, lambda: shard_starts(range(early))
+    )
+    shard_starts(range(early, half))
+    assemble_dense(at, rows_own, mats, tall, land, w_ref, gain_ref, router_ref)
+    w_copy = pltpu.make_async_copy(w_ref, w_keep, keep_sem.at[5])
+    w_copy.start()
 
     dense = (
         (x_zero_buf, x_zero_out), (a_one_buf, a_one_out), (qkv_buf, qkv_out), (att_buf, att_out), (x_one_buf, x_one_out),
     )
 
-    def dense_copies(row):
-        slot = lax.rem(row, 2)
+    def dense_copy(row, index):
         here = pl.ds(pl.multiple_of(row * span, 16), span)
-        return [
-            pltpu.make_async_copy(buf.at[slot], out.at[here], dense_sem.at[index, slot])
-            for index, (buf, out) in enumerate(dense)
-        ]
+        buf, out = dense[index]
+        return pltpu.make_async_copy(buf, out.at[here], dense_sem.at[index])
+
+    def keep_dense(row, index, value):
+        @pl.when(row > 0)
+        def _():
+            dense_copy(row - 1, index).wait()
+
+        dense[index][0][...] = value
+        dense_copy(row, index).start()
 
     pool_ref[...] = jnp.zeros_like(pool_ref)
     imp_ref[...] = jnp.zeros_like(imp_ref)
@@ -814,26 +830,31 @@
     lane = lax.broadcasted_iota(jnp.int32, (span, 128), 1)
 
     def dense_row(row, carry):
-        @pl.when(row >= 2)
-        def _():
-            for copy in dense_copies(row - 2):
-                copy.wait()
-
-        slot = lax.rem(row, 2)
         here = pl.ds(pl.multiple_of(row * span, 16), span)
         x_zero = dot_f32(patch_ref[here], w_ref[0], NN)
-        x_zero_buf[slot] = x_zero
+        keep_dense(row, 0, x_zero)
         a_one = (norm_parts(x_zero)[0] * gain_ref[0:1] + gain_ref[3:4]).astype(jnp.bfloat16)
-        a_one_buf[slot] = a_one
+        keep_dense(row, 1, a_one)
+
+        @pl.when(row > 0)
+        def _():
+            dense_copy(row - 1, 2).wait()
+
         for part in range(3):
-            qkv_buf[slot, :, part * width : (part + 1) * width] = dot_f32(
+            qkv_buf[:, part * width : (part + 1) * width] = dot_f32(
                 a_one, w_ref[1 + part], NN
             ).astype(jnp.bfloat16)
-        open_to = allowed_slots(length_ref, row, images, mask_ref[row], span)
+        dense_copy(row, 2).start()
+        open_to = allowed_slots(length_ref, row, images, mask_ref[pl.ds(row, 1)], span)
         logs = jnp.zeros((span, 128), jnp.float32)
+
+        @pl.when(row > 0)
+        def _():
+            dense_copy(row - 1, 3).wait()
+
         for pair in range(width // 128):
             query, key, value = (
-                qkv_buf[slot, :, part * width + pair * 128 : part * width + (pair + 1) * 128]
+                qkv_buf[:, part * width + pair * 128 : part * width + (pair + 1) * 128]
                 for part in range(3)
             )
             outs = []
@@ -846,12 +867,13 @@
                 probs = (powers * (1.0 / whole_sum)).astype(jnp.bfloat16)
                 outs.append(dot_f32(probs, value, NN))
                 logs = jnp.where(lane == 2 * pair + side, top + jnp.log(whole_sum), logs)
-            att_buf[slot, :, pair * 128 : (pair + 1) * 128] = jnp.where(
+            att_buf[:, pair * 128 : (pair + 1) * 128] = jnp.where(
                 lane < 64, outs[0], outs[1]
             ).astype(jnp.bfloat16)
         lse_ref[here] = logs
-        x_one = x_zero + dot_f32(att_buf[slot], w_ref[4], NN)
-        x_one_buf[slot] = x_one
+        dense_copy(row, 3).start()
+        x_one = x_zero + dot_f32(att_buf[...], w_ref[4], NN)
+        keep_dense(row, 4, x_one)
         a_two = (norm_parts(x_one)[0] * gain_ref[1:2] + gain_ref[4:5]).astype(jnp.bfloat16)
         a_two_ref[here] = a_two
         logits = jnp.where(lane < n_experts, dot_f32(a_two, routers, NT), mask_fill)
@@ -867,8 +889,6 @@
             weight = jnp.where(image == number.astype(jnp.float32), pool, 0.0)
             pooled = jnp.sum(x_one * weight, 0, keepdims=True)
             pool_ref[...] = jnp.where(line == number, pooled, pool_ref[...])
-        for copy in dense_copies(row):
-            copy.start()
         return carry
 
     lax.fori_loop(0, rows_here, dense_row, 0)
@@ -927,39 +947,35 @@
         return carry
 
     lax.fori_loop(1, n_experts, dispatch_step, 0)
-    shard_starts(range(early, middle))
     rows_in[at.member] = rows_of(at.member)
     detail_in[at.member] = send_detail[at.member]
     a_two_copy = pltpu.make_async_copy(a_two_ref, a_two_out, keep_sem.at[0])
     a_two_copy.start()
-    for row in range(max(rows_here - 2, 0), rows_here):
-        for copy in dense_copies(row):
-            copy.wait()
+    for index in range(len(dense)):
+        dense_copy(rows_here - 1, index).wait()
 
     shard_waits(range(early))
     for step in range(early):
         swap_copy(step).wait_recv()
 
-    many = act_buf.shape[2] // padded
+    many = act_buf.shape[1] // padded
     count = many * padded
     rounds = n_experts // many
-    part = act_buf.shape[3]
-
-    def hidden_copies(index):
-        slot, turn = lax.rem(index, 2), lax.div(index, rounds)
-        block = block_of(index)
+
+    def hidden_copies(index, chunk):
+        block, turn = block_of(index), lax.div(index, rounds)
         here = pl.ds(pl.multiple_of(block * count, 16), count)
-        there = pl.ds(turn * half, half)
+        there = turn * half + chunk
         return (
-            pltpu.make_async_copy(act_buf.at[slot], act_out.at[there, here], act_sem.at[slot]),
-            pltpu.make_async_copy(slope_buf.at[slot], slope_out.at[there, here], slope_sem.at[slot]),
+            pltpu.make_async_copy(act_buf.at[chunk], act_out.at[there, here], act_sem.at[chunk]),
+            pltpu.make_async_copy(slope_buf.at[chunk], slope_out.at[there, here], slope_sem.at[chunk]),
         )
 
     def block_of(index):
         return lax.rem(lax.div(at.member, many) + index, rounds)
 
     def expert_step(index, carry):
-        slot, turn = lax.rem(index, 2), lax.div(index, rounds)
+        turn = lax.div(index, rounds)
         block = block_of(index)
 
         @pl.when(turn == 0)
@@ -972,18 +988,9 @@
                     row_copy(source, source).wait_recv()
                     detail_copy(source, source).wait_recv()
 
-        @pl.when(index == 0)
-        def _():
-            shard_starts(range(middle, half))
-
         @pl.when(index == rounds)
         def _():
             shard_waits(range(early, half))
-
-        @pl.when(index >= 2)
-        def _():
-            for copy in hidden_copies(index - 2):
-                copy.wait()
 
         rows = rows_in[pl.ds(block * many, many)].reshape(count, width)
         for chunk in range(half):
@@ -993,8 +1000,15 @@
                 def _():
                     for step in range(early, half):
                         swap_copy(step).wait_recv()
+                    keeps[2].start()
 
             hidden_all = dot_f32(rows, weights[turn, chunk, 0], NT)
+
+            @pl.when(index > 0)
+            def _():
+                for copy in hidden_copies(index - 1, chunk):
+                    copy.wait()
+
             for spot in tiles(count):
                 hidden = hidden_all[spot]
                 square = hidden * hidden
@@ -1004,11 +1018,11 @@
                 slope = upper + gelu * (1.0 - upper) * (
                     2.0 * 0.7978845608 + 6.0 * 0.7978845608 * 0.044715 * square
                 )
-                act_buf[slot, chunk, spot] = gelu.astype(jnp.bfloat16)
-                slope_buf[slot, chunk, spot] = slope.astype(jnp.bfloat16)
-        for copy in hidden_copies(index):
-            copy.start()
-        acts = jnp.concatenate([act_buf[slot, chunk] for chunk in range(half)], 1)
+                act_buf[chunk, spot] = gelu.astype(jnp.bfloat16)
+                slope_buf[chunk, spot] = slope.astype(jnp.bfloat16)
+            for copy in hidden_copies(index, chunk):
+                copy.start()
+        acts = jnp.concatenate([act_buf[chunk] for chunk in range(half)], 1)
         ends = jnp.concatenate([weights[turn, chunk, 1] for chunk in range(half)], 0)
         found = dot_f32(acts, ends, NN)
         here = pl.ds(pl.multiple_of(block * count, 16), count)
@@ -1038,20 +1052,21 @@
             for member in others(at.member, n_experts):
                 row_copy(member, at.member).wait_send()
                 detail_copy(member, at.member).wait_send()
+            for copy in keeps[:2]:
+                copy.start()
 
         return carry
 
-    lax.fori_loop(0, 2 * rounds, expert_step, 0)
     keeps = [
         pltpu.make_async_copy(rows_in, rows_out, keep_sem.at[1]),
         pltpu.make_async_copy(detail_in, detail_out, keep_sem.at[2]),
+        pltpu.make_async_copy(weights, weight_out, keep_sem.at[4]),
         pltpu.make_async_copy(send_rows, y_out, keep_sem.at[3]),
-        pltpu.make_async_copy(weights, weight_out, keep_sem.at[4]),
     ]
-    for copy in keeps:
-        copy.start()
-    for index in range(2 * rounds - 2, 2 * rounds):
-        for copy in hidden_copies(index):
+    lax.fori_loop(0, 2 * rounds, expert_step, 0)
+    keeps[3].start()
+    for chunk in range(half):
+        for copy in hidden_copies(2 * rounds - 1, chunk):
             copy.wait()
     for step in range(half):
         own = team.target(step)[2]
@@ -1062,21 +1077,29 @@
             shard_copy(step).wait_send()
 
     a_two_copy.wait()
+    w_copy.wait()
     for copy in keeps:
         copy.wait()
-
-
-def forward(sizes, n_experts, padded, lengths, slot_mask, patches, weights, gains, routers, columns, shards):
+    for copy in gathers:
+        copy.wait_send()
+
+
+def forward(sizes, n_experts, padded, lengths, slot_mask, picks, ranks, patches, dense, norms, routers, expert_in, expert_out):
     rows_here, span = slot_mask.shape
     tokens, width = patches.shape
-    part = shards.shape[2]
+    part = expert_in.shape[1]
+    mats, rows_own, unused = dense.shape
+    tall = max(8, n_experts)
+    depth = round_up(mats * rows_own + tall, 16)
+    Z, Y, X = QUAD, sizes["g"], sizes["x"]
     half = 2 * sizes["g"]
     lanes = round_up(padded, 128)
-    many = max(1, 576 // padded)
+    many = max(1, (144 if part % 128 else 576) // padded)
     count = n_experts * padded
     f32, kind = jnp.float32, jnp.bfloat16
     dma = pltpu.SemaphoreType.DMA
     each, parts, two = dma((n_experts,)), dma((half,)), dma((2,))
+    by_y, by_x, by_z = dma((Z, Y)), dma((Z, X)), dma((Z,))
 
     def out(wide, dtype):
         return jax.ShapeDtypeStruct((tokens, wide), dtype)
@@ -1086,6 +1109,8 @@
     return pl.pallas_call(
         functools.partial(forward_kernel, sizes, n_experts, lengths.shape[1], padded),
         out_shape=(
+            jax.ShapeDtypeStruct((mats, width, width), kind), jax.ShapeDtypeStruct((8, width), f32),
+            jax.ShapeDtypeStruct((tall, width), f32), out(128, f32),
             out(width, f32), out(width, kind), out(3 * width, kind), out(width, kind), out(width, f32),
             out(width, kind), out(128, f32), out(128, f32),
             jax.ShapeDtypeStruct((IMAGE_PAD, width), f32), jax.ShapeDtypeStruct((8, width), f32),
@@ -1094,23 +1119,25 @@
             jax.ShapeDtypeStruct((n_experts, IMAGE_PAD, width), f32),
             jax.ShapeDtypeStruct((2, half, 2, part, width), kind),
         ),
-        in_specs=[whole(pltpu.SMEM)] + [whole()] * 6 + [whole(ANY)],
-        out_specs=(whole(ANY),) * 6 + (whole(),) * 4 + (whole(ANY),) * 5 + (whole(), whole(ANY)),
+        in_specs=[whole(pltpu.SMEM)] + [whole()] * 8 + [whole(ANY)] * 2,
+        out_specs=(whole(ANY), whole(), whole(), whole()) + (whole(ANY),) * 6 + (whole(),) * 4 + (whole(ANY),) * 5 + (whole(), whole(ANY)),
         scratch_shapes=[
-            VMEM((2, span, width), f32), VMEM((2, span, width), kind), VMEM((2, span, 3 * width), kind),
-            VMEM((2, span, width), kind), VMEM((2, span, width), f32), VMEM((tokens, width), kind),
+            VMEM((2, Z, X, Y, depth, width), kind), VMEM((mats, width, width), kind), VMEM((2, 2, part, width), kind),
+            VMEM((span, width), f32), VMEM((span, width), kind), VMEM((span, 3 * width), kind),
+            VMEM((span, width), kind), VMEM((span, width), f32), VMEM((tokens, width), kind),
             VMEM((2, half, 2, part, width), kind), VMEM(rows, kind), VMEM((n_experts, 8, lanes), f32),
             VMEM((8, tokens), f32), VMEM(rows, kind), VMEM((n_experts, 8, lanes), f32),
-            VMEM((count, width), f32), VMEM((2, half, many * padded, part), kind),
-            VMEM((2, half, many * padded, part), kind), dma((5, 2)), dma((5,)), two,
-            parts, parts, parts, parts, each, each, each, each, two, two,
+            VMEM((count, width), f32), VMEM((half, many * padded, part), kind),
+            VMEM((half, many * padded, part), kind), dma((5,)), dma((6,)), two,
+            parts, parts, parts, parts, each, each, each, each, parts, parts, dma((2, 2)),
+            by_z, by_z, by_y, by_y, by_x, by_x, by_x, by_x, by_y, by_y, by_z, by_z,
         ],
         compiler_params=pltpu.CompilerParams(
-            collective_id=5, has_side_effects=True, vmem_limit_bytes=60 * MIB
+            collective_id=5, has_side_effects=True, vmem_limit_bytes=62 * MIB
         ),
         cost_estimate=cost(120),
         name="forward",
-    )(lengths, slot_mask[:, None, :], patches, weights, gains, routers, columns, shards)
+    )(lengths, lengths, slot_mask, picks.T, ranks, patches, dense, norms, routers, expert_in, expert_out)
 
 
 def chunk_at(index, half):
@@ -1485,7 +1512,7 @@
 def shard_moves(n_blocks):
     span = 2 * n_blocks
     moves = []
-    for step in range(span):
+    for step in step_order(n_blocks):
         pairs = []
         for place in range(QUAD * n_blocks):
             for core in range(2):
@@ -1539,31 +1566,18 @@
     n_blocks = lax.axis_size("g")
     sizes = {name: lax.axis_size(name) for name in ALL}
     rows_own, n_experts = router_weights.shape
-    n_tail = max(8, n_experts)
-    tail = jnp.zeros((n_tail, dense_weights.shape[2]), jnp.float32)
-    tail = tail.at[:6, :rows_own].set(norm_params)
-    tail = tail.at[:n_experts, 128 : 128 + rows_own].set(router_weights.T)
     rows_here, n_slots_row = slot_mask.shape
     tokens, model_width = patches.shape
     n_images = lengths.shape[0] * lengths.shape[1]
     capacity = (21 * tokens * TOP + 20 * n_experts - 1) // (20 * n_experts)
     padded = round_up(capacity, 16)
-    layer_b, gain_rows, router_t, columns = gather_weights(
-        sizes,
-        (lengths.shape[1], n_experts, capacity, padded),
-        dense_weights,
-        tail,
-        expert_picks,
-        priority_rank,
-        slot_mask,
-        lengths,
-    )
-    shards = jnp.stack([expert_in, expert_out], 1).astype(jnp.bfloat16)
     (
+        layer_b, gain_rows, router_t, columns,
         x_zero, a_one, qkv, att_out, x_one, a_two, router_probs, logs, pooled, part_importance,
         arrived, details, activated, slope, result, part_pooled, expert_weights
     ) = forward(
-        sizes, n_experts, padded, lengths, slot_mask, patches, layer_b, gain_rows, router_t, columns, shards
+        sizes, n_experts, padded, lengths, slot_mask, expert_picks, priority_rank, patches, dense_weights, norm_params,
+        router_weights, expert_in, expert_out
     )
     g_head, d_pooled_all, d_pooled, g_norm_three, head_sums, total_importance = head_step(
         sizes,

time: 513 us -> 479 us (0.934); the launches traced: 504 us -> 476 us
  other arithmetic: 31.7 us -> 21.3 us
  waiting for transfers between devices: 6.9 us -> 0.01 us
    pallas_call x1 -> x0, Pallas kernels: 44.7 us -> none  [gather_weights(): pl.pallas_call(functools.partial(gather_kernel, sizes, rows, mats, routin...]
    pallas_call x1, Pallas kernels: 158 us -> 187 us  [forward(): pl.pallas_call(functools.partial(forward_kernel, sizes, n_experts, length...]
    pallas_call x1, Pallas kernels: 49 us -> 60.3 us  [head_step(): pl.pallas_call(functools.partial(head_kernel, sizes, images), out_shape=(...]
    ppermute x4, waiting for transfers between devices: 6.9 us -> 0.01 us  [return_experts(): lax.ppermute(part, ('g', 'r', 'c'), [(dst, src) for src, dst in pairs])]
    another operation x4 -> x0, other arithmetic: 6.21 us -> none  [the longest x2 4.22 us: body(): shards = jnp.stack([expert_in, expert_out], 1).astype(jnp.bfloat16)]
    add x6 -> x5, other arithmetic: 24.7 us -> 20.6 us  [adam_update(): polyak_decay * average_state + (1.0 - polyak_decay) * weight_new]
  transfers between devices with their start and end apart: 4 -> 4, of which waited for: 1 -> 0; matrix products, arithmetic and copies ran while one was open for 0% -> 0% of each run, Pallas kernels for 22% -> 24%
where the time goes in v9:
time: 479 us; the launch traced here: 476 us
  Pallas kernels  442 us (92%)
  other arithmetic  21.3 us (4%)
  local copies, waits for them, and re-layouts  5.95 us (1%)
  starting transfers between devices  5.45 us (1%)
    pallas_call x1, Pallas kernels, forward(): pl.pallas_call(functools.partial(forward_kernel, sizes, n_experts, length...  187 us
    pallas_call x1, Pallas kernels, expert_backward(): pl.pallas_call(functools.partial(expert_backward_kernel, sizes, padded),...  65.7 us
    pallas_call x1, Pallas kernels, head_step(): pl.pallas_call(functools.partial(head_kernel, sizes, images), out_shape=(...  60.3 us
    pallas_call x1, Pallas kernels, scatter_dense(): pl.pallas_call(functools.partial(scatter_kernel, sizes), out_shape=(jax.S...  58.7 us
    pallas_call x1, Pallas kernels, dense_backward(): pl.pallas_call(functools.partial(dense_backward_kernel, sizes, n_experts,...  56.2 us
    add x5, other arithmetic, adam_update(): polyak_decay * average_state + (1.0 - polyak_decay) * weight_new  20.6 us
    pallas_call x1, Pallas kernels, finish(): pl.pallas_call(functools.partial(finish_kernel, sizes, n_experts), out_sh...  13.7 us
  transfers between devices with their start and end apart: 4, of which 0 were waited for; matrix products, arithmetic and copies ran while one was open for 0% of the time, Pallas kernels for 24%

profile of v9, /device:TPU:0, one launch (start us, length us, event | category | flops | bytes accessed | tf_op | source)
XLA Modules:
  0.0 475.9 jit_solution(3731957605394900728)
XLA Ops:
  0.7 1.4 copy.57.routing_ref
  2.0 187.3 %forward.1 = (bf16[5,768,768]{2,1,0:T(8,128)(2,1)}, f32[8,768]{1,0:T(8,128)}, f32[8,768]{1,0:T(8,128)}, f32[1024,128]{1,0:T(8,128)}, f32[1024,768]{1,0:T(8,128)}...) custom-call(s32[4,3]{1,0:T(4,128)} %length_ref.3, ...), custom_call_target="tpu_custom_call" | custom-call | flops 138000007168 | tf_op jit(solution)/shard_map/forward/pallas_call | solution.py:1109
  189.4 60.3 %head_step.1 = (f32[576,768]{1,0:T(8,128)}, f32[8,16,768]{2,1,0:T(8,128)}, f32[16,768]{1,0:T(8,128)}, f32[8,768]{1,0:T(8,128)}, f32[8,128]{1,0:T(8,128)}, /*index=5*/f32[8,768]{1,0:T(8,128)}) custom-call(f32[8,16,768]{2,1,0:T(8,128)} %get-tuple-element.65.part_ref, f32[16,768]{1,0:T(8,128)} %get-tuple-element.66.own_ref, ...), custom_call_target="tpu_custom_call" | custom-call | flops 48299999232 | tf_op jit(solution)/shard_map/head_step/pallas_call | solution.py:546
  249.7 65.7 %expert_backward.1 = (bf16[8,272,768]{2,1,0:T(8,128)(2,1)}, f32[8,8,384]{2,1,0:T(8,128)}, bf16[2,384,768]{2,1,0:T(8,128)(2,1)}, bf16[2,384,768]{2,1,0:T(8,128)(2...) custom-call(bf16[8,272,768]{2,1,0:T(8,128)(2,1)} %get-tuple-element.81.rows_ref, ...), custom_call_target="tpu_custom_call" | custom-call | flops 74750001152 | tf_op jit(solution)/shard_map/expert_backward/pallas_call | solution.py:1305
  315.3 1.9 collective-permute-start
  317.3 1.5 collective-permute-start.1
  318.8 1.6 collective-permute-start.2
  320.3 0.5 collective-permute-start.3
  320.8 0.6 broadcast_in_dim.3.mask_ref
  321.4 56.2 %dense_backward.1.g_ref = bf16[2,4,2,2,128,768]{5,4,3,2,1,0:T(8,128)(2,1)} custom-call(s32[4,3]{1,0:T(4,128)} %length_ref.3, s32[4,1,256]{2,1,0:T(1,128)} %broadcast_in_dim.3.mask_ref, bf16[1024,768]{1,0:T(8,128)(2,1)} %patch_ref.3, f32[1024,768]{1,0:T(8,128)} %get-tuple-element.70.x_zero_ref, bf16[1024,768]{1,0:T(8,128)(2,1)} %get-tuple-element.71.a_one_ref, ...), custom_call_target="tpu_custom_call" | custom-call | flops 57500000256 | tf_op jit(solution)/shard_map/dense_backward/pallas_call | solution.py:1484
  377.6 2.8 copy-done.1
  380.4 58.7 %scatter_dense.1 = (f32[128,768]{1,0:T(8,128)S(1)}, f32[8,128]{1,0:T(8,128)S(1)}) custom-call(bf16[2,4,2,2,128,768]{5,4,3,2,1,0:T(8,128)(2,1)S(1)} %copy-done.1), custom_call_target="tpu_custom_call" | custom-call | flops 51749998592 | tf_op jit(solution)/shard_map/scatter_dense/pallas_call | solution.py:304
  439.1 0.5 slice_bitcast_fusion
  439.6 0.0 copy-start.15
  439.6 0.0 copy-start.16
  439.7 0.0 copy-start.13
  439.8 13.7 %finish.1 = (f32[2,384,768]{2,1,0:T(8,128)S(1)}, f32[2,384,768]{2,1,0:T(8,128)S(1)}, f32[8,128]{1,0:T(8,128)S(1)}) custom-call(f32[8,128]{1,0:T(8,128)S(1)} %copy-done.2, f32[8,128]{1,0:T(8,128)S(1)} %get-tuple-element.93.dense_ref, f32[8,768]{1,0:T(8,128)S(1)} %copy-done, bf16[2,384,768]{2,1,0:T(8,128)(2,1)S(1)} %collective-permute-done.refs_0_, ...), custom_call_target="tpu_custom_call" | custom-call | flops 11500000256 | tf_op jit(solution)/shard_map/finish/pallas_call | solution.py:384
  453.5 0.6 fusion.14
  454.1 0.7 slice_multiply_fusion
  454.8 1.3 multiply_add_fusion.8
  456.2 1.3 multiply_add_fusion.10
  457.5 4.9 %multiply_add_fusion.4 = (f32[576,768]{1,0:T(8,128)}, f32[576,768]{1,0:T(8,128)}, f32[576,768]{1,0:T(8,128)}, f32[576,768]{1,0:T(8,128)}) fusion(f32[576,768]{1,0:T(8,128)S(1)} %copy-done.8, f32[576,768]{1,0:T(8,128)S(1)} %copy-done.7, f32[576,768]{1,0:T(8,128)S(1)} %copy-done.11, f32[]{:T(128)} %bitcast.4, f32[576,768]{1,0:T(8,128)S(1)} %copy-done.9, ...), kind=kLoop, calls=%fused_computation.12 | loop fusion | flops 8404992 | bytes 15925252 | tf_op jit(solution)/shard_map/add | solution.py:43
  462.4 2.7 multiply_add_fusion.6
  465.1 10.5 %multiply_add_fusion = (f32[2,384,768]{2,1,0:T(8,128)}, f32[2,384,768]{2,1,0:T(8,128)}, f32[2,384,768]{2,1,0:T(8,128)}, f32[2,384,768]{2,1,0:T(8,128)}, f32[2,38...) fusion(f32[2,384,768]{2,1,0:T(8,128)S(1)} %copy-done.5, ...), kind=kLoop, calls=%fused_computation.5 | loop fusion | flops 22413312 | bytes 42467332 | tf_op jit(solution)/shard_map/add | solution.py:43
  (44 shorter events, 0.1 us)
Async XLA Ops:
  249.7 71.2 %copy-start.21 = (s32[4,256]{1,0:T(4,128)S(1)}, s32[4,256]{1,0:T(4,128)}, u32[]{:S(2)}) copy-start(s32[4,256]{1,0:T(4,128)} %mask_ref.1) | copy-start | bytes 12292
  315.3 124.2 %collective-permute-start = (bf16[2,384,768]{2,1,0:T(8,128)(2,1)}, bf16[2,384,768]{2,1,0:T(8,128)(2,1)S(1)}, u32[]{:S(2)}, u32[]{:S(2)}) collective-permute-start(bf16[2,384,768]{2,1,0:T(8,128)(2,1)} %get-tuple-element.94), channel_id=1, source_target_pairs={{0,0},{8,1},{4,4},{12,5},{16,8},{24,9},{20,12},{28,13},{1,16},{9,1... | collective-permute-start | bytes 3538952 | tf_op jit(solution)/shard_map/ppermute | solution.py:1529
  317.3 122.3 %collective-permute-start.1 = (bf16[2,384,768]{2,1,0:T(8,128)(2,1)}, bf16[2,384,768]{2,1,0:T(8,128)(2,1)S(1)}, u32[]{:S(2)}, u32[]{:S(2)}) collective-permute-start(bf16[2,384,768]{2,1,0:T(8,128)(2,1)} %get-tuple-element.95), channel_id=1, source_target_pairs={{16,0},{24,1},{20,4},{28,5},{0,8},{8,9},{4,12},{12,13},{17,16},{25... | collective-permute-start | bytes 3538952 | tf_op jit(solution)/shard_map/ppermute | solution.py:1529
  318.8 120.8 %collective-permute-start.2 = (bf16[2,384,768]{2,1,0:T(8,128)(2,1)}, bf16[2,384,768]{2,1,0:T(8,128)(2,1)S(1)}, u32[]{:S(2)}, u32[]{:S(2)}) collective-permute-start(bf16[2,384,768]{2,1,0:T(8,128)(2,1)} %get-tuple-element.96), channel_id=1, source_target_pairs={{4,0},{12,1},{16,4},{24,5},{20,8},{28,9},{0,12},{8,13},{5,16},{13,... | collective-permute-start | bytes 3538952 | tf_op jit(solution)/shard_map/ppermute | solution.py:1529
  320.3 119.3 %collective-permute-start.3 = (bf16[2,384,768]{2,1,0:T(8,128)(2,1)}, bf16[2,384,768]{2,1,0:T(8,128)(2,1)}, u32[]{:S(2)}, u32[]{:S(2)}) collective-permute-start(bf16[2,384,768]{2,1,0:T(8,128)(2,1)} %get-tuple-element.97), channel_id=1, source_target_pairs={{20,0},{28,1},{0,4},{8,5},{4,8},{12,9},{16,12},{24,13},{21,16},{29... | collective-permute-start | bytes 3538952 | tf_op jit(solution)/shard_map/ppermute | solution.py:1529
  380.4 58.7 %copy-start = (f32[8,768]{1,0:T(8,128)S(1)}, f32[8,768]{1,0:T(8,128)}, u32[]{:S(2)}) copy-start(f32[8,768]{1,0:T(8,128)} %get-tuple-element.91.imp_ref) | copy-start | bytes 73732
  380.4 59.2 %copy-start.2 = (f32[8,128]{1,0:T(8,128)S(1)}, f32[8,128]{1,0:T(8,128)}, u32[]{:S(2)}) copy-start(f32[8,128]{1,0:T(8,128)} %get-tuple-element.69.head_ref) | copy-start | bytes 12292
  439.6 15.2 %copy-start.14 = (f32[6,24]{1,0:T(8,128)S(1)}, f32[6,24]{1,0:T(8,128)}, u32[]{:S(2)}) copy-start(f32[6,24]{1,0:T(8,128)} %norm_ref.1) | copy-start | bytes 1732
  439.6 15.2 %copy-start.15 = (f32[6,24]{1,0:T(8,128)S(1)}, f32[6,24]{1,0:T(8,128)}, u32[]{:S(2)}) copy-start(f32[6,24]{1,0:T(8,128)} %param.47) | copy-start | bytes 1732
  439.6 15.2 %copy-start.16 = (f32[6,24]{1,0:T(8,128)S(1)}, f32[6,24]{1,0:T(8,128)}, u32[]{:S(2)}) copy-start(f32[6,24]{1,0:T(8,128)} %param.45) | copy-start | bytes 1732
  439.6 15.2 %copy-start.17 = (f32[6,24]{1,0:T(8,128)S(1)}, f32[6,24]{1,0:T(8,128)}, u32[]{:S(2)}) copy-start(f32[6,24]{1,0:T(8,128)} %param.46) | copy-start | bytes 1732
  439.7 16.5 %copy-start.13 = (f32[24,8]{0,1:T(8,128)S(1)}, f32[24,8]{0,1:T(8,128)}, u32[]{:S(2)}) copy-start(f32[24,8]{0,1:T(8,128)} %param.40) | copy-start | bytes 2308
  439.7 16.5 %copy-start.18 = (f32[24,8]{0,1:T(8,128)S(1)}, f32[24,8]{0,1:T(8,128)}, u32[]{:S(2)}) copy-start(f32[24,8]{0,1:T(8,128)} %param.43) | copy-start | bytes 2308
  439.7 16.5 %copy-start.19 = (f32[24,8]{0,1:T(8,128)S(1)}, f32[24,8]{0,1:T(8,128)}, u32[]{:S(2)}) copy-start(f32[24,8]{0,1:T(8,128)} %param.41) | copy-start | bytes 2308
  439.7 16.5 %copy-start.20 = (f32[24,8]{0,1:T(8,128)S(1)}, f32[24,8]{0,1:T(8,128)}, u32[]{:S(2)}) copy-start(f32[24,8]{0,1:T(8,128)} %param.42) | copy-start | bytes 2308
  439.7 17.7 %copy-start.7 = (f32[576,768]{1,0:T(8,128)S(1)}, f32[576,768]{1,0:T(8,128)}, u32[]{:S(2)}) copy-start(f32[576,768]{1,0:T(8,128)} %head_ref.1) | copy-start | bytes 5308420
  439.7 17.7 %copy-start.8 = (f32[576,768]{1,0:T(8,128)S(1)}, f32[576,768]{1,0:T(8,128)}, u32[]{:S(2)}) copy-start(f32[576,768]{1,0:T(8,128)} %param.59) | copy-start | bytes 5308420
  439.7 17.7 %copy-start.9 = (f32[576,768]{1,0:T(8,128)S(1)}, f32[576,768]{1,0:T(8,128)}, u32[]{:S(2)}) copy-start(f32[576,768]{1,0:T(8,128)} %param.57) | copy-start | bytes 5308420
  439.7 17.7 %copy-start.10 = (f32[576,768]{1,0:T(8,128)S(1)}, f32[576,768]{1,0:T(8,128)}, u32[]{:S(2)}) copy-start(f32[576,768]{1,0:T(8,128)} %param.58) | copy-start | bytes 5308420
  439.8 17.7 %copy-start.11 = (f32[576,768]{1,0:T(8,128)S(1)}, f32[576,768]{1,0:T(8,128)}, u32[]{:S(2)}) copy-start(f32[576,768]{1,0:T(8,128)} %get-tuple-element.102) | copy-start | bytes 5308420
  457.5 4.9 %copy-start.12 = (f32[5,24,768]{2,1,0:T(8,128)S(1)}, f32[5,24,768]{2,1,0:T(8,128)}, u32[]{:S(2)}) copy-start(f32[5,24,768]{2,1,0:T(8,128)} %dense_ref.1) | copy-start | bytes 1105924
  457.5 7.6 %copy-start.4 = (f32[2,384,768]{2,1,0:T(8,128)S(1)}, f32[2,384,768]{2,1,0:T(8,128)}, u32[]{:S(2)}) copy-start(f32[2,384,768]{2,1,0:T(8,128)} %out_ref.1) | copy-start | bytes 7077892
  457.5 7.6 %copy-start.5 = (f32[2,384,768]{2,1,0:T(8,128)S(1)}, f32[2,384,768]{2,1,0:T(8,128)}, u32[]{:S(2)}) copy-start(f32[2,384,768]{2,1,0:T(8,128)} %param.55) | copy-start | bytes 7077892
  457.5 7.6 %copy-start.6 = (f32[2,384,768]{2,1,0:T(8,128)S(1)}, f32[2,384,768]{2,1,0:T(8,128)}, u32[]{:S(2)}) copy-start(f32[2,384,768]{2,1,0:T(8,128)} %param.53) | copy-start | bytes 7077892
  (2 other events, 5.5 us)

commit v10 on v9

--- a/solution.py
+++ b/solution.py
@@ -644,14 +644,15 @@
         bound = bound + lengths[row, image]
         query_seg = query_seg + jnp.where(query >= bound, 1, 0)
         key_seg = key_seg + jnp.where(key >= bound, 1, 0)
-    return (query_seg == key_seg) & ((valid_row > 0) | (query == key))
+    allowed = (query_seg == key_seg) & ((valid_row > 0) | (query == key))
+    return jnp.where(allowed, 1.0, 0.0)
 
 
 TILE = 32
 
 
-def tiles(count):
-    return [slice(start, min(start + TILE, count)) for start in range(0, count, TILE)]
+def tiles(count, size=TILE):
+    return [slice(start, min(start + size, count)) for start in range(0, count, size)]
 
 
 def step_order(blocks):
@@ -860,13 +861,17 @@
             outs = []
             for side in range(2):
                 held = jnp.where((lane < 64) == (side == 0), query, jnp.zeros_like(query))
-                scores = jnp.where(open_to, dot_f32(held, key, NT) * 64**-0.5, mask_fill)
-                top = jnp.max(scores, 1, keepdims=True)
-                powers = jnp.exp(scores - top)
-                whole_sum = jnp.sum(powers, 1, keepdims=True)
-                probs = (powers * (1.0 / whole_sum)).astype(jnp.bfloat16)
-                outs.append(dot_f32(probs, value, NN))
-                logs = jnp.where(lane == 2 * pair + side, top + jnp.log(whole_sum), logs)
+                raw = dot_f32(held, key, NT)
+                probs, sums = [], []
+                for spot in tiles(span, 64):
+                    scores = jnp.where(open_to[spot] > 0.0, raw[spot] * 64**-0.5, mask_fill)
+                    top = jnp.max(scores, 1, keepdims=True)
+                    powers = jnp.exp(scores - top)
+                    whole_sum = jnp.sum(powers, 1, keepdims=True)
+                    probs.append((powers * (1.0 / whole_sum)).astype(jnp.bfloat16))
+                    sums.append(top + jnp.log(whole_sum))
+                outs.append(dot_f32(jnp.concatenate(probs, 0), value, NN))
+                logs = jnp.where(lane == 2 * pair + side, jnp.concatenate(sums, 0), logs)
             att_buf[:, pair * 128 : (pair + 1) * 128] = jnp.where(
                 lane < 64, outs[0], outs[1]
             ).astype(jnp.bfloat16)
@@ -895,6 +900,30 @@
 
     columns = col_ref[...]
     places[...] = columns.T[:8]
+    def rows_of(member):
+        slots = lax.broadcasted_iota(jnp.int32, (padded, tokens), 0) + member * padded
+        slots = slots.astype(jnp.float32)
+        match = (slots == places[0:1]) | (slots == places[1:2])
+        match = jnp.where(match, 1.0, 0.0).astype(jnp.bfloat16)
+        return dot_f32(match, a_two_ref[...], NN).astype(jnp.bfloat16)
+
+    def row_copy(member, source):
+        return send(
+            send_rows.at[member], rows_in.at[source], r_out.at[member], r_in.at[source], at.of_member(member)
+        )
+
+    def detail_copy(member, source):
+        return send(
+            send_detail.at[member], detail_in.at[source], m_out.at[member], m_in.at[source], at.of_member(member)
+        )
+
+    def dispatch_step(index, carry):
+        member = lax.rem(at.member + index, n_experts)
+        send_rows[member] = rows_of(member)
+        row_copy(member, at.member).start()
+        return carry
+
+    lax.fori_loop(1, n_experts, dispatch_step, 0)
     lane = lax.broadcasted_iota(jnp.int32, (tokens, 128), 1)
     kind, expert = lax.div(lane, n_experts), lax.rem(lane, n_experts).astype(jnp.float32)
     slot_lane = lax.broadcasted_iota(jnp.int32, (tokens, send_detail.shape[2]), 1).astype(jnp.float32)
@@ -922,31 +951,8 @@
             send_detail[index, spot : spot + 1] = value[index : index + 1]
         send_detail[index, 3:8] = jnp.zeros((5, send_detail.shape[2]), jnp.float32)
 
-    def rows_of(member):
-        slots = lax.broadcasted_iota(jnp.int32, (padded, tokens), 0) + member * padded
-        slots = slots.astype(jnp.float32)
-        match = (slots == places[0:1]) | (slots == places[1:2])
-        match = jnp.where(match, 1.0, 0.0).astype(jnp.bfloat16)
-        return dot_f32(match, a_two_ref[...], NN).astype(jnp.bfloat16)
-
-    def row_copy(member, source):
-        return send(
-            send_rows.at[member], rows_in.at[source], r_out.at[member], r_in.at[source], at.of_member(member)
-        )
-
-    def detail_copy(member, source):
-        return send(
-            send_detail.at[member], detail_in.at[source], m_out.at[member], m_in.at[source], at.of_member(member)
-        )
-
-    def dispatch_step(index, carry):
-        member = lax.rem(at.member + index, n_experts)
-        send_rows[member] = rows_of(member)
-        row_copy(member, at.member).start()
+    for member in others(at.member, n_experts):
         detail_copy(member, at.member).start()
-        return carry
-
-    lax.fori_loop(1, n_experts, dispatch_step, 0)
     rows_in[at.member] = rows_of(at.member)
     detail_in[at.member] = send_detail[at.member]
     a_two_copy = pltpu.make_async_copy(a_two_ref, a_two_out, keep_sem.at[0])
@@ -1338,16 +1344,16 @@
 def dense_backward_kernel(
     sizes, n_experts, images, padded, length_ref, mask_ref, patch_ref, x_zero_ref, a_one_ref, qkv_ref, att_ref,
     x_one_ref, a_two_ref, prob_ref, lse_ref, col_ref, w_ref, gain_ref, router_ref, back_ref, gate_ref,
-    pool_ref, imp_ref, third_ref, out_ref, grads, g_router, g_norm, d_qkv
+    pool_ref, imp_ref, third_ref, out_ref, grads, g_norm, d_qkv, d_atts, d_zeros, d_routers
 ):
     row = pl.program_id(0)
-    span, width = patch_ref.shape
+    span, width = x_zero_ref.shape
     mats, rows = grads.shape[0], width // (8 * sizes["g"] * sizes["x"])
+
+    here = pl.ds(pl.multiple_of(row * span, 16), span)
 
     @pl.when(row == 0)
     def _():
-        grads[...] = jnp.zeros_like(grads)
-        g_router[...] = jnp.zeros_like(g_router)
         g_norm[...] = third_ref[...]
 
     columns = col_ref[...]
@@ -1384,7 +1390,7 @@
     d_probs = d_probs + jnp.where(number == columns[:, 6:7], d_gate_two, 0.0)
     probs = prob_ref[...]
     d_router = (probs * (d_probs - jnp.sum(probs * d_probs, 1, keepdims=True))).astype(jnp.bfloat16)
-    g_router[...] += dot_f32(d_router, a_two_ref[...], TN)
+    d_routers[here] = d_router
     routers = router_ref[...].astype(jnp.bfloat16)
     if routers.shape[0] < 128:
         routers = jnp.concatenate(
@@ -1400,7 +1406,7 @@
         weight = jnp.where(image == place.astype(jnp.float32), pool, 0.0)
         d_x_one = d_x_one + weight * pool_ref[pl.ds(place, 1)]
     d_att = d_x_one.astype(jnp.bfloat16)
-    grads[4] += dot_f32(att_ref[...], d_att, TN)
+    d_atts[here] = d_att
     d_out = dot_f32(d_att, w_ref[4], NT).astype(jnp.bfloat16)
     open_to = allowed_slots(length_ref, row, images, mask_ref[0], span)
     logs = lse_ref[...]
@@ -1414,35 +1420,45 @@
         for side in range(2):
             left = (lane < 64) == (side == 0)
             held = jnp.where(left, query, jnp.zeros_like(query))
-            scores = jnp.where(open_to, dot_f32(held, key, NT) * 64**-0.5, mask_fill)
-            total = logs[:, 2 * pair + side : 2 * pair + side + 1]
-            chance = jnp.exp(scores - total)
+            raw = dot_f32(held, key, NT)
             d_held = jnp.where(left, d_pair, jnp.zeros_like(d_pair))
-            d_chance = dot_f32(d_held, value, NT)
-            d_value = dot_f32(chance.astype(jnp.bfloat16), d_pair, TN)
-            d_scores = chance * (d_chance - jnp.sum(chance * d_chance, 1, keepdims=True))
-            d_scores = d_scores.astype(jnp.bfloat16)
+            d_raw = dot_f32(d_held, value, NT)
+            chances, d_scores = [], []
+            for spot in tiles(span, 64):
+                scores = jnp.where(open_to[spot] > 0.0, raw[spot] * 64**-0.5, mask_fill)
+                chance = jnp.exp(scores - logs[spot, 2 * pair + side : 2 * pair + side + 1])
+                chances.append(chance.astype(jnp.bfloat16))
+                d_chance = d_raw[spot]
+                d_score = chance * (d_chance - jnp.sum(chance * d_chance, 1, keepdims=True))
+                d_scores.append(d_score.astype(jnp.bfloat16))
+            d_value = dot_f32(jnp.concatenate(chances, 0), d_pair, TN)
+            d_scores = jnp.concatenate(d_scores, 0)
             d_query = dot_f32(d_scores, key, NN) * 64**-0.5
             d_key = dot_f32(d_scores, query, TN) * 64**-0.5
             found.append((d_query, d_key, d_value))
         for part in range(3):
-            d_qkv[:, part * width + pair * 128 : part * width + (pair + 1) * 128] = jnp.where(
+            d_qkv[here, part * width + pair * 128 : part * width + (pair + 1) * 128] = jnp.where(
                 lane < 64, found[0][part], found[1][part]
             ).astype(jnp.bfloat16)
     d_a_one = None
     for part in range(3):
-        piece = d_qkv[:, part * width : (part + 1) * width]
-        grads[1 + part] += dot_f32(a_one_ref[...], piece, TN)
+        piece = d_qkv[here, part * width : (part + 1) * width]
         found = dot_f32(piece, w_ref[1 + part], NT)
         d_a_one = found if d_a_one is None else d_a_one + found
     scaled, scale = norm_parts(x_zero_ref[...])
     g_norm[0:1] += jnp.sum(d_a_one * scaled, 0, keepdims=True)
     g_norm[3:4] += jnp.sum(d_a_one, 0, keepdims=True)
     d_x_zero = norm_back(d_a_one, scaled, scale, gain_ref[0:1]) + d_x_one
-    grads[0] += dot_f32(patch_ref[...], d_x_zero.astype(jnp.bfloat16), TN)
+    d_zeros[here] = d_x_zero.astype(jnp.bfloat16)
 
     @pl.when(row == pl.num_programs(0) - 1)
     def _():
+        grads[0] = dot_f32(patch_ref[...], d_zeros[...], TN)
+        for part in range(3):
+            piece = d_qkv[:, part * width : (part + 1) * width]
+            grads[1 + part] = dot_f32(a_one_ref[...], piece, TN)
+        grads[4] = dot_f32(att_ref[...], d_atts[...], TN)
+        g_router = dot_f32(d_routers[...], a_two_ref[...], TN)
         Z, Y, X = QUAD, sizes["g"], sizes["x"]
         tall = max(8, n_experts)
         norms = g_norm[...]
@@ -1488,17 +1504,19 @@
             (2, QUAD, sizes["x"], sizes["g"], depth, width), jnp.bfloat16
         ),
         in_specs=[
-            whole(pltpu.SMEM), pl.BlockSpec((1, 1, span), lambda i: (i, 0, 0)), block(width),
-            block(width), block(width), block(3 * width), block(width), block(width), block(width),
+            whole(pltpu.SMEM), pl.BlockSpec((1, 1, span), lambda i: (i, 0, 0)), whole(),
+            block(width), whole(), block(3 * width), whole(), block(width), whole(),
             block(128), block(128), block(128),
         ]
         + [whole()] * 8,
         out_specs=whole(),
         scratch_shapes=[
             VMEM((mats, width, width), jnp.float32),
-            VMEM((128, width), jnp.float32),
             VMEM((8, width), jnp.float32),
-            VMEM((span, 3 * width), jnp.bfloat16),
+            VMEM((tokens, 3 * width), jnp.bfloat16),
+            VMEM((tokens, width), jnp.bfloat16),
+            VMEM((tokens, width), jnp.bfloat16),
+            VMEM((tokens, 128), jnp.bfloat16),
         ],
         compiler_params=pltpu.CompilerParams(vmem_limit_bytes=60 * MIB),
         cost_estimate=cost(50),

time: 479 us -> 477 us (level)
    pallas_call x1, Pallas kernels: 60.3 us -> 51.2 us  [head_step(): pl.pallas_call(functools.partial(head_kernel, sizes, images), out_shape=(...]
    pallas_call x1, Pallas kernels: 187 us -> 195 us  [forward(): pl.pallas_call(functools.partial(forward_kernel, sizes, n_experts, length...]
where the time goes in v10:
time: 477 us; the launch traced here: 474 us
  Pallas kernels  440 us (92%)
  other arithmetic  21.3 us (4%)
  local copies, waits for them, and re-layouts  5.95 us (1%)
  starting transfers between devices  5.46 us (1%)
    pallas_call x1, Pallas kernels, forward(): pl.pallas_call(functools.partial(forward_kernel, sizes, n_experts, length...  195 us
    pallas_call x1, Pallas kernels, expert_backward(): pl.pallas_call(functools.partial(expert_backward_kernel, sizes, padded),...  65.9 us
    pallas_call x1, Pallas kernels, dense_backward(): pl.pallas_call(functools.partial(dense_backward_kernel, sizes, n_experts,...  59.1 us
    pallas_call x1, Pallas kernels, scatter_dense(): pl.pallas_call(functools.partial(scatter_kernel, sizes), out_shape=(jax.S...  55.7 us
    pallas_call x1, Pallas kernels, head_step(): pl.pallas_call(functools.partial(head_kernel, sizes, images), out_shape=(...  51.2 us
    add x5, other arithmetic, adam_update(): polyak_decay * average_state + (1.0 - polyak_decay) * weight_new  20.6 us
    pallas_call x1, Pallas kernels, finish(): pl.pallas_call(functools.partial(finish_kernel, sizes, n_experts), out_sh...  13.1 us
  transfers between devices with their start and end apart: 4, of which 0 were waited for; matrix products, arithmetic and copies ran while one was open for 0% of the time, Pallas kernels for 24%

profile of v10, /device:TPU:0, one launch (start us, length us, event | category | flops | bytes accessed | tf_op | source)
XLA Modules:
  0.0 473.8 jit_solution(5459068444347320567)
XLA Ops:
  0.7 1.4 copy.57.routing_ref
  2.0 194.8 %forward.1 = (bf16[5,768,768]{2,1,0:T(8,128)(2,1)}, f32[8,768]{1,0:T(8,128)}, f32[8,768]{1,0:T(8,128)}, f32[1024,128]{1,0:T(8,128)}, f32[1024,768]{1,0:T(8,128)}...) custom-call(s32[4,3]{1,0:T(4,128)} %length_ref.3, ...), custom_call_target="tpu_custom_call" | custom-call | flops 138000007168 | tf_op jit(solution)/shard_map/forward/pallas_call | solution.py:1115
  196.8 51.2 %head_step.1 = (f32[576,768]{1,0:T(8,128)}, f32[8,16,768]{2,1,0:T(8,128)}, f32[16,768]{1,0:T(8,128)}, f32[8,768]{1,0:T(8,128)}, f32[8,128]{1,0:T(8,128)}, /*index=5*/f32[8,768]{1,0:T(8,128)}) custom-call(f32[8,16,768]{2,1,0:T(8,128)} %get-tuple-element.65.part_ref, f32[16,768]{1,0:T(8,128)} %get-tuple-element.66.own_ref, ...), custom_call_target="tpu_custom_call" | custom-call | flops 48299999232 | tf_op jit(solution)/shard_map/head_step/pallas_call | solution.py:546
  248.0 65.9 %expert_backward.1 = (bf16[8,272,768]{2,1,0:T(8,128)(2,1)}, f32[8,8,384]{2,1,0:T(8,128)}, bf16[2,384,768]{2,1,0:T(8,128)(2,1)}, bf16[2,384,768]{2,1,0:T(8,128)(2...) custom-call(bf16[8,272,768]{2,1,0:T(8,128)(2,1)} %get-tuple-element.81.rows_ref, ...), custom_call_target="tpu_custom_call" | custom-call | flops 74750001152 | tf_op jit(solution)/shard_map/expert_backward/pallas_call | solution.py:1311
  313.9 1.9 collective-permute-start
  315.9 1.5 collective-permute-start.1
  317.4 1.6 collective-permute-start.2
  318.9 0.5 collective-permute-start.3
  319.4 0.6 broadcast_in_dim.3.mask_ref
  320.0 59.1 %dense_backward.1.g_ref = bf16[2,4,2,2,128,768]{5,4,3,2,1,0:T(8,128)(2,1)} custom-call(s32[4,3]{1,0:T(4,128)} %length_ref.3, s32[4,1,256]{2,1,0:T(1,128)} %broadcast_in_dim.3.mask_ref, bf16[1024,768]{1,0:T(8,128)(2,1)} %patch_ref.3, f32[1024,768]{1,0:T(8,128)} %get-tuple-element.70.x_zero_ref, bf16[1024,768]{1,0:T(8,128)(2,1)} %get-tuple-element.71.a_one_ref, ...), custom_call_target="tpu_custom_call" | custom-call | flops 57500000256 | tf_op jit(solution)/shard_map/dense_backward/pallas_call | solution.py:1500
  379.2 2.8 copy-done.1
  381.9 55.7 %scatter_dense.1 = (f32[128,768]{1,0:T(8,128)S(1)}, f32[8,128]{1,0:T(8,128)S(1)}) custom-call(bf16[2,4,2,2,128,768]{5,4,3,2,1,0:T(8,128)(2,1)S(1)} %copy-done.1), custom_call_target="tpu_custom_call" | custom-call | flops 51749998592 | tf_op jit(solution)/shard_map/scatter_dense/pallas_call | solution.py:304
  437.7 0.5 slice_bitcast_fusion
  438.2 0.0 copy-start.15
  438.2 0.0 copy-start.16
  438.3 0.0 copy-start.13
  438.4 13.1 %finish.1 = (f32[2,384,768]{2,1,0:T(8,128)S(1)}, f32[2,384,768]{2,1,0:T(8,128)S(1)}, f32[8,128]{1,0:T(8,128)S(1)}) custom-call(f32[8,128]{1,0:T(8,128)S(1)} %copy-done.2, f32[8,128]{1,0:T(8,128)S(1)} %get-tuple-element.93.dense_ref, f32[8,768]{1,0:T(8,128)S(1)} %copy-done, bf16[2,384,768]{2,1,0:T(8,128)(2,1)S(1)} %collective-permute-done.refs_0_, ...), custom_call_target="tpu_custom_call" | custom-call | flops 11500000256 | tf_op jit(solution)/shard_map/finish/pallas_call | solution.py:384
  451.5 0.6 fusion.14
  452.1 0.7 slice_multiply_fusion
  452.8 1.3 multiply_add_fusion.8
  454.1 1.3 multiply_add_fusion.10
  455.5 4.9 %multiply_add_fusion.4 = (f32[576,768]{1,0:T(8,128)}, f32[576,768]{1,0:T(8,128)}, f32[576,768]{1,0:T(8,128)}, f32[576,768]{1,0:T(8,128)}) fusion(f32[576,768]{1,0:T(8,128)S(1)} %copy-done.8, f32[576,768]{1,0:T(8,128)S(1)} %copy-done.7, f32[576,768]{1,0:T(8,128)S(1)} %copy-done.11, f32[]{:T(128)} %bitcast.4, f32[576,768]{1,0:T(8,128)S(1)} %copy-done.9, ...), kind=kLoop, calls=%fused_computation.12 | loop fusion | flops 8404992 | bytes 15925252 | tf_op jit(solution)/shard_map/add | solution.py:43
  460.4 2.7 multiply_add_fusion.6
  463.1 10.5 %multiply_add_fusion = (f32[2,384,768]{2,1,0:T(8,128)}, f32[2,384,768]{2,1,0:T(8,128)}, f32[2,384,768]{2,1,0:T(8,128)}, f32[2,384,768]{2,1,0:T(8,128)}, f32[2,38...) fusion(f32[2,384,768]{2,1,0:T(8,128)S(1)} %copy-done.5, ...), kind=kLoop, calls=%fused_computation.5 | loop fusion | flops 22413312 | bytes 42467332 | tf_op jit(solution)/shard_map/add | solution.py:43
  (44 shorter events, 0.1 us)
Async XLA Ops:
  248.0 71.4 %copy-start.21 = (s32[4,256]{1,0:T(4,128)S(1)}, s32[4,256]{1,0:T(4,128)}, u32[]{:S(2)}) copy-start(s32[4,256]{1,0:T(4,128)} %mask_ref.1) | copy-start | bytes 12292
  313.9 124.2 %collective-permute-start = (bf16[2,384,768]{2,1,0:T(8,128)(2,1)}, bf16[2,384,768]{2,1,0:T(8,128)(2,1)S(1)}, u32[]{:S(2)}, u32[]{:S(2)}) collective-permute-start(bf16[2,384,768]{2,1,0:T(8,128)(2,1)} %get-tuple-element.94), channel_id=1, source_target_pairs={{0,0},{8,1},{4,4},{12,5},{16,8},{24,9},{20,12},{28,13},{1,16},{9,1... | collective-permute-start | bytes 3538952 | tf_op jit(solution)/shard_map/ppermute | solution.py:1547
  315.9 122.3 %collective-permute-start.1 = (bf16[2,384,768]{2,1,0:T(8,128)(2,1)}, bf16[2,384,768]{2,1,0:T(8,128)(2,1)S(1)}, u32[]{:S(2)}, u32[]{:S(2)}) collective-permute-start(bf16[2,384,768]{2,1,0:T(8,128)(2,1)} %get-tuple-element.95), channel_id=1, source_target_pairs={{16,0},{24,1},{20,4},{28,5},{0,8},{8,9},{4,12},{12,13},{17,16},{25... | collective-permute-start | bytes 3538952 | tf_op jit(solution)/shard_map/ppermute | solution.py:1547
  317.4 120.8 %collective-permute-start.2 = (bf16[2,384,768]{2,1,0:T(8,128)(2,1)}, bf16[2,384,768]{2,1,0:T(8,128)(2,1)S(1)}, u32[]{:S(2)}, u32[]{:S(2)}) collective-permute-start(bf16[2,384,768]{2,1,0:T(8,128)(2,1)} %get-tuple-element.96), channel_id=1, source_target_pairs={{4,0},{12,1},{16,4},{24,5},{20,8},{28,9},{0,12},{8,13},{5,16},{13,... | collective-permute-start | bytes 3538952 | tf_op jit(solution)/shard_map/ppermute | solution.py:1547
  318.9 119.3 %collective-permute-start.3 = (bf16[2,384,768]{2,1,0:T(8,128)(2,1)}, bf16[2,384,768]{2,1,0:T(8,128)(2,1)}, u32[]{:S(2)}, u32[]{:S(2)}) collective-permute-start(bf16[2,384,768]{2,1,0:T(8,128)(2,1)} %get-tuple-element.97), channel_id=1, source_target_pairs={{20,0},{28,1},{0,4},{8,5},{4,8},{12,9},{16,12},{24,13},{21,16},{29... | collective-permute-start | bytes 3538952 | tf_op jit(solution)/shard_map/ppermute | solution.py:1547
  381.9 55.7 %copy-start = (f32[8,768]{1,0:T(8,128)S(1)}, f32[8,768]{1,0:T(8,128)}, u32[]{:S(2)}) copy-start(f32[8,768]{1,0:T(8,128)} %get-tuple-element.91.imp_ref) | copy-start | bytes 73732
  381.9 56.3 %copy-start.2 = (f32[8,128]{1,0:T(8,128)S(1)}, f32[8,128]{1,0:T(8,128)}, u32[]{:S(2)}) copy-start(f32[8,128]{1,0:T(8,128)} %get-tuple-element.69.head_ref) | copy-start | bytes 12292
  438.2 14.6 %copy-start.14 = (f32[6,24]{1,0:T(8,128)S(1)}, f32[6,24]{1,0:T(8,128)}, u32[]{:S(2)}) copy-start(f32[6,24]{1,0:T(8,128)} %norm_ref.1) | copy-start | bytes 1732
  438.2 14.6 %copy-start.15 = (f32[6,24]{1,0:T(8,128)S(1)}, f32[6,24]{1,0:T(8,128)}, u32[]{:S(2)}) copy-start(f32[6,24]{1,0:T(8,128)} %param.47) | copy-start | bytes 1732
  438.2 14.6 %copy-start.16 = (f32[6,24]{1,0:T(8,128)S(1)}, f32[6,24]{1,0:T(8,128)}, u32[]{:S(2)}) copy-start(f32[6,24]{1,0:T(8,128)} %param.45) | copy-start | bytes 1732
  438.3 14.6 %copy-start.17 = (f32[6,24]{1,0:T(8,128)S(1)}, f32[6,24]{1,0:T(8,128)}, u32[]{:S(2)}) copy-start(f32[6,24]{1,0:T(8,128)} %param.46) | copy-start | bytes 1732
  438.3 15.8 %copy-start.13 = (f32[24,8]{0,1:T(8,128)S(1)}, f32[24,8]{0,1:T(8,128)}, u32[]{:S(2)}) copy-start(f32[24,8]{0,1:T(8,128)} %param.40) | copy-start | bytes 2308
  438.3 15.8 %copy-start.18 = (f32[24,8]{0,1:T(8,128)S(1)}, f32[24,8]{0,1:T(8,128)}, u32[]{:S(2)}) copy-start(f32[24,8]{0,1:T(8,128)} %param.43) | copy-start | bytes 2308
  438.3 15.8 %copy-start.19 = (f32[24,8]{0,1:T(8,128)S(1)}, f32[24,8]{0,1:T(8,128)}, u32[]{:S(2)}) copy-start(f32[24,8]{0,1:T(8,128)} %param.41) | copy-start | bytes 2308
  438.3 15.8 %copy-start.20 = (f32[24,8]{0,1:T(8,128)S(1)}, f32[24,8]{0,1:T(8,128)}, u32[]{:S(2)}) copy-start(f32[24,8]{0,1:T(8,128)} %param.42) | copy-start | bytes 2308
  438.3 17.1 %copy-start.7 = (f32[576,768]{1,0:T(8,128)S(1)}, f32[576,768]{1,0:T(8,128)}, u32[]{:S(2)}) copy-start(f32[576,768]{1,0:T(8,128)} %head_ref.1) | copy-start | bytes 5308420
  438.3 17.1 %copy-start.8 = (f32[576,768]{1,0:T(8,128)S(1)}, f32[576,768]{1,0:T(8,128)}, u32[]{:S(2)}) copy-start(f32[576,768]{1,0:T(8,128)} %param.59) | copy-start | bytes 5308420
  438.3 17.1 %copy-start.9 = (f32[576,768]{1,0:T(8,128)S(1)}, f32[576,768]{1,0:T(8,128)}, u32[]{:S(2)}) copy-start(f32[576,768]{1,0:T(8,128)} %param.57) | copy-start | bytes 5308420
  438.4 17.1 %copy-start.10 = (f32[576,768]{1,0:T(8,128)S(1)}, f32[576,768]{1,0:T(8,128)}, u32[]{:S(2)}) copy-start(f32[576,768]{1,0:T(8,128)} %param.58) | copy-start | bytes 5308420
  438.4 17.1 %copy-start.11 = (f32[576,768]{1,0:T(8,128)S(1)}, f32[576,768]{1,0:T(8,128)}, u32[]{:S(2)}) copy-start(f32[576,768]{1,0:T(8,128)} %get-tuple-element.102) | copy-start | bytes 5308420
  455.5 4.9 %copy-start.12 = (f32[5,24,768]{2,1,0:T(8,128)S(1)}, f32[5,24,768]{2,1,0:T(8,128)}, u32[]{:S(2)}) copy-start(f32[5,24,768]{2,1,0:T(8,128)} %dense_ref.1) | copy-start | bytes 1105924
  455.5 7.6 %copy-start.4 = (f32[2,384,768]{2,1,0:T(8,128)S(1)}, f32[2,384,768]{2,1,0:T(8,128)}, u32[]{:S(2)}) copy-start(f32[2,384,768]{2,1,0:T(8,128)} %out_ref.1) | copy-start | bytes 7077892
  455.5 7.6 %copy-start.5 = (f32[2,384,768]{2,1,0:T(8,128)S(1)}, f32[2,384,768]{2,1,0:T(8,128)}, u32[]{:S(2)}) copy-start(f32[2,384,768]{2,1,0:T(8,128)} %param.55) | copy-start | bytes 7077892
  455.5 7.6 %copy-start.6 = (f32[2,384,768]{2,1,0:T(8,128)S(1)}, f32[2,384,768]{2,1,0:T(8,128)}, u32[]{:S(2)}) copy-start(f32[2,384,768]{2,1,0:T(8,128)} %param.53) | copy-start | bytes 7077892
  (2 other events, 5.5 us)

commit v11 on v10

--- a/solution.py
+++ b/solution.py
@@ -133,7 +133,7 @@
     return peers + [at.sibling()]
 
 
-def gather_dense(at, rows, mats, count, land, sems, started, beside, idle):
+def gather_dense(at, rows, mats, land, w_ref, sems, started, beside, idle):
     Z, Y, X = at.Z, at.Y, at.X
     depth = land.shape[4]
     cut = depth // 2 // 16 * 16
@@ -179,6 +179,22 @@
             send(line, line, yb_out.at[z, y], yb_in.at[z, y], at.at(y=y)).wait_recv()
         plane = land.at[at.c, z]
         begin(send(plane, plane, c_out.at[z], c_in.at[z], at.sibling()))
+
+    def place(z):
+        plane = land.at[1 - at.c, z]
+        send(plane, plane, c_out.at[z], c_in.at[z], at.sibling()).wait_recv()
+        group = 16 // math.gcd(16, rows)
+        cores = [(c, x, y) for y in range(Y) for x in range(X) for c in range(2)]
+        for start in range(0, len(cores), group):
+            spot = pl.multiple_of((z * len(cores) + start) * rows, 16)
+            for mat in range(mats):
+                w_ref[mat, pl.ds(spot, group * rows)] = jnp.concatenate(
+                    [
+                        land[c, z, x, y, mat * rows : (mat + 1) * rows]
+                        for c, x, y in cores[start : start + group]
+                    ],
+                    0,
+                )
 
     for step in range(Z + 2):
         if step < Z:
@@ -195,20 +211,14 @@
             two(order[step - 1])
         if 0 <= step - 2 < Z:
             three(order[step - 2])
-    for z in order:
-        plane = land.at[1 - at.c, z]
-        send(plane, plane, c_out.at[z], c_in.at[z], at.sibling()).wait_recv()
-
-
-def assemble_dense(at, rows, mats, count, land, w_ref, gain_ref, router_ref):
+        if 0 <= step - 3 < Z:
+            place(order[step - 3])
+    place(order[Z - 1])
+
+
+def gather_small(at, rows, mats, count, land, gain_ref, router_ref):
     chips = [(z, y, x) for z in range(at.Z) for y in range(at.Y) for x in range(at.X)]
     cores = [(c, z, x, y) for z, y, x in chips for c in range(2)]
-    group = 16 // math.gcd(16, rows)
-    for start in range(0, len(cores), group):
-        for mat in range(mats):
-            w_ref[mat, start * rows : (start + group) * rows] = jnp.concatenate(
-                [land[spot][mat * rows : (mat + 1) * rows] for spot in cores[start : start + group]], 0
-            )
     base = mats * rows
     tails = [land[spot][base : base + count].astype(jnp.float32) for spot in cores]
     gain_ref[...] = jnp.concatenate([tail[:8, :rows] for tail in tails], 1)
@@ -569,7 +579,7 @@
         + [by_member, by_member, by_chip, by_chip, dma((2,)), dma((2,)), by_chip, by_chip]
         + [by_member, by_member],
         compiler_params=pltpu.CompilerParams(
-            collective_id=4, has_side_effects=True, vmem_limit_bytes=56 * MIB
+            collective_id=4, has_side_effects=True, vmem_limit_bytes=(56 if wide > 1024 else 28) * MIB
         ),
         cost_estimate=cost(42),
         name="head_step",
@@ -724,13 +734,14 @@
         copy.start()
     depth = land.shape[4]
     routing = routing_ref[...]
-    routing = jnp.concatenate([routing, jnp.zeros((rows_own, 128 - n_experts), jnp.float32)], 1)
-    routing = jnp.concatenate([routing, jnp.zeros((128 - rows_own, 128), jnp.float32)], 0).T
+    routing = jnp.concatenate([routing, jnp.zeros((n_experts, 128 - rows_own), jnp.float32)], 1)
+    if n_experts < tall:
+        routing = jnp.concatenate([routing, jnp.zeros((tall - n_experts, 128), jnp.float32)], 0)
     norms = norm_ref[...]
     norms = jnp.concatenate([norms, jnp.zeros((norms.shape[0], 128 - rows_own), jnp.float32)], 1)
     norms = jnp.concatenate([norms, jnp.zeros((tall - norms.shape[0], 128), jnp.float32)], 0)
     tail = jnp.concatenate(
-        [norms, routing[:tall], jnp.zeros((tall, width - 256), jnp.float32)], 1
+        [norms, routing, jnp.zeros((tall, width - 256), jnp.float32)], 1
     )
     block = jnp.concatenate([dense_ref[...].reshape(mats * rows_own, width), tail], 0)
     if block.shape[0] < depth:
@@ -797,10 +808,10 @@
 
     gathers = []
     gather_dense(
-        at, rows_own, mats, tall, land, gather_sems, gathers, beside_gather, lambda: shard_starts(range(early))
+        at, rows_own, mats, land, w_ref, gather_sems, gathers, beside_gather, lambda: shard_starts(range(early))
     )
     shard_starts(range(early, half))
-    assemble_dense(at, rows_own, mats, tall, land, w_ref, gain_ref, router_ref)
+    gather_small(at, rows_own, mats, tall, land, gain_ref, router_ref)
     w_copy = pltpu.make_async_copy(w_ref, w_keep, keep_sem.at[5])
     w_copy.start()
 
@@ -1143,7 +1154,7 @@
         ),
         cost_estimate=cost(120),
         name="forward",
-    )(lengths, lengths, slot_mask, picks.T, ranks, patches, dense, norms, routers, expert_in, expert_out)
+    )(lengths, lengths, slot_mask, picks.T, ranks, patches, dense, norms, routers.T, expert_in, expert_out)
 
 
 def chunk_at(index, half):
@@ -1344,16 +1355,16 @@
 def dense_backward_kernel(
     sizes, n_experts, images, padded, length_ref, mask_ref, patch_ref, x_zero_ref, a_one_ref, qkv_ref, att_ref,
     x_one_ref, a_two_ref, prob_ref, lse_ref, col_ref, w_ref, gain_ref, router_ref, back_ref, gate_ref,
-    pool_ref, imp_ref, third_ref, out_ref, grads, g_norm, d_qkv, d_atts, d_zeros, d_routers
+    pool_ref, imp_ref, third_ref, out_ref, grads, g_router, g_norm, d_qkv
 ):
     row = pl.program_id(0)
     span, width = x_zero_ref.shape
     mats, rows = grads.shape[0], width // (8 * sizes["g"] * sizes["x"])
 
-    here = pl.ds(pl.multiple_of(row * span, 16), span)
-
     @pl.when(row == 0)
     def _():
+        grads[...] = jnp.zeros_like(grads)
+        g_router[...] = jnp.zeros_like(g_router)
         g_norm[...] = third_ref[...]
 
     columns = col_ref[...]
@@ -1390,7 +1401,7 @@
     d_probs = d_probs + jnp.where(number == columns[:, 6:7], d_gate_two, 0.0)
     probs = prob_ref[...]
     d_router = (probs * (d_probs - jnp.sum(probs * d_probs, 1, keepdims=True))).astype(jnp.bfloat16)
-    d_routers[here] = d_router
+    g_router[...] += dot_f32(d_router, a_two_ref[...], TN)
     routers = router_ref[...].astype(jnp.bfloat16)
     if routers.shape[0] < 128:
         routers = jnp.concatenate(
@@ -1406,9 +1417,9 @@
         weight = jnp.where(image == place.astype(jnp.float32), pool, 0.0)
         d_x_one = d_x_one + weight * pool_ref[pl.ds(place, 1)]
     d_att = d_x_one.astype(jnp.bfloat16)
-    d_atts[here] = d_att
+    grads[4] += dot_f32(att_ref[...], d_att, TN)
     d_out = dot_f32(d_att, w_ref[4], NT).astype(jnp.bfloat16)
-    open_to = allowed_slots(length_ref, row, images, mask_ref[0], span)
+    open_to = allowed_slots(length_ref, row, images, mask_ref[pl.ds(row, 1)], span)
     logs = lse_ref[...]
     for pair in range(width // 128):
         query, key, value = (
@@ -1437,28 +1448,23 @@
             d_key = dot_f32(d_scores, query, TN) * 64**-0.5
             found.append((d_query, d_key, d_value))
         for part in range(3):
-            d_qkv[here, part * width + pair * 128 : part * width + (pair + 1) * 128] = jnp.where(
+            d_qkv[:, part * width + pair * 128 : part * width + (pair + 1) * 128] = jnp.where(
                 lane < 64, found[0][part], found[1][part]
             ).astype(jnp.bfloat16)
     d_a_one = None
     for part in range(3):
-        piece = d_qkv[here, part * width : (part + 1) * width]
+        piece = d_qkv[:, part * width : (part + 1) * width]
+        grads[1 + part] += dot_f32(a_one_ref[...], piece, TN)
         found = dot_f32(piece, w_ref[1 + part], NT)
         d_a_one = found if d_a_one is None else d_a_one + found
     scaled, scale = norm_parts(x_zero_ref[...])
     g_norm[0:1] += jnp.sum(d_a_one * scaled, 0, keepdims=True)
     g_norm[3:4] += jnp.sum(d_a_one, 0, keepdims=True)
     d_x_zero = norm_back(d_a_one, scaled, scale, gain_ref[0:1]) + d_x_one
-    d_zeros[here] = d_x_zero.astype(jnp.bfloat16)
+    grads[0] += dot_f32(patch_ref[...], d_x_zero.astype(jnp.bfloat16), TN)
 
     @pl.when(row == pl.num_programs(0) - 1)
     def _():
-        grads[0] = dot_f32(patch_ref[...], d_zeros[...], TN)
-        for part in range(3):
-            piece = d_qkv[:, part * width : (part + 1) * width]
-            grads[1 + part] = dot_f32(a_one_ref[...], piece, TN)
-        grads[4] = dot_f32(att_ref[...], d_atts[...], TN)
-        g_router = dot_f32(d_routers[...], a_two_ref[...], TN)
         Z, Y, X = QUAD, sizes["g"], sizes["x"]
         tall = max(8, n_experts)
         norms = g_norm[...]
@@ -1504,25 +1510,23 @@
             (2, QUAD, sizes["x"], sizes["g"], depth, width), jnp.bfloat16
         ),
         in_specs=[
-            whole(pltpu.SMEM), pl.BlockSpec((1, 1, span), lambda i: (i, 0, 0)), whole(),
-            block(width), whole(), block(3 * width), whole(), block(width), whole(),
+            whole(pltpu.SMEM), whole(), block(width),
+            block(width), block(width), block(3 * width), block(width), block(width), block(width),
             block(128), block(128), block(128),
         ]
         + [whole()] * 8,
         out_specs=whole(),
         scratch_shapes=[
             VMEM((mats, width, width), jnp.float32),
+            VMEM((128, width), jnp.float32),
             VMEM((8, width), jnp.float32),
-            VMEM((tokens, 3 * width), jnp.bfloat16),
-            VMEM((tokens, width), jnp.bfloat16),
-            VMEM((tokens, width), jnp.bfloat16),
-            VMEM((tokens, 128), jnp.bfloat16),
+            VMEM((span, 3 * width), jnp.bfloat16),
         ],
         compiler_params=pltpu.CompilerParams(vmem_limit_bytes=60 * MIB),
         cost_estimate=cost(50),
         name="dense_backward",
     )(
-        lengths, slot_mask[:, None, :], patches, x_zero, a_one, qkv, att, x_one, a_two, probs, logs, columns,
+        lengths, slot_mask, patches, x_zero, a_one, qkv, att, x_one, a_two, probs, logs, columns,
         weights, gains, routers, back, gates, pooled, importance, third,
     )
 

time: 477 us -> 482 us (1.010)
  local copies, waits for them, and re-layouts: 5.95 us -> 12.2 us
    unnamed x45 -> x62, local copies, waits for them, and re-layouts: 4.26 us -> 11.1 us
where the time goes in v11:
time: 482 us; the launch traced here: 478 us
  Pallas kernels  438 us (91%)
  other arithmetic  21 us (4%)
  local copies, waits for them, and re-layouts  12.2 us (3%)
  starting transfers between devices  5.47 us (1%)
    pallas_call x1, Pallas kernels, forward(): pl.pallas_call(functools.partial(forward_kernel, sizes, n_experts, length...  195 us
    pallas_call x1, Pallas kernels, expert_backward(): pl.pallas_call(functools.partial(expert_backward_kernel, sizes, padded),...  65.6 us
    pallas_call x1, Pallas kernels, scatter_dense(): pl.pallas_call(functools.partial(scatter_kernel, sizes), out_shape=(jax.S...  58.8 us
    pallas_call x1, Pallas kernels, dense_backward(): pl.pallas_call(functools.partial(dense_backward_kernel, sizes, n_experts,...  56.6 us
    pallas_call x1, Pallas kernels, head_step(): pl.pallas_call(functools.partial(head_kernel, sizes, images), out_shape=(...  47.9 us
    add x5, other arithmetic, adam_update(): polyak_decay * average_state + (1.0 - polyak_decay) * weight_new  20 us
    pallas_call x1, Pallas kernels, finish(): pl.pallas_call(functools.partial(finish_kernel, sizes, n_experts), out_sh...  14.4 us
    unnamed x62, local copies, waits for them, and re-layouts  11.1 us
  transfers between devices with their start and end apart: 4, of which 0 were waited for; matrix products, arithmetic and copies ran while one was open for 0% of the time, Pallas kernels for 24%

profile of v11, /device:TPU:0, one launch (start us, length us, event | category | flops | bytes accessed | tf_op | source)
XLA Modules:
  0.0 478.2 jit_solution(6098189372723991008)
XLA Ops:
  0.7 194.8 %forward.1 = (bf16[5,768,768]{2,1,0:T(8,128)(2,1)}, f32[8,768]{1,0:T(8,128)}, f32[8,768]{1,0:T(8,128)}, f32[1024,128]{1,0:T(8,128)}, f32[1024,768]{1,0:T(8,128)}...) custom-call(s32[4,3]{1,0:T(4,128)} %length_ref.3, ...), custom_call_target="tpu_custom_call" | custom-call | flops 138000007168 | tf_op jit(solution)/shard_map/forward/pallas_call | solution.py:1126
  195.5 1.2 copy-done.3
  196.7 1.0 copy-done.7
  197.7 0.8 copy-done.10
  198.5 0.7 copy-done.11
  199.2 0.7 copy-done.13
  200.0 47.9 %head_step.1 = (f32[576,768]{1,0:T(8,128)S(1)}, f32[8,16,768]{2,1,0:T(8,128)S(1)}, f32[16,768]{1,0:T(8,128)S(1)}, f32[8,768]{1,0:T(8,128)S(1)}, f32[8,128]{1,0:T(8,128)S(1)}, /*index=5*/f32[8,768]{1,0:T(8,128)S(1)}) custom-call(f32[8,16,768]{2,1,0:T(8,128)S(1)} %copy-done.7, f32[16,768]{1,0:T(8,128)S(1)} %copy-done.10, f32[8,768]{1,0:T(8,128)S(1)} %copy-done.13, ...), custom_call_target="tpu_custom_call" | custom-call | flops 48299999232 | tf_op jit(solution)/shard_map/head_step/pallas_call | solution.py:556
  247.9 1.2 copy-done.1
  249.7 0.7 copy-done.8
  250.4 0.6 copy-done.9
  251.6 65.6 %expert_backward.1 = (bf16[8,272,768]{2,1,0:T(8,128)(2,1)}, f32[8,8,384]{2,1,0:T(8,128)}, bf16[2,384,768]{2,1,0:T(8,128)(2,1)}, bf16[2,384,768]{2,1,0:T(8,128)(2...) custom-call(bf16[8,272,768]{2,1,0:T(8,128)(2,1)} %get-tuple-element.81.rows_ref, ...), custom_call_target="tpu_custom_call" | custom-call | flops 74750001152 | tf_op jit(solution)/shard_map/expert_backward/pallas_call | solution.py:1322
  317.3 1.9 collective-permute-start
  319.2 1.5 collective-permute-start.1
  320.7 1.5 collective-permute-start.2
  322.8 56.6 %dense_backward.1.g_ref = bf16[2,4,2,2,128,768]{5,4,3,2,1,0:T(8,128)(2,1)} custom-call(s32[4,3]{1,0:T(4,128)} %length_ref.3, s32[4,256]{1,0:T(4,128)} %mask_ref.3, bf16[1024,768]{1,0:T(8,128)(2,1)} %patch_ref.3, f32[1024,768]{1,0:T(8,128)} %get-tuple-element.70.x_zero_ref, bf16[1024,768]{1,0:T(8,128)(2,1)} %get-tuple-element.71.a_one_ref, ...), custom_call_target="tpu_custom_call" | custom-call | flops 57500000256 | tf_op jit(solution)/shard_map/dense_backward/pallas_call | solution.py:1506
  379.3 2.8 copy-done.6
  382.1 58.8 %scatter_dense.1 = (f32[128,768]{1,0:T(8,128)S(1)}, f32[8,128]{1,0:T(8,128)S(1)}) custom-call(bf16[2,4,2,2,128,768]{5,4,3,2,1,0:T(8,128)(2,1)S(1)} %copy-done.6), custom_call_target="tpu_custom_call" | custom-call | flops 51749998592 | tf_op jit(solution)/shard_map/scatter_dense/pallas_call | solution.py:314
  441.7 14.4 %finish.1 = (f32[2,384,768]{2,1,0:T(8,128)S(1)}, f32[2,384,768]{2,1,0:T(8,128)S(1)}, f32[8,128]{1,0:T(8,128)S(1)}) custom-call(f32[8,128]{1,0:T(8,128)S(1)} %get-tuple-element.69.head_ref, f32[8,128]{1,0:T(8,128)S(1)} %get-tuple-element.93.dense_ref, f32[8,768]{1,0:T(8,128)S(1)} %copy-done.5, bf16[2,384,768]{2,1,0:T(8,128)(2,1)S(1)} %collective-permute-done.refs_0_, ...), custom_call_target="tpu_custom_call" | custom-call | flops 11500000256 | tf_op jit(solution)/shard_map/finish/pallas_call | solution.py:394
  456.8 1.0 slice_multiply_fusion
  457.8 1.3 multiply_add_fusion.8
  459.1 1.3 multiply_add_fusion.10
  460.4 1.3 multiply_add_fusion.6
  461.8 4.8 %multiply_add_fusion.4 = (f32[576,768]{1,0:T(8,128)}, f32[576,768]{1,0:T(8,128)}, f32[576,768]{1,0:T(8,128)}, f32[576,768]{1,0:T(8,128)}) fusion(f32[576,768]{1,0:T(8,128)S(1)} %copy-done.16, f32[576,768]{1,0:T(8,128)S(1)} %copy-done, f32[576,768]{1,0:T(8,128)S(1)} %copy-done.2, f32[]{:T(128)} %bitcast.5, f32[576,768]{1,0:T(8,128)S(1)} %copy-done.17, ...), kind=kLoop, calls=%fused_computation.12 | loop fusion | flops 8404992 | bytes 15925252 | tf_op jit(solution)/shard_map/add | solution.py:43
  466.6 11.2 %multiply_add_fusion = (f32[2,384,768]{2,1,0:T(8,128)}, f32[2,384,768]{2,1,0:T(8,128)}, f32[2,384,768]{2,1,0:T(8,128)}, f32[2,384,768]{2,1,0:T(8,128)}, f32[2,38...) fusion(f32[2,384,768]{2,1,0:T(8,128)} %param.55, ...), kind=kLoop, calls=%fused_computation.5 | loop fusion | flops 22413312 | bytes 42467332 | tf_op jit(solution)/shard_map/add | solution.py:43
  (60 shorter events, 3.0 us)
Async XLA Ops:
  0.7 194.8 %copy-start = (f32[576,768]{1,0:T(8,128)S(1)}, f32[576,768]{1,0:T(8,128)}, u32[]{:S(2)}) copy-start(f32[576,768]{1,0:T(8,128)} %head_ref.1) | copy-start | bytes 5308420
  317.3 124.2 %collective-permute-start = (bf16[2,384,768]{2,1,0:T(8,128)(2,1)}, bf16[2,384,768]{2,1,0:T(8,128)(2,1)S(1)}, u32[]{:S(2)}, u32[]{:S(2)}) collective-permute-start(bf16[2,384,768]{2,1,0:T(8,128)(2,1)} %get-tuple-element.94), channel_id=1, source_target_pairs={{0,0},{8,1},{4,4},{12,5},{16,8},{24,9},{20,12},{28,13},{1,16},{9,1... | collective-permute-start | bytes 3538952 | tf_op jit(solution)/shard_map/ppermute | solution.py:1551
  319.2 122.3 %collective-permute-start.1 = (bf16[2,384,768]{2,1,0:T(8,128)(2,1)}, bf16[2,384,768]{2,1,0:T(8,128)(2,1)}, u32[]{:S(2)}, u32[]{:S(2)}) collective-permute-start(bf16[2,384,768]{2,1,0:T(8,128)(2,1)} %get-tuple-element.95), channel_id=1, source_target_pairs={{16,0},{24,1},{20,4},{28,5},{0,8},{8,9},{4,12},{12,13},{17,16},{25... | collective-permute-start | bytes 3538952 | tf_op jit(solution)/shard_map/ppermute | solution.py:1551
  320.7 120.8 %collective-permute-start.2 = (bf16[2,384,768]{2,1,0:T(8,128)(2,1)}, bf16[2,384,768]{2,1,0:T(8,128)(2,1)}, u32[]{:S(2)}, u32[]{:S(2)}) collective-permute-start(bf16[2,384,768]{2,1,0:T(8,128)(2,1)} %get-tuple-element.96), channel_id=1, source_target_pairs={{4,0},{12,1},{16,4},{24,5},{20,8},{28,9},{0,12},{8,13},{5,16},{13,... | collective-permute-start | bytes 3538952 | tf_op jit(solution)/shard_map/ppermute | solution.py:1551
  322.3 119.2 %collective-permute-start.3 = (bf16[2,384,768]{2,1,0:T(8,128)(2,1)}, bf16[2,384,768]{2,1,0:T(8,128)(2,1)}, u32[]{:S(2)}, u32[]{:S(2)}) collective-permute-start(bf16[2,384,768]{2,1,0:T(8,128)(2,1)} %get-tuple-element.97), channel_id=1, source_target_pairs={{20,0},{28,1},{0,4},{8,5},{4,8},{12,9},{16,12},{24,13},{21,16},{29... | collective-permute-start | bytes 3538952 | tf_op jit(solution)/shard_map/ppermute | solution.py:1551
  382.1 58.8 %copy-start.5 = (f32[8,768]{1,0:T(8,128)S(1)}, f32[8,768]{1,0:T(8,128)}, u32[]{:S(2)}) copy-start(f32[8,768]{1,0:T(8,128)} %copy-done.4) | copy-start | bytes 73732
  441.5 16.2 %copy-start.23 = (f32[6,24]{1,0:T(8,128)S(1)}, f32[6,24]{1,0:T(8,128)}, u32[]{:S(2)}) copy-start(f32[6,24]{1,0:T(8,128)} %norm_ref.1) | copy-start | bytes 1732
  441.5 16.2 %copy-start.24 = (f32[6,24]{1,0:T(8,128)S(1)}, f32[6,24]{1,0:T(8,128)}, u32[]{:S(2)}) copy-start(f32[6,24]{1,0:T(8,128)} %param.47) | copy-start | bytes 1732
  441.5 16.2 %copy-start.25 = (f32[6,24]{1,0:T(8,128)S(1)}, f32[6,24]{1,0:T(8,128)}, u32[]{:S(2)}) copy-start(f32[6,24]{1,0:T(8,128)} %param.45) | copy-start | bytes 1732
  441.6 16.2 %copy-start.26 = (f32[6,24]{1,0:T(8,128)S(1)}, f32[6,24]{1,0:T(8,128)}, u32[]{:S(2)}) copy-start(f32[6,24]{1,0:T(8,128)} %param.46) | copy-start | bytes 1732
  441.6 17.5 %copy-start.27 = (f32[24,8]{0,1:T(8,128)S(1)}, f32[24,8]{0,1:T(8,128)}, u32[]{:S(2)}) copy-start(f32[24,8]{0,1:T(8,128)} %param.40) | copy-start | bytes 2308
  441.6 17.5 %copy-start.28 = (f32[24,8]{0,1:T(8,128)S(1)}, f32[24,8]{0,1:T(8,128)}, u32[]{:S(2)}) copy-start(f32[24,8]{0,1:T(8,128)} %param.43) | copy-start | bytes 2308
  441.6 17.5 %copy-start.29 = (f32[24,8]{0,1:T(8,128)S(1)}, f32[24,8]{0,1:T(8,128)}, u32[]{:S(2)}) copy-start(f32[24,8]{0,1:T(8,128)} %param.41) | copy-start | bytes 2308
  441.6 17.5 %copy-start.30 = (f32[24,8]{0,1:T(8,128)S(1)}, f32[24,8]{0,1:T(8,128)}, u32[]{:S(2)}) copy-start(f32[24,8]{0,1:T(8,128)} %param.42) | copy-start | bytes 2308
  441.6 18.8 %copy-start.19 = (f32[5,24,768]{2,1,0:T(8,128)S(1)}, f32[5,24,768]{2,1,0:T(8,128)}, u32[]{:S(2)}) copy-start(f32[5,24,768]{2,1,0:T(8,128)} %dense_ref.1) | copy-start | bytes 1105924
  441.6 18.8 %copy-start.20 = (f32[5,24,768]{2,1,0:T(8,128)S(1)}, f32[5,24,768]{2,1,0:T(8,128)}, u32[]{:S(2)}) copy-start(f32[5,24,768]{2,1,0:T(8,128)} %param.39) | copy-start | bytes 1105924
  441.6 18.8 %copy-start.21 = (f32[5,24,768]{2,1,0:T(8,128)S(1)}, f32[5,24,768]{2,1,0:T(8,128)}, u32[]{:S(2)}) copy-start(f32[5,24,768]{2,1,0:T(8,128)} %param.37) | copy-start | bytes 1105924
  441.6 18.8 %copy-start.22 = (f32[5,24,768]{2,1,0:T(8,128)S(1)}, f32[5,24,768]{2,1,0:T(8,128)}, u32[]{:S(2)}) copy-start(f32[5,24,768]{2,1,0:T(8,128)} %param.38) | copy-start | bytes 1105924
  441.7 20.1 %copy-start.17 = (f32[576,768]{1,0:T(8,128)S(1)}, f32[576,768]{1,0:T(8,128)}, u32[]{:S(2)}) copy-start(f32[576,768]{1,0:T(8,128)} %param.57) | copy-start | bytes 5308420
  441.7 20.1 %copy-start.18 = (f32[576,768]{1,0:T(8,128)S(1)}, f32[576,768]{1,0:T(8,128)}, u32[]{:S(2)}) copy-start(f32[576,768]{1,0:T(8,128)} %param.58) | copy-start | bytes 5308420
  456.1 5.6 %copy-start.2 = (f32[576,768]{1,0:T(8,128)S(1)}, f32[576,768]{1,0:T(8,128)}, u32[]{:S(2)}) copy-start(f32[576,768]{1,0:T(8,128)} %copy-done.1) | copy-start | bytes 5308420
  456.2 5.6 %copy-start.16 = (f32[576,768]{1,0:T(8,128)S(1)}, f32[576,768]{1,0:T(8,128)}, u32[]{:S(2)}) copy-start(f32[576,768]{1,0:T(8,128)} %param.59) | copy-start | bytes 5308420
  461.8 4.9 %copy-start.14 = (f32[2,384,768]{2,1,0:T(8,128)S(1)}, f32[2,384,768]{2,1,0:T(8,128)}, u32[]{:S(2)}) copy-start(f32[2,384,768]{2,1,0:T(8,128)} %in_ref.1) | copy-start | bytes 7077892
  461.8 4.9 %copy-start.15 = (f32[2,384,768]{2,1,0:T(8,128)S(1)}, f32[2,384,768]{2,1,0:T(8,128)}, u32[]{:S(2)}) copy-start(f32[2,384,768]{2,1,0:T(8,128)} %out_ref.1) | copy-start | bytes 7077892
  (11 other events, 11.0 us)

commit v12 on v11

--- a/solution.py
+++ b/solution.py
@@ -579,7 +579,7 @@
         + [by_member, by_member, by_chip, by_chip, dma((2,)), dma((2,)), by_chip, by_chip]
         + [by_member, by_member],
         compiler_params=pltpu.CompilerParams(
-            collective_id=4, has_side_effects=True, vmem_limit_bytes=(56 if wide > 1024 else 28) * MIB
+            collective_id=4, has_side_effects=True, vmem_limit_bytes=56 * MIB
         ),
         cost_estimate=cost(42),
         name="head_step",
@@ -716,7 +716,7 @@
     at = Place(sizes)
     team = Team(at)
     half = weights.shape[1]
-    early = half // 2
+    early, middle = half // 2, half * 3 // 4
     rows_here, span = mask_ref.shape
     width = patch_ref.shape[1]
     tokens = rows_here * span
@@ -810,7 +810,7 @@
     gather_dense(
         at, rows_own, mats, land, w_ref, gather_sems, gathers, beside_gather, lambda: shard_starts(range(early))
     )
-    shard_starts(range(early, half))
+    shard_starts(range(early, middle))
     gather_small(at, rows_own, mats, tall, land, gain_ref, router_ref)
     w_copy = pltpu.make_async_copy(w_ref, w_keep, keep_sem.at[5])
     w_copy.start()
@@ -1004,6 +1004,10 @@
                 def _():
                     row_copy(source, source).wait_recv()
                     detail_copy(source, source).wait_recv()
+
+        @pl.when(index == 0)
+        def _():
+            shard_starts(range(middle, half))
 
         @pl.when(index == rounds)
         def _():

time: 482 us -> 472 us (0.979)
  local copies, waits for them, and re-layouts: 12.2 us -> 5.14 us
    unnamed x62 -> x48, local copies, waits for them, and re-layouts: 11.1 us -> 4.11 us
  transfers between devices with their start and end apart: 4 -> 4, of which waited for: 0 -> 0; matrix products, arithmetic and copies ran while one was open for 0% -> 0% of each run, Pallas kernels for 24% -> 25%
where the time goes in v12:
time: 472 us; the launch traced here: 469 us
  Pallas kernels  437 us (93%)
  other arithmetic  20.1 us (4%)
  starting transfers between devices  5.47 us (1%)
  local copies, waits for them, and re-layouts  5.14 us (1%)
    pallas_call x1, Pallas kernels, forward(): pl.pallas_call(functools.partial(forward_kernel, sizes, n_experts, length...  193 us
    pallas_call x1, Pallas kernels, expert_backward(): pl.pallas_call(functools.partial(expert_backward_kernel, sizes, padded),...  66.8 us
    pallas_call x1, Pallas kernels, scatter_dense(): pl.pallas_call(functools.partial(scatter_kernel, sizes), out_shape=(jax.S...  58.7 us
    pallas_call x1, Pallas kernels, dense_backward(): pl.pallas_call(functools.partial(dense_backward_kernel, sizes, n_experts,...  56.6 us
    pallas_call x1, Pallas kernels, head_step(): pl.pallas_call(functools.partial(head_kernel, sizes, images), out_shape=(...  49.3 us
    add x5, other arithmetic, adam_update(): polyak_decay * average_state + (1.0 - polyak_decay) * weight_new  19.2 us
    pallas_call x1, Pallas kernels, finish(): pl.pallas_call(functools.partial(finish_kernel, sizes, n_experts), out_sh...  12.8 us
  transfers between devices with their start and end apart: 4, of which 0 were waited for; matrix products, arithmetic and copies ran while one was open for 0% of the time, Pallas kernels for 25%

profile of v12, /device:TPU:0, one launch (start us, length us, event | category | flops | bytes accessed | tf_op | source)
XLA Modules:
  0.0 469.1 jit_solution(15250298818254857827)
XLA Ops:
  0.7 193.0 %forward.1 = (bf16[5,768,768]{2,1,0:T(8,128)(2,1)}, f32[8,768]{1,0:T(8,128)}, f32[8,768]{1,0:T(8,128)}, f32[1024,128]{1,0:T(8,128)}, f32[1024,768]{1,0:T(8,128)}...) custom-call(s32[4,3]{1,0:T(4,128)} %length_ref.3, ...), custom_call_target="tpu_custom_call" | custom-call | flops 138000007168 | tf_op jit(solution)/shard_map/forward/pallas_call | solution.py:1130
  193.6 49.3 %head_step.1 = (f32[576,768]{1,0:T(8,128)}, f32[8,16,768]{2,1,0:T(8,128)}, f32[16,768]{1,0:T(8,128)}, f32[8,768]{1,0:T(8,128)}, f32[8,128]{1,0:T(8,128)}, /*index=5*/f32[8,768]{1,0:T(8,128)}) custom-call(f32[8,16,768]{2,1,0:T(8,128)} %get-tuple-element.65.part_ref, f32[16,768]{1,0:T(8,128)} %get-tuple-element.66.own_ref, ...), custom_call_target="tpu_custom_call" | custom-call | flops 48299999232 | tf_op jit(solution)/shard_map/head_step/pallas_call | solution.py:556
  243.0 66.8 %expert_backward.1 = (bf16[8,272,768]{2,1,0:T(8,128)(2,1)}, f32[8,8,384]{2,1,0:T(8,128)}, bf16[2,384,768]{2,1,0:T(8,128)(2,1)}, bf16[2,384,768]{2,1,0:T(8,128)(2...) custom-call(bf16[8,272,768]{2,1,0:T(8,128)(2,1)} %get-tuple-element.81.rows_ref, ...), custom_call_target="tpu_custom_call" | custom-call | flops 74750001152 | tf_op jit(solution)/shard_map/expert_backward/pallas_call | solution.py:1326
  309.8 1.9 collective-permute-start
  311.7 1.5 collective-permute-start.1
  313.2 1.7 collective-permute-start.2
  315.0 0.3 collective-permute-start.3
  315.3 56.6 %dense_backward.1.g_ref = bf16[2,4,2,2,128,768]{5,4,3,2,1,0:T(8,128)(2,1)} custom-call(s32[4,3]{1,0:T(4,128)} %length_ref.3, s32[4,256]{1,0:T(4,128)} %mask_ref.3, bf16[1024,768]{1,0:T(8,128)(2,1)} %patch_ref.3, f32[1024,768]{1,0:T(8,128)} %get-tuple-element.70.x_zero_ref, bf16[1024,768]{1,0:T(8,128)(2,1)} %get-tuple-element.71.a_one_ref, ...), custom_call_target="tpu_custom_call" | custom-call | flops 57500000256 | tf_op jit(solution)/shard_map/dense_backward/pallas_call | solution.py:1510
  371.9 2.8 copy-done.1
  374.6 58.7 %scatter_dense.1 = (f32[128,768]{1,0:T(8,128)S(1)}, f32[8,128]{1,0:T(8,128)S(1)}) custom-call(bf16[2,4,2,2,128,768]{5,4,3,2,1,0:T(8,128)(2,1)S(1)} %copy-done.1), custom_call_target="tpu_custom_call" | custom-call | flops 51749998592 | tf_op jit(solution)/shard_map/scatter_dense/pallas_call | solution.py:314
  433.3 0.5 slice_bitcast_fusion
  433.9 0.0 copy-start.16
  433.9 0.0 copy-start.19
  433.9 0.0 copy-start.20
  433.9 0.0 copy-start.23
  434.0 12.8 %finish.1 = (f32[2,384,768]{2,1,0:T(8,128)S(1)}, f32[2,384,768]{2,1,0:T(8,128)S(1)}, f32[8,128]{1,0:T(8,128)S(1)}) custom-call(f32[8,128]{1,0:T(8,128)S(1)} %copy-done.2, f32[8,128]{1,0:T(8,128)S(1)} %get-tuple-element.93.dense_ref, f32[8,768]{1,0:T(8,128)S(1)} %copy-done, bf16[2,384,768]{2,1,0:T(8,128)(2,1)S(1)} %collective-permute-done.refs_0_, ...), custom_call_target="tpu_custom_call" | custom-call | flops 11500000256 | tf_op jit(solution)/shard_map/finish/pallas_call | solution.py:394
  446.8 0.5 fusion.14
  447.4 0.9 slice_multiply_fusion
  448.3 1.2 multiply_add_fusion.8
  449.5 1.2 multiply_add_fusion.10
  450.7 1.3 multiply_add_fusion.6
  452.1 5.1 %multiply_add_fusion.4 = (f32[576,768]{1,0:T(8,128)}, f32[576,768]{1,0:T(8,128)}, f32[576,768]{1,0:T(8,128)}, f32[576,768]{1,0:T(8,128)}) fusion(f32[576,768]{1,0:T(8,128)S(1)} %copy-done.8, f32[576,768]{1,0:T(8,128)S(1)} %copy-done.7, f32[576,768]{1,0:T(8,128)S(1)} %copy-done.11, f32[]{:T(128)} %bitcast.5, f32[576,768]{1,0:T(8,128)S(1)} %copy-done.9, ...), kind=kLoop, calls=%fused_computation.12 | loop fusion | flops 8404992 | bytes 15925252 | tf_op jit(solution)/shard_map/add | solution.py:43
  457.2 1.2 copy-done.6
  458.4 10.4 %multiply_add_fusion = (f32[2,384,768]{2,1,0:T(8,128)}, f32[2,384,768]{2,1,0:T(8,128)}, f32[2,384,768]{2,1,0:T(8,128)}, f32[2,384,768]{2,1,0:T(8,128)}, f32[2,38...) fusion(f32[2,384,768]{2,1,0:T(8,128)S(1)} %copy-done.5, ...), kind=kLoop, calls=%fused_computation.5 | loop fusion | flops 22413312 | bytes 42467332 | tf_op jit(solution)/shard_map/add | solution.py:43
  (46 shorter events, 0.1 us)
Async XLA Ops:
  309.8 124.0 %collective-permute-start = (bf16[2,384,768]{2,1,0:T(8,128)(2,1)}, bf16[2,384,768]{2,1,0:T(8,128)(2,1)S(1)}, u32[]{:S(2)}, u32[]{:S(2)}) collective-permute-start(bf16[2,384,768]{2,1,0:T(8,128)(2,1)} %get-tuple-element.94), channel_id=1, source_target_pairs={{0,0},{8,1},{4,4},{12,5},{16,8},{24,9},{20,12},{28,13},{1,16},{9,1... | collective-permute-start | bytes 3538952 | tf_op jit(solution)/shard_map/ppermute | solution.py:1555
  311.7 122.1 %collective-permute-start.1 = (bf16[2,384,768]{2,1,0:T(8,128)(2,1)}, bf16[2,384,768]{2,1,0:T(8,128)(2,1)S(1)}, u32[]{:S(2)}, u32[]{:S(2)}) collective-permute-start(bf16[2,384,768]{2,1,0:T(8,128)(2,1)} %get-tuple-element.95), channel_id=1, source_target_pairs={{16,0},{24,1},{20,4},{28,5},{0,8},{8,9},{4,12},{12,13},{17,16},{25... | collective-permute-start | bytes 3538952 | tf_op jit(solution)/shard_map/ppermute | solution.py:1555
  313.2 120.6 %collective-permute-start.2 = (bf16[2,384,768]{2,1,0:T(8,128)(2,1)}, bf16[2,384,768]{2,1,0:T(8,128)(2,1)S(1)}, u32[]{:S(2)}, u32[]{:S(2)}) collective-permute-start(bf16[2,384,768]{2,1,0:T(8,128)(2,1)} %get-tuple-element.96), channel_id=1, source_target_pairs={{4,0},{12,1},{16,4},{24,5},{20,8},{28,9},{0,12},{8,13},{5,16},{13,... | collective-permute-start | bytes 3538952 | tf_op jit(solution)/shard_map/ppermute | solution.py:1555
  315.0 118.9 %collective-permute-start.3 = (bf16[2,384,768]{2,1,0:T(8,128)(2,1)}, bf16[2,384,768]{2,1,0:T(8,128)(2,1)}, u32[]{:S(2)}, u32[]{:S(2)}) collective-permute-start(bf16[2,384,768]{2,1,0:T(8,128)(2,1)} %get-tuple-element.97), channel_id=1, source_target_pairs={{20,0},{28,1},{0,4},{8,5},{4,8},{12,9},{16,12},{24,13},{21,16},{29... | collective-permute-start | bytes 3538952 | tf_op jit(solution)/shard_map/ppermute | solution.py:1555
  374.6 58.7 %copy-start = (f32[8,768]{1,0:T(8,128)S(1)}, f32[8,768]{1,0:T(8,128)}, u32[]{:S(2)}) copy-start(f32[8,768]{1,0:T(8,128)} %get-tuple-element.91.imp_ref) | copy-start | bytes 73732
  374.6 59.2 %copy-start.2 = (f32[8,128]{1,0:T(8,128)S(1)}, f32[8,128]{1,0:T(8,128)}, u32[]{:S(2)}) copy-start(f32[8,128]{1,0:T(8,128)} %get-tuple-element.69.head_ref) | copy-start | bytes 12292
  433.9 14.4 %copy-start.16 = (f32[6,24]{1,0:T(8,128)S(1)}, f32[6,24]{1,0:T(8,128)}, u32[]{:S(2)}) copy-start(f32[6,24]{1,0:T(8,128)} %norm_ref.1) | copy-start | bytes 1732
  433.9 14.4 %copy-start.17 = (f32[6,24]{1,0:T(8,128)S(1)}, f32[6,24]{1,0:T(8,128)}, u32[]{:S(2)}) copy-start(f32[6,24]{1,0:T(8,128)} %param.47) | copy-start | bytes 1732
  433.9 14.4 %copy-start.18 = (f32[6,24]{1,0:T(8,128)S(1)}, f32[6,24]{1,0:T(8,128)}, u32[]{:S(2)}) copy-start(f32[6,24]{1,0:T(8,128)} %param.45) | copy-start | bytes 1732
  433.9 14.4 %copy-start.19 = (f32[6,24]{1,0:T(8,128)S(1)}, f32[6,24]{1,0:T(8,128)}, u32[]{:S(2)}) copy-start(f32[6,24]{1,0:T(8,128)} %param.46) | copy-start | bytes 1732
  433.9 15.6 %copy-start.20 = (f32[24,8]{0,1:T(8,128)S(1)}, f32[24,8]{0,1:T(8,128)}, u32[]{:S(2)}) copy-start(f32[24,8]{0,1:T(8,128)} %param.40) | copy-start | bytes 2308
  433.9 15.5 %copy-start.21 = (f32[24,8]{0,1:T(8,128)S(1)}, f32[24,8]{0,1:T(8,128)}, u32[]{:S(2)}) copy-start(f32[24,8]{0,1:T(8,128)} %param.43) | copy-start | bytes 2308
  433.9 15.5 %copy-start.22 = (f32[24,8]{0,1:T(8,128)S(1)}, f32[24,8]{0,1:T(8,128)}, u32[]{:S(2)}) copy-start(f32[24,8]{0,1:T(8,128)} %param.41) | copy-start | bytes 2308
  433.9 15.5 %copy-start.23 = (f32[24,8]{0,1:T(8,128)S(1)}, f32[24,8]{0,1:T(8,128)}, u32[]{:S(2)}) copy-start(f32[24,8]{0,1:T(8,128)} %param.42) | copy-start | bytes 2308
  434.0 16.7 %copy-start.12 = (f32[5,24,768]{2,1,0:T(8,128)S(1)}, f32[5,24,768]{2,1,0:T(8,128)}, u32[]{:S(2)}) copy-start(f32[5,24,768]{2,1,0:T(8,128)} %dense_ref.1) | copy-start | bytes 1105924
  434.0 16.7 %copy-start.13 = (f32[5,24,768]{2,1,0:T(8,128)S(1)}, f32[5,24,768]{2,1,0:T(8,128)}, u32[]{:S(2)}) copy-start(f32[5,24,768]{2,1,0:T(8,128)} %param.39) | copy-start | bytes 1105924
  434.0 16.7 %copy-start.14 = (f32[5,24,768]{2,1,0:T(8,128)S(1)}, f32[5,24,768]{2,1,0:T(8,128)}, u32[]{:S(2)}) copy-start(f32[5,24,768]{2,1,0:T(8,128)} %param.37) | copy-start | bytes 1105924
  434.0 16.7 %copy-start.15 = (f32[5,24,768]{2,1,0:T(8,128)S(1)}, f32[5,24,768]{2,1,0:T(8,128)}, u32[]{:S(2)}) copy-start(f32[5,24,768]{2,1,0:T(8,128)} %param.38) | copy-start | bytes 1105924
  434.0 18.0 %copy-start.9 = (f32[576,768]{1,0:T(8,128)S(1)}, f32[576,768]{1,0:T(8,128)}, u32[]{:S(2)}) copy-start(f32[576,768]{1,0:T(8,128)} %param.57) | copy-start | bytes 5308420
  434.0 18.0 %copy-start.10 = (f32[576,768]{1,0:T(8,128)S(1)}, f32[576,768]{1,0:T(8,128)}, u32[]{:S(2)}) copy-start(f32[576,768]{1,0:T(8,128)} %param.58) | copy-start | bytes 5308420
  434.0 18.0 %copy-start.11 = (f32[576,768]{1,0:T(8,128)S(1)}, f32[576,768]{1,0:T(8,128)}, u32[]{:S(2)}) copy-start(f32[576,768]{1,0:T(8,128)} %get-tuple-element.102) | copy-start | bytes 5308420
  446.8 5.2 %copy-start.7 = (f32[576,768]{1,0:T(8,128)S(1)}, f32[576,768]{1,0:T(8,128)}, u32[]{:S(2)}) copy-start(f32[576,768]{1,0:T(8,128)} %head_ref.1) | copy-start | bytes 5308420
  446.8 5.2 %copy-start.8 = (f32[576,768]{1,0:T(8,128)S(1)}, f32[576,768]{1,0:T(8,128)}, u32[]{:S(2)}) copy-start(f32[576,768]{1,0:T(8,128)} %param.59) | copy-start | bytes 5308420
  452.1 6.3 %copy-start.6 = (f32[2,384,768]{2,1,0:T(8,128)S(1)}, f32[2,384,768]{2,1,0:T(8,128)}, u32[]{:S(2)}) copy-start(f32[2,384,768]{2,1,0:T(8,128)} %param.53) | copy-start | bytes 7077892
  (4 other events, 18.2 us)
